TPU v7x, 32 devices: a whole 2x2x4 slice. The times are simulated.
32 devices in a mesh: leaf: 4 (over y, core), blk: 8 (over z, x).
Axes of the slice: x: 2, y: 2, z: 4, core: 2. Of those that a mesh axis runs over, the one named last changes fastest.
Arguments:
- ln_rate: float32 [16384], P(('leaf', 'blk')), may hold values from -1 to 0.5
- log_state: float32 [16384], P(('leaf', 'blk')), may hold values from -1 to 1
- sigma: float32 [16384], P(('leaf', 'blk')), may hold values from 40 to 120
- fric_a: float32 [16384], P(('leaf', 'blk')), may hold values from 0.005 to 0.015
- fric_b: float32 [16384], P(('leaf', 'blk')), may hold values from 0.006 to 0.02
- slip_dist: float32 [16384], P(('leaf', 'blk')), may hold values from 1 to 4
- leaf_of_elem: int32 [16384], P(('leaf', 'blk')), may hold values from 0 to 16383, as said below
- near_blocks: bfloat16 [96, 512, 512], P(('leaf', 'blk')), may hold values from -0.25 to 0.25
- near_col: int32 [96], P(('leaf', 'blk')), may hold values from 0 to 7, as said below
- near_count: int32 [32], P(('leaf', 'blk')), may hold values from 1 to 3, as said below
- far_u: bfloat16 [128, 16, 512], P(('leaf', 'blk')), may hold values from -0.75 to 0.75
- far_v: bfloat16 [128, 16, 512], P(('leaf', 'blk')), may hold values from -0.25 to 0.25
- far_col: int32 [128], P(('leaf', 'blk')), may hold values from 0 to 7
- far_rank: int32 [128], P(('leaf', 'blk')), may hold values from 4 to 16, as said below
- coarse_u: bfloat16 [4, 16, 16384], P(None, None, ('leaf', 'blk')), may hold values from -0.75 to 0.75
- coarse_v: bfloat16 [4, 16, 16384], P(None, None, ('leaf', 'blk')), may hold values from -0.09375 to 0.09375
Outputs:
- ln_rate_next: float32 [16384], P(('leaf', 'blk'))
- log_state_next: float32 [16384], P(('leaf', 'blk'))
Inputs may be any that keep to these rules, and one draw needn't show every extreme that they name: `leaf_of_elem`: A bijection; an element's leaf-order row lies in the group of the element's own device, and the rows owned by one device take exactly 64 elements from each device of that group. `near_col`: within two blocks of the slot's row block; equal to it in a device's first 1 slots. Slots of a device from position near_count on hold no block. In every group some device has all 3 slots live. `far_rank`: every device has a block of rank 16.
All inputs are finite; a program needn't handle non-finite values.
Results may differ from a plain program's by a relative error of at most 0.00076.
Values may be sent and summed in bfloat16 or wider, within the bound.
No kernel may reach another device: no remote copies, remote signals or barrier semaphores. Data moves between devices by JAX's collectives and lax.ppermute only.
A program may use at most 64 MiB of HBM per device.

v0:
```python
import jax
import jax.numpy as jnp
from jax import lax
from jax.sharding import PartitionSpec as P

DAMPING = 0.5
PLATE_RATE = 1.0
TIME_STEP = 0.2


def near_products(leaf_deficit, near_blocks, near_col, near_count, group_blocks, blocks_mine):
    leaf_size = near_blocks.shape[1]
    slot_count = near_blocks.shape[0]
    blocks = leaf_deficit.reshape(group_blocks, leaf_size)
    sources = blocks[near_col]
    products = jnp.einsum("sij,sj->si", near_blocks, sources, preferred_element_type=jnp.float32)
    slot_index = jnp.arange(slot_count, dtype=jnp.int32)
    live_slots = slot_index < near_count[0]
    products = jnp.where(live_slots[:, None], products, 0.0)
    return (
        jnp.zeros((blocks_mine, leaf_size), jnp.float32).at[slot_index % blocks_mine].add(products)
    )


def far_products(leaf_deficit, far_u, far_v, far_col, far_rank, group_blocks, blocks_mine):
    leaf_size = far_u.shape[2]
    rank_top = far_u.shape[1]
    sources = leaf_deficit.reshape(group_blocks, leaf_size)[far_col]
    project = jnp.einsum("srj,sj->sr", far_v, sources, preferred_element_type=jnp.float32)
    kept_ranks = jnp.arange(rank_top, dtype=jnp.int32)[None, :] < far_rank[:, None]
    project = jnp.where(kept_ranks, project, 0.0).astype(jnp.bfloat16)
    values = jnp.einsum("sr,srj->sj", project, far_u, preferred_element_type=jnp.float32)
    return values.reshape(blocks_mine, -1, leaf_size).sum(axis=1)


def coarse_partial(own_deficit, coarse_v, group_index):
    partial_value = jnp.einsum(
        "grq,q->gr", coarse_v, own_deficit, preferred_element_type=jnp.float32
    )
    foreign = jnp.arange(coarse_v.shape[0], dtype=jnp.int32) != group_index
    return jnp.where(foreign[:, None], partial_value, 0.0)


def body(
    ln_rate,
    log_state,
    sigma,
    fric_a,
    fric_b,
    slip_dist,
    leaf_of_elem,
    near_blocks,
    near_col,
    near_count,
    far_u,
    far_v,
    far_col,
    far_rank,
    coarse_u,
    coarse_v,
):
    members = lax.axis_size("blk")
    group_index = lax.axis_index("leaf")
    elem_count = ln_rate.shape[0]
    leaf_size = near_blocks.shape[1]
    blocks_mine = elem_count // leaf_size
    group_blocks = members * blocks_mine
    group_rows = group_blocks * leaf_size
    group_local = leaf_of_elem - group_index * group_rows
    peer_rows = elem_count // members
    target = group_local // elem_count
    target_row = group_local % elem_count
    onehot = (target[:, None] == jnp.arange(members, dtype=jnp.int32)[None, :]).astype(jnp.int32)
    earlier = jnp.cumsum(onehot, axis=0) - onehot
    rank_within = jnp.sum(earlier * onehot, axis=1)
    slot_index = target * peer_rows + rank_within
    sent_rows = (
        jnp.zeros((elem_count,), jnp.int32)
        .at[slot_index]
        .set(target_row)
        .reshape(members, peer_rows)
    )

    def coarse_coefficients(partial_value):
        summed = lax.psum(partial_value, "blk")
        return lax.all_to_all(
            summed.astype(jnp.bfloat16), "leaf", split_axis=0, concat_axis=0, tiled=True
        )

    def stress_rates(deficit):
        sent_values = (
            jnp.zeros((elem_count,), jnp.bfloat16)
            .at[slot_index]
            .set(deficit)
            .reshape(members, peer_rows)
        )
        got_values, got_rows = (
            lax.all_to_all(sent_values, "blk", split_axis=0, concat_axis=0, tiled=True),
            lax.all_to_all(sent_rows, "blk", split_axis=0, concat_axis=0, tiled=True),
        )
        own_deficit = (
            jnp.zeros((elem_count,), jnp.bfloat16)
            .at[got_rows.reshape(-1)]
            .set(got_values.reshape(-1))
        )
        leaf_deficit = lax.all_gather(own_deficit, "blk", axis=0, tiled=True)
        coefficients = coarse_coefficients(coarse_partial(own_deficit, coarse_v, group_index))
        own_rows = far_products(
            leaf_deficit, far_u, far_v, far_col, far_rank, group_blocks, blocks_mine
        )
        own_rows = own_rows + near_products(
            leaf_deficit, near_blocks, near_col, near_count, group_blocks, blocks_mine
        )
        coarse_rows = jnp.einsum(
            "hrp,hr->p", coarse_u, coefficients, preferred_element_type=jnp.float32
        )
        leaf_totals = own_rows.reshape(-1) + coarse_rows
        returned = lax.all_to_all(
            leaf_totals[got_rows], "blk", split_axis=0, concat_axis=0, tiled=True
        )
        return returned.reshape(-1)[slot_index]

    def derivatives(ln_now, state_now):
        velocity = jnp.exp(ln_now)
        stress_rate = stress_rates((PLATE_RATE - velocity).astype(jnp.bfloat16))
        state_rate = (jnp.exp(-state_now) - velocity) / slip_dist
        log_rate = (stress_rate - sigma * fric_b * state_rate) / (
            sigma * fric_a + DAMPING * velocity
        )
        return (log_rate, state_rate)

    first_ln, first_state = derivatives(ln_rate, log_state)
    second_ln, second_state = derivatives(
        ln_rate + TIME_STEP * first_ln, log_state + TIME_STEP * first_state
    )
    ln_rate_next = ln_rate + 0.5 * TIME_STEP * (first_ln + second_ln)
    log_state_next = log_state + 0.5 * TIME_STEP * (first_state + second_state)
    return (ln_rate_next, log_state_next)


def solution(mesh):
    in_specs = (
        P(("leaf", "blk")),
        P(("leaf", "blk")),
        P(("leaf", "blk")),
        P(("leaf", "blk")),
        P(("leaf", "blk")),
        P(("leaf", "blk")),
        P(("leaf", "blk")),
        P(("leaf", "blk"), None, None),
        P(("leaf", "blk")),
        P(("leaf", "blk")),
        P(("leaf", "blk"), None, None),
        P(("leaf", "blk"), None, None),
        P(("leaf", "blk")),
        P(("leaf", "blk")),
        P(None, None, ("leaf", "blk")),
        P(None, None, ("leaf", "blk")),
    )
    out_specs = (P(("leaf", "blk")), P(("leaf", "blk")))
    return jax.shard_map(body, mesh=mesh, in_specs=in_specs, out_specs=out_specs, check_vma=False)
```

profile of v0, /device:TPU:0, one launch (start us, length us, event | category | flops | bytes accessed | tf_op | source)
XLA Modules:
  0.0 198.3 jit_solution(1611504463744347669)
XLA Ops:
  3.7 3.8 %scatter_custom_fusion.1 = bf16[512]{0:T(512)(128)(2,1)S(1)} fusion(s32[512]{0:T(512)S(1)} %compare_select_fusion.2, bf16[512]{0:T(512)(128)(2,1)S(1)} %subtract_convert_fusion.1, bf16[]{:T(256)} %constant.66.clone.1), kind=kCustom, calls=%fused_computation.95 | custom fusion | bytes 1026 | tf_op jit(solution)/shard_map/scatter | solution.py:94
  8.2 7.3 %all-to-all-start.1 = ((bf16[8,1,64]{2,1,0:T(2,128)(2,1)}), bf16[8,1,64]{2,1,0:T(2,128)(2,1)S(1)}, u32[]{:S(2)}, u32[]{:S(2)}) async-start(bf16[8,1,64]{2,1,0:T(2,128)(2,1)} %all_to_all.66), calls=%async_computation.1 | async-start | bytes 8192 | tf_op jit(solution)/shard_map/all_to_all | solution.py:98
  16.8 2.4 %scatter_custom_fusion = s32[512]{0:T(512)S(1)} fusion(s32[512]{0:T(512)S(1)} %compare_select_fusion.2, s32[512]{0:T(512)S(1)} %get-tuple-element.6, s32[]{:T(128)} %constant.67.clone.1), kind=kCustom, calls=%fused_computation.84 | custom fusion | bytes 2052 | tf_op jit(solution)/shard_map/scatter | solution.py:80
  21.9 4.7 %all-to-all-start = ((s32[8,1,64]{2,1,0:T(1,128)}), s32[8,1,64]{2,1,0:T(1,128)S(1)}, u32[]{:S(2)}, u32[]{:S(2)}) async-start(s32[8,1,64]{2,1,0:T(1,128)} %all_to_all.49), calls=%async_computation | async-start | bytes 8192 | tf_op jit(solution)/shard_map/all_to_all | solution.py:99
  26.7 6.3 %all-to-all-done = s32[8,1,64]{2,1,0:T(1,128)S(1)} async-done(((s32[8,1,64]{2,1,0:T(1,128)}), s32[8,1,64]{2,1,0:T(1,128)S(1)}, u32[]{:S(2)}, u32[]{:S(2)}) %all-to-all-start) | async-done | bytes 2080 | tf_op jit(solution)/shard_map/all_to_all | solution.py:99
  34.3 3.8 %scatter_custom_fusion.2 = bf16[512]{0:T(512)(128)(2,1)S(1)} fusion(s32[512]{0:T(512)S(1)} %bitcast.97, bf16[512]{0:T(512)(128)(2,1)S(1)} %reshape.242, bf16[]{:T(256)} %constant.66.clone.1), kind=kCustom, calls=%fused_computation.93 | custom fusion | bytes 1026 | tf_op jit(solution)/shard_map/scatter | solution.py:104
  38.1 26.0 %all-gather = bf16[8,1,512]{2,1,0:T(2,128)(2,1)S(1)} all-gather(bf16[1,1,512]{2,1,0:T(2,128)(2,1)S(1)} %reshape.299), channel_id=1, replica_groups=mesh['leaf'=4,'blk'=8] {'blk'}, dimensions={0}, use_global_device_ids=true | all-gather | bytes 9216 | tf_op jit(solution)/shard_map/all_gather | solution.py:106
  66.3 17.1 %psum.14 = bf16[4,16]{1,0:T(4,128)(2,1)S(1)} all-reduce(f32[4,16]{1,0:T(4,128)S(1)} %broadcast_select_fusion.1), channel_id=1, replica_groups=mesh['leaf'=4,'blk'=8] {'blk'}, use_global_device_ids=true, to_apply=%region_7.8 | all-reduce | flops 64 | bytes 384 | tf_op jit(solution)/shard_map/psum | solution.py:85
  84.0 3.2 %all-to-all-start.2 = ((bf16[4,1,16]{2,1,0:T(2,128)(2,1)}), bf16[4,1,16]{2,1,0:T(2,128)(2,1)S(1)}, u32[]{:S(2)}, u32[]{:S(2)}) async-start(bf16[4,1,16]{2,1,0:T(2,128)(2,1)} %copy.23), calls=%async_computation.2 | async-start | bytes 4096 | tf_op jit(solution)/shard_map/all_to_all | solution.py:86
  89.0 1.9 all-to-all-done.2
  91.1 3.5 %gather_fusion.2 = f32[512]{0:T(512)S(1)} fusion(f32[512]{0:T(512)S(1)} %add.107, s32[1024]{0:T(1024)S(1)} %pad_clamp_fusion.1), kind=kCustom, calls=%fused_computation.2 | custom fusion | bytes 6144 | tf_op jit(solution)/shard_map/gather | solution.py:119
  95.3 3.5 %all-to-all-start.3 = ((f32[8,1,64]{2,1,0:T(1,128)}), f32[8,1,64]{2,1,0:T(1,128)S(1)}, u32[]{:S(2)}, u32[]{:S(2)}) async-start(f32[8,1,64]{2,1,0:T(1,128)} %all_to_all.57), calls=%async_computation.3 | async-start | bytes 8192 | tf_op jit(solution)/shard_map/all_to_all | solution.py:118
  98.9 6.2 %all-to-all-done.3 = f32[8,1,64]{2,1,0:T(1,128)S(1)} async-done(((f32[8,1,64]{2,1,0:T(1,128)}), f32[8,1,64]{2,1,0:T(1,128)S(1)}, u32[]{:S(2)}, u32[]{:S(2)}) %all-to-all-start.3) | async-done | bytes 2080 | tf_op jit(solution)/shard_map/all_to_all | solution.py:118
  106.5 3.5 %gather_fusion.3 = f32[512]{0:T(512)S(1)} fusion(f32[512]{0:T(512)S(1)} %reshape.153, s32[1024]{0:T(1024)S(1)} %pad_clamp_fusion), kind=kCustom, calls=%fused_computation.3 | custom fusion | bytes 6144 | tf_op jit(solution)/shard_map/gather | solution.py:121
  110.6 3.8 %scatter_custom_fusion.4 = bf16[512]{0:T(512)(128)(2,1)S(1)} fusion(s32[512]{0:T(512)S(1)} %compare_select_fusion.2, bf16[512]{0:T(512)(128)(2,1)S(1)} %subtract_convert_fusion, bf16[]{:T(256)} %constant.66.clone.1), kind=kCustom, calls=%fused_computation.91 | custom fusion | bytes 1026 | tf_op jit(solution)/shard_map/scatter | solution.py:94
  114.5 8.8 %all_to_all.75 = bf16[8,1,64]{2,1,0:T(2,128)(2,1)S(1)} all-to-all(bf16[8,1,64]{2,1,0:T(2,128)(2,1)S(1)} %all_to_all.67), channel_id=1, replica_groups=mesh['leaf'=4,'blk'=8] {'blk'}, dimensions={0} | all-to-all | bytes 2048 | tf_op jit(solution)/shard_map/all_to_all | solution.py:98
  123.4 3.8 %scatter_custom_fusion.5 = bf16[512]{0:T(512)(128)(2,1)S(1)} fusion(s32[512]{0:T(512)S(1)} %bitcast.98, bf16[512]{0:T(512)(128)(2,1)S(1)} %reshape.268, bf16[]{:T(256)} %constant.66.clone.1), kind=kCustom, calls=%fused_computation.89 | custom fusion | bytes 1026 | tf_op jit(solution)/shard_map/scatter | solution.py:104
  127.2 26.0 %all-gather.1 = bf16[8,1,512]{2,1,0:T(2,128)(2,1)S(1)} all-gather(bf16[1,1,512]{2,1,0:T(2,128)(2,1)S(1)} %reshape.301), channel_id=1, replica_groups=mesh['leaf'=4,'blk'=8] {'blk'}, dimensions={0}, use_global_device_ids=true | all-gather | bytes 9216 | tf_op jit(solution)/shard_map/all_gather | solution.py:106
  155.5 17.1 %psum.15 = bf16[4,16]{1,0:T(4,128)(2,1)S(1)} all-reduce(f32[4,16]{1,0:T(4,128)S(1)} %broadcast_select_fusion), channel_id=1, replica_groups=mesh['leaf'=4,'blk'=8] {'blk'}, use_global_device_ids=true, to_apply=%region_11.12 | all-reduce | flops 64 | bytes 384 | tf_op jit(solution)/shard_map/psum | solution.py:85
  173.3 3.2 %all-to-all-start.5 = ((bf16[4,1,16]{2,1,0:T(2,128)(2,1)}), bf16[4,1,16]{2,1,0:T(2,128)(2,1)S(1)}, u32[]{:S(2)}, u32[]{:S(2)}) async-start(bf16[4,1,16]{2,1,0:T(2,128)(2,1)} %copy.25), calls=%async_computation.5 | async-start | bytes 4096 | tf_op jit(solution)/shard_map/all_to_all | solution.py:86
  177.2 3.0 %all-to-all-done.5 = bf16[4,1,16]{2,1,0:T(2,128)(2,1)S(1)} async-done(((bf16[4,1,16]{2,1,0:T(2,128)(2,1)}), bf16[4,1,16]{2,1,0:T(2,128)(2,1)S(1)}, u32[]{:S(2)}, u32[]{:S(2)}) %all-to-all-start.5) | async-done | bytes 160 | tf_op jit(solution)/shard_map/all_to_all | solution.py:86
  180.3 3.5 %gather_fusion.6 = f32[512]{0:T(512)S(1)} fusion(f32[512]{0:T(512)S(1)} %add.111, s32[1024]{0:T(1024)S(1)} %pad_clamp_fusion.1), kind=kCustom, calls=%fused_computation.6 | custom fusion | bytes 6144 | tf_op jit(solution)/shard_map/gather | solution.py:119
  183.9 9.5 %all_to_all.76 = f32[8,1,64]{2,1,0:T(1,128)S(1)} all-to-all(f32[8,1,64]{2,1,0:T(1,128)S(1)} %all_to_all.64), channel_id=1, replica_groups=mesh['leaf'=4,'blk'=8] {'blk'}, dimensions={0} | all-to-all | bytes 4096 | tf_op jit(solution)/shard_map/all_to_all | solution.py:118
  194.2 3.5 %gather_fusion.7 = f32[512]{0:T(512)S(1)} fusion(f32[512]{0:T(512)S(1)} %reshape.157, s32[1024]{0:T(1024)S(1)} %pad_clamp_fusion), kind=kCustom, calls=%fused_computation.7 | custom fusion | bytes 6144 | tf_op jit(solution)/shard_map/gather | solution.py:121
  (96 shorter events, 21.3 us)
Async XLA Ops:
  0.6 86.7 %copy-start = (bf16[3,512,512]{2,1,0:T(8,128)(2,1)S(1)}, bf16[3,512,512]{2,1,0:T(8,128)(2,1)}, u32[]{:S(2)}) copy-start(bf16[3,512,512]{2,1,0:T(8,128)(2,1)} %param.23) | copy-start | bytes 4718596
  0.6 87.2 %copy-start.8 = (bf16[4,16,512]{2,1,0:T(8,128)(2,1)S(1)}, bf16[4,16,512]{2,1,0:T(8,128)(2,1)}, u32[]{:S(2)}) copy-start(bf16[4,16,512]{2,1,0:T(8,128)(2,1)} %param.27) | copy-start | bytes 196612
  0.7 87.3 %copy-start.4 = (s32[4]{0:T(128)S(1)}, s32[4]{0:T(128)}, u32[]{:S(2)}) copy-start(s32[4]{0:T(128)} %param.29) | copy-start | bytes 52
  0.7 87.4 %copy-start.9 = (bf16[4,16,512]{2,1,0:T(8,128)(2,1)S(1)}, bf16[4,16,512]{2,1,0:T(8,128)(2,1)}, u32[]{:S(2)}) copy-start(bf16[4,16,512]{2,1,0:T(8,128)(2,1)} %param.26) | copy-start | bytes 196612
  0.7 90.2 %copy-start.11 = (bf16[4,16,512]{2,1,0:T(8,128)(2,1)S(1)}, bf16[4,16,512]{2,1,0:T(8,128)(2,1)}, u32[]{:S(2)}) copy-start(bf16[4,16,512]{2,1,0:T(8,128)(2,1)} %param.30) | copy-start | bytes 196612
  8.2 13.7 %all-to-all-start.1 = ((bf16[8,1,64]{2,1,0:T(2,128)(2,1)}), bf16[8,1,64]{2,1,0:T(2,128)(2,1)S(1)}, u32[]{:S(2)}, u32[]{:S(2)}) async-start(bf16[8,1,64]{2,1,0:T(2,128)(2,1)} %all_to_all.66), calls=%async_computation.1 | async-start | bytes 8192 | tf_op jit(solution)/shard_map/all_to_all | solution.py:98
  21.9 11.1 %all-to-all-start = ((s32[8,1,64]{2,1,0:T(1,128)}), s32[8,1,64]{2,1,0:T(1,128)S(1)}, u32[]{:S(2)}, u32[]{:S(2)}) async-start(s32[8,1,64]{2,1,0:T(1,128)} %all_to_all.49), calls=%async_computation | async-start | bytes 8192 | tf_op jit(solution)/shard_map/all_to_all | solution.py:99
  84.0 6.9 %all-to-all-start.2 = ((bf16[4,1,16]{2,1,0:T(2,128)(2,1)}), bf16[4,1,16]{2,1,0:T(2,128)(2,1)S(1)}, u32[]{:S(2)}, u32[]{:S(2)}) async-start(bf16[4,1,16]{2,1,0:T(2,128)(2,1)} %copy.23), calls=%async_computation.2 | async-start | bytes 4096 | tf_op jit(solution)/shard_map/all_to_all | solution.py:86
  94.6 15.4 %copy-start.1 = (f32[512]{0:T(512)S(1)}, f32[512]{0:T(512)}, u32[]{:S(2)}) copy-start(f32[512]{0:T(512)} %param.16) | copy-start | bytes 6148
  94.6 15.4 %copy-start.2 = (f32[512]{0:T(512)S(1)}, f32[512]{0:T(512)}, u32[]{:S(2)}) copy-start(f32[512]{0:T(512)} %param.17) | copy-start | bytes 6148
  94.6 15.4 %copy-start.3 = (f32[512]{0:T(512)S(1)}, f32[512]{0:T(512)}, u32[]{:S(2)}) copy-start(f32[512]{0:T(512)} %param.21) | copy-start | bytes 6148
  94.6 15.4 %copy-start.5 = (f32[512]{0:T(512)S(1)}, f32[512]{0:T(512)}, u32[]{:S(2)}) copy-start(f32[512]{0:T(512)} %param.18) | copy-start | bytes 6148
  94.6 15.4 %copy-start.6 = (f32[512]{0:T(512)S(1)}, f32[512]{0:T(512)}, u32[]{:S(2)}) copy-start(f32[512]{0:T(512)} %param.20) | copy-start | bytes 6148
  94.6 15.4 %copy-start.7 = (f32[512]{0:T(512)S(1)}, f32[512]{0:T(512)}, u32[]{:S(2)}) copy-start(f32[512]{0:T(512)} %param.19) | copy-start | bytes 6148
  95.3 9.8 %all-to-all-start.3 = ((f32[8,1,64]{2,1,0:T(1,128)}), f32[8,1,64]{2,1,0:T(1,128)S(1)}, u32[]{:S(2)}, u32[]{:S(2)}) async-start(f32[8,1,64]{2,1,0:T(1,128)} %all_to_all.57), calls=%async_computation.3 | async-start | bytes 8192 | tf_op jit(solution)/shard_map/all_to_all | solution.py:118
  106.5 48.8 %copy-start.10 = (bf16[4,16,512]{2,1,0:T(8,128)(2,1)S(1)}, bf16[4,16,512]{2,1,0:T(8,128)(2,1)}, u32[]{:S(2)}) copy-start(bf16[4,16,512]{2,1,0:T(8,128)(2,1)} %param.31) | copy-start | bytes 196612
  173.3 6.9 %all-to-all-start.5 = ((bf16[4,1,16]{2,1,0:T(2,128)(2,1)}), bf16[4,1,16]{2,1,0:T(2,128)(2,1)S(1)}, u32[]{:S(2)}, u32[]{:S(2)}) async-start(bf16[4,1,16]{2,1,0:T(2,128)(2,1)} %copy.25), calls=%async_computation.5 | async-start | bytes 4096 | tf_op jit(solution)/shard_map/all_to_all | solution.py:86
where the time goes:
time: 199 us; the launch traced here: 198 us
  blocking collectives  105 us (53%)
  local copies, waits for them, and re-layouts  39 us (20%)
  starting transfers between devices  21.9 us (11%)
  waiting for transfers between devices  18.8 us (9%)
  other arithmetic  9.14 us (5%)
  matrix products  3.26 us (2%)
    all_gather x2, blocking collectives, stress_rates(): leaf_deficit = lax.all_gather(own_deficit, 'blk', axis=0, tiled=True)  52 us
    psum x2, blocking collectives, coarse_coefficients(): summed = lax.psum(partial_value, 'blk')  34.3 us
    all_to_all x1, blocking collectives, stress_rates(): lax.all_to_all(leaf_totals[got_rows], 'blk', split_axis=0, concat_axis=0,...  9.54 us
    all_to_all x1, blocking collectives, stress_rates(): lax.all_to_all(sent_values, 'blk', split_axis=0, concat_axis=0, tiled=True)  8.82 us
    scatter x4, local copies, waits for them, and re-layouts, stress_rates(): own_deficit = jnp.zeros((elem_count,), jnp.bfloat16).at[got_rows.reshape(...  7.54 us
    scatter x2, local copies, waits for them, and re-layouts, stress_rates(): sent_values = jnp.zeros((elem_count,), jnp.bfloat16).at[slot_index].set(d...  7.54 us
    all_to_all x1, starting transfers between devices, stress_rates(): lax.all_to_all(sent_values, 'blk', split_axis=0, concat_axis=0, tiled=True)  7.25 us
    gather x2, local copies, waits for them, and re-layouts, stress_rates(): leaf_totals[got_rows]  6.97 us
  transfers between devices with their start and end apart: 5, of which 5 were waited for; matrix products, arithmetic and copies ran while one was open for 3% of the time, Pallas kernels for 0%

commit v1 on v0

v1 whole, which is shorter than its diff:
```python
import functools

import jax
import jax.numpy as jnp
from jax import lax
from jax.experimental import pallas as pl
from jax.experimental.pallas import tpu as pltpu
from jax.sharding import PartitionSpec as P

DAMPING = 0.5
PLATE_RATE = 1.0
TIME_STEP = 0.2

NN = (((1,), (0,)), ((), ()))
NT = (((1,), (1,)), ((), ()))
VMEM = pltpu.VMEM
SMEM = pltpu.SMEM


def dot(left, right, dims):
    return lax.dot_general(left, right, dims, preferred_element_type=jnp.float32)


def selection(index_row, count):
    rows = lax.broadcasted_iota(jnp.int32, (count, index_row.shape[1]), 0)
    return jnp.where(rows == index_row, 1.0, 0.0).astype(jnp.bfloat16)


def select_columns(values, matrix, dims):
    high = values.astype(jnp.bfloat16).astype(jnp.float32)
    rest = values - high
    middle = rest.astype(jnp.bfloat16).astype(jnp.float32)
    parts = jnp.concatenate([high, middle, rest - middle], axis=0).astype(jnp.bfloat16)
    moved = dot(parts, matrix, dims)
    return moved[0:8] + moved[8:16] + moved[16:24]


def sort_kernel(members, index_ref, u_ref, phi_ref, sigma_ref, a_ref, b_ref, dist_ref, leaf_ref, sent_ref, slot_ref):
    elem_count = u_ref.shape[1]
    peer_rows = elem_count // members
    local = leaf_ref[...] - index_ref[0] * (members * elem_count)
    target = local // elem_count
    target_row = local - target * elem_count
    onehot = selection(target, members)
    before = lax.broadcasted_iota(jnp.int32, (elem_count, elem_count), 0)
    after = lax.broadcasted_iota(jnp.int32, (elem_count, elem_count), 1)
    earlier = dot(onehot, jnp.where(before < after, 1.0, 0.0).astype(jnp.bfloat16), NN)
    rank = jnp.sum(earlier * onehot.astype(jnp.float32), axis=0, keepdims=True)
    slot = target * peer_rows + rank.astype(jnp.int32)
    slot_ref[...] = slot
    sigma = sigma_ref[...]
    rows = [
        u_ref[...],
        phi_ref[...],
        sigma * a_ref[...],
        sigma * b_ref[...],
        dist_ref[...],
        target_row.astype(jnp.float32),
    ]
    pad = jnp.zeros((8 - len(rows), elem_count), jnp.float32)
    sent = select_columns(jnp.concatenate(rows + [pad], axis=0), selection(slot, elem_count), NT)
    for peer in range(members):
        sent_ref[peer] = sent[:, peer * peer_rows:(peer + 1) * peer_rows]


def outgoing(deficit, coarse_v_ref, out_ref):
    elem_count = deficit.shape[1]
    pieces = elem_count // 128
    wide = jnp.broadcast_to(deficit, (8, elem_count))
    partial = dot(wide.astype(jnp.bfloat16), coarse_v_ref[...], NT)
    out_ref[...] = jnp.zeros(out_ref.shape, jnp.float32)
    for piece in range(pieces):
        out_ref[piece:piece + 1, :] = deficit[:, piece * 128:(piece + 1) * 128]
    width = partial.shape[1]
    for piece in range(pl.cdiv(width, 128)):
        span = min(128, width - piece * 128)
        out_ref[pieces + piece:pieces + piece + 1, 0:span] = partial[0:1, piece * 128:piece * 128 + span]


def place_kernel(members, got_ref, coarse_v_ref, state_ref, rows_ref, out_ref, flat_ref):
    peer_rows = got_ref.shape[2]
    elem_count = members * peer_rows
    for peer in range(members):
        flat_ref[:, peer * peer_rows:(peer + 1) * peer_rows] = got_ref[peer]
    flat = flat_ref[...]
    rows = flat[5:6].astype(jnp.int32)
    rows_ref[...] = rows
    state = select_columns(flat, selection(rows, elem_count), NT)
    state_ref[...] = state
    deficit = (PLATE_RATE - jnp.exp(state[0:1])).astype(jnp.bfloat16).astype(jnp.float32)
    outgoing(deficit, coarse_v_ref, out_ref)


def coef_kernel(groups, rank, pieces, index_ref, got_ref, coef_ref):
    total = jnp.sum(got_ref[...], axis=0)
    coef_ref[...] = jnp.zeros(coef_ref.shape, jnp.float32)
    per_row = 128 // rank
    for group in range(groups):
        row, place = pieces + group // per_row, (group % per_row) * rank
        keep = jnp.where(index_ref[0] == group, 0.0, 1.0)
        coef_ref[group, 0:1, 0:rank] = total[row:row + 1, place:place + rank] * keep


def inside_kernel(
    got_ref, near_ref, far_u_ref, far_v_ref, near_col_ref, near_count_ref, far_col_ref, far_rank_ref, out_ref, flat_ref
):
    members = got_ref.shape[0]
    near_slots, leaf_size = near_ref.shape[0], near_ref.shape[2]
    far_slots, rank = far_col_ref.shape[0], far_u_ref.shape[0] // far_col_ref.shape[0]
    for piece in range(leaf_size // 128):
        flat_ref[:, piece * 128:(piece + 1) * 128] = got_ref[:, piece, :]
    deficits = flat_ref[...]
    block = lax.broadcasted_iota(jnp.int32, (members, leaf_size), 0)
    total = jnp.zeros((members, leaf_size), jnp.float32)
    for slot in range(near_slots):
        column = jnp.where(slot < near_count_ref[0], near_col_ref[slot], -1)
        source = jnp.where(block == column, deficits, 0.0).astype(jnp.bfloat16)
        total = total + dot(source, near_ref[slot], NT)
    project = dot(deficits.astype(jnp.bfloat16), far_v_ref[...], NT)
    block = lax.broadcasted_iota(jnp.int32, project.shape, 0)
    lane = lax.broadcasted_iota(jnp.int32, project.shape, 1)
    column = jnp.full(project.shape, -1, jnp.int32)
    for slot in range(far_slots):
        low = slot * rank
        mine = (lane >= low) & (lane < low + far_rank_ref[slot])
        column = jnp.where(mine, far_col_ref[slot], column)
    project = jnp.sum(jnp.where(block == column, project, 0.0), axis=0, keepdims=True)
    project = jnp.broadcast_to(project, (8, project.shape[1])).astype(jnp.bfloat16)
    far = dot(project, far_u_ref[...], NN)
    out_ref[...] = jnp.sum(total, axis=0, keepdims=True) + far[0:1]


def rates(load, ln_now, state_now, sa, sb, dist):
    velocity = jnp.exp(ln_now)
    state_rate = (jnp.exp(-state_now) - velocity) / dist
    log_rate = (load - sb * state_rate) / (sa + DAMPING * velocity)
    return log_rate, state_rate


def coarse_rows(coef_ref, coarse_u_ref):
    groups, leaf_size = coef_ref.shape[0], coarse_u_ref.shape[1]
    rank = coarse_u_ref.shape[0] // groups
    total = jnp.zeros((8, leaf_size), jnp.float32)
    for group in range(groups):
        weights = coef_ref[group][:, 0:rank].astype(jnp.bfloat16)
        total = total + dot(weights, coarse_u_ref[group * rank:(group + 1) * rank, :], NN)
    return total[0:1]


def first_kernel(state_ref, inside_ref, coef_ref, coarse_u_ref, coarse_v_ref, next_ref, out_ref):
    state = state_ref[...]
    load = inside_ref[...] + coarse_rows(coef_ref, coarse_u_ref)
    u, phi, sa, sb, dist = (state[i:i + 1] for i in range(5))
    k1u, k1p = rates(load, u, phi, sa, sb, dist)
    u2 = u + TIME_STEP * k1u
    phi2 = phi + TIME_STEP * k1p
    deficit = (PLATE_RATE - jnp.exp(u2)).astype(jnp.bfloat16).astype(jnp.float32)
    outgoing(deficit, coarse_v_ref, out_ref)
    next_ref[...] = jnp.concatenate([u2, phi2, k1u, k1p, jnp.zeros((4, u.shape[1]), jnp.float32)], axis=0)


def second_kernel(state_ref, next_ref, rows_ref, inside_ref, coef_ref, coarse_u_ref, sent_ref):
    state = state_ref[...]
    later = next_ref[...]
    load = inside_ref[...] + coarse_rows(coef_ref, coarse_u_ref)
    u, phi, sa, sb, dist = (state[i:i + 1] for i in range(5))
    u2, phi2, k1u, k1p = (later[i:i + 1] for i in range(4))
    k2u, k2p = rates(load, u2, phi2, sa, sb, dist)
    u = u + 0.5 * TIME_STEP * (k1u + k2u)
    phi = phi + 0.5 * TIME_STEP * (k1p + k2p)
    elem_count = u.shape[1]
    values = jnp.concatenate([u, phi, jnp.zeros((6, elem_count), jnp.float32)], axis=0)
    sent = select_columns(values, selection(rows_ref[...], elem_count), NN)
    members = sent_ref.shape[0]
    peer_rows = elem_count // members
    for peer in range(members):
        sent_ref[peer] = sent[:, peer * peer_rows:(peer + 1) * peer_rows]


def unsort_kernel(got_ref, slot_ref, u_ref, phi_ref, flat_ref):
    members, _, peer_rows = got_ref.shape
    for peer in range(members):
        flat_ref[:, peer * peer_rows:(peer + 1) * peer_rows] = got_ref[peer]
    out = select_columns(flat_ref[...], selection(slot_ref[...], members * peer_rows), NN)
    u_ref[...] = out[0:1]
    phi_ref[...] = out[1:2]


def call(kernel, outs, *args, scalars=(), scratch=(), flops=1000, moved=1000):
    specs = [
        pl.BlockSpec(memory_space=SMEM if i in scalars else VMEM) for i in range(len(args))
    ]
    return pl.pallas_call(
        kernel,
        out_shape=outs,
        in_specs=specs,
        out_specs=jax.tree.map(lambda _: pl.BlockSpec(memory_space=VMEM), outs),
        scratch_shapes=list(scratch),
        cost_estimate=pl.CostEstimate(flops=flops, bytes_accessed=moved, transcendentals=0),
        compiler_params=pltpu.CompilerParams(vmem_limit_bytes=32 * 1024 * 1024),
    )(*args)


def shape(*dims, dtype=jnp.float32):
    return jax.ShapeDtypeStruct(dims, dtype)


def body(
    ln_rate,
    log_state,
    sigma,
    fric_a,
    fric_b,
    slip_dist,
    leaf_of_elem,
    near_blocks,
    near_col,
    near_count,
    far_u,
    far_v,
    far_col,
    far_rank,
    coarse_u,
    coarse_v,
):
    members = lax.axis_size("blk")
    group_index = lax.axis_index("leaf").astype(jnp.int32).reshape(1)
    elems = ln_rate.shape[0]
    leaf_size = near_blocks.shape[1]
    groups, rank = coarse_v.shape[0], coarse_v.shape[1]
    peer_rows = elems // members
    pieces = elems // 128
    out_rows = pl.cdiv(pieces + pl.cdiv(groups * rank, 128), 8) * 8
    far_u = far_u.reshape(-1, leaf_size)
    far_v = far_v.reshape(-1, leaf_size)
    coarse_u = coarse_u.reshape(-1, elems)
    coarse_v = coarse_v.reshape(-1, elems)

    def swap(value, axis):
        return lax.all_to_all(value, axis, split_axis=0, concat_axis=0, tiled=True)

    def flat(value):
        return value.reshape(1, elems)

    sent, slot = call(
        functools.partial(sort_kernel, members),
        (shape(members, 8, peer_rows), shape(1, elems, dtype=jnp.int32)),
        group_index, flat(ln_rate), flat(log_state), flat(sigma), flat(fric_a), flat(fric_b),
        flat(slip_dist), flat(leaf_of_elem), scalars=(0,),
    )
    got = swap(sent, "blk")
    state, rows, out = call(
        functools.partial(place_kernel, members),
        (shape(8, elems), shape(1, elems, dtype=jnp.int32), shape(out_rows, 128)),
        got, coarse_v, scratch=[VMEM((8, elems), jnp.float32)],
    )

    def section(out):
        everyone = swap(jnp.broadcast_to(out[None], (members,) + out.shape), "blk")
        coef = call(
            functools.partial(coef_kernel, groups, rank, pieces),
            shape(groups, 8, 128), group_index, everyone, scalars=(0,),
        )
        coef = swap(coef, "leaf")
        inside = call(
            inside_kernel, shape(1, elems),
            everyone, near_blocks, far_u, far_v, near_col, near_count, far_col, far_rank,
            scalars=(4, 5, 6, 7), scratch=[VMEM((members, leaf_size), jnp.float32)],
            flops=2 * members * near_blocks.size, moved=2 * near_blocks.size,
        )
        return coef, inside

    coef, inside = section(out)
    later, out = call(
        first_kernel, (shape(8, elems), shape(out_rows, 128)), state, inside, coef, coarse_u, coarse_v
    )
    coef, inside = section(out)
    sent = call(
        second_kernel, shape(members, 8, peer_rows), state, later, rows, inside, coef, coarse_u
    )
    got = swap(sent, "blk")
    u, phi = call(
        unsort_kernel, (shape(1, elems), shape(1, elems)),
        got, slot, scratch=[VMEM((8, elems), jnp.float32)],
    )
    return u.reshape(elems), phi.reshape(elems)


def solution(mesh):
    each = P(("leaf", "blk"))
    blocks = P(("leaf", "blk"), None, None)
    last = P(None, None, ("leaf", "blk"))
    in_specs = (each,) * 7 + (blocks, each, each, blocks, blocks, each, each, last, last)
    return jax.shard_map(body, mesh=mesh, in_specs=in_specs, out_specs=(each, each), check_vma=False)
```

time: 199 us -> 71.4 us (0.36)
  blocking collectives: 105 us -> 40.7 us
  local copies, waits for them, and re-layouts: 39 us -> 11.7 us
  waiting for transfers between devices: 18.8 us -> 2.59 us
  starting transfers between devices: 21.9 us -> 6.5 us
  other arithmetic: 9.14 us -> 1.37 us
  Pallas kernels: 0 us -> 6.26 us
  matrix products: 3.26 us -> 0 us
    all_gather x2 -> x0, blocking collectives: 52 us -> none  [stress_rates(): leaf_deficit = lax.all_gather(own_deficit, 'blk', axis=0, tiled=True)]
    psum x2 -> x0, blocking collectives: 34.3 us -> none  [coarse_coefficients(): summed = lax.psum(partial_value, 'blk')]
    all_to_all x2 -> x4, blocking collectives: 18.4 us -> 40.7 us  [swap(): return lax.all_to_all(value, axis, split_axis=0, concat_axis=0, tiled=True)]
    scatter x7 -> x0, local copies, waits for them, and re-layouts: 17.5 us -> none  [the longest x4 7.54 us: stress_rates(): own_deficit = jnp.zeros((elem_count,), jnp.bfloat16).at[got_rows.reshape(...]
    all_to_all x5 -> x2, waiting for transfers between devices: 18.8 us -> 2.59 us  [swap(): return lax.all_to_all(value, axis, split_axis=0, concat_axis=0, tiled=True)]
    gather x8 -> x0, local copies, waits for them, and re-layouts: 16.2 us -> none  [the longest x2 6.97 us: stress_rates(): leaf_totals[got_rows]]
    all_to_all x5 -> x2, starting transfers between devices: 21.9 us -> 6.5 us  [swap(): return lax.all_to_all(value, axis, split_axis=0, concat_axis=0, tiled=True)]
    unnamed x28 -> x48, local copies, waits for them, and re-layouts: 0.09 us -> 11.2 us
  transfers between devices with their start and end apart: 5 -> 2, of which waited for: 5 -> 1; matrix products, arithmetic and copies ran while one was open for 3% -> 0% of each run, Pallas kernels for 0% -> 3%
where the time goes in v1:
time: 71.4 us; the launch traced here: 70.6 us
  blocking collectives  40.7 us (57%)
  local copies, waits for them, and re-layouts  11.7 us (16%)
  starting transfers between devices  6.5 us (9%)
  Pallas kernels  6.26 us (9%)
  waiting for transfers between devices  2.59 us (4%)
  between operations  1.47 us (2%)
  other arithmetic  1.37 us (2%)
    all_to_all x4, blocking collectives, swap(): return lax.all_to_all(value, axis, split_axis=0, concat_axis=0, tiled=True)  40.7 us
    unnamed x48, local copies, waits for them, and re-layouts  11.2 us
    all_to_all x2, starting transfers between devices, swap(): return lax.all_to_all(value, axis, split_axis=0, concat_axis=0, tiled=True)  6.5 us
    pallas_call x9, Pallas kernels, call(): pl.pallas_call(kernel, out_shape=outs, in_specs=specs, out_specs=jax.tree...  6.26 us
    all_to_all x2, waiting for transfers between devices, swap(): return lax.all_to_all(value, axis, split_axis=0, concat_axis=0, tiled=True)  2.59 us
  transfers between devices with their start and end apart: 2, of which 1 were waited for; matrix products, arithmetic and copies ran while one was open for 0% of the time, Pallas kernels for 3%

profile of v1, /device:TPU:0, one launch (start us, length us, event | category | flops | bytes accessed | tf_op | source)
XLA Modules:
  0.0 70.6 jit_solution(5453984514922295266)
XLA Ops:
  0.7 0.7 %copy-done.15 = f32[512]{0:T(512)S(1)} copy-done((f32[512]{0:T(512)S(1)}, f32[512]{0:T(512)}, u32[]{:S(2)}) %copy-start.15) | copy-done | bytes 2072
  1.5 0.7 copy-done.16
  2.1 0.7 copy-done.17
  2.8 0.7 copy-done.18
  3.5 0.7 copy-done.19
  4.2 0.7 copy-done.20
  4.9 0.7 copy-done.21
  6.2 13.6 %all_to_all.30 = f32[8,1,512]{2,1,0:T(1,128)S(1)} all-to-all(f32[8,1,512]{2,1,0:T(1,128)S(1)} %reshape.62), channel_id=1, replica_groups=mesh['leaf'=4,'blk'=8] {'blk'}, dimensions={0} | all-to-all | bytes 32768 | tf_op jit(solution)/shard_map/all_to_all | solution.py:240
  20.3 0.7 reduce
  21.1 0.8 %copy-done.3 = bf16[4,16,512]{2,1,0:T(8,128)(2,1)S(1)} copy-done((bf16[4,16,512]{2,1,0:T(8,128)(2,1)S(1)}, bf16[4,16,512]{2,1,0:T(8,128)(2,1)}, u32[]{:S(2)}) %copy-start.3) | copy-done | bytes 65560
  22.4 9.1 %all_to_all.31.got_ref = f32[8,8,128]{2,1,0:T(8,128)S(1)} all-to-all(f32[8,8,128]{2,1,0:T(8,128)S(1)} %broadcast_in_dim.4), channel_id=1, replica_groups=mesh['leaf'=4,'blk'=8] {'blk'}, dimensions={0} | all-to-all | bytes 65536 | tf_op jit(solution)/shard_map/all_to_all | solution.py:240
  31.5 0.7 shard_map.170
  32.2 3.2 %all-to-all-start.2 = ((f32[4,8,128]{2,1,0:T(8,128)}), f32[4,8,128]{2,1,0:T(8,128)S(1)}, u32[]{:S(2)}, u32[]{:S(2)}) async-start(f32[4,8,128]{2,1,0:T(8,128)} %shard_map.170), calls=%async_computation.2 | async-start | bytes 32768 | tf_op jit(solution)/shard_map/all_to_all | solution.py:240
  36.1 1.4 %copy-done = bf16[3,512,512]{2,1,0:T(8,128)(2,1)S(1)} copy-done((bf16[3,512,512]{2,1,0:T(8,128)(2,1)S(1)}, bf16[3,512,512]{2,1,0:T(8,128)(2,1)}, u32[]{:S(2)}) %copy-start) | copy-done | bytes 1572888
  37.5 0.8 %copy-done.5 = bf16[4,16,512]{2,1,0:T(8,128)(2,1)S(1)} copy-done((bf16[4,16,512]{2,1,0:T(8,128)(2,1)S(1)}, bf16[4,16,512]{2,1,0:T(8,128)(2,1)}, u32[]{:S(2)}) %copy-start.5) | copy-done | bytes 65560
  38.3 0.8 %copy-done.7 = bf16[4,16,512]{2,1,0:T(8,128)(2,1)S(1)} copy-done((bf16[4,16,512]{2,1,0:T(8,128)(2,1)S(1)}, bf16[4,16,512]{2,1,0:T(8,128)(2,1)}, u32[]{:S(2)}) %copy-start.7) | copy-done | bytes 65560
  41.1 1.2 %shard_map.169.inside_ref = f32[1,512]{1,0:T(1,128)S(1)} custom-call(f32[8,8,128]{2,1,0:T(8,128)S(1)} %all_to_all.31.got_ref, bf16[3,512,512]{2,1,0:T(8,128)(2,1)S(1)} %copy-done, bf16[64,512]{1,0:T(8,128)(2,1)S(1)} %bitcast.18, bf16[64,512]{1,0:T(8,128)(2,1)S(1)} %bitcast.20, s32[3]{0:T(128)S(1)} %copy-done.9, s32[1]{0:T(128)S(6)} %copy.18.near_count_ref, ...), custom_call_target="tpu_custom_call" | custom-call | flops 12582912 | bytes 1572864 | tf_op jit(solution)/shard_map/pallas_call | solution.py:193
  42.7 9.1 %all_to_all.32.got_ref = f32[8,8,128]{2,1,0:T(8,128)S(1)} all-to-all(f32[8,8,128]{2,1,0:T(8,128)S(1)} %broadcast_in_dim.5), channel_id=1, replica_groups=mesh['leaf'=4,'blk'=8] {'blk'}, dimensions={0} | all-to-all | bytes 65536 | tf_op jit(solution)/shard_map/all_to_all | solution.py:240
  52.4 3.3 %all-to-all-start.4 = ((f32[4,8,128]{2,1,0:T(8,128)}), f32[4,8,128]{2,1,0:T(8,128)S(1)}, u32[]{:S(2)}, u32[]{:S(2)}) async-start(f32[4,8,128]{2,1,0:T(8,128)} %shard_map.173), calls=%async_computation.4 | async-start | bytes 32768 | tf_op jit(solution)/shard_map/all_to_all | solution.py:240
  55.7 1.2 %shard_map.172.inside_ref = f32[1,512]{1,0:T(1,128)S(1)} custom-call(f32[8,8,128]{2,1,0:T(8,128)S(1)} %all_to_all.32.got_ref, bf16[3,512,512]{2,1,0:T(8,128)(2,1)S(1)} %copy-done.1, bf16[64,512]{1,0:T(8,128)(2,1)S(1)} %bitcast.19, bf16[64,512]{1,0:T(8,128)(2,1)S(1)} %bitcast.21, s32[3]{0:T(128)S(1)} %copy-done.10, s32[1]{0:T(128)S(6)} %copy.18.near_count_ref, ...), custom_call_target="tpu_custom_call" | custom-call | flops 12582912 | bytes 1572864 | tf_op jit(solution)/shard_map/pallas_call | solution.py:193
  56.9 2.6 %all-to-all-done.4.coef_ref = f32[4,8,128]{2,1,0:T(8,128)S(1)} async-done(((f32[4,8,128]{2,1,0:T(8,128)}), f32[4,8,128]{2,1,0:T(8,128)S(1)}, u32[]{:S(2)}, u32[]{:S(2)}) %all-to-all-start.4) | async-done | bytes 16416 | tf_op jit(solution)/shard_map/all_to_all | solution.py:240
  60.0 8.9 %all_to_all.33 = f32[8,1,512]{2,1,0:T(1,128)S(1)} all-to-all(f32[8,1,512]{2,1,0:T(1,128)S(1)} %reshape.64), channel_id=1, replica_groups=mesh['leaf'=4,'blk'=8] {'blk'}, dimensions={0} | all-to-all | bytes 32768 | tf_op jit(solution)/shard_map/all_to_all | solution.py:240
  69.0 0.7 reduce.1
  69.7 0.8 %shard_map.175 = (f32[1,512]{1,0:T(1,128)}, f32[1,512]{1,0:T(1,128)}) custom-call(f32[8,8,64]{2,1,0:T(8,128)S(1)} %reshape.65.got_ref, s32[1,512]{1,0:T(1,128)S(1)} %get-tuple-element.17.slot_ref), custom_call_target="tpu_custom_call" | custom-call | flops 1000 | bytes 1000 | tf_op jit(solution)/shard_map/pallas_call | solution.py:193
  (46 shorter events, 5.3 us)
Async XLA Ops:
  0.6 41.7 %copy-start.4 = (bf16[4,16,512]{2,1,0:T(8,128)(2,1)S(1)}, bf16[4,16,512]{2,1,0:T(8,128)(2,1)}, u32[]{:S(2)}) copy-start(bf16[4,16,512]{2,1,0:T(8,128)(2,1)} %param.31) | copy-start | bytes 196612
  0.6 55.0 %copy-start.14 = (s32[4]{0:T(128)S(1)}, s32[4]{0:T(128)}, u32[]{:S(2)}) copy-start(s32[4]{0:T(128)} %far_rank_ref.3) | copy-start | bytes 52
  0.7 55.0 %copy-start.12 = (s32[4]{0:T(128)S(1)}, s32[4]{0:T(128)}, u32[]{:S(2)}) copy-start(s32[4]{0:T(128)} %far_col_ref.3) | copy-start | bytes 52
  0.7 55.0 %copy-start.10 = (s32[3]{0:T(128)S(1)}, s32[3]{0:T(128)}, u32[]{:S(2)}) copy-start(s32[3]{0:T(128)} %near_col_ref.3) | copy-start | bytes 40
  0.7 55.0 %copy-start.6 = (bf16[4,16,512]{2,1,0:T(8,128)(2,1)S(1)}, bf16[4,16,512]{2,1,0:T(8,128)(2,1)}, u32[]{:S(2)}) copy-start(bf16[4,16,512]{2,1,0:T(8,128)(2,1)} %param.26) | copy-start | bytes 196612
  0.7 41.7 %copy-start.2 = (bf16[4,16,512]{2,1,0:T(8,128)(2,1)S(1)}, bf16[4,16,512]{2,1,0:T(8,128)(2,1)}, u32[]{:S(2)}) copy-start(bf16[4,16,512]{2,1,0:T(8,128)(2,1)} %param.30) | copy-start | bytes 196612
  0.7 0.7 %copy-start.15 = (f32[512]{0:T(512)S(1)}, f32[512]{0:T(512)}, u32[]{:S(2)}) copy-start(f32[512]{0:T(512)} %param.16) | copy-start | bytes 6148
  1.5 0.7 copy-start.16
  2.1 0.7 copy-start.17
  2.8 0.7 copy-start.18
  3.5 0.7 copy-start.19
  4.2 0.7 copy-start.20
  4.9 0.7 copy-start.21
  21.1 0.8 %copy-start.3 = (bf16[4,16,512]{2,1,0:T(8,128)(2,1)S(1)}, bf16[4,16,512]{2,1,0:T(8,128)(2,1)}, u32[]{:S(2)}) copy-start(bf16[4,16,512]{2,1,0:T(8,128)(2,1)} %param.31) | copy-start | bytes 196612
  21.9 33.8 %copy-start.8 = (bf16[4,16,512]{2,1,0:T(8,128)(2,1)S(1)}, bf16[4,16,512]{2,1,0:T(8,128)(2,1)}, u32[]{:S(2)}) copy-start(bf16[4,16,512]{2,1,0:T(8,128)(2,1)} %param.27) | copy-start | bytes 196612
  32.2 10.2 %all-to-all-start.2 = ((f32[4,8,128]{2,1,0:T(8,128)}), f32[4,8,128]{2,1,0:T(8,128)S(1)}, u32[]{:S(2)}, u32[]{:S(2)}) async-start(f32[4,8,128]{2,1,0:T(8,128)} %shard_map.170), calls=%async_computation.2 | async-start | bytes 32768 | tf_op jit(solution)/shard_map/all_to_all | solution.py:240
  36.1 1.4 %copy-start = (bf16[3,512,512]{2,1,0:T(8,128)(2,1)S(1)}, bf16[3,512,512]{2,1,0:T(8,128)(2,1)}, u32[]{:S(2)}) copy-start(bf16[3,512,512]{2,1,0:T(8,128)(2,1)} %near_ref.3) | copy-start | bytes 4718596
  37.5 0.8 %copy-start.5 = (bf16[4,16,512]{2,1,0:T(8,128)(2,1)S(1)}, bf16[4,16,512]{2,1,0:T(8,128)(2,1)}, u32[]{:S(2)}) copy-start(bf16[4,16,512]{2,1,0:T(8,128)(2,1)} %param.26) | copy-start | bytes 196612
  38.3 0.8 %copy-start.7 = (bf16[4,16,512]{2,1,0:T(8,128)(2,1)S(1)}, bf16[4,16,512]{2,1,0:T(8,128)(2,1)}, u32[]{:S(2)}) copy-start(bf16[4,16,512]{2,1,0:T(8,128)(2,1)} %param.27) | copy-start | bytes 196612
  39.2 0.7 copy-start.9
  39.8 0.7 copy-start.11
  40.5 0.7 copy-start.13
  41.1 14.6 %copy-start.1 = (bf16[3,512,512]{2,1,0:T(8,128)(2,1)S(1)}, bf16[3,512,512]{2,1,0:T(8,128)(2,1)}, u32[]{:S(2)}) copy-start(bf16[3,512,512]{2,1,0:T(8,128)(2,1)} %near_ref.3) | copy-start | bytes 4718596
  52.4 7.1 %all-to-all-start.4 = ((f32[4,8,128]{2,1,0:T(8,128)}), f32[4,8,128]{2,1,0:T(8,128)S(1)}, u32[]{:S(2)}, u32[]{:S(2)}) async-start(f32[4,8,128]{2,1,0:T(8,128)} %shard_map.173), calls=%async_computation.4 | async-start | bytes 32768 | tf_op jit(solution)/shard_map/all_to_all | solution.py:240

commit v2 on v1

v2 whole, which is shorter than its diff:
```python
import functools

import jax
import jax.numpy as jnp
from jax import lax
from jax.experimental import pallas as pl
from jax.experimental.pallas import tpu as pltpu
from jax.sharding import PartitionSpec as P

DAMPING = 0.5
PLATE_RATE = 1.0
TIME_STEP = 0.2

NN = (((1,), (0,)), ((), ()))
NT = (((1,), (1,)), ((), ()))
VMEM = pltpu.VMEM
SMEM = pltpu.SMEM


def dot(left, right, dims):
    return lax.dot_general(left, right, dims, preferred_element_type=jnp.float32)


def selection(index_row, count):
    rows = lax.broadcasted_iota(jnp.int32, (count, index_row.shape[1]), 0)
    return jnp.where(rows == index_row, 1.0, 0.0).astype(jnp.bfloat16)


def select_columns(values, matrix, dims):
    high = values.astype(jnp.bfloat16).astype(jnp.float32)
    rest = values - high
    middle = rest.astype(jnp.bfloat16).astype(jnp.float32)
    parts = jnp.concatenate([high, middle, rest - middle], axis=0).astype(jnp.bfloat16)
    moved = dot(parts, matrix, dims)
    return moved[0:8] + moved[8:16] + moved[16:24]


def sort_kernel(members, index_ref, near_count, *refs):
    elem_refs, weight_refs, scalar_refs = refs[:7], refs[7:12], refs[12:15]
    sent_ref, slot_ref, near_mask_ref, far_mask_ref = refs[15:19]
    weight_outs = refs[19:24]
    elem_bufs, scalar_bufs, sems = refs[24:31], refs[31:34], refs[34]
    sources = elem_refs + scalar_refs + weight_refs
    targets = elem_bufs + scalar_bufs + weight_outs
    copies = [
        pltpu.make_async_copy(source, target, sems.at[i])
        for i, (source, target) in enumerate(zip(sources, targets))
    ]
    for copy in copies:
        copy.start()
    elem_count = elem_bufs[0].shape[1]
    peer_rows = elem_count // members
    before = lax.broadcasted_iota(jnp.int32, (elem_count, elem_count), 0)
    after = lax.broadcasted_iota(jnp.int32, (elem_count, elem_count), 1)
    triangle = jnp.where(before < after, 1.0, 0.0).astype(jnp.bfloat16)
    for copy in copies[:7]:
        copy.wait()
    u, phi, sigma, fric_a, fric_b, dist, leaf = (buf[...] for buf in elem_bufs)
    local = leaf - index_ref[0] * (members * elem_count)
    target = local // elem_count
    target_row = local - target * elem_count
    onehot = selection(target, members)
    earlier = dot(onehot, triangle, NN)
    rank = jnp.sum(earlier * onehot.astype(jnp.float32), axis=0, keepdims=True)
    slot = target * peer_rows + rank.astype(jnp.int32)
    slot_ref[...] = slot
    rows = [u, phi, sigma * fric_a, sigma * fric_b, dist, target_row.astype(jnp.float32)]
    pad = jnp.zeros((8 - len(rows), elem_count), jnp.float32)
    sent = select_columns(jnp.concatenate(rows + [pad], axis=0), selection(slot, elem_count), NT)
    for peer in range(members):
        sent_ref[peer, :, 0:peer_rows] = sent[:, peer * peer_rows:(peer + 1) * peer_rows]
    for copy in copies[7:]:
        copy.wait()
    near_col, far_col, far_rank = scalar_bufs
    near_slots = near_mask_ref.shape[0]
    far_slots = far_col.shape[0]
    far_width = far_mask_ref.shape[1] // far_slots

    def owner(dims):
        shift = lax.broadcasted_iota(jnp.int32, dims, 0)
        block = index_ref[1] - shift
        return jnp.where(block < 0, block + members, block)

    block = owner(near_mask_ref.shape[1:])
    for number in range(near_slots):
        column = jnp.where(number < near_count[0], near_col[number], -1)
        near_mask_ref[number] = jnp.where(block == column, 1.0, 0.0)
    block = owner(far_mask_ref.shape)
    lane = lax.broadcasted_iota(jnp.int32, far_mask_ref.shape, 1)
    column = jnp.full(far_mask_ref.shape, -1, jnp.int32)
    for number in range(far_slots):
        low = number * far_width
        mine = (lane >= low) & (lane < low + far_rank[number])
        column = jnp.where(mine, far_col[number], column)
    far_mask_ref[...] = jnp.where(block == column, 1.0, 0.0)


def outgoing(deficit, coarse_v_ref, out_ref):
    elem_count = deficit.shape[1]
    pieces = elem_count // 128
    wide = jnp.broadcast_to(deficit, (8, elem_count))
    partial = dot(wide.astype(jnp.bfloat16), coarse_v_ref[...], NT)
    out_ref[...] = jnp.zeros(out_ref.shape, jnp.float32)
    for piece in range(pieces):
        out_ref[piece:piece + 1, :] = deficit[:, piece * 128:(piece + 1) * 128]
    width = partial.shape[1]
    for piece in range(pl.cdiv(width, 128)):
        span = min(128, width - piece * 128)
        out_ref[pieces + piece:pieces + piece + 1, 0:span] = partial[0:1, piece * 128:piece * 128 + span]


def place_kernel(members, got_ref, coarse_v_ref, state_ref, rows_ref, out_ref, flat_ref):
    elem_count = state_ref.shape[1]
    peer_rows = elem_count // members
    for peer in range(members):
        flat_ref[:, peer * peer_rows:(peer + 1) * peer_rows] = got_ref[peer, :, 0:peer_rows]
    flat = flat_ref[...]
    rows = flat[5:6].astype(jnp.int32)
    rows_ref[...] = rows
    state = select_columns(flat, selection(rows, elem_count), NT)
    state_ref[...] = state
    deficit = (PLATE_RATE - jnp.exp(state[0:1])).astype(jnp.bfloat16).astype(jnp.float32)
    outgoing(deficit, coarse_v_ref, out_ref)


def coef_kernel(pieces, *refs):
    out_ref = refs[-1]
    total = refs[0][...]
    for ref in refs[1:-1]:
        total = total + ref[...]
    out_ref[...] = total


def inside_kernel(members, *refs):
    got_refs = refs[:members]
    near_ref, far_u_ref, far_v_ref, near_mask_ref, far_mask_ref, out_ref, flat_ref = refs[members:]
    leaf_size = near_ref.shape[2]
    for member in range(members):
        for piece in range(leaf_size // 128):
            span = slice(piece * 128, (piece + 1) * 128)
            flat_ref[member:member + 1, span] = got_refs[member][piece:piece + 1, :]
    deficits = flat_ref[...]
    total = jnp.zeros((members, leaf_size), jnp.float32)
    for slot in range(near_ref.shape[0]):
        source = (deficits * near_mask_ref[slot]).astype(jnp.bfloat16)
        total = total + dot(source, near_ref[slot], NT)
    project = dot(deficits.astype(jnp.bfloat16), far_v_ref[...], NT) * far_mask_ref[...]
    project = jnp.sum(project, axis=0, keepdims=True)
    project = jnp.broadcast_to(project, (8, project.shape[1])).astype(jnp.bfloat16)
    far = dot(project, far_u_ref[...], NN)
    out_ref[...] = jnp.sum(total, axis=0, keepdims=True) + far[0:1]


def rates(load, ln_now, state_now, sa, sb, dist):
    velocity = jnp.exp(ln_now)
    state_rate = (jnp.exp(-state_now) - velocity) / dist
    log_rate = (load - sb * state_rate) / (sa + DAMPING * velocity)
    return log_rate, state_rate


def coarse_rows(index_ref, coef_refs, pieces, coarse_u_ref):
    groups = len(coef_refs) + 1
    width, leaf_size = coarse_u_ref.shape
    rank = width // groups
    lane = lax.broadcasted_iota(jnp.int32, (1, width), 1)
    low = index_ref[0] * rank
    mine = (lane >= low) & (lane < low + rank)
    weights = jnp.zeros((1, width), jnp.float32)
    for shift in range(1, groups):
        got = coef_refs[shift - 1]
        count = pl.cdiv(width, 128)
        row = jnp.concatenate([got[pieces + i:pieces + i + 1, :] for i in range(count)], axis=1)
        row = jnp.where(mine, row[:, 0:width], 0.0)
        twice = jnp.concatenate([row, row], axis=1)
        weights = weights + twice[:, shift * rank:shift * rank + width]
    weights = jnp.broadcast_to(weights, (8, width)).astype(jnp.bfloat16)
    return dot(weights, coarse_u_ref[...], NN)[0:1]


def first_kernel(pieces, index_ref, state_ref, inside_ref, coarse_u_ref, coarse_v_ref, *refs):
    coef_refs, next_ref, out_ref = refs[:-2], refs[-2], refs[-1]
    state = state_ref[...]
    load = inside_ref[...] + coarse_rows(index_ref, coef_refs, pieces, coarse_u_ref)
    u, phi, sa, sb, dist = (state[i:i + 1] for i in range(5))
    k1u, k1p = rates(load, u, phi, sa, sb, dist)
    u2 = u + TIME_STEP * k1u
    phi2 = phi + TIME_STEP * k1p
    deficit = (PLATE_RATE - jnp.exp(u2)).astype(jnp.bfloat16).astype(jnp.float32)
    outgoing(deficit, coarse_v_ref, out_ref)
    next_ref[...] = jnp.concatenate([u2, phi2, k1u, k1p, jnp.zeros((4, u.shape[1]), jnp.float32)], axis=0)


def second_kernel(pieces, index_ref, state_ref, next_ref, rows_ref, inside_ref, coarse_u_ref, *refs):
    coef_refs, sent_ref = refs[:-1], refs[-1]
    state = state_ref[...]
    later = next_ref[...]
    load = inside_ref[...] + coarse_rows(index_ref, coef_refs, pieces, coarse_u_ref)
    u, phi, sa, sb, dist = (state[i:i + 1] for i in range(5))
    u2, phi2, k1u, k1p = (later[i:i + 1] for i in range(4))
    k2u, k2p = rates(load, u2, phi2, sa, sb, dist)
    u = u + 0.5 * TIME_STEP * (k1u + k2u)
    phi = phi + 0.5 * TIME_STEP * (k1p + k2p)
    elem_count = u.shape[1]
    values = jnp.concatenate([u, phi, jnp.zeros((6, elem_count), jnp.float32)], axis=0)
    sent = select_columns(values, selection(rows_ref[...], elem_count), NN)
    members = sent_ref.shape[0]
    peer_rows = elem_count // members
    for peer in range(members):
        sent_ref[peer, :, 0:peer_rows] = sent[:, peer * peer_rows:(peer + 1) * peer_rows]


def unsort_kernel(got_ref, slot_ref, u_ref, phi_ref, flat_ref):
    members, elem_count = got_ref.shape[0], u_ref.shape[1]
    peer_rows = elem_count // members
    for peer in range(members):
        flat_ref[:, peer * peer_rows:(peer + 1) * peer_rows] = got_ref[peer, :, 0:peer_rows]
    out = select_columns(flat_ref[...], selection(slot_ref[...], elem_count), NN)
    u_ref[...] = out[0:1]
    phi_ref[...] = out[1:2]


def call(kernel, outs, *args, scalars=(), far=(), scratch=(), flops=1000, moved=1000):
    spaces = [SMEM if i in scalars else pl.ANY if i in far else VMEM for i in range(len(args))]
    return pl.pallas_call(
        kernel,
        out_shape=outs,
        in_specs=[pl.BlockSpec(memory_space=space) for space in spaces],
        out_specs=jax.tree.map(lambda _: pl.BlockSpec(memory_space=VMEM), outs),
        scratch_shapes=list(scratch),
        cost_estimate=pl.CostEstimate(flops=flops, bytes_accessed=moved, transcendentals=0),
        compiler_params=pltpu.CompilerParams(vmem_limit_bytes=32 * 1024 * 1024),
    )(*[pltpu.with_memory_space_constraint(v, pltpu.HBM) if i in far else v for i, v in enumerate(args)])


def shape(*dims, dtype=jnp.float32):
    return jax.ShapeDtypeStruct(dims, dtype)


def body(
    ln_rate,
    log_state,
    sigma,
    fric_a,
    fric_b,
    slip_dist,
    leaf_of_elem,
    near_blocks,
    near_col,
    near_count,
    far_u,
    far_v,
    far_col,
    far_rank,
    coarse_u,
    coarse_v,
):
    members = lax.axis_size("blk")
    place = jnp.stack([lax.axis_index("leaf"), lax.axis_index("blk")]).astype(jnp.int32)
    elems = ln_rate.shape[0]
    leaf_size = near_blocks.shape[1]
    groups, rank = coarse_v.shape[0], coarse_v.shape[1]
    pieces = elems // 128
    out_rows = pl.cdiv(pieces + pl.cdiv(groups * rank, 128), 8) * 8

    def swap(value):
        return lax.all_to_all(value, "blk", split_axis=0, concat_axis=0, tiled=True)

    def shifted(value, axis):
        count = lax.axis_size(axis)
        moved = [
            lax.ppermute(value, axis, [(i, (i + shift) % count) for i in range(count)])
            for shift in range(1, count)
        ]
        return [value] + moved

    elem_args = [
        value.reshape(1, elems)
        for value in (ln_rate, log_state, sigma, fric_a, fric_b, slip_dist, leaf_of_elem)
    ]
    weights = [near_blocks] + [
        value.reshape(-1, value.shape[2]) for value in (far_u, far_v, coarse_u, coarse_v)
    ]
    scalar_args = [near_col, far_col, far_rank]
    whole = [shape(*value.shape, dtype=value.dtype) for value in weights]
    sent, slot, near_mask, far_mask, near, far_u, far_v, coarse_u, coarse_v = call(
        functools.partial(sort_kernel, members),
        (
            shape(members, 8, 128),
            shape(1, elems, dtype=jnp.int32),
            shape(near_blocks.shape[0], members, leaf_size),
            shape(members, far_u.shape[0] * far_u.shape[1]),
            *whole,
        ),
        place, near_count, *elem_args, *weights, *scalar_args, scalars=(0, 1), far=range(2, 17),
        scratch=[VMEM(value.shape, value.dtype) for value in elem_args]
        + [SMEM(value.shape, value.dtype) for value in scalar_args]
        + [pltpu.SemaphoreType.DMA((15,))],
    )
    got = swap(sent)
    state, rows, out = call(
        functools.partial(place_kernel, members),
        (shape(8, elems), shape(1, elems, dtype=jnp.int32), shape(out_rows, 128)),
        got, coarse_v, scratch=[VMEM((8, elems), jnp.float32)],
    )

    def section(out):
        everyone = shifted(out, "blk")
        total = call(functools.partial(coef_kernel, pieces), shape(out_rows, 128), *everyone)
        coefs = shifted(total, "leaf")[1:]
        inside = call(
            functools.partial(inside_kernel, members), shape(1, elems),
            *everyone, near, far_u, far_v, near_mask, far_mask,
            scratch=[VMEM((members, leaf_size), jnp.float32)],
            flops=2 * members * near.size, moved=2 * near.size,
        )
        return coefs, inside

    coefs, inside = section(out)
    later, out = call(
        functools.partial(first_kernel, pieces), (shape(8, elems), shape(out_rows, 128)),
        place, state, inside, coarse_u, coarse_v, *coefs, scalars=(0,),
    )
    coefs, inside = section(out)
    sent = call(
        functools.partial(second_kernel, pieces), shape(members, 8, 128),
        place, state, later, rows, inside, coarse_u, *coefs, scalars=(0,),
    )
    u, phi = call(
        unsort_kernel, (shape(1, elems), shape(1, elems)),
        swap(sent), slot, scratch=[VMEM((8, elems), jnp.float32)],
    )
    return u.reshape(elems), phi.reshape(elems)


def solution(mesh):
    each = P(("leaf", "blk"))
    blocks = P(("leaf", "blk"), None, None)
    last = P(None, None, ("leaf", "blk"))
    in_specs = (each,) * 7 + (blocks, each, each, blocks, blocks, each, each, last, last)
    return jax.shard_map(body, mesh=mesh, in_specs=in_specs, out_specs=(each, each), check_vma=False)
```

time: 71.4 us -> 65.5 us (0.917)
  blocking collectives: 40.7 us -> 22.8 us
  waiting for transfers between devices: 2.59 us -> 15.1 us
  starting transfers between devices: 6.5 us -> 19 us
  local copies, waits for them, and re-layouts: 11.7 us -> 0 us
  other arithmetic: 1.37 us -> 0.08 us
  Pallas kernels: 6.26 us -> 7.02 us
    ppermute x0 -> x20, starting transfers between devices: none -> 19 us  [shifted(): lax.ppermute(value, axis, [(i, (i + shift) % count) for i in range(count)])]
    all_to_all x4 -> x2, blocking collectives: 40.7 us -> 22.8 us  [swap(): return lax.all_to_all(value, 'blk', split_axis=0, concat_axis=0, tiled=True)]
    ppermute x0 -> x20, waiting for transfers between devices: none -> 15.1 us  [shifted(): lax.ppermute(value, axis, [(i, (i + shift) % count) for i in range(count)])]
    unnamed x48 -> x0, local copies, waits for them, and re-layouts: 11.2 us -> none
    all_to_all x2 -> x0, starting transfers between devices: 6.5 us -> none  [swap(): return lax.all_to_all(value, axis, split_axis=0, concat_axis=0, tiled=True)]
    all_to_all x2 -> x0, waiting for transfers between devices: 2.59 us -> none  [swap(): return lax.all_to_all(value, axis, split_axis=0, concat_axis=0, tiled=True)]
    all_to_all x2 -> x0, other arithmetic: 1.37 us -> none  [swap(): return lax.all_to_all(value, axis, split_axis=0, concat_axis=0, tiled=True)]
    pallas_call x9, Pallas kernels: 6.26 us -> 7.02 us  [call(): pl.pallas_call(kernel, out_shape=outs, in_specs=[pl.BlockSpec(memory_spac...]
  transfers between devices with their start and end apart: 2 -> 20, of which waited for: 1 -> 8; matrix products, arithmetic and copies ran while one was open for 0% -> 0% of each run, Pallas kernels for 3% -> 2%
where the time goes in v2:
time: 65.5 us; the launch traced here: 65.3 us
  blocking collectives  22.8 us (35%)
  starting transfers between devices  19 us (29%)
  waiting for transfers between devices  15.1 us (23%)
  Pallas kernels  7.02 us (11%)
  between operations  1.34 us (2%)
    all_to_all x2, blocking collectives, swap(): return lax.all_to_all(value, 'blk', split_axis=0, concat_axis=0, tiled=True)  22.8 us
    ppermute x20, starting transfers between devices, shifted(): lax.ppermute(value, axis, [(i, (i + shift) % count) for i in range(count)])  19 us
    ppermute x20, waiting for transfers between devices, shifted(): lax.ppermute(value, axis, [(i, (i + shift) % count) for i in range(count)])  15.1 us
    pallas_call x9, Pallas kernels, call(): pl.pallas_call(kernel, out_shape=outs, in_specs=[pl.BlockSpec(memory_spac...  7.02 us
  transfers between devices with their start and end apart: 20, of which 8 were waited for; matrix products, arithmetic and copies ran while one was open for 0% of the time, Pallas kernels for 2%

profile of v2, /device:TPU:0, one launch (start us, length us, event | category | flops | bytes accessed | tf_op | source)
XLA Modules:
  0.0 65.3 jit_solution(17116003697806052954)
XLA Ops:
  1.4 2.2 %shard_map.167 = (f32[8,8,128]{2,1,0:T(8,128)S(1)}, s32[1,512]{1,0:T(1,128)S(1)}, f32[3,8,512]{2,1,0:T(8,128)S(1)}, f32[8,64]{1,0:T(8,128)S(1)}, bf16[3,512,512]...) custom-call(s32[2]{0:T(128)S(1)} %pad_add_fusion.index_ref, ...), custom_call_target="tpu_custom_call" | custom-call | flops 1000 | bytes 1000 | tf_op jit(solution)/shard_map/pallas_call | solution.py:224
  3.6 13.7 %all_to_all.10.got_ref = f32[8,8,128]{2,1,0:T(8,128)S(1)} all-to-all(f32[8,8,128]{2,1,0:T(8,128)S(1)} %get-tuple-element.18), channel_id=1, replica_groups=mesh['leaf'=4,'blk'=8] {'blk'}, dimensions={0} | all-to-all | bytes 65536 | tf_op jit(solution)/shard_map/all_to_all | solution.py:266
  18.5 1.2 %collective-permute-start.5 = (f32[8,128]{1,0:T(8,128)S(1)}, f32[8,128]{1,0:T(8,128)S(1)}, u32[]{:S(2)}, u32[]{:S(2)}) collective-permute-start(f32[8,128]{1,0:T(8,128)S(1)} %get-tuple-element.21.refs_0_), channel_id=1, source_target_pairs={{0,6},{1,7},{2,0},{3,1},{4,2},{5,3},{6,4},{7,5},{8,14},{9,15},{10,... | collective-permute-start | bytes 12296 | tf_op jit(solution)/shard_map/ppermute | solution.py:271
  19.7 1.4 %collective-permute-start.4 = (f32[8,128]{1,0:T(8,128)S(1)}, f32[8,128]{1,0:T(8,128)S(1)}, u32[]{:S(2)}, u32[]{:S(2)}) collective-permute-start(f32[8,128]{1,0:T(8,128)S(1)} %get-tuple-element.21.refs_0_), channel_id=1, source_target_pairs={{0,5},{1,6},{2,7},{3,0},{4,1},{5,2},{6,3},{7,4},{8,13},{9,14},{10,... | collective-permute-start | bytes 12296 | tf_op jit(solution)/shard_map/ppermute | solution.py:271
  21.2 1.6 %collective-permute-start.3 = (f32[8,128]{1,0:T(8,128)S(1)}, f32[8,128]{1,0:T(8,128)S(1)}, u32[]{:S(2)}, u32[]{:S(2)}) collective-permute-start(f32[8,128]{1,0:T(8,128)S(1)} %get-tuple-element.21.refs_0_), channel_id=1, source_target_pairs={{0,4},{1,5},{2,6},{3,7},{4,0},{5,1},{6,2},{7,3},{8,12},{9,13},{10,... | collective-permute-start | bytes 12296 | tf_op jit(solution)/shard_map/ppermute | solution.py:271
  22.8 1.4 %collective-permute-start.2 = (f32[8,128]{1,0:T(8,128)S(1)}, f32[8,128]{1,0:T(8,128)S(1)}, u32[]{:S(2)}, u32[]{:S(2)}) collective-permute-start(f32[8,128]{1,0:T(8,128)S(1)} %get-tuple-element.21.refs_0_), channel_id=1, source_target_pairs={{0,3},{1,4},{2,5},{3,6},{4,7},{5,0},{6,1},{7,2},{8,11},{9,12},{10,... | collective-permute-start | bytes 12296 | tf_op jit(solution)/shard_map/ppermute | solution.py:271
  24.2 1.6 %collective-permute-start.1 = (f32[8,128]{1,0:T(8,128)S(1)}, f32[8,128]{1,0:T(8,128)S(1)}, u32[]{:S(2)}, u32[]{:S(2)}) collective-permute-start(f32[8,128]{1,0:T(8,128)S(1)} %get-tuple-element.21.refs_0_), channel_id=1, source_target_pairs={{0,2},{1,3},{2,4},{3,5},{4,6},{5,7},{6,0},{7,1},{8,10},{9,11},{10,... | collective-permute-start | bytes 12296 | tf_op jit(solution)/shard_map/ppermute | solution.py:271
  26.2 1.9 %collective-permute-done.2.refs_3_ = f32[8,128]{1,0:T(8,128)S(1)} collective-permute-done((f32[8,128]{1,0:T(8,128)S(1)}, f32[8,128]{1,0:T(8,128)S(1)}, u32[]{:S(2)}, u32[]{:S(2)}) %collective-permute-start.2) | collective-permute-done | bytes 4128 | tf_op jit(solution)/shard_map/ppermute | solution.py:271
  28.2 1.4 %collective-permute-done.1.refs_2_ = f32[8,128]{1,0:T(8,128)S(1)} collective-permute-done((f32[8,128]{1,0:T(8,128)S(1)}, f32[8,128]{1,0:T(8,128)S(1)}, u32[]{:S(2)}, u32[]{:S(2)}) %collective-permute-start.1) | collective-permute-done | bytes 4128 | tf_op jit(solution)/shard_map/ppermute | solution.py:271
  29.6 2.5 %collective-permute-done.refs_1_ = f32[8,128]{1,0:T(8,128)S(1)} collective-permute-done((f32[8,128]{1,0:T(8,128)S(1)}, f32[8,128]{1,0:T(8,128)S(1)}, u32[]{:S(2)}, u32[]{:S(2)}) %collective-permute-start) | collective-permute-done | bytes 4128 | tf_op jit(solution)/shard_map/ppermute | solution.py:271
  32.1 1.6 %collective-permute-start.8 = (f32[8,128]{1,0:T(8,128)S(1)}, f32[8,128]{1,0:T(8,128)S(1)}, u32[]{:S(2)}, u32[]{:S(2)}) collective-permute-start(f32[8,128]{1,0:T(8,128)S(1)} %shard_map.170), channel_id=1, source_target_pairs={{0,16},{8,24},{16,0},{24,8},{1,17},{9,25},{17,1},{25,9},{2,18},{10... | collective-permute-start | bytes 12296 | tf_op jit(solution)/shard_map/ppermute | solution.py:271
  34.6 1.2 %collective-permute-done.8.refs_1_ = f32[8,128]{1,0:T(8,128)S(1)} collective-permute-done((f32[8,128]{1,0:T(8,128)S(1)}, f32[8,128]{1,0:T(8,128)S(1)}, u32[]{:S(2)}, u32[]{:S(2)}) %collective-permute-start.8) | collective-permute-done | bytes 4128 | tf_op jit(solution)/shard_map/ppermute | solution.py:271
  35.8 0.9 %collective-permute-done.7.refs_0_ = f32[8,128]{1,0:T(8,128)S(1)} collective-permute-done((f32[8,128]{1,0:T(8,128)S(1)}, f32[8,128]{1,0:T(8,128)S(1)}, u32[]{:S(2)}, u32[]{:S(2)}) %collective-permute-start.7) | collective-permute-done | bytes 4128 | tf_op jit(solution)/shard_map/ppermute | solution.py:271
  36.8 1.0 %shard_map.171 = (f32[8,512]{1,0:T(8,128)S(1)}, f32[8,128]{1,0:T(8,128)S(1)}) custom-call(s32[2]{0:T(128)S(1)} %pad_add_fusion.index_ref, f32[8,512]{1,0:T(8,128)S(1)} %get-tuple-element.20.state_ref, f32[1,512]{1,0:T(1,128)S(1)} %shard_map.169.inside_ref, bf16[64,512]{1,0:T(8,128)(2,1)S(1)} %get-tuple-element.27.coarse_u_ref, ...), custom_call_target="tpu_custom_call" | custom-call | flops 1000 | bytes 1000 | tf_op jit(solution)/shard_map/pallas_call | solution.py:224
  38.1 0.7 %collective-permute-start.15 = (f32[8,128]{1,0:T(8,128)S(1)}, f32[8,128]{1,0:T(8,128)S(1)}, u32[]{:S(2)}, u32[]{:S(2)}) collective-permute-start(f32[8,128]{1,0:T(8,128)S(1)} %get-tuple-element.30.refs_0_), channel_id=1, source_target_pairs={{0,6},{1,7},{2,0},{3,1},{4,2},{5,3},{6,4},{7,5},{8,14},{9,15},{10,... | collective-permute-start | bytes 12296 | tf_op jit(solution)/shard_map/ppermute | solution.py:271
  39.3 3.3 %collective-permute-start.13 = (f32[8,128]{1,0:T(8,128)S(1)}, f32[8,128]{1,0:T(8,128)S(1)}, u32[]{:S(2)}, u32[]{:S(2)}) collective-permute-start(f32[8,128]{1,0:T(8,128)S(1)} %get-tuple-element.30.refs_0_), channel_id=1, source_target_pairs={{0,4},{1,5},{2,6},{3,7},{4,0},{5,1},{6,2},{7,3},{8,12},{9,13},{10,... | collective-permute-start | bytes 12296 | tf_op jit(solution)/shard_map/ppermute | solution.py:271
  42.6 1.6 %collective-permute-start.11 = (f32[8,128]{1,0:T(8,128)S(1)}, f32[8,128]{1,0:T(8,128)S(1)}, u32[]{:S(2)}, u32[]{:S(2)}) collective-permute-start(f32[8,128]{1,0:T(8,128)S(1)} %get-tuple-element.30.refs_0_), channel_id=1, source_target_pairs={{0,2},{1,3},{2,4},{3,5},{4,6},{5,7},{6,0},{7,1},{8,10},{9,11},{10,... | collective-permute-start | bytes 12296 | tf_op jit(solution)/shard_map/ppermute | solution.py:271
  44.2 1.5 %collective-permute-start.10 = (f32[8,128]{1,0:T(8,128)S(1)}, f32[8,128]{1,0:T(8,128)S(1)}, u32[]{:S(2)}, u32[]{:S(2)}) collective-permute-start(f32[8,128]{1,0:T(8,128)S(1)} %get-tuple-element.30.refs_0_), channel_id=1, source_target_pairs={{0,1},{1,2},{2,3},{3,4},{4,5},{5,6},{6,7},{7,0},{8,9},{9,10},{10,1... | collective-permute-start | bytes 12296 | tf_op jit(solution)/shard_map/ppermute | solution.py:271
  45.7 2.3 %collective-permute-done.12.refs_3_ = f32[8,128]{1,0:T(8,128)S(1)} collective-permute-done((f32[8,128]{1,0:T(8,128)S(1)}, f32[8,128]{1,0:T(8,128)S(1)}, u32[]{:S(2)}, u32[]{:S(2)}) %collective-permute-start.12) | collective-permute-done | bytes 4128 | tf_op jit(solution)/shard_map/ppermute | solution.py:271
  48.0 2.5 %collective-permute-done.10.refs_1_ = f32[8,128]{1,0:T(8,128)S(1)} collective-permute-done((f32[8,128]{1,0:T(8,128)S(1)}, f32[8,128]{1,0:T(8,128)S(1)}, u32[]{:S(2)}, u32[]{:S(2)}) %collective-permute-start.10) | collective-permute-done | bytes 4128 | tf_op jit(solution)/shard_map/ppermute | solution.py:271
  52.1 2.2 %collective-permute-done.18.refs_1_ = f32[8,128]{1,0:T(8,128)S(1)} collective-permute-done((f32[8,128]{1,0:T(8,128)S(1)}, f32[8,128]{1,0:T(8,128)S(1)}, u32[]{:S(2)}, u32[]{:S(2)}) %collective-permute-start.18) | collective-permute-done | bytes 4128 | tf_op jit(solution)/shard_map/ppermute | solution.py:271
  54.3 1.1 %shard_map.174 = f32[8,8,128]{2,1,0:T(8,128)S(1)} custom-call(s32[2]{0:T(128)S(1)} %pad_add_fusion.index_ref, f32[8,512]{1,0:T(8,128)S(1)} %get-tuple-element.20.state_ref, f32[8,512]{1,0:T(8,128)S(1)} %get-tuple-element.28.next_ref, s32[1,512]{1,0:T(1,128)S(1)} %get-tuple-element.29.rows_ref, f32[1,512]{1,0:T(1,128)S(1)} %shard_map.172.inside_ref, ...), custom_call_target="tpu_custom_call" | custom-call | flops 1000 | bytes 1000 | tf_op jit(solution)/shard_map/pallas_call | solution.py:224
  55.4 9.1 %all_to_all.11.got_ref = f32[8,8,128]{2,1,0:T(8,128)S(1)} all-to-all(f32[8,8,128]{2,1,0:T(8,128)S(1)} %shard_map.174), channel_id=1, replica_groups=mesh['leaf'=4,'blk'=8] {'blk'}, dimensions={0} | all-to-all | bytes 65536 | tf_op jit(solution)/shard_map/all_to_all | solution.py:266
  64.5 0.8 %shard_map.175 = (f32[1,512]{1,0:T(1,128)}, f32[1,512]{1,0:T(1,128)}) custom-call(f32[8,8,128]{2,1,0:T(8,128)S(1)} %all_to_all.11.got_ref, s32[1,512]{1,0:T(1,128)S(1)} %get-tuple-element.31.slot_ref), custom_call_target="tpu_custom_call" | custom-call | flops 1000 | bytes 1000 | tf_op jit(solution)/shard_map/pallas_call | solution.py:224
  (28 shorter events, 5.1 us)
Async XLA Ops:
  17.8 6.3 %collective-permute-start.6 = (f32[8,128]{1,0:T(8,128)S(1)}, f32[8,128]{1,0:T(8,128)S(1)}, u32[]{:S(2)}, u32[]{:S(2)}) collective-permute-start(f32[8,128]{1,0:T(8,128)S(1)} %get-tuple-element.21.refs_0_), channel_id=1, source_target_pairs={{0,7},{1,0},{2,1},{3,2},{4,3},{5,4},{6,5},{7,6},{8,15},{9,8},{10,9... | collective-permute-start | bytes 12296 | tf_op jit(solution)/shard_map/ppermute | solution.py:271
  18.5 7.2 %collective-permute-start.5 = (f32[8,128]{1,0:T(8,128)S(1)}, f32[8,128]{1,0:T(8,128)S(1)}, u32[]{:S(2)}, u32[]{:S(2)}) collective-permute-start(f32[8,128]{1,0:T(8,128)S(1)} %get-tuple-element.21.refs_0_), channel_id=1, source_target_pairs={{0,6},{1,7},{2,0},{3,1},{4,2},{5,3},{6,4},{7,5},{8,14},{9,15},{10,... | collective-permute-start | bytes 12296 | tf_op jit(solution)/shard_map/ppermute | solution.py:271
  19.7 6.5 %collective-permute-start.4 = (f32[8,128]{1,0:T(8,128)S(1)}, f32[8,128]{1,0:T(8,128)S(1)}, u32[]{:S(2)}, u32[]{:S(2)}) collective-permute-start(f32[8,128]{1,0:T(8,128)S(1)} %get-tuple-element.21.refs_0_), channel_id=1, source_target_pairs={{0,5},{1,6},{2,7},{3,0},{4,1},{5,2},{6,3},{7,4},{8,13},{9,14},{10,... | collective-permute-start | bytes 12296 | tf_op jit(solution)/shard_map/ppermute | solution.py:271
  21.2 5.1 %collective-permute-start.3 = (f32[8,128]{1,0:T(8,128)S(1)}, f32[8,128]{1,0:T(8,128)S(1)}, u32[]{:S(2)}, u32[]{:S(2)}) collective-permute-start(f32[8,128]{1,0:T(8,128)S(1)} %get-tuple-element.21.refs_0_), channel_id=1, source_target_pairs={{0,4},{1,5},{2,6},{3,7},{4,0},{5,1},{6,2},{7,3},{8,12},{9,13},{10,... | collective-permute-start | bytes 12296 | tf_op jit(solution)/shard_map/ppermute | solution.py:271
  22.8 5.4 %collective-permute-start.2 = (f32[8,128]{1,0:T(8,128)S(1)}, f32[8,128]{1,0:T(8,128)S(1)}, u32[]{:S(2)}, u32[]{:S(2)}) collective-permute-start(f32[8,128]{1,0:T(8,128)S(1)} %get-tuple-element.21.refs_0_), channel_id=1, source_target_pairs={{0,3},{1,4},{2,5},{3,6},{4,7},{5,0},{6,1},{7,2},{8,11},{9,12},{10,... | collective-permute-start | bytes 12296 | tf_op jit(solution)/shard_map/ppermute | solution.py:271
  24.2 5.4 %collective-permute-start.1 = (f32[8,128]{1,0:T(8,128)S(1)}, f32[8,128]{1,0:T(8,128)S(1)}, u32[]{:S(2)}, u32[]{:S(2)}) collective-permute-start(f32[8,128]{1,0:T(8,128)S(1)} %get-tuple-element.21.refs_0_), channel_id=1, source_target_pairs={{0,2},{1,3},{2,4},{3,5},{4,6},{5,7},{6,0},{7,1},{8,10},{9,11},{10,... | collective-permute-start | bytes 12296 | tf_op jit(solution)/shard_map/ppermute | solution.py:271
  25.8 6.3 %collective-permute-start = (f32[8,128]{1,0:T(8,128)S(1)}, f32[8,128]{1,0:T(8,128)S(1)}, u32[]{:S(2)}, u32[]{:S(2)}) collective-permute-start(f32[8,128]{1,0:T(8,128)S(1)} %get-tuple-element.21.refs_0_), channel_id=1, source_target_pairs={{0,1},{1,2},{2,3},{3,4},{4,5},{5,6},{6,7},{7,0},{8,9},{9,10},{10,1... | collective-permute-start | bytes 12296 | tf_op jit(solution)/shard_map/ppermute | solution.py:271
  32.1 2.5 %collective-permute-start.9 = (f32[8,128]{1,0:T(8,128)S(1)}, f32[8,128]{1,0:T(8,128)S(1)}, u32[]{:S(2)}, u32[]{:S(2)}) collective-permute-start(f32[8,128]{1,0:T(8,128)S(1)} %shard_map.170), channel_id=1, source_target_pairs={{0,24},{8,0},{16,8},{24,16},{1,25},{9,1},{17,9},{25,17},{2,26},{10... | collective-permute-start | bytes 12296 | tf_op jit(solution)/shard_map/ppermute | solution.py:271
  32.1 3.7 %collective-permute-start.8 = (f32[8,128]{1,0:T(8,128)S(1)}, f32[8,128]{1,0:T(8,128)S(1)}, u32[]{:S(2)}, u32[]{:S(2)}) collective-permute-start(f32[8,128]{1,0:T(8,128)S(1)} %shard_map.170), channel_id=1, source_target_pairs={{0,16},{8,24},{16,0},{24,8},{1,17},{9,25},{17,1},{25,9},{2,18},{10... | collective-permute-start | bytes 12296 | tf_op jit(solution)/shard_map/ppermute | solution.py:271
  33.7 3.0 %collective-permute-start.7 = (f32[8,128]{1,0:T(8,128)S(1)}, f32[8,128]{1,0:T(8,128)S(1)}, u32[]{:S(2)}, u32[]{:S(2)}) collective-permute-start(f32[8,128]{1,0:T(8,128)S(1)} %shard_map.170), channel_id=1, source_target_pairs={{0,8},{8,16},{16,24},{24,0},{1,9},{9,17},{17,25},{25,1},{2,10},{10... | collective-permute-start | bytes 12296 | tf_op jit(solution)/shard_map/ppermute | solution.py:271
  37.8 4.8 %collective-permute-start.16 = (f32[8,128]{1,0:T(8,128)S(1)}, f32[8,128]{1,0:T(8,128)S(1)}, u32[]{:S(2)}, u32[]{:S(2)}) collective-permute-start(f32[8,128]{1,0:T(8,128)S(1)} %get-tuple-element.30.refs_0_), channel_id=1, source_target_pairs={{0,7},{1,0},{2,1},{3,2},{4,3},{5,4},{6,5},{7,6},{8,15},{9,8},{10,9... | collective-permute-start | bytes 12296 | tf_op jit(solution)/shard_map/ppermute | solution.py:271
  38.1 6.1 %collective-permute-start.15 = (f32[8,128]{1,0:T(8,128)S(1)}, f32[8,128]{1,0:T(8,128)S(1)}, u32[]{:S(2)}, u32[]{:S(2)}) collective-permute-start(f32[8,128]{1,0:T(8,128)S(1)} %get-tuple-element.30.refs_0_), channel_id=1, source_target_pairs={{0,6},{1,7},{2,0},{3,1},{4,2},{5,3},{6,4},{7,5},{8,14},{9,15},{10,... | collective-permute-start | bytes 12296 | tf_op jit(solution)/shard_map/ppermute | solution.py:271
  38.9 6.8 %collective-permute-start.14 = (f32[8,128]{1,0:T(8,128)S(1)}, f32[8,128]{1,0:T(8,128)S(1)}, u32[]{:S(2)}, u32[]{:S(2)}) collective-permute-start(f32[8,128]{1,0:T(8,128)S(1)} %get-tuple-element.30.refs_0_), channel_id=1, source_target_pairs={{0,5},{1,6},{2,7},{3,0},{4,1},{5,2},{6,3},{7,4},{8,13},{9,14},{10,... | collective-permute-start | bytes 12296 | tf_op jit(solution)/shard_map/ppermute | solution.py:271
  39.3 6.4 %collective-permute-start.13 = (f32[8,128]{1,0:T(8,128)S(1)}, f32[8,128]{1,0:T(8,128)S(1)}, u32[]{:S(2)}, u32[]{:S(2)}) collective-permute-start(f32[8,128]{1,0:T(8,128)S(1)} %get-tuple-element.30.refs_0_), channel_id=1, source_target_pairs={{0,4},{1,5},{2,6},{3,7},{4,0},{5,1},{6,2},{7,3},{8,12},{9,13},{10,... | collective-permute-start | bytes 12296 | tf_op jit(solution)/shard_map/ppermute | solution.py:271
  42.6 5.4 %collective-permute-start.12 = (f32[8,128]{1,0:T(8,128)S(1)}, f32[8,128]{1,0:T(8,128)S(1)}, u32[]{:S(2)}, u32[]{:S(2)}) collective-permute-start(f32[8,128]{1,0:T(8,128)S(1)} %get-tuple-element.30.refs_0_), channel_id=1, source_target_pairs={{0,3},{1,4},{2,5},{3,6},{4,7},{5,0},{6,1},{7,2},{8,11},{9,12},{10,... | collective-permute-start | bytes 12296 | tf_op jit(solution)/shard_map/ppermute | solution.py:271
  42.6 5.4 %collective-permute-start.11 = (f32[8,128]{1,0:T(8,128)S(1)}, f32[8,128]{1,0:T(8,128)S(1)}, u32[]{:S(2)}, u32[]{:S(2)}) collective-permute-start(f32[8,128]{1,0:T(8,128)S(1)} %get-tuple-element.30.refs_0_), channel_id=1, source_target_pairs={{0,2},{1,3},{2,4},{3,5},{4,6},{5,7},{6,0},{7,1},{8,10},{9,11},{10,... | collective-permute-start | bytes 12296 | tf_op jit(solution)/shard_map/ppermute | solution.py:271
  44.2 6.3 %collective-permute-start.10 = (f32[8,128]{1,0:T(8,128)S(1)}, f32[8,128]{1,0:T(8,128)S(1)}, u32[]{:S(2)}, u32[]{:S(2)}) collective-permute-start(f32[8,128]{1,0:T(8,128)S(1)} %get-tuple-element.30.refs_0_), channel_id=1, source_target_pairs={{0,1},{1,2},{2,3},{3,4},{4,5},{5,6},{6,7},{7,0},{8,9},{9,10},{10,1... | collective-permute-start | bytes 12296 | tf_op jit(solution)/shard_map/ppermute | solution.py:271
  50.5 1.6 %collective-permute-start.19 = (f32[8,128]{1,0:T(8,128)S(1)}, f32[8,128]{1,0:T(8,128)S(1)}, u32[]{:S(2)}, u32[]{:S(2)}) collective-permute-start(f32[8,128]{1,0:T(8,128)S(1)} %shard_map.173), channel_id=1, source_target_pairs={{0,24},{8,0},{16,8},{24,16},{1,25},{9,1},{17,9},{25,17},{2,26},{10... | collective-permute-start | bytes 12296 | tf_op jit(solution)/shard_map/ppermute | solution.py:271
  50.6 3.7 %collective-permute-start.18 = (f32[8,128]{1,0:T(8,128)S(1)}, f32[8,128]{1,0:T(8,128)S(1)}, u32[]{:S(2)}, u32[]{:S(2)}) collective-permute-start(f32[8,128]{1,0:T(8,128)S(1)} %shard_map.173), channel_id=1, source_target_pairs={{0,16},{8,24},{16,0},{24,8},{1,17},{9,25},{17,1},{25,9},{2,18},{10... | collective-permute-start | bytes 12296 | tf_op jit(solution)/shard_map/ppermute | solution.py:271
  51.2 3.1 %collective-permute-start.17 = (f32[8,128]{1,0:T(8,128)S(1)}, f32[8,128]{1,0:T(8,128)S(1)}, u32[]{:S(2)}, u32[]{:S(2)}) collective-permute-start(f32[8,128]{1,0:T(8,128)S(1)} %shard_map.173), channel_id=1, source_target_pairs={{0,8},{8,16},{16,24},{24,0},{1,9},{9,17},{17,25},{25,1},{2,10},{10... | collective-permute-start | bytes 12296 | tf_op jit(solution)/shard_map/ppermute | solution.py:271

commit v3 on v2

v3 whole, which is shorter than its diff:
```python
import functools

import jax
import jax.numpy as jnp
from jax import lax
from jax.experimental import pallas as pl
from jax.experimental.pallas import tpu as pltpu
from jax.sharding import PartitionSpec as P

DAMPING = 0.5
PLATE_RATE = 1.0
TIME_STEP = 0.2

NN = (((1,), (0,)), ((), ()))
NT = (((1,), (1,)), ((), ()))
VMEM = pltpu.VMEM
SMEM = pltpu.SMEM


def dot(left, right, dims):
    return lax.dot_general(left, right, dims, preferred_element_type=jnp.float32)


def selection(index_row, count):
    rows = lax.broadcasted_iota(jnp.int32, (count, index_row.shape[1]), 0)
    return jnp.where(rows == index_row, 1.0, 0.0).astype(jnp.bfloat16)


def select_columns(values, matrix, dims):
    high = values.astype(jnp.bfloat16).astype(jnp.float32)
    rest = values - high
    middle = rest.astype(jnp.bfloat16).astype(jnp.float32)
    parts = jnp.concatenate([high, middle, rest - middle], axis=0).astype(jnp.bfloat16)
    moved = dot(parts, matrix, dims)
    return moved[0:8] + moved[8:16] + moved[16:24]


def merged(held, came, width, bit):
    block = lax.broadcasted_iota(jnp.int32, held.shape, 1) // width
    return jnp.where((block >> bit) & 1 == 1, came, held)


def merge_kernel(width, bit, held_ref, came_ref, out_ref):
    out_ref[...] = merged(held_ref[...], came_ref[...], width, bit)


def stack_kernel(held_ref, came_ref, out_ref):
    count = held_ref.shape[0]
    out_ref[0:count, :] = held_ref[...]
    out_ref[count:2 * count, :] = came_ref[...]


def start_copies(sources, targets, sems):
    copies = [
        pltpu.make_async_copy(source, target, sems.at[i])
        for i, (source, target) in enumerate(zip(sources, targets))
    ]
    for copy in copies:
        copy.start()
    return copies


def sort_kernel(members, index_ref, *refs):
    elem_refs, sent_ref, slot_ref, bufs, sems = refs[:7], refs[7], refs[8], refs[9:16], refs[16]
    copies = start_copies(elem_refs, bufs, sems)
    elem_count = bufs[0].shape[1]
    peer_rows = elem_count // members
    before = lax.broadcasted_iota(jnp.int32, (elem_count, elem_count), 0)
    after = lax.broadcasted_iota(jnp.int32, (elem_count, elem_count), 1)
    triangle = jnp.where(before < after, 1.0, 0.0).astype(jnp.bfloat16)
    for copy in copies:
        copy.wait()
    u, phi, sigma, fric_a, fric_b, dist, leaf = (buf[...] for buf in bufs)
    local = leaf - index_ref[0] * (members * elem_count)
    target = local // elem_count
    target_row = local - target * elem_count
    onehot = selection(target, members)
    earlier = dot(onehot, triangle, NN)
    rank = jnp.sum(earlier * onehot.astype(jnp.float32), axis=0, keepdims=True)
    slot = (target ^ index_ref[1]) * peer_rows + rank.astype(jnp.int32)
    slot_ref[...] = slot
    rows = [u, phi, sigma * fric_a, sigma * fric_b, dist, target_row.astype(jnp.float32)]
    pad = jnp.zeros((8 - len(rows), elem_count), jnp.float32)
    values = jnp.concatenate(rows + [pad], axis=0)
    sent_ref[...] = select_columns(values, selection(slot, elem_count), NT)


def load_kernel(members, index_ref, near_count, *refs):
    near_ref, far_u_ref, far_v_ref, coarse_u_ref, coarse_v_ref = refs[:5]
    scalar_refs, outs, scalar_bufs, sems = refs[5:8], refs[8:15], refs[15:18], refs[18]
    near_mask_ref, far_mask_ref, near_out, far_u_out, far_v_out, coarse_u_out, coarse_v_out = outs
    groups, rank = coarse_u_ref.shape[0], coarse_u_ref.shape[1]
    sources = [*scalar_refs, near_ref, far_u_ref, far_v_ref]
    targets = [*scalar_bufs, near_out, far_u_out, far_v_out]
    for shift in range(groups):
        group = index_ref[0] ^ shift
        span = pl.ds(shift * rank, rank)
        sources += [coarse_u_ref.at[group], coarse_v_ref.at[group]]
        targets += [coarse_u_out.at[span, :], coarse_v_out.at[span, :]]
    copies = start_copies(sources, targets, sems)
    for copy in copies[:3]:
        copy.wait()
    near_col, far_col, far_rank = scalar_bufs
    far_slots = far_col.shape[0]
    far_width = far_mask_ref.shape[1] // far_slots
    block = lax.broadcasted_iota(jnp.int32, near_mask_ref.shape[1:], 0) ^ index_ref[1]
    for number in range(near_mask_ref.shape[0]):
        column = jnp.where(number < near_count[0], near_col[number], -1)
        near_mask_ref[number] = jnp.where(block == column, 1.0, 0.0)
    block = lax.broadcasted_iota(jnp.int32, far_mask_ref.shape, 0) ^ index_ref[1]
    lane = lax.broadcasted_iota(jnp.int32, far_mask_ref.shape, 1)
    column = jnp.full(far_mask_ref.shape, -1, jnp.int32)
    for number in range(far_slots):
        low = number * far_width
        mine = (lane >= low) & (lane < low + far_rank[number])
        column = jnp.where(mine, far_col[number], column)
    far_mask_ref[...] = jnp.where(block == column, 1.0, 0.0)
    for copy in copies[3:]:
        copy.wait()


def outgoing(deficit, coarse_v_ref, out_ref):
    elem_count = deficit.shape[1]
    wide = jnp.broadcast_to(deficit, (8, elem_count)).astype(jnp.bfloat16)
    partial = dot(wide, coarse_v_ref[...], NT)[0:1]
    width = partial.shape[1]
    out_ref[:, 0:elem_count] = deficit
    if elem_count + width < out_ref.shape[1]:
        out_ref[:, elem_count + width:] = jnp.zeros((1, out_ref.shape[1] - elem_count - width), jnp.float32)
    out_ref[:, elem_count:elem_count + width] = partial


def place_kernel(members, bit, held_ref, came_ref, coarse_v_ref, state_ref, rows_ref, out_ref):
    elem_count = held_ref.shape[1]
    flat = merged(held_ref[...], came_ref[...], elem_count // members, bit)
    rows = flat[5:6].astype(jnp.int32)
    rows_ref[...] = rows
    state = select_columns(flat, selection(rows, elem_count), NT)
    state_ref[...] = state
    deficit = (PLATE_RATE - jnp.exp(state[0:1])).astype(jnp.bfloat16).astype(jnp.float32)
    outgoing(deficit, coarse_v_ref, out_ref)


def gather_kernel(held_ref, came_ref, all_ref, total_ref):
    stack_kernel(held_ref, came_ref, all_ref)
    low = all_ref.shape[1] - total_ref.shape[1]
    total_ref[...] = jnp.sum(all_ref[:, low:], axis=0, keepdims=True)


def inside_kernel(all_ref, near_ref, far_u_ref, far_v_ref, near_mask_ref, far_mask_ref, out_ref):
    leaf_size = near_ref.shape[2]
    deficits = all_ref[:, 0:leaf_size]
    total = jnp.zeros(deficits.shape, jnp.float32)
    for slot in range(near_ref.shape[0]):
        source = (deficits * near_mask_ref[slot]).astype(jnp.bfloat16)
        total = total + dot(source, near_ref[slot], NT)
    project = dot(deficits.astype(jnp.bfloat16), far_v_ref[...], NT) * far_mask_ref[...]
    project = jnp.sum(project, axis=0, keepdims=True)
    project = jnp.broadcast_to(project, (8, project.shape[1])).astype(jnp.bfloat16)
    far = dot(project, far_u_ref[...], NN)
    out_ref[...] = jnp.sum(total, axis=0, keepdims=True) + far[0:1]


def rates(load, ln_now, state_now, sa, sb, dist):
    velocity = jnp.exp(ln_now)
    state_rate = (jnp.exp(-state_now) - velocity) / dist
    log_rate = (load - sb * state_rate) / (sa + DAMPING * velocity)
    return log_rate, state_rate


def coarse_rows(rank, bit, held_ref, came_ref, coarse_u_ref):
    width = coarse_u_ref.shape[0]
    weights = merged(held_ref[...], came_ref[...], rank, bit)[:, 0:width]
    lane = lax.broadcasted_iota(jnp.int32, weights.shape, 1)
    weights = jnp.where(lane >= rank, weights, 0.0)
    weights = jnp.broadcast_to(weights, (8, width)).astype(jnp.bfloat16)
    return dot(weights, coarse_u_ref[...], NN)[0:1]


def first_kernel(rank, bit, state_ref, inside_ref, held_ref, came_ref, coarse_u_ref, coarse_v_ref, next_ref, out_ref):
    state = state_ref[...]
    load = inside_ref[...] + coarse_rows(rank, bit, held_ref, came_ref, coarse_u_ref)
    u, phi, sa, sb, dist = (state[i:i + 1] for i in range(5))
    k1u, k1p = rates(load, u, phi, sa, sb, dist)
    u2 = u + TIME_STEP * k1u
    phi2 = phi + TIME_STEP * k1p
    deficit = (PLATE_RATE - jnp.exp(u2)).astype(jnp.bfloat16).astype(jnp.float32)
    outgoing(deficit, coarse_v_ref, out_ref)
    next_ref[...] = jnp.concatenate([u2, phi2, k1u, k1p, jnp.zeros((4, u.shape[1]), jnp.float32)], axis=0)


def second_kernel(rank, bit, state_ref, next_ref, rows_ref, inside_ref, held_ref, came_ref, coarse_u_ref, sent_ref):
    state = state_ref[...]
    later = next_ref[...]
    load = inside_ref[...] + coarse_rows(rank, bit, held_ref, came_ref, coarse_u_ref)
    u, phi, sa, sb, dist = (state[i:i + 1] for i in range(5))
    u2, phi2, k1u, k1p = (later[i:i + 1] for i in range(4))
    k2u, k2p = rates(load, u2, phi2, sa, sb, dist)
    u = u + 0.5 * TIME_STEP * (k1u + k2u)
    phi = phi + 0.5 * TIME_STEP * (k1p + k2p)
    elem_count = u.shape[1]
    values = jnp.concatenate([u, phi, jnp.zeros((6, elem_count), jnp.float32)], axis=0)
    sent_ref[...] = select_columns(values, selection(rows_ref[...], elem_count), NN)[0:2]


def unsort_kernel(members, bit, held_ref, came_ref, slot_ref, u_ref, phi_ref):
    elem_count = held_ref.shape[1]
    flat = merged(held_ref[...], came_ref[...], elem_count // members, bit)
    flat = jnp.concatenate([flat, jnp.zeros((6, elem_count), jnp.float32)], axis=0)
    out = select_columns(flat, selection(slot_ref[...], elem_count), NN)
    u_ref[...] = out[0:1]
    phi_ref[...] = out[1:2]


def call(kernel, outs, *args, scalars=(), far=(), scratch=(), flops=1000, moved=1000):
    spaces = [SMEM if i in scalars else pl.ANY if i in far else VMEM for i in range(len(args))]
    args = [
        pltpu.with_memory_space_constraint(arg, pltpu.HBM) if i in far else arg
        for i, arg in enumerate(args)
    ]
    return pl.pallas_call(
        kernel,
        out_shape=outs,
        in_specs=[pl.BlockSpec(memory_space=space) for space in spaces],
        out_specs=jax.tree.map(lambda _: pl.BlockSpec(memory_space=VMEM), outs),
        scratch_shapes=list(scratch),
        cost_estimate=pl.CostEstimate(flops=flops, bytes_accessed=moved, transcendentals=0),
        compiler_params=pltpu.CompilerParams(vmem_limit_bytes=32 * 1024 * 1024),
    )(*args)


def shape(*dims, dtype=jnp.float32):
    return jax.ShapeDtypeStruct(dims, dtype)


def body(
    ln_rate,
    log_state,
    sigma,
    fric_a,
    fric_b,
    slip_dist,
    leaf_of_elem,
    near_blocks,
    near_col,
    near_count,
    far_u,
    far_v,
    far_col,
    far_rank,
    coarse_u,
    coarse_v,
):
    members = lax.axis_size("blk")
    place = jnp.stack([lax.axis_index("leaf"), lax.axis_index("blk")]).astype(jnp.int32)
    elems = ln_rate.shape[0]
    leaf_size = near_blocks.shape[1]
    groups, rank = coarse_v.shape[0], coarse_v.shape[1]
    width = pl.cdiv(groups * rank, 128) * 128
    block_bits = range(members.bit_length() - 1)
    group_bits = range(groups.bit_length() - 1)

    def partner(value, axis, bit):
        count = lax.axis_size(axis)
        return lax.ppermute(value, axis, [(i, i ^ (1 << bit)) for i in range(count)])

    def trade(value, axis, bits, lanes):
        for bit in bits[:-1]:
            came = partner(value, axis, bit)
            value = call(
                functools.partial(merge_kernel, lanes, bit), shape(*value.shape), value, came
            )
        return value, partner(value, axis, bits[-1])

    elem_args = [
        value.reshape(1, elems)
        for value in (ln_rate, log_state, sigma, fric_a, fric_b, slip_dist, leaf_of_elem)
    ]
    sent, slot = call(
        functools.partial(sort_kernel, members),
        (shape(8, elems), shape(1, elems, dtype=jnp.int32)),
        place, *elem_args, scalars=(0,), far=range(1, 8),
        scratch=[VMEM(value.shape, value.dtype) for value in elem_args]
        + [pltpu.SemaphoreType.DMA((7,))],
    )
    weights = [
        near_blocks, far_u.reshape(-1, leaf_size), far_v.reshape(-1, leaf_size), coarse_u, coarse_v
    ]
    scalar_args = [near_col, far_col, far_rank]
    far_rows = weights[1].shape[0]
    near_mask, far_mask, near, far_u, far_v, coarse_u, coarse_v = call(
        functools.partial(load_kernel, members),
        (
            shape(near_blocks.shape[0], members, leaf_size),
            shape(members, far_rows),
            shape(*near_blocks.shape, dtype=jnp.bfloat16),
            shape(far_rows, leaf_size, dtype=jnp.bfloat16),
            shape(far_rows, leaf_size, dtype=jnp.bfloat16),
            shape(groups * rank, elems, dtype=jnp.bfloat16),
            shape(groups * rank, elems, dtype=jnp.bfloat16),
        ),
        place, near_count, *weights, *scalar_args, scalars=(0, 1), far=range(2, 10),
        scratch=[SMEM(value.shape, value.dtype) for value in scalar_args]
        + [pltpu.SemaphoreType.DMA((6 + 2 * groups,))],
        flops=2 * near_blocks.size, moved=2 * near_blocks.size * 2,
    )
    held, came = trade(sent, "blk", block_bits, elems // members)
    state, rows, out = call(
        functools.partial(place_kernel, members, block_bits[-1]),
        (shape(8, elems), shape(1, elems, dtype=jnp.int32), shape(1, elems + width)),
        held, came, coarse_v,
    )

    def section(out):
        for bit in block_bits[:-1]:
            out = call(
                stack_kernel, shape(2 * out.shape[0], out.shape[1]), out, partner(out, "blk", bit)
            )
        everyone, total = call(
            gather_kernel, (shape(members, elems + width), shape(1, width)),
            out, partner(out, "blk", block_bits[-1]),
        )
        coefs = trade(total, "leaf", group_bits, rank)
        inside = call(
            inside_kernel, shape(1, elems), everyone, near, far_u, far_v, near_mask, far_mask,
            flops=2 * members * near.size, moved=2 * near.size,
        )
        return coefs, inside

    coefs, inside = section(out)
    later, out = call(
        functools.partial(first_kernel, rank, group_bits[-1]),
        (shape(8, elems), shape(1, elems + width)),
        state, inside, *coefs, coarse_u, coarse_v,
    )
    coefs, inside = section(out)
    sent = call(
        functools.partial(second_kernel, rank, group_bits[-1]), shape(2, elems),
        state, later, rows, inside, *coefs, coarse_u,
    )
    held, came = trade(sent, "blk", block_bits, elems // members)
    u, phi = call(
        functools.partial(unsort_kernel, members, block_bits[-1]),
        (shape(1, elems), shape(1, elems)),
        held, came, slot,
    )
    return u.reshape(elems), phi.reshape(elems)


def solution(mesh):
    each = P(("leaf", "blk"))
    blocks = P(("leaf", "blk"), None, None)
    last = P(None, None, ("leaf", "blk"))
    in_specs = (each,) * 7 + (blocks, each, each, blocks, blocks, each, each, last, last)
    return jax.shard_map(body, mesh=mesh, in_specs=in_specs, out_specs=(each, each), check_vma=False)
```

time: 65.5 us -> 64.1 us (0.979)
  blocking collectives: 22.8 us -> 0 us
  waiting for transfers between devices: 15.1 us -> 28.7 us
  starting transfers between devices: 19 us -> 26.5 us
    all_to_all x2 -> x0, blocking collectives: 22.8 us -> none  [swap(): return lax.all_to_all(value, 'blk', split_axis=0, concat_axis=0, tiled=True)]
    ppermute x20 -> x16, waiting for transfers between devices: 15.1 us -> 28.7 us  [partner(): return lax.ppermute(value, axis, [(i, i ^ 1 << bit) for i in range(count)])]
    ppermute x20 -> x16, starting transfers between devices: 19 us -> 26.5 us  [partner(): return lax.ppermute(value, axis, [(i, i ^ 1 << bit) for i in range(count)])]
    pallas_call x9 -> x20, Pallas kernels: 7.02 us -> 7.14 us  [call(): pl.pallas_call(kernel, out_shape=outs, in_specs=[pl.BlockSpec(memory_spac...]
  transfers between devices with their start and end apart: 20 -> 16, of which waited for: 8 -> 15; matrix products, arithmetic and copies ran while one was open for 0% -> 0% of each run, Pallas kernels for 2% -> 5%
where the time goes in v3:
time: 64.1 us; the launch traced here: 63.9 us
  waiting for transfers between devices  28.7 us (45%)
  starting transfers between devices  26.5 us (41%)
  Pallas kernels  7.14 us (11%)
  between operations  1.37 us (2%)
    ppermute x16, waiting for transfers between devices, partner(): return lax.ppermute(value, axis, [(i, i ^ 1 << bit) for i in range(count)])  28.7 us
    ppermute x16, starting transfers between devices, partner(): return lax.ppermute(value, axis, [(i, i ^ 1 << bit) for i in range(count)])  26.5 us
    pallas_call x20, Pallas kernels, call(): pl.pallas_call(kernel, out_shape=outs, in_specs=[pl.BlockSpec(memory_spac...  7.14 us
  transfers between devices with their start and end apart: 16, of which 15 were waited for; matrix products, arithmetic and copies ran while one was open for 0% of the time, Pallas kernels for 5%

profile of v3, /device:TPU:0, one launch (start us, length us, event | category | flops | bytes accessed | tf_op | source)
XLA Modules:
  0.0 63.9 jit_solution(12022104110666614302)
XLA Ops:
  0.7 1.8 %shard_map.167 = (f32[8,512]{1,0:T(8,128)S(1)}, s32[1,512]{1,0:T(1,128)S(1)}) custom-call(s32[2]{0:T(128)S(1)} %pad_add_fusion.index_ref, f32[1,512]{1,0:T(1,128)} %bitcast.15, f32[1,512]{1,0:T(1,128)} %bitcast.16, f32[1,512]{1,0:T(1,128)} %bitcast.17, f32[1,512]{1,0:T(1,128)} %bitcast.18, f32[1,512]{1,0:T(1,128)} %bitcast.19, f32[1,512]{1,0:T(1,128)} %bitcast.20, ...), custom_call_target="tpu_custom_call" | custom-call | flops 1000 | bytes 1000 | tf_op jit(solution)/shard_map/pallas_call | solution.py:221
  2.6 3.0 %collective-permute-start = (f32[8,512]{1,0:T(8,128)S(1)}, f32[8,512]{1,0:T(8,128)S(1)}, u32[]{:S(2)}, u32[]{:S(2)}) collective-permute-start(f32[8,512]{1,0:T(8,128)S(1)} %get-tuple-element.22.held_ref), channel_id=1, source_target_pairs={{0,1},{1,0},{2,3},{3,2},{4,5},{5,4},{6,7},{7,6},{8,9},{9,8},{10,11... | collective-permute-start | bytes 49160 | tf_op jit(solution)/shard_map/ppermute | solution.py:265
  5.6 1.7 %collective-permute-done.came_ref = f32[8,512]{1,0:T(8,128)S(1)} collective-permute-done((f32[8,512]{1,0:T(8,128)S(1)}, f32[8,512]{1,0:T(8,128)S(1)}, u32[]{:S(2)}, u32[]{:S(2)}) %collective-permute-start) | collective-permute-done | bytes 16416 | tf_op jit(solution)/shard_map/ppermute | solution.py:265
  7.3 2.2 %collective-permute-start.1 = (f32[8,512]{1,0:T(8,128)S(1)}, f32[8,512]{1,0:T(8,128)S(1)}, u32[]{:S(2)}, u32[]{:S(2)}) collective-permute-start(f32[8,512]{1,0:T(8,128)S(1)} %shard_map.168.held_ref), channel_id=1, source_target_pairs={{0,2},{1,3},{2,0},{3,1},{4,6},{5,7},{6,4},{7,5},{8,10},{9,11},{10,... | collective-permute-start | bytes 49160 | tf_op jit(solution)/shard_map/ppermute | solution.py:265
  9.5 1.7 %collective-permute-done.1.came_ref = f32[8,512]{1,0:T(8,128)S(1)} collective-permute-done((f32[8,512]{1,0:T(8,128)S(1)}, f32[8,512]{1,0:T(8,128)S(1)}, u32[]{:S(2)}, u32[]{:S(2)}) %collective-permute-start.1) | collective-permute-done | bytes 16416 | tf_op jit(solution)/shard_map/ppermute | solution.py:265
  11.2 3.1 %collective-permute-start.2 = (f32[8,512]{1,0:T(8,128)S(1)}, f32[8,512]{1,0:T(8,128)S(1)}, u32[]{:S(2)}, u32[]{:S(2)}) collective-permute-start(f32[8,512]{1,0:T(8,128)S(1)} %shard_map.169.held_ref), channel_id=1, source_target_pairs={{0,4},{1,5},{2,6},{3,7},{4,0},{5,1},{6,2},{7,3},{8,12},{9,13},{10,... | collective-permute-start | bytes 49160 | tf_op jit(solution)/shard_map/ppermute | solution.py:265
  14.9 2.1 %shard_map.170 = (f32[3,8,512]{2,1,0:T(8,128)S(1)}, f32[8,64]{1,0:T(8,128)S(1)}, bf16[3,512,512]{2,1,0:T(8,128)(2,1)S(1)}, bf16[64,512]{1,0:T(8,128)(2,1)S(1)}, ...) custom-call(s32[2]{0:T(128)S(1)} %pad_add_fusion.index_ref, ...), custom_call_target="tpu_custom_call" | custom-call | flops 1572864 | bytes 3145728 | tf_op jit(solution)/shard_map/pallas_call | solution.py:221
  19.0 2.1 %collective-permute-done.3.came_ref = f32[1,640]{1,0:T(1,128)S(1)} collective-permute-done((f32[1,640]{1,0:T(1,128)S(1)}, f32[1,640]{1,0:T(1,128)S(1)}, u32[]{:S(2)}, u32[]{:S(2)}) %collective-permute-start.3) | collective-permute-done | bytes 2592 | tf_op jit(solution)/shard_map/ppermute | solution.py:265
  21.1 1.6 %collective-permute-start.4 = (f32[2,640]{1,0:T(2,128)S(1)}, f32[2,640]{1,0:T(2,128)S(1)}, u32[]{:S(2)}, u32[]{:S(2)}) collective-permute-start(f32[2,640]{1,0:T(2,128)S(1)} %shard_map.172.held_ref), channel_id=1, source_target_pairs={{0,2},{1,3},{2,0},{3,1},{4,6},{5,7},{6,4},{7,5},{8,10},{9,11},{10,... | collective-permute-start | bytes 15368 | tf_op jit(solution)/shard_map/ppermute | solution.py:265
  22.7 2.0 %collective-permute-done.4.came_ref = f32[2,640]{1,0:T(2,128)S(1)} collective-permute-done((f32[2,640]{1,0:T(2,128)S(1)}, f32[2,640]{1,0:T(2,128)S(1)}, u32[]{:S(2)}, u32[]{:S(2)}) %collective-permute-start.4) | collective-permute-done | bytes 5152 | tf_op jit(solution)/shard_map/ppermute | solution.py:265
  24.7 1.9 %collective-permute-start.5 = (f32[4,640]{1,0:T(4,128)S(1)}, f32[4,640]{1,0:T(4,128)S(1)}, u32[]{:S(2)}, u32[]{:S(2)}) collective-permute-start(f32[4,640]{1,0:T(4,128)S(1)} %shard_map.173.held_ref), channel_id=1, source_target_pairs={{0,4},{1,5},{2,6},{3,7},{4,0},{5,1},{6,2},{7,3},{8,12},{9,13},{10,... | collective-permute-start | bytes 30728 | tf_op jit(solution)/shard_map/ppermute | solution.py:265
  26.6 2.7 %collective-permute-done.5.came_ref = f32[4,640]{1,0:T(4,128)S(1)} collective-permute-done((f32[4,640]{1,0:T(4,128)S(1)}, f32[4,640]{1,0:T(4,128)S(1)}, u32[]{:S(2)}, u32[]{:S(2)}) %collective-permute-start.5) | collective-permute-done | bytes 10272 | tf_op jit(solution)/shard_map/ppermute | solution.py:265
  35.8 2.1 %collective-permute-done.8.came_ref = f32[1,640]{1,0:T(1,128)S(1)} collective-permute-done((f32[1,640]{1,0:T(1,128)S(1)}, f32[1,640]{1,0:T(1,128)S(1)}, u32[]{:S(2)}, u32[]{:S(2)}) %collective-permute-start.8) | collective-permute-done | bytes 2592 | tf_op jit(solution)/shard_map/ppermute | solution.py:265
  37.9 1.6 %collective-permute-start.9 = (f32[2,640]{1,0:T(2,128)S(1)}, f32[2,640]{1,0:T(2,128)S(1)}, u32[]{:S(2)}, u32[]{:S(2)}) collective-permute-start(f32[2,640]{1,0:T(2,128)S(1)} %shard_map.178.held_ref), channel_id=1, source_target_pairs={{0,2},{1,3},{2,0},{3,1},{4,6},{5,7},{6,4},{7,5},{8,10},{9,11},{10,... | collective-permute-start | bytes 15368 | tf_op jit(solution)/shard_map/ppermute | solution.py:265
  39.5 2.0 %collective-permute-done.9.came_ref = f32[2,640]{1,0:T(2,128)S(1)} collective-permute-done((f32[2,640]{1,0:T(2,128)S(1)}, f32[2,640]{1,0:T(2,128)S(1)}, u32[]{:S(2)}, u32[]{:S(2)}) %collective-permute-start.9) | collective-permute-done | bytes 5152 | tf_op jit(solution)/shard_map/ppermute | solution.py:265
  41.5 1.9 %collective-permute-start.10 = (f32[4,640]{1,0:T(4,128)S(1)}, f32[4,640]{1,0:T(4,128)S(1)}, u32[]{:S(2)}, u32[]{:S(2)}) collective-permute-start(f32[4,640]{1,0:T(4,128)S(1)} %shard_map.179.held_ref), channel_id=1, source_target_pairs={{0,4},{1,5},{2,6},{3,7},{4,0},{5,1},{6,2},{7,3},{8,12},{9,13},{10,... | collective-permute-start | bytes 30728 | tf_op jit(solution)/shard_map/ppermute | solution.py:265
  43.4 2.7 %collective-permute-done.10.came_ref = f32[4,640]{1,0:T(4,128)S(1)} collective-permute-done((f32[4,640]{1,0:T(4,128)S(1)}, f32[4,640]{1,0:T(4,128)S(1)}, u32[]{:S(2)}, u32[]{:S(2)}) %collective-permute-start.10) | collective-permute-done | bytes 10272 | tf_op jit(solution)/shard_map/ppermute | solution.py:265
  47.3 1.5 %collective-permute-start.12 = (f32[1,128]{1,0:T(1,128)S(1)}, f32[1,128]{1,0:T(1,128)S(1)}, u32[]{:S(2)}, u32[]{:S(2)}) collective-permute-start(f32[1,128]{1,0:T(1,128)S(1)} %shard_map.182.held_ref), channel_id=1, source_target_pairs={{0,16},{8,24},{16,0},{24,8},{1,17},{9,25},{17,1},{25,9},{2,18},{10... | collective-permute-start | bytes 1544 | tf_op jit(solution)/shard_map/ppermute | solution.py:265
  51.1 1.6 %collective-permute-start.13 = (f32[2,512]{1,0:T(2,128)S(1)}, f32[2,512]{1,0:T(2,128)S(1)}, u32[]{:S(2)}, u32[]{:S(2)}) collective-permute-start(f32[2,512]{1,0:T(2,128)S(1)} %shard_map.183.held_ref), channel_id=1, source_target_pairs={{0,1},{1,0},{2,3},{3,2},{4,5},{5,4},{6,7},{7,6},{8,9},{9,8},{10,11... | collective-permute-start | bytes 12296 | tf_op jit(solution)/shard_map/ppermute | solution.py:265
  52.7 2.1 %collective-permute-done.13.came_ref = f32[2,512]{1,0:T(2,128)S(1)} collective-permute-done((f32[2,512]{1,0:T(2,128)S(1)}, f32[2,512]{1,0:T(2,128)S(1)}, u32[]{:S(2)}, u32[]{:S(2)}) %collective-permute-start.13) | collective-permute-done | bytes 4128 | tf_op jit(solution)/shard_map/ppermute | solution.py:265
  54.8 1.6 %collective-permute-start.14 = (f32[2,512]{1,0:T(2,128)S(1)}, f32[2,512]{1,0:T(2,128)S(1)}, u32[]{:S(2)}, u32[]{:S(2)}) collective-permute-start(f32[2,512]{1,0:T(2,128)S(1)} %shard_map.184.held_ref), channel_id=1, source_target_pairs={{0,2},{1,3},{2,0},{3,1},{4,6},{5,7},{6,4},{7,5},{8,10},{9,11},{10,... | collective-permute-start | bytes 12296 | tf_op jit(solution)/shard_map/ppermute | solution.py:265
  56.4 2.0 %collective-permute-done.14.came_ref = f32[2,512]{1,0:T(2,128)S(1)} collective-permute-done((f32[2,512]{1,0:T(2,128)S(1)}, f32[2,512]{1,0:T(2,128)S(1)}, u32[]{:S(2)}, u32[]{:S(2)}) %collective-permute-start.14) | collective-permute-done | bytes 4128 | tf_op jit(solution)/shard_map/ppermute | solution.py:265
  58.5 2.0 %collective-permute-start.15 = (f32[2,512]{1,0:T(2,128)S(1)}, f32[2,512]{1,0:T(2,128)S(1)}, u32[]{:S(2)}, u32[]{:S(2)}) collective-permute-start(f32[2,512]{1,0:T(2,128)S(1)} %shard_map.185.held_ref), channel_id=1, source_target_pairs={{0,4},{1,5},{2,6},{3,7},{4,0},{5,1},{6,2},{7,3},{8,12},{9,13},{10,... | collective-permute-start | bytes 12296 | tf_op jit(solution)/shard_map/ppermute | solution.py:265
  60.5 2.6 %collective-permute-done.15.came_ref = f32[2,512]{1,0:T(2,128)S(1)} collective-permute-done((f32[2,512]{1,0:T(2,128)S(1)}, f32[2,512]{1,0:T(2,128)S(1)}, u32[]{:S(2)}, u32[]{:S(2)}) %collective-permute-start.15) | collective-permute-done | bytes 4128 | tf_op jit(solution)/shard_map/ppermute | solution.py:265
  (29 shorter events, 12.8 us)
Async XLA Ops:
  2.6 4.7 %collective-permute-start = (f32[8,512]{1,0:T(8,128)S(1)}, f32[8,512]{1,0:T(8,128)S(1)}, u32[]{:S(2)}, u32[]{:S(2)}) collective-permute-start(f32[8,512]{1,0:T(8,128)S(1)} %get-tuple-element.22.held_ref), channel_id=1, source_target_pairs={{0,1},{1,0},{2,3},{3,2},{4,5},{5,4},{6,7},{7,6},{8,9},{9,8},{10,11... | collective-permute-start | bytes 49160 | tf_op jit(solution)/shard_map/ppermute | solution.py:265
  7.3 3.9 %collective-permute-start.1 = (f32[8,512]{1,0:T(8,128)S(1)}, f32[8,512]{1,0:T(8,128)S(1)}, u32[]{:S(2)}, u32[]{:S(2)}) collective-permute-start(f32[8,512]{1,0:T(8,128)S(1)} %shard_map.168.held_ref), channel_id=1, source_target_pairs={{0,2},{1,3},{2,0},{3,1},{4,6},{5,7},{6,4},{7,5},{8,10},{9,11},{10,... | collective-permute-start | bytes 49160 | tf_op jit(solution)/shard_map/ppermute | solution.py:265
  11.2 5.9 %collective-permute-start.2 = (f32[8,512]{1,0:T(8,128)S(1)}, f32[8,512]{1,0:T(8,128)S(1)}, u32[]{:S(2)}, u32[]{:S(2)}) collective-permute-start(f32[8,512]{1,0:T(8,128)S(1)} %shard_map.169.held_ref), channel_id=1, source_target_pairs={{0,4},{1,5},{2,6},{3,7},{4,0},{5,1},{6,2},{7,3},{8,12},{9,13},{10,... | collective-permute-start | bytes 49160 | tf_op jit(solution)/shard_map/ppermute | solution.py:265
  17.5 3.6 %collective-permute-start.3 = (f32[1,640]{1,0:T(1,128)S(1)}, f32[1,640]{1,0:T(1,128)S(1)}, u32[]{:S(2)}, u32[]{:S(2)}) collective-permute-start(f32[1,640]{1,0:T(1,128)S(1)} %get-tuple-element.25.held_ref), channel_id=1, source_target_pairs={{0,1},{1,0},{2,3},{3,2},{4,5},{5,4},{6,7},{7,6},{8,9},{9,8},{10,11... | collective-permute-start | bytes 7688 | tf_op jit(solution)/shard_map/ppermute | solution.py:265
  21.1 3.6 %collective-permute-start.4 = (f32[2,640]{1,0:T(2,128)S(1)}, f32[2,640]{1,0:T(2,128)S(1)}, u32[]{:S(2)}, u32[]{:S(2)}) collective-permute-start(f32[2,640]{1,0:T(2,128)S(1)} %shard_map.172.held_ref), channel_id=1, source_target_pairs={{0,2},{1,3},{2,0},{3,1},{4,6},{5,7},{6,4},{7,5},{8,10},{9,11},{10,... | collective-permute-start | bytes 15368 | tf_op jit(solution)/shard_map/ppermute | solution.py:265
  24.7 4.6 %collective-permute-start.5 = (f32[4,640]{1,0:T(4,128)S(1)}, f32[4,640]{1,0:T(4,128)S(1)}, u32[]{:S(2)}, u32[]{:S(2)}) collective-permute-start(f32[4,640]{1,0:T(4,128)S(1)} %shard_map.173.held_ref), channel_id=1, source_target_pairs={{0,4},{1,5},{2,6},{3,7},{4,0},{5,1},{6,2},{7,3},{8,12},{9,13},{10,... | collective-permute-start | bytes 30728 | tf_op jit(solution)/shard_map/ppermute | solution.py:265
  29.3 1.2 %collective-permute-start.6 = (f32[1,128]{1,0:T(1,128)S(1)}, f32[1,128]{1,0:T(1,128)S(1)}, u32[]{:S(2)}, u32[]{:S(2)}) collective-permute-start(f32[1,128]{1,0:T(1,128)S(1)} %get-tuple-element.32.held_ref), channel_id=1, source_target_pairs={{0,8},{8,0},{16,24},{24,16},{1,9},{9,1},{17,25},{25,17},{2,10},{10... | collective-permute-start | bytes 1544 | tf_op jit(solution)/shard_map/ppermute | solution.py:265
  30.5 3.5 %collective-permute-start.7 = (f32[1,128]{1,0:T(1,128)S(1)}, f32[1,128]{1,0:T(1,128)S(1)}, u32[]{:S(2)}, u32[]{:S(2)}) collective-permute-start(f32[1,128]{1,0:T(1,128)S(1)} %shard_map.176.held_ref), channel_id=1, source_target_pairs={{0,16},{8,24},{16,0},{24,8},{1,17},{9,25},{17,1},{25,9},{2,18},{10... | collective-permute-start | bytes 1544 | tf_op jit(solution)/shard_map/ppermute | solution.py:265
  34.3 3.6 %collective-permute-start.8 = (f32[1,640]{1,0:T(1,128)S(1)}, f32[1,640]{1,0:T(1,128)S(1)}, u32[]{:S(2)}, u32[]{:S(2)}) collective-permute-start(f32[1,640]{1,0:T(1,128)S(1)} %get-tuple-element.36.held_ref), channel_id=1, source_target_pairs={{0,1},{1,0},{2,3},{3,2},{4,5},{5,4},{6,7},{7,6},{8,9},{9,8},{10,11... | collective-permute-start | bytes 7688 | tf_op jit(solution)/shard_map/ppermute | solution.py:265
  37.9 3.6 %collective-permute-start.9 = (f32[2,640]{1,0:T(2,128)S(1)}, f32[2,640]{1,0:T(2,128)S(1)}, u32[]{:S(2)}, u32[]{:S(2)}) collective-permute-start(f32[2,640]{1,0:T(2,128)S(1)} %shard_map.178.held_ref), channel_id=1, source_target_pairs={{0,2},{1,3},{2,0},{3,1},{4,6},{5,7},{6,4},{7,5},{8,10},{9,11},{10,... | collective-permute-start | bytes 15368 | tf_op jit(solution)/shard_map/ppermute | solution.py:265
  41.5 4.6 %collective-permute-start.10 = (f32[4,640]{1,0:T(4,128)S(1)}, f32[4,640]{1,0:T(4,128)S(1)}, u32[]{:S(2)}, u32[]{:S(2)}) collective-permute-start(f32[4,640]{1,0:T(4,128)S(1)} %shard_map.179.held_ref), channel_id=1, source_target_pairs={{0,4},{1,5},{2,6},{3,7},{4,0},{5,1},{6,2},{7,3},{8,12},{9,13},{10,... | collective-permute-start | bytes 30728 | tf_op jit(solution)/shard_map/ppermute | solution.py:265
  46.1 1.2 %collective-permute-start.11 = (f32[1,128]{1,0:T(1,128)S(1)}, f32[1,128]{1,0:T(1,128)S(1)}, u32[]{:S(2)}, u32[]{:S(2)}) collective-permute-start(f32[1,128]{1,0:T(1,128)S(1)} %get-tuple-element.38.held_ref), channel_id=1, source_target_pairs={{0,8},{8,0},{16,24},{24,16},{1,9},{9,1},{17,25},{25,17},{2,10},{10... | collective-permute-start | bytes 1544 | tf_op jit(solution)/shard_map/ppermute | solution.py:265
  47.3 3.5 %collective-permute-start.12 = (f32[1,128]{1,0:T(1,128)S(1)}, f32[1,128]{1,0:T(1,128)S(1)}, u32[]{:S(2)}, u32[]{:S(2)}) collective-permute-start(f32[1,128]{1,0:T(1,128)S(1)} %shard_map.182.held_ref), channel_id=1, source_target_pairs={{0,16},{8,24},{16,0},{24,8},{1,17},{9,25},{17,1},{25,9},{2,18},{10... | collective-permute-start | bytes 1544 | tf_op jit(solution)/shard_map/ppermute | solution.py:265
  51.1 3.7 %collective-permute-start.13 = (f32[2,512]{1,0:T(2,128)S(1)}, f32[2,512]{1,0:T(2,128)S(1)}, u32[]{:S(2)}, u32[]{:S(2)}) collective-permute-start(f32[2,512]{1,0:T(2,128)S(1)} %shard_map.183.held_ref), channel_id=1, source_target_pairs={{0,1},{1,0},{2,3},{3,2},{4,5},{5,4},{6,7},{7,6},{8,9},{9,8},{10,11... | collective-permute-start | bytes 12296 | tf_op jit(solution)/shard_map/ppermute | solution.py:265
  54.8 3.7 %collective-permute-start.14 = (f32[2,512]{1,0:T(2,128)S(1)}, f32[2,512]{1,0:T(2,128)S(1)}, u32[]{:S(2)}, u32[]{:S(2)}) collective-permute-start(f32[2,512]{1,0:T(2,128)S(1)} %shard_map.184.held_ref), channel_id=1, source_target_pairs={{0,2},{1,3},{2,0},{3,1},{4,6},{5,7},{6,4},{7,5},{8,10},{9,11},{10,... | collective-permute-start | bytes 12296 | tf_op jit(solution)/shard_map/ppermute | solution.py:265
  58.5 4.6 %collective-permute-start.15 = (f32[2,512]{1,0:T(2,128)S(1)}, f32[2,512]{1,0:T(2,128)S(1)}, u32[]{:S(2)}, u32[]{:S(2)}) collective-permute-start(f32[2,512]{1,0:T(2,128)S(1)} %shard_map.185.held_ref), channel_id=1, source_target_pairs={{0,4},{1,5},{2,6},{3,7},{4,0},{5,1},{6,2},{7,3},{8,12},{9,13},{10,... | collective-permute-start | bytes 12296 | tf_op jit(solution)/shard_map/ppermute | solution.py:265

commit v4 on v3

--- a/solution.py
+++ b/solution.py
@@ -35,19 +35,17 @@
     return moved[0:8] + moved[8:16] + moved[16:24]
 
 
-def merged(held, came, width, bit):
-    block = lax.broadcasted_iota(jnp.int32, held.shape, 1) // width
-    return jnp.where((block >> bit) & 1 == 1, came, held)
-
-
-def merge_kernel(width, bit, held_ref, came_ref, out_ref):
-    out_ref[...] = merged(held_ref[...], came_ref[...], width, bit)
-
-
-def stack_kernel(held_ref, came_ref, out_ref):
-    count = held_ref.shape[0]
-    out_ref[0:count, :] = held_ref[...]
-    out_ref[count:2 * count, :] = came_ref[...]
+def spread(flat, sent_ref):
+    members = sent_ref.shape[0]
+    peer_rows = flat.shape[1] // members
+    for peer in range(members):
+        sent_ref[peer, :, 0:peer_rows] = flat[:, peer * peer_rows:(peer + 1) * peer_rows]
+
+
+def flattened(got_ref, elem_count):
+    members = got_ref.shape[0]
+    peer_rows = elem_count // members
+    return jnp.concatenate([got_ref[peer, :, 0:peer_rows] for peer in range(members)], axis=1)
 
 
 def start_copies(sources, targets, sems):
@@ -77,15 +75,15 @@
     onehot = selection(target, members)
     earlier = dot(onehot, triangle, NN)
     rank = jnp.sum(earlier * onehot.astype(jnp.float32), axis=0, keepdims=True)
-    slot = (target ^ index_ref[1]) * peer_rows + rank.astype(jnp.int32)
+    slot = target * peer_rows + rank.astype(jnp.int32)
     slot_ref[...] = slot
     rows = [u, phi, sigma * fric_a, sigma * fric_b, dist, target_row.astype(jnp.float32)]
     pad = jnp.zeros((8 - len(rows), elem_count), jnp.float32)
     values = jnp.concatenate(rows + [pad], axis=0)
-    sent_ref[...] = select_columns(values, selection(slot, elem_count), NT)
-
-
-def load_kernel(members, index_ref, near_count, *refs):
+    spread(select_columns(values, selection(slot, elem_count), NT), sent_ref)
+
+
+def load_kernel(index_ref, near_count, *refs):
     near_ref, far_u_ref, far_v_ref, coarse_u_ref, coarse_v_ref = refs[:5]
     scalar_refs, outs, scalar_bufs, sems = refs[5:8], refs[8:15], refs[15:18], refs[18]
     near_mask_ref, far_mask_ref, near_out, far_u_out, far_v_out, coarse_u_out, coarse_v_out = outs
@@ -103,11 +101,11 @@
     near_col, far_col, far_rank = scalar_bufs
     far_slots = far_col.shape[0]
     far_width = far_mask_ref.shape[1] // far_slots
-    block = lax.broadcasted_iota(jnp.int32, near_mask_ref.shape[1:], 0) ^ index_ref[1]
+    block = lax.broadcasted_iota(jnp.int32, near_mask_ref.shape[1:], 0)
     for number in range(near_mask_ref.shape[0]):
         column = jnp.where(number < near_count[0], near_col[number], -1)
         near_mask_ref[number] = jnp.where(block == column, 1.0, 0.0)
-    block = lax.broadcasted_iota(jnp.int32, far_mask_ref.shape, 0) ^ index_ref[1]
+    block = lax.broadcasted_iota(jnp.int32, far_mask_ref.shape, 0)
     lane = lax.broadcasted_iota(jnp.int32, far_mask_ref.shape, 1)
     column = jnp.full(far_mask_ref.shape, -1, jnp.int32)
     for number in range(far_slots):
@@ -123,16 +121,16 @@
     elem_count = deficit.shape[1]
     wide = jnp.broadcast_to(deficit, (8, elem_count)).astype(jnp.bfloat16)
     partial = dot(wide, coarse_v_ref[...], NT)[0:1]
-    width = partial.shape[1]
-    out_ref[:, 0:elem_count] = deficit
-    if elem_count + width < out_ref.shape[1]:
-        out_ref[:, elem_count + width:] = jnp.zeros((1, out_ref.shape[1] - elem_count - width), jnp.float32)
-    out_ref[:, elem_count:elem_count + width] = partial
-
-
-def place_kernel(members, bit, held_ref, came_ref, coarse_v_ref, state_ref, rows_ref, out_ref):
-    elem_count = held_ref.shape[1]
-    flat = merged(held_ref[...], came_ref[...], elem_count // members, bit)
+    pieces = [deficit, partial]
+    rest = out_ref.shape[2] - elem_count - partial.shape[1]
+    if rest:
+        pieces.append(jnp.zeros((1, rest), jnp.float32))
+    out_ref[...] = jnp.broadcast_to(jnp.concatenate(pieces, axis=1)[None], out_ref.shape)
+
+
+def place_kernel(got_ref, coarse_v_ref, state_ref, rows_ref, out_ref):
+    elem_count = state_ref.shape[1]
+    flat = flattened(got_ref, elem_count)
     rows = flat[5:6].astype(jnp.int32)
     rows_ref[...] = rows
     state = select_columns(flat, selection(rows, elem_count), NT)
@@ -141,15 +139,14 @@
     outgoing(deficit, coarse_v_ref, out_ref)
 
 
-def gather_kernel(held_ref, came_ref, all_ref, total_ref):
-    stack_kernel(held_ref, came_ref, all_ref)
-    low = all_ref.shape[1] - total_ref.shape[1]
-    total_ref[...] = jnp.sum(all_ref[:, low:], axis=0, keepdims=True)
-
-
-def inside_kernel(all_ref, near_ref, far_u_ref, far_v_ref, near_mask_ref, far_mask_ref, out_ref):
-    leaf_size = near_ref.shape[2]
-    deficits = all_ref[:, 0:leaf_size]
+def load_rows(
+    index_ref, all_ref, near_ref, far_u_ref, far_v_ref, near_mask_ref, far_mask_ref, coarse_u_ref, groups
+):
+    members, leaf_size = near_mask_ref.shape[1], near_ref.shape[2]
+    coarse_width = coarse_u_ref.shape[0]
+    rank = coarse_width // groups
+    mine = index_ref[0]
+    deficits = all_ref[pl.ds(mine * members, members), 0, 0:leaf_size]
     total = jnp.zeros(deficits.shape, jnp.float32)
     for slot in range(near_ref.shape[0]):
         source = (deficits * near_mask_ref[slot]).astype(jnp.bfloat16)
@@ -158,7 +155,16 @@
     project = jnp.sum(project, axis=0, keepdims=True)
     project = jnp.broadcast_to(project, (8, project.shape[1])).astype(jnp.bfloat16)
     far = dot(project, far_u_ref[...], NN)
-    out_ref[...] = jnp.sum(total, axis=0, keepdims=True) + far[0:1]
+    lane = lax.broadcasted_iota(jnp.int32, (members, coarse_width), 1)
+    weights = jnp.zeros((members, coarse_width), jnp.float32)
+    for shift in range(1, groups):
+        start = (mine ^ shift) * members
+        part = all_ref[pl.ds(start, members), 0, leaf_size:leaf_size + coarse_width]
+        weights = jnp.where(lane // rank == shift, part, weights)
+    weights = jnp.sum(weights, axis=0, keepdims=True)
+    weights = jnp.broadcast_to(weights, (8, coarse_width)).astype(jnp.bfloat16)
+    coarse = dot(weights, coarse_u_ref[...], NN)
+    return jnp.sum(total, axis=0, keepdims=True) + far[0:1] + coarse[0:1]
 
 
 def rates(load, ln_now, state_now, sa, sb, dist):
@@ -168,18 +174,10 @@
     return log_rate, state_rate
 
 
-def coarse_rows(rank, bit, held_ref, came_ref, coarse_u_ref):
-    width = coarse_u_ref.shape[0]
-    weights = merged(held_ref[...], came_ref[...], rank, bit)[:, 0:width]
-    lane = lax.broadcasted_iota(jnp.int32, weights.shape, 1)
-    weights = jnp.where(lane >= rank, weights, 0.0)
-    weights = jnp.broadcast_to(weights, (8, width)).astype(jnp.bfloat16)
-    return dot(weights, coarse_u_ref[...], NN)[0:1]
-
-
-def first_kernel(rank, bit, state_ref, inside_ref, held_ref, came_ref, coarse_u_ref, coarse_v_ref, next_ref, out_ref):
+def first_kernel(groups, index_ref, state_ref, coarse_v_ref, *refs):
+    field_refs, next_ref, out_ref = refs[:-2], refs[-2], refs[-1]
     state = state_ref[...]
-    load = inside_ref[...] + coarse_rows(rank, bit, held_ref, came_ref, coarse_u_ref)
+    load = load_rows(index_ref, *field_refs, groups)
     u, phi, sa, sb, dist = (state[i:i + 1] for i in range(5))
     k1u, k1p = rates(load, u, phi, sa, sb, dist)
     u2 = u + TIME_STEP * k1u
@@ -189,10 +187,11 @@
     next_ref[...] = jnp.concatenate([u2, phi2, k1u, k1p, jnp.zeros((4, u.shape[1]), jnp.float32)], axis=0)
 
 
-def second_kernel(rank, bit, state_ref, next_ref, rows_ref, inside_ref, held_ref, came_ref, coarse_u_ref, sent_ref):
+def second_kernel(groups, index_ref, state_ref, next_ref, rows_ref, *refs):
+    field_refs, sent_ref = refs[:-1], refs[-1]
     state = state_ref[...]
     later = next_ref[...]
-    load = inside_ref[...] + coarse_rows(rank, bit, held_ref, came_ref, coarse_u_ref)
+    load = load_rows(index_ref, *field_refs, groups)
     u, phi, sa, sb, dist = (state[i:i + 1] for i in range(5))
     u2, phi2, k1u, k1p = (later[i:i + 1] for i in range(4))
     k2u, k2p = rates(load, u2, phi2, sa, sb, dist)
@@ -200,12 +199,12 @@
     phi = phi + 0.5 * TIME_STEP * (k1p + k2p)
     elem_count = u.shape[1]
     values = jnp.concatenate([u, phi, jnp.zeros((6, elem_count), jnp.float32)], axis=0)
-    sent_ref[...] = select_columns(values, selection(rows_ref[...], elem_count), NN)[0:2]
-
-
-def unsort_kernel(members, bit, held_ref, came_ref, slot_ref, u_ref, phi_ref):
-    elem_count = held_ref.shape[1]
-    flat = merged(held_ref[...], came_ref[...], elem_count // members, bit)
+    spread(select_columns(values, selection(rows_ref[...], elem_count), NN)[0:2], sent_ref)
+
+
+def unsort_kernel(got_ref, slot_ref, u_ref, phi_ref):
+    elem_count = slot_ref.shape[1]
+    flat = flattened(got_ref, elem_count)
     flat = jnp.concatenate([flat, jnp.zeros((6, elem_count), jnp.float32)], axis=0)
     out = select_columns(flat, selection(slot_ref[...], elem_count), NN)
     u_ref[...] = out[0:1]
@@ -257,20 +256,10 @@
     leaf_size = near_blocks.shape[1]
     groups, rank = coarse_v.shape[0], coarse_v.shape[1]
     width = pl.cdiv(groups * rank, 128) * 128
-    block_bits = range(members.bit_length() - 1)
-    group_bits = range(groups.bit_length() - 1)
-
-    def partner(value, axis, bit):
-        count = lax.axis_size(axis)
-        return lax.ppermute(value, axis, [(i, i ^ (1 << bit)) for i in range(count)])
-
-    def trade(value, axis, bits, lanes):
-        for bit in bits[:-1]:
-            came = partner(value, axis, bit)
-            value = call(
-                functools.partial(merge_kernel, lanes, bit), shape(*value.shape), value, came
-            )
-        return value, partner(value, axis, bits[-1])
+    devices = groups * members
+
+    def swap(value, axes):
+        return lax.all_to_all(value, axes, split_axis=0, concat_axis=0, tiled=True)
 
     elem_args = [
         value.reshape(1, elems)
@@ -278,7 +267,7 @@
     ]
     sent, slot = call(
         functools.partial(sort_kernel, members),
-        (shape(8, elems), shape(1, elems, dtype=jnp.int32)),
+        (shape(members, 8, 128), shape(1, elems, dtype=jnp.int32)),
         place, *elem_args, scalars=(0,), far=range(1, 8),
         scratch=[VMEM(value.shape, value.dtype) for value in elem_args]
         + [pltpu.SemaphoreType.DMA((7,))],
@@ -289,7 +278,7 @@
     scalar_args = [near_col, far_col, far_rank]
     far_rows = weights[1].shape[0]
     near_mask, far_mask, near, far_u, far_v, coarse_u, coarse_v = call(
-        functools.partial(load_kernel, members),
+        load_kernel,
         (
             shape(near_blocks.shape[0], members, leaf_size),
             shape(members, far_rows),
@@ -304,45 +293,26 @@
         + [pltpu.SemaphoreType.DMA((6 + 2 * groups,))],
         flops=2 * near_blocks.size, moved=2 * near_blocks.size * 2,
     )
-    held, came = trade(sent, "blk", block_bits, elems // members)
     state, rows, out = call(
-        functools.partial(place_kernel, members, block_bits[-1]),
-        (shape(8, elems), shape(1, elems, dtype=jnp.int32), shape(1, elems + width)),
-        held, came, coarse_v,
-    )
-
-    def section(out):
-        for bit in block_bits[:-1]:
-            out = call(
-                stack_kernel, shape(2 * out.shape[0], out.shape[1]), out, partner(out, "blk", bit)
-            )
-        everyone, total = call(
-            gather_kernel, (shape(members, elems + width), shape(1, width)),
-            out, partner(out, "blk", block_bits[-1]),
-        )
-        coefs = trade(total, "leaf", group_bits, rank)
-        inside = call(
-            inside_kernel, shape(1, elems), everyone, near, far_u, far_v, near_mask, far_mask,
-            flops=2 * members * near.size, moved=2 * near.size,
-        )
-        return coefs, inside
-
-    coefs, inside = section(out)
+        place_kernel,
+        (shape(8, elems), shape(1, elems, dtype=jnp.int32), shape(devices, 1, elems + width)),
+        swap(sent, "blk"), coarse_v,
+    )
+    fields = near, far_u, far_v, near_mask, far_mask, coarse_u
+
+    def share(out):
+        return swap(out, ("leaf", "blk"))
+
     later, out = call(
-        functools.partial(first_kernel, rank, group_bits[-1]),
-        (shape(8, elems), shape(1, elems + width)),
-        state, inside, *coefs, coarse_u, coarse_v,
-    )
-    coefs, inside = section(out)
+        functools.partial(first_kernel, groups), (shape(8, elems), shape(devices, 1, elems + width)),
+        place, state, coarse_v, share(out), *fields, scalars=(0,),
+    )
     sent = call(
-        functools.partial(second_kernel, rank, group_bits[-1]), shape(2, elems),
-        state, later, rows, inside, *coefs, coarse_u,
-    )
-    held, came = trade(sent, "blk", block_bits, elems // members)
+        functools.partial(second_kernel, groups), shape(members, 2, 128),
+        place, state, later, rows, share(out), *fields, scalars=(0,),
+    )
     u, phi = call(
-        functools.partial(unsort_kernel, members, block_bits[-1]),
-        (shape(1, elems), shape(1, elems)),
-        held, came, slot,
+        unsort_kernel, (shape(1, elems), shape(1, elems)), swap(sent, "blk"), slot
     )
     return u.reshape(elems), phi.reshape(elems)
 

time: 64.1 us -> 49.2 us (0.77)
  blocking collectives: 0 us -> 27.4 us
  waiting for transfers between devices: 28.7 us -> 3.93 us
  starting transfers between devices: 26.5 us -> 7.26 us
  Pallas kernels: 7.14 us -> 8.78 us
    ppermute x16 -> x0, waiting for transfers between devices: 28.7 us -> none  [partner(): return lax.ppermute(value, axis, [(i, i ^ 1 << bit) for i in range(count)])]
    all_to_all x0 -> x3, blocking collectives: none -> 27.4 us  [swap(): return lax.all_to_all(value, axes, split_axis=0, concat_axis=0, tiled=True)]
    ppermute x16 -> x0, starting transfers between devices: 26.5 us -> none  [partner(): return lax.ppermute(value, axis, [(i, i ^ 1 << bit) for i in range(count)])]
    all_to_all x0 -> x1, starting transfers between devices: none -> 7.26 us  [swap(): return lax.all_to_all(value, axes, split_axis=0, concat_axis=0, tiled=True)]
    all_to_all x0 -> x1, waiting for transfers between devices: none -> 3.93 us  [swap(): return lax.all_to_all(value, axes, split_axis=0, concat_axis=0, tiled=True)]
    pallas_call x20 -> x6, Pallas kernels: 7.14 us -> 8.78 us  [call(): pl.pallas_call(kernel, out_shape=outs, in_specs=[pl.BlockSpec(memory_spac...]
  transfers between devices with their start and end apart: 16 -> 1, of which waited for: 15 -> 1; matrix products, arithmetic and copies ran while one was open for 0% -> 0% of each run, Pallas kernels for 5% -> 4%
where the time goes in v4:
time: 49.2 us; the launch traced here: 48.8 us
  blocking collectives  27.4 us (56%)
  Pallas kernels  8.78 us (18%)
  starting transfers between devices  7.26 us (15%)
  waiting for transfers between devices  3.93 us (8%)
  between operations  1.32 us (3%)
    all_to_all x3, blocking collectives, swap(): return lax.all_to_all(value, axes, split_axis=0, concat_axis=0, tiled=True)  27.4 us
    pallas_call x6, Pallas kernels, call(): pl.pallas_call(kernel, out_shape=outs, in_specs=[pl.BlockSpec(memory_spac...  8.78 us
    all_to_all x1, starting transfers between devices, swap(): return lax.all_to_all(value, axes, split_axis=0, concat_axis=0, tiled=True)  7.26 us
    all_to_all x1, waiting for transfers between devices, swap(): return lax.all_to_all(value, axes, split_axis=0, concat_axis=0, tiled=True)  3.93 us
  transfers between devices with their start and end apart: 1, of which 1 were waited for; matrix products, arithmetic and copies ran while one was open for 0% of the time, Pallas kernels for 4%

profile of v4, /device:TPU:0, one launch (start us, length us, event | category | flops | bytes accessed | tf_op | source)
XLA Modules:
  0.0 48.8 jit_solution(7027971509712994449)
XLA Ops:
  0.6 0.1 pad_add_fusion.index_ref
  0.7 2.5 %shard_map.167 = (f32[8,8,128]{2,1,0:T(8,128)}, s32[1,512]{1,0:T(1,128)S(1)}) custom-call(s32[2]{0:T(128)S(1)} %pad_add_fusion.index_ref, f32[1,512]{1,0:T(1,128)} %bitcast.15, f32[1,512]{1,0:T(1,128)} %bitcast.16, f32[1,512]{1,0:T(1,128)} %bitcast.17, f32[1,512]{1,0:T(1,128)} %bitcast.18, f32[1,512]{1,0:T(1,128)} %bitcast.19, f32[1,512]{1,0:T(1,128)} %bitcast.20, ...), custom_call_target="tpu_custom_call" | custom-call | flops 1000 | bytes 1000 | tf_op jit(solution)/shard_map/pallas_call | solution.py:220
  3.2 7.3 %all-to-all-start = ((f32[8,8,128]{2,1,0:T(8,128)}), f32[8,8,128]{2,1,0:T(8,128)S(1)}, u32[]{:S(2)}, u32[]{:S(2)}) async-start(f32[8,8,128]{2,1,0:T(8,128)} %get-tuple-element.18), calls=%async_computation | async-start | bytes 65536 | tf_op jit(solution)/shard_map/all_to_all | solution.py:262
  11.2 2.1 %shard_map.168 = (f32[3,8,512]{2,1,0:T(8,128)S(1)}, f32[8,64]{1,0:T(8,128)S(1)}, bf16[3,512,512]{2,1,0:T(8,128)(2,1)S(1)}, bf16[64,512]{1,0:T(8,128)(2,1)S(1)}, ...) custom-call(s32[2]{0:T(128)S(1)} %pad_add_fusion.index_ref, ...), custom_call_target="tpu_custom_call" | custom-call | flops 1572864 | bytes 3145728 | tf_op jit(solution)/shard_map/pallas_call | solution.py:220
  13.3 3.9 %all-to-all-done.got_ref = f32[8,8,128]{2,1,0:T(8,128)S(1)} async-done(((f32[8,8,128]{2,1,0:T(8,128)}), f32[8,8,128]{2,1,0:T(8,128)S(1)}, u32[]{:S(2)}, u32[]{:S(2)}) %all-to-all-start) | async-done | bytes 32800 | tf_op jit(solution)/shard_map/all_to_all | solution.py:262
  17.2 0.5 %shard_map.169 = (f32[8,512]{1,0:T(8,128)S(1)}, s32[1,512]{1,0:T(1,128)S(1)}, f32[32,1,640]{2,1,0:T(1,128)S(1)}) custom-call(f32[8,8,128]{2,1,0:T(8,128)S(1)} %all-to-all-done.got_ref, bf16[64,512]{1,0:T(8,128)(2,1)S(1)} %get-tuple-element.19.coarse_v_ref), custom_call_target="tpu_custom_call" | custom-call | flops 1000 | bytes 1000 | tf_op jit(solution)/shard_map/pallas_call | solution.py:220
  17.7 9.4 %all_to_all.20.refs_0_ = f32[32,1,640]{2,1,0:T(1,128)S(1)} all-to-all(f32[32,1,640]{2,1,0:T(1,128)S(1)} %get-tuple-element.21), channel_id=1, replica_groups=mesh['leaf'=4,'blk'=8] {'leaf','blk'}, dimensions={0} | all-to-all | bytes 163840 | tf_op jit(solution)/shard_map/all_to_all | solution.py:262
  27.1 1.4 %shard_map.170 = (f32[8,512]{1,0:T(8,128)S(1)}, f32[32,1,640]{2,1,0:T(1,128)S(1)}) custom-call(s32[2]{0:T(128)S(1)} %pad_add_fusion.index_ref, f32[8,512]{1,0:T(8,128)S(1)} %get-tuple-element.20.state_ref, bf16[64,512]{1,0:T(8,128)(2,1)S(1)} %get-tuple-element.19.coarse_v_ref, f32[32,1,640]{2,1,0:T(1,128)S(1)} %all_to_all.20.refs_0_, ...), custom_call_target="tpu_custom_call" | custom-call | flops 1000 | bytes 1000 | tf_op jit(solution)/shard_map/pallas_call | solution.py:220
  28.5 9.1 %all_to_all.21.refs_0_ = f32[32,1,640]{2,1,0:T(1,128)S(1)} all-to-all(f32[32,1,640]{2,1,0:T(1,128)S(1)} %get-tuple-element.30), channel_id=1, replica_groups=mesh['leaf'=4,'blk'=8] {'leaf','blk'}, dimensions={0} | all-to-all | bytes 163840 | tf_op jit(solution)/shard_map/all_to_all | solution.py:262
  37.6 1.4 %shard_map.171 = f32[8,2,128]{2,1,0:T(2,128)S(1)} custom-call(s32[2]{0:T(128)S(1)} %pad_add_fusion.index_ref, f32[8,512]{1,0:T(8,128)S(1)} %get-tuple-element.20.state_ref, f32[8,512]{1,0:T(8,128)S(1)} %get-tuple-element.28.next_ref, s32[1,512]{1,0:T(1,128)S(1)} %get-tuple-element.29.rows_ref, f32[32,1,640]{2,1,0:T(1,128)S(1)} %all_to_all.21.refs_0_, ...), custom_call_target="tpu_custom_call" | custom-call | flops 1000 | bytes 1000 | tf_op jit(solution)/shard_map/pallas_call | solution.py:220
  39.0 8.9 %all_to_all.22.got_ref = f32[8,2,128]{2,1,0:T(2,128)S(1)} all-to-all(f32[8,2,128]{2,1,0:T(2,128)S(1)} %shard_map.171), channel_id=1, replica_groups=mesh['leaf'=4,'blk'=8] {'blk'}, dimensions={0} | all-to-all | bytes 16384 | tf_op jit(solution)/shard_map/all_to_all | solution.py:262
  48.0 0.8 %shard_map.172 = (f32[1,512]{1,0:T(1,128)}, f32[1,512]{1,0:T(1,128)}) custom-call(f32[8,2,128]{2,1,0:T(2,128)S(1)} %all_to_all.22.got_ref, s32[1,512]{1,0:T(1,128)S(1)} %get-tuple-element.31.slot_ref), custom_call_target="tpu_custom_call" | custom-call | flops 1000 | bytes 1000 | tf_op jit(solution)/shard_map/pallas_call | solution.py:220
Async XLA Ops:
  3.2 13.9 %all-to-all-start = ((f32[8,8,128]{2,1,0:T(8,128)}), f32[8,8,128]{2,1,0:T(8,128)S(1)}, u32[]{:S(2)}, u32[]{:S(2)}) async-start(f32[8,8,128]{2,1,0:T(8,128)} %get-tuple-element.18), calls=%async_computation | async-start | bytes 65536 | tf_op jit(solution)/shard_map/all_to_all | solution.py:262

commit v5 on v4

--- a/solution.py
+++ b/solution.py
@@ -58,45 +58,46 @@
     return copies
 
 
-def sort_kernel(members, index_ref, *refs):
-    elem_refs, sent_ref, slot_ref, bufs, sems = refs[:7], refs[7], refs[8], refs[9:16], refs[16]
-    copies = start_copies(elem_refs, bufs, sems)
-    elem_count = bufs[0].shape[1]
+def sort_kernel(members, near_count, *refs):
+    elem_refs, scalar_refs, weight_refs = refs[:7], refs[7:10], refs[10:15]
+    sent_ref, order_ref, near_mask_ref, far_mask_ref = refs[15:19]
+    weight_outs, elem_bufs, scalar_bufs, sems = refs[19:24], refs[24:31], refs[31:34], refs[34]
+    mine = lax.axis_index("leaf")
+    coarse_u_ref, coarse_v_ref = weight_refs[3:]
+    coarse_u_out, coarse_v_out = weight_outs[3:]
+    groups, rank = coarse_u_ref.shape[0], coarse_u_ref.shape[1]
+    sources = [*elem_refs, *scalar_refs, *weight_refs[:3]]
+    targets = [*elem_bufs, *scalar_bufs, *weight_outs[:3]]
+    for shift in range(groups):
+        group = mine ^ shift
+        span = pl.ds(shift * rank, rank)
+        sources += [coarse_u_ref.at[group], coarse_v_ref.at[group]]
+        targets += [coarse_u_out.at[span, :], coarse_v_out.at[span, :]]
+    copies = start_copies(sources, targets, sems)
+
+    elem_count = elem_bufs[0].shape[1]
     peer_rows = elem_count // members
     before = lax.broadcasted_iota(jnp.int32, (elem_count, elem_count), 0)
     after = lax.broadcasted_iota(jnp.int32, (elem_count, elem_count), 1)
     triangle = jnp.where(before < after, 1.0, 0.0).astype(jnp.bfloat16)
-    for copy in copies:
-        copy.wait()
-    u, phi, sigma, fric_a, fric_b, dist, leaf = (buf[...] for buf in bufs)
-    local = leaf - index_ref[0] * (members * elem_count)
+    copies[0].wait()
+    local = elem_bufs[0][...] - mine * (members * elem_count)
     target = local // elem_count
     target_row = local - target * elem_count
     onehot = selection(target, members)
     earlier = dot(onehot, triangle, NN)
-    rank = jnp.sum(earlier * onehot.astype(jnp.float32), axis=0, keepdims=True)
-    slot = target * peer_rows + rank.astype(jnp.int32)
-    slot_ref[...] = slot
+    rank_within = jnp.sum(earlier * onehot.astype(jnp.float32), axis=0, keepdims=True)
+    slot = target * peer_rows + rank_within.astype(jnp.int32)
+    order = selection(slot, elem_count)
+    order_ref[...] = order
+    for copy in copies[1:7]:
+        copy.wait()
+    u, phi, sigma, fric_a, fric_b, dist = (buf[...] for buf in elem_bufs[1:])
     rows = [u, phi, sigma * fric_a, sigma * fric_b, dist, target_row.astype(jnp.float32)]
     pad = jnp.zeros((8 - len(rows), elem_count), jnp.float32)
-    values = jnp.concatenate(rows + [pad], axis=0)
-    spread(select_columns(values, selection(slot, elem_count), NT), sent_ref)
-
-
-def load_kernel(index_ref, near_count, *refs):
-    near_ref, far_u_ref, far_v_ref, coarse_u_ref, coarse_v_ref = refs[:5]
-    scalar_refs, outs, scalar_bufs, sems = refs[5:8], refs[8:15], refs[15:18], refs[18]
-    near_mask_ref, far_mask_ref, near_out, far_u_out, far_v_out, coarse_u_out, coarse_v_out = outs
-    groups, rank = coarse_u_ref.shape[0], coarse_u_ref.shape[1]
-    sources = [*scalar_refs, near_ref, far_u_ref, far_v_ref]
-    targets = [*scalar_bufs, near_out, far_u_out, far_v_out]
-    for shift in range(groups):
-        group = index_ref[0] ^ shift
-        span = pl.ds(shift * rank, rank)
-        sources += [coarse_u_ref.at[group], coarse_v_ref.at[group]]
-        targets += [coarse_u_out.at[span, :], coarse_v_out.at[span, :]]
-    copies = start_copies(sources, targets, sems)
-    for copy in copies[:3]:
+    spread(select_columns(jnp.concatenate(rows + [pad], axis=0), order, NT), sent_ref)
+
+    for copy in copies[7:10]:
         copy.wait()
     near_col, far_col, far_rank = scalar_bufs
     far_slots = far_col.shape[0]
@@ -110,10 +111,10 @@
     column = jnp.full(far_mask_ref.shape, -1, jnp.int32)
     for number in range(far_slots):
         low = number * far_width
-        mine = (lane >= low) & (lane < low + far_rank[number])
-        column = jnp.where(mine, far_col[number], column)
+        kept = (lane >= low) & (lane < low + far_rank[number])
+        column = jnp.where(kept, far_col[number], column)
     far_mask_ref[...] = jnp.where(block == column, 1.0, 0.0)
-    for copy in copies[3:]:
+    for copy in copies[10:]:
         copy.wait()
 
 
@@ -128,24 +129,24 @@
     out_ref[...] = jnp.broadcast_to(jnp.concatenate(pieces, axis=1)[None], out_ref.shape)
 
 
-def place_kernel(got_ref, coarse_v_ref, state_ref, rows_ref, out_ref):
+def place_kernel(got_ref, coarse_v_ref, state_ref, order_ref, out_ref):
     elem_count = state_ref.shape[1]
     flat = flattened(got_ref, elem_count)
-    rows = flat[5:6].astype(jnp.int32)
-    rows_ref[...] = rows
-    state = select_columns(flat, selection(rows, elem_count), NT)
+    order = selection(flat[5:6].astype(jnp.int32), elem_count)
+    order_ref[...] = order
+    state = select_columns(flat, order, NT)
     state_ref[...] = state
     deficit = (PLATE_RATE - jnp.exp(state[0:1])).astype(jnp.bfloat16).astype(jnp.float32)
     outgoing(deficit, coarse_v_ref, out_ref)
 
 
 def load_rows(
-    index_ref, all_ref, near_ref, far_u_ref, far_v_ref, near_mask_ref, far_mask_ref, coarse_u_ref, groups
+    all_ref, near_ref, far_u_ref, far_v_ref, near_mask_ref, far_mask_ref, coarse_u_ref, groups
 ):
     members, leaf_size = near_mask_ref.shape[1], near_ref.shape[2]
     coarse_width = coarse_u_ref.shape[0]
     rank = coarse_width // groups
-    mine = index_ref[0]
+    mine = lax.axis_index("leaf")
     deficits = all_ref[pl.ds(mine * members, members), 0, 0:leaf_size]
     total = jnp.zeros(deficits.shape, jnp.float32)
     for slot in range(near_ref.shape[0]):
@@ -174,10 +175,10 @@
     return log_rate, state_rate
 
 
-def first_kernel(groups, index_ref, state_ref, coarse_v_ref, *refs):
+def first_kernel(groups, state_ref, coarse_v_ref, *refs):
     field_refs, next_ref, out_ref = refs[:-2], refs[-2], refs[-1]
     state = state_ref[...]
-    load = load_rows(index_ref, *field_refs, groups)
+    load = load_rows(*field_refs, groups)
     u, phi, sa, sb, dist = (state[i:i + 1] for i in range(5))
     k1u, k1p = rates(load, u, phi, sa, sb, dist)
     u2 = u + TIME_STEP * k1u
@@ -187,11 +188,11 @@
     next_ref[...] = jnp.concatenate([u2, phi2, k1u, k1p, jnp.zeros((4, u.shape[1]), jnp.float32)], axis=0)
 
 
-def second_kernel(groups, index_ref, state_ref, next_ref, rows_ref, *refs):
+def second_kernel(groups, state_ref, next_ref, order_ref, *refs):
     field_refs, sent_ref = refs[:-1], refs[-1]
     state = state_ref[...]
     later = next_ref[...]
-    load = load_rows(index_ref, *field_refs, groups)
+    load = load_rows(*field_refs, groups)
     u, phi, sa, sb, dist = (state[i:i + 1] for i in range(5))
     u2, phi2, k1u, k1p = (later[i:i + 1] for i in range(4))
     k2u, k2p = rates(load, u2, phi2, sa, sb, dist)
@@ -199,14 +200,14 @@
     phi = phi + 0.5 * TIME_STEP * (k1p + k2p)
     elem_count = u.shape[1]
     values = jnp.concatenate([u, phi, jnp.zeros((6, elem_count), jnp.float32)], axis=0)
-    spread(select_columns(values, selection(rows_ref[...], elem_count), NN)[0:2], sent_ref)
-
-
-def unsort_kernel(got_ref, slot_ref, u_ref, phi_ref):
-    elem_count = slot_ref.shape[1]
+    spread(select_columns(values, order_ref[...], NN)[0:2], sent_ref)
+
+
+def unsort_kernel(got_ref, order_ref, u_ref, phi_ref):
+    elem_count = order_ref.shape[1]
     flat = flattened(got_ref, elem_count)
     flat = jnp.concatenate([flat, jnp.zeros((6, elem_count), jnp.float32)], axis=0)
-    out = select_columns(flat, selection(slot_ref[...], elem_count), NN)
+    out = select_columns(flat, order_ref[...], NN)
     u_ref[...] = out[0:1]
     phi_ref[...] = out[1:2]
 
@@ -251,7 +252,6 @@
     coarse_v,
 ):
     members = lax.axis_size("blk")
-    place = jnp.stack([lax.axis_index("leaf"), lax.axis_index("blk")]).astype(jnp.int32)
     elems = ln_rate.shape[0]
     leaf_size = near_blocks.shape[1]
     groups, rank = coarse_v.shape[0], coarse_v.shape[1]
@@ -263,39 +263,35 @@
 
     elem_args = [
         value.reshape(1, elems)
-        for value in (ln_rate, log_state, sigma, fric_a, fric_b, slip_dist, leaf_of_elem)
+        for value in (leaf_of_elem, ln_rate, log_state, sigma, fric_a, fric_b, slip_dist)
     ]
-    sent, slot = call(
-        functools.partial(sort_kernel, members),
-        (shape(members, 8, 128), shape(1, elems, dtype=jnp.int32)),
-        place, *elem_args, scalars=(0,), far=range(1, 8),
-        scratch=[VMEM(value.shape, value.dtype) for value in elem_args]
-        + [pltpu.SemaphoreType.DMA((7,))],
-    )
+    scalar_args = [near_col, far_col, far_rank]
     weights = [
         near_blocks, far_u.reshape(-1, leaf_size), far_v.reshape(-1, leaf_size), coarse_u, coarse_v
     ]
-    scalar_args = [near_col, far_col, far_rank]
     far_rows = weights[1].shape[0]
-    near_mask, far_mask, near, far_u, far_v, coarse_u, coarse_v = call(
-        load_kernel,
+    bases = [near_blocks.shape] + [(far_rows, leaf_size)] * 2 + [(groups * rank, elems)] * 2
+    sent, elem_order, near_mask, far_mask, near, far_u, far_v, coarse_u, coarse_v = call(
+        functools.partial(sort_kernel, members),
         (
+            shape(members, 8, 128),
+            shape(elems, elems, dtype=jnp.bfloat16),
             shape(near_blocks.shape[0], members, leaf_size),
             shape(members, far_rows),
-            shape(*near_blocks.shape, dtype=jnp.bfloat16),
-            shape(far_rows, leaf_size, dtype=jnp.bfloat16),
-            shape(far_rows, leaf_size, dtype=jnp.bfloat16),
-            shape(groups * rank, elems, dtype=jnp.bfloat16),
-            shape(groups * rank, elems, dtype=jnp.bfloat16),
+            *[shape(*dims, dtype=jnp.bfloat16) for dims in bases],
         ),
-        place, near_count, *weights, *scalar_args, scalars=(0, 1), far=range(2, 10),
-        scratch=[SMEM(value.shape, value.dtype) for value in scalar_args]
-        + [pltpu.SemaphoreType.DMA((6 + 2 * groups,))],
-        flops=2 * near_blocks.size, moved=2 * near_blocks.size * 2,
-    )
-    state, rows, out = call(
+        near_count, *elem_args, *scalar_args, *weights, scalars=(0,), far=range(1, 16),
+        scratch=[VMEM(value.shape, value.dtype) for value in elem_args]
+        + [SMEM(value.shape, value.dtype) for value in scalar_args]
+        + [pltpu.SemaphoreType.DMA((13 + 2 * groups,))],
+    )
+    state, leaf_order, out = call(
         place_kernel,
-        (shape(8, elems), shape(1, elems, dtype=jnp.int32), shape(devices, 1, elems + width)),
+        (
+            shape(8, elems),
+            shape(elems, elems, dtype=jnp.bfloat16),
+            shape(devices, 1, elems + width),
+        ),
         swap(sent, "blk"), coarse_v,
     )
     fields = near, far_u, far_v, near_mask, far_mask, coarse_u
@@ -305,14 +301,14 @@
 
     later, out = call(
         functools.partial(first_kernel, groups), (shape(8, elems), shape(devices, 1, elems + width)),
-        place, state, coarse_v, share(out), *fields, scalars=(0,),
+        state, coarse_v, share(out), *fields,
     )
     sent = call(
         functools.partial(second_kernel, groups), shape(members, 2, 128),
-        place, state, later, rows, share(out), *fields, scalars=(0,),
+        state, later, leaf_order, share(out), *fields,
     )
     u, phi = call(
-        unsort_kernel, (shape(1, elems), shape(1, elems)), swap(sent, "blk"), slot
+        unsort_kernel, (shape(1, elems), shape(1, elems)), swap(sent, "blk"), elem_order
     )
     return u.reshape(elems), phi.reshape(elems)
 

time: 49.2 us -> 47.5 us (0.965)
  blocking collectives: 27.4 us -> 41.1 us
  starting transfers between devices: 7.26 us -> 0 us
  Pallas kernels: 8.78 us -> 4.83 us
  waiting for transfers between devices: 3.93 us -> 0 us
    all_to_all x3 -> x4, blocking collectives: 27.4 us -> 41.1 us  [swap(): return lax.all_to_all(value, axes, split_axis=0, concat_axis=0, tiled=True)]
    all_to_all x1 -> x0, starting transfers between devices: 7.26 us -> none  [swap(): return lax.all_to_all(value, axes, split_axis=0, concat_axis=0, tiled=True)]
    pallas_call x6 -> x5, Pallas kernels: 8.78 us -> 4.83 us  [call(): pl.pallas_call(kernel, out_shape=outs, in_specs=[pl.BlockSpec(memory_spac...]
    all_to_all x1 -> x0, waiting for transfers between devices: 3.93 us -> none  [swap(): return lax.all_to_all(value, axes, split_axis=0, concat_axis=0, tiled=True)]
  transfers between devices with their start and end apart: 1 -> 0, of which waited for: 1 -> 0; matrix products, arithmetic and copies ran while one was open for 0% -> 0% of each run, Pallas kernels for 4% -> 0%
where the time goes in v5:
time: 47.5 us; the launch traced here: 47.2 us
  blocking collectives  41.1 us (87%)
  Pallas kernels  4.83 us (10%)
  between operations  1.31 us (3%)
    all_to_all x4, blocking collectives, swap(): return lax.all_to_all(value, axes, split_axis=0, concat_axis=0, tiled=True)  41.1 us
    pallas_call x5, Pallas kernels, call(): pl.pallas_call(kernel, out_shape=outs, in_specs=[pl.BlockSpec(memory_spac...  4.83 us

profile of v5, /device:TPU:0, one launch (start us, length us, event | category | flops | bytes accessed | tf_op | source)
XLA Modules:
  0.0 47.2 jit_solution(13207178776456608535)
XLA Ops:
  1.3 1.7 %shard_map.167 = (f32[8,8,128]{2,1,0:T(8,128)S(1)}, bf16[512,512]{1,0:T(8,128)(2,1)S(1)}, f32[3,8,512]{2,1,0:T(8,128)S(1)}, f32[8,64]{1,0:T(8,128)S(1)}, bf16[3,...) custom-call(s32[1]{0:T(128)S(6)} %copy.18.near_count, ...), custom_call_target="tpu_custom_call" | custom-call | flops 1000 | bytes 1000 | tf_op jit(solution)/shard_map/pallas_call | solution.py:221
  3.0 13.7 %all_to_all.20.got_ref = f32[8,8,128]{2,1,0:T(8,128)S(1)} all-to-all(f32[8,8,128]{2,1,0:T(8,128)S(1)} %get-tuple-element.18), channel_id=1, replica_groups=mesh['leaf'=4,'blk'=8] {'blk'}, dimensions={0} | all-to-all | bytes 65536 | tf_op jit(solution)/shard_map/all_to_all | solution.py:262
  16.8 0.6 %shard_map.168 = (f32[8,512]{1,0:T(8,128)S(1)}, bf16[512,512]{1,0:T(8,128)(2,1)S(1)}, f32[32,1,640]{2,1,0:T(1,128)S(1)}) custom-call(f32[8,8,128]{2,1,0:T(8,128)S(1)} %all_to_all.20.got_ref, bf16[64,512]{1,0:T(8,128)(2,1)S(1)} %get-tuple-element.19.coarse_v_ref), custom_call_target="tpu_custom_call" | custom-call | flops 1000 | bytes 1000 | tf_op jit(solution)/shard_map/pallas_call | solution.py:221
  17.3 9.3 %all_to_all.21.refs_0_ = f32[32,1,640]{2,1,0:T(1,128)S(1)} all-to-all(f32[32,1,640]{2,1,0:T(1,128)S(1)} %get-tuple-element.21), channel_id=1, replica_groups=mesh['leaf'=4,'blk'=8] {'leaf','blk'}, dimensions={0} | all-to-all | bytes 163840 | tf_op jit(solution)/shard_map/all_to_all | solution.py:262
  26.6 0.8 %shard_map.169 = (f32[8,512]{1,0:T(8,128)S(1)}, f32[32,1,640]{2,1,0:T(1,128)S(1)}) custom-call(f32[8,512]{1,0:T(8,128)S(1)} %get-tuple-element.20.state_ref, bf16[64,512]{1,0:T(8,128)(2,1)S(1)} %get-tuple-element.19.coarse_v_ref, f32[32,1,640]{2,1,0:T(1,128)S(1)} %all_to_all.21.refs_0_, bf16[3,512,512]{2,1,0:T(8,128)(2,1)S(1)} %get-tuple-element.22.refs_1_, ...), custom_call_target="tpu_custom_call" | custom-call | flops 1000 | bytes 1000 | tf_op jit(solution)/shard_map/pallas_call | solution.py:221
  27.4 9.1 %all_to_all.22.refs_0_ = f32[32,1,640]{2,1,0:T(1,128)S(1)} all-to-all(f32[32,1,640]{2,1,0:T(1,128)S(1)} %get-tuple-element.30), channel_id=1, replica_groups=mesh['leaf'=4,'blk'=8] {'leaf','blk'}, dimensions={0} | all-to-all | bytes 163840 | tf_op jit(solution)/shard_map/all_to_all | solution.py:262
  36.6 0.9 %shard_map.170 = f32[8,2,128]{2,1,0:T(2,128)S(1)} custom-call(f32[8,512]{1,0:T(8,128)S(1)} %get-tuple-element.20.state_ref, f32[8,512]{1,0:T(8,128)S(1)} %get-tuple-element.28.next_ref, bf16[512,512]{1,0:T(8,128)(2,1)S(1)} %get-tuple-element.29.order_ref, f32[32,1,640]{2,1,0:T(1,128)S(1)} %all_to_all.22.refs_0_, ...), custom_call_target="tpu_custom_call" | custom-call | flops 1000 | bytes 1000 | tf_op jit(solution)/shard_map/pallas_call | solution.py:221
  37.4 8.9 %all_to_all.23.got_ref = f32[8,2,128]{2,1,0:T(2,128)S(1)} all-to-all(f32[8,2,128]{2,1,0:T(2,128)S(1)} %shard_map.170), channel_id=1, replica_groups=mesh['leaf'=4,'blk'=8] {'blk'}, dimensions={0} | all-to-all | bytes 16384 | tf_op jit(solution)/shard_map/all_to_all | solution.py:262
  46.4 0.8 %shard_map.171 = (f32[1,512]{1,0:T(1,128)}, f32[1,512]{1,0:T(1,128)}) custom-call(f32[8,2,128]{2,1,0:T(2,128)S(1)} %all_to_all.23.got_ref, bf16[512,512]{1,0:T(8,128)(2,1)S(1)} %get-tuple-element.31.order_ref), custom_call_target="tpu_custom_call" | custom-call | flops 1000 | bytes 1000 | tf_op jit(solution)/shard_map/pallas_call | solution.py:221

commit v6 on v5

v6 whole, which is shorter than its diff:
```python
import functools

import jax
import jax.numpy as jnp
from jax import lax
from jax.experimental import pallas as pl
from jax.experimental.pallas import tpu as pltpu
from jax.sharding import PartitionSpec as P

DAMPING = 0.5
PLATE_RATE = 1.0
TIME_STEP = 0.2

NN = (((1,), (0,)), ((), ()))
NT = (((1,), (1,)), ((), ()))
VMEM = pltpu.VMEM
SMEM = pltpu.SMEM

LANES = 128


def dot(left, right, dims):
    return lax.dot_general(left, right, dims, preferred_element_type=jnp.float32)


def low_matrix(index_row):
    rows = lax.broadcasted_iota(jnp.int32, (LANES, index_row.shape[1]), 0)
    return jnp.where(rows == (index_row & (LANES - 1)), 1.0, 0.0).astype(jnp.bfloat16)


def three_parts(values):
    high = values.astype(jnp.bfloat16).astype(jnp.float32)
    rest = values - high
    middle = rest.astype(jnp.bfloat16).astype(jnp.float32)
    return jnp.concatenate([high, middle, rest - middle], axis=0)


def joined(parts):
    count = parts.shape[0] // 3
    return parts[0:count] + parts[count:2 * count] + parts[2 * count:]


def scattered(values, index_row):
    parts = three_parts(values)
    count = parts.shape[0]
    high = index_row // LANES
    pieces = values.shape[1] // LANES
    left = jnp.concatenate([jnp.where(high == piece, parts, 0.0) for piece in range(pieces)], axis=0)
    moved = dot(left.astype(jnp.bfloat16), low_matrix(index_row), NT)
    return jnp.concatenate(
        [joined(moved[piece * count:(piece + 1) * count]) for piece in range(pieces)], axis=1
    )


def gathered(values, index_row):
    parts = three_parts(values)
    count = parts.shape[0]
    high = index_row // LANES
    pieces = values.shape[1] // LANES
    left = jnp.concatenate(
        [parts[:, piece * LANES:(piece + 1) * LANES] for piece in range(pieces)], axis=0
    )
    moved = dot(left.astype(jnp.bfloat16), low_matrix(index_row), NN)
    total = jnp.zeros((count, index_row.shape[1]), jnp.float32)
    for piece in range(pieces):
        total = jnp.where(high == piece, moved[piece * count:(piece + 1) * count], total)
    return joined(total)


def padded(rows, count):
    missing = count - len(rows)
    if missing:
        rows = rows + [jnp.zeros((missing, rows[0].shape[1]), jnp.float32)]
    return jnp.concatenate(rows, axis=0)


def as_lines(row):
    return jnp.concatenate(
        [row[:, i * LANES:(i + 1) * LANES] for i in range(row.shape[1] // LANES)], axis=0
    )


def peer_lanes(ref, first, members, rows, elem_count):
    width = elem_count // members
    return jnp.concatenate([ref[first + peer, 0:rows, 0:width] for peer in range(members)], axis=1)


def start_copies(sources, targets, sems):
    copies = [
        pltpu.make_async_copy(source, target, sems.at[i])
        for i, (source, target) in enumerate(zip(sources, targets))
    ]
    for copy in copies:
        copy.start()
    return copies


def sort_kernel(members, near_count, *refs):
    elem_refs, scalar_refs, weight_refs = refs[:7], refs[7:10], refs[10:14]
    sent_ref, slot_ref, slot_row_ref, near_mask_ref, far_mask_ref = refs[14:19]
    weight_outs, elem_bufs, scalar_bufs, sems = refs[19:23], refs[23:30], refs[30:33], refs[33]
    copies = start_copies(
        [*elem_refs, *scalar_refs, *weight_refs], [*elem_bufs, *scalar_bufs, *weight_outs], sems
    )
    mine = lax.axis_index("leaf")
    elem_count = elem_bufs[0].shape[1]
    peer_rows = elem_count // members
    pieces = elem_count // LANES
    before = lax.broadcasted_iota(jnp.int32, (LANES, LANES), 0)
    after = lax.broadcasted_iota(jnp.int32, (LANES, LANES), 1)
    triangle = jnp.where(before < after, 1.0, 0.0).astype(jnp.bfloat16)
    copies[0].wait()
    local = elem_bufs[0][...] - mine * (members * elem_count)
    target = local // elem_count
    target_row = local - target * elem_count
    peers = lax.broadcasted_iota(jnp.int32, (members, elem_count), 0)
    onehot = jnp.where(peers == target, 1.0, 0.0)
    lines = [onehot[:, i * LANES:(i + 1) * LANES] for i in range(pieces)]
    inside = dot(jnp.concatenate(lines, axis=0).astype(jnp.bfloat16), triangle, NN)
    passed = jnp.zeros((members, 1), jnp.float32)
    ranks = []
    for i, line in enumerate(lines):
        earlier = inside[i * members:(i + 1) * members] + passed
        ranks.append(jnp.sum(earlier * line, axis=0, keepdims=True))
        passed = passed + jnp.sum(line, axis=1, keepdims=True)
    slot = target * peer_rows + jnp.concatenate(ranks, axis=1).astype(jnp.int32)
    slot_ref[...] = slot
    for copy in copies[1:7]:
        copy.wait()
    u, phi, sigma, fric_a, fric_b, dist = (buf[...] for buf in elem_bufs[1:])
    deficit = (PLATE_RATE - jnp.exp(u)).astype(jnp.bfloat16).astype(jnp.float32)
    rows = [u, phi, sigma * fric_a, sigma * fric_b, dist, target_row.astype(jnp.float32), deficit]
    values = scattered(padded(rows, 8), slot)
    slot_row_ref[...] = values[5:6].astype(jnp.int32)
    everyone = jnp.concatenate([as_lines(values[6:7]), as_lines(values[5:6])], axis=0)
    for peer in range(members):
        sent_ref[peer, 0:8, 0:peer_rows] = values[:, peer * peer_rows:(peer + 1) * peer_rows]
        sent_ref[peer, 8:8 + 2 * pieces, :] = everyone

    for copy in copies[7:10]:
        copy.wait()
    near_col, far_col, far_rank = scalar_bufs
    far_slots = far_col.shape[0]
    far_width = far_mask_ref.shape[1] // far_slots
    block = lax.broadcasted_iota(jnp.int32, near_mask_ref.shape[1:], 0)
    for number in range(near_mask_ref.shape[0]):
        column = jnp.where(number < near_count[0], near_col[number], -1)
        near_mask_ref[number] = jnp.where(block == column, 1.0, 0.0)
    block = lax.broadcasted_iota(jnp.int32, far_mask_ref.shape, 0)
    lane = lax.broadcasted_iota(jnp.int32, far_mask_ref.shape, 1)
    column = jnp.full(far_mask_ref.shape, -1, jnp.int32)
    for number in range(far_slots):
        low = number * far_width
        kept = (lane >= low) & (lane < low + far_rank[number])
        column = jnp.where(kept, far_col[number], column)
    far_mask_ref[...] = jnp.where(block == column, 1.0, 0.0)
    for copy in copies[10:]:
        copy.wait()


def partial_row(deficit, coarse_v_ref):
    wide = jnp.broadcast_to(deficit, (8, deficit.shape[1])).astype(jnp.bfloat16)
    partial = dot(wide, coarse_v_ref[...], NT)[0:1]
    rest = -partial.shape[1] % LANES
    if rest:
        partial = jnp.concatenate([partial, jnp.zeros((1, rest), jnp.float32)], axis=1)
    return partial


def inside_rows(deficits, near_ref, far_u_ref, far_v_ref, near_mask_ref, far_mask_ref):
    total = jnp.zeros(deficits.shape, jnp.float32)
    for slot in range(near_ref.shape[0]):
        source = (deficits * near_mask_ref[slot]).astype(jnp.bfloat16)
        total = total + dot(source, near_ref[slot], NT)
    project = dot(deficits.astype(jnp.bfloat16), far_v_ref[...], NT) * far_mask_ref[...]
    project = jnp.sum(project, axis=0, keepdims=True)
    project = jnp.broadcast_to(project, (8, project.shape[1])).astype(jnp.bfloat16)
    far = dot(project, far_u_ref[...], NN)
    return jnp.sum(total, axis=0, keepdims=True) + far[0:1]


def coefficients(sums, rank):
    groups, width = len(sums), sums[0].shape[1]
    mine = lax.axis_index("leaf")
    table = padded(sums, -(-groups // 8) * 8)
    lane = lax.broadcasted_iota(jnp.int32, table.shape, 1) // rank
    row = lax.broadcasted_iota(jnp.int32, table.shape, 0)
    table = jnp.where(lane == mine, table, 0.0).astype(jnp.bfloat16)
    across = lax.broadcasted_iota(jnp.int32, (width, width), 0) % rank
    down = lax.broadcasted_iota(jnp.int32, (width, width), 1) % rank
    spread = dot(table, jnp.where(across == down, 1.0, 0.0).astype(jnp.bfloat16), NN)
    kept = (lane == row) & (row != mine)
    return jnp.sum(jnp.where(kept, spread, 0.0), axis=0, keepdims=True)


def coarse_all(weights, members, bases_ref):
    width = weights.shape[1]
    tiled = jnp.concatenate([weights] * members, axis=1)
    lane = lax.broadcasted_iota(jnp.int32, (members, members * width), 1) // width
    row = lax.broadcasted_iota(jnp.int32, (members, members * width), 0)
    left = jnp.where(lane == row, tiled, 0.0).astype(jnp.bfloat16)
    return dot(left, bases_ref[...], NN)


def place_kernel(got_ref, coarse_v_ref, *refs):
    field_refs, state_ref, rows_ref, out_ref, lines_ref = refs[:5], refs[5], refs[6], refs[7], refs[8]
    members = got_ref.shape[0]
    elem_count = state_ref.shape[1]
    pieces = elem_count // LANES
    peer_rows = elem_count // members
    per_line = LANES // peer_rows
    line_block = lax.broadcasted_iota(jnp.int32, (per_line * pieces, LANES), 0) // pieces
    line_piece = lax.broadcasted_iota(jnp.int32, (per_line * pieces, LANES), 0) % pieces
    lane_block = lax.broadcasted_iota(jnp.int32, (per_line * pieces, LANES), 1) // peer_rows
    own_lane = line_block == lane_block
    for line in range(pieces):
        left, right = [], []
        for peer in range(members):
            value = got_ref[peer, 8 + line:9 + line, :]
            row = got_ref[peer, 8 + pieces + line:9 + pieces + line, :].astype(jnp.int32)
            left.append(jnp.where(own_lane & (line_piece == row // LANES), value, 0.0))
            right.append(low_matrix(row))
        left = jnp.concatenate(left, axis=1).astype(jnp.bfloat16)
        count = per_line * pieces
        lines_ref[line * count:(line + 1) * count, :] = dot(left, jnp.concatenate(right, axis=1), NT)
    deficits = jnp.concatenate(
        [lines_ref[pl.ds(piece, members, stride=pieces), :] for piece in range(pieces)], axis=1
    )
    inside = inside_rows(deficits, *field_refs)

    flat = peer_lanes(got_ref, 0, members, 8, elem_count)
    rows = flat[5:6].astype(jnp.int32)
    rows_ref[...] = rows
    state = scattered(flat, rows)
    u, phi, sa, sb, dist = (state[i:i + 1] for i in range(5))
    velocity = jnp.exp(u)
    k1p = (jnp.exp(-phi) - velocity) / dist
    inverse = 1.0 / (sa + DAMPING * velocity)
    u2 = u + TIME_STEP * ((inside - sb * k1p) * inverse)
    factor = TIME_STEP * inverse
    state_ref[...] = jnp.concatenate([u, phi, sa, sb, dist, k1p, u2, factor], axis=0)
    sent = jnp.concatenate([u2, factor, partial_row(state[6:7], coarse_v_ref)], axis=1)
    out_ref[...] = jnp.broadcast_to(sent[None], out_ref.shape)


def second_kernel(
    groups, state_ref, rows_ref, all_ref, bases_ref, coarse_v_ref, *refs
):
    field_refs, sent_ref, bases_out, sem = refs[:5], refs[5], refs[6], refs[7]
    copy = pltpu.make_async_copy(bases_ref, bases_out, sem.at[0])
    copy.start()
    members, elem_count = refs[3].shape[1], state_ref.shape[1]
    width = coarse_v_ref.shape[0]
    mine, me = lax.axis_index("leaf"), lax.axis_index("blk")
    sums = [
        jnp.sum(
            all_ref[group * members:(group + 1) * members, 0, 2 * elem_count:2 * elem_count + width],
            axis=0, keepdims=True,
        )
        for group in range(groups)
    ]
    weights = coefficients(sums, width // groups)
    own = all_ref[pl.ds(mine * members, members), 0, 0:2 * elem_count]
    copy.wait()
    coarse = coarse_all(weights, members, bases_out)
    u2_all = own[:, 0:elem_count] + own[:, elem_count:] * coarse
    deficits = (PLATE_RATE - jnp.exp(u2_all)).astype(jnp.bfloat16).astype(jnp.float32)
    inside = inside_rows(deficits, *field_refs)

    state = state_ref[...]
    u, phi, sa, sb, dist, k1p = (state[i:i + 1] for i in range(6))
    here = lax.broadcasted_iota(jnp.int32, u2_all.shape, 0) == me
    u2 = jnp.sum(jnp.where(here, u2_all, 0.0), axis=0, keepdims=True)
    deficit = jnp.sum(jnp.where(here, deficits, 0.0), axis=0, keepdims=True)
    phi2 = phi + TIME_STEP * k1p
    velocity = jnp.exp(u2)
    k2p = (jnp.exp(-phi2) - velocity) / dist
    inverse = 0.5 * TIME_STEP / (sa + DAMPING * velocity)
    u_next = 0.5 * (u + u2) + (inside - sb * k2p) * inverse
    phi_next = phi + 0.5 * TIME_STEP * (k1p + k2p)
    sent = gathered(padded([u_next, inverse, phi_next], 8), rows_ref[...])
    partial = as_lines(partial_row(deficit, coarse_v_ref))
    peer_rows = elem_count // members
    for device in range(groups * members):
        peer = device % members
        sent_ref[device, 0:3, 0:peer_rows] = sent[0:3, peer * peer_rows:(peer + 1) * peer_rows]
        sent_ref[device, 3:3 + partial.shape[0], :] = partial


def finish_kernel(groups, width, got_ref, bases_ref, slot_ref, slot_row_ref, u_ref, phi_ref, *scratch):
    if scratch:
        copy = pltpu.make_async_copy(bases_ref, scratch[0], scratch[1].at[0])
        copy.start()
        copy.wait()
        bases_ref = scratch[0]
    elem_count = slot_ref.shape[1]
    members = got_ref.shape[0] // groups
    sums = []
    for group in range(groups):
        total = jnp.sum(got_ref[group * members:(group + 1) * members], axis=0)
        lines = [total[3 + i:4 + i, :] for i in range(pl.cdiv(width, LANES))]
        sums.append(jnp.concatenate(lines, axis=1)[:, 0:width])
    coarse = coarse_all(coefficients(sums, width // groups), members, bases_ref)
    row = slot_row_ref[...]
    block = lax.broadcasted_iota(jnp.int32, (members, elem_count), 0)
    lane_block = lax.broadcasted_iota(jnp.int32, (members, elem_count), 1) // (elem_count // members)
    rows = gathered(coarse, row)
    found = jnp.sum(jnp.where(block == lane_block, rows, 0.0), axis=0, keepdims=True)
    first = lax.axis_index("leaf") * members
    flat = peer_lanes(got_ref, first, members, 3, elem_count)
    u_next = flat[0:1] + flat[1:2] * found
    out = gathered(padded([u_next, flat[2:3]], 8), slot_ref[...])
    u_ref[...] = out[0:1]
    phi_ref[...] = out[1:2]


def call(kernel, outs, *args, scalars=(), far=(), scratch=(), flops=1000, moved=1000):
    spaces = [SMEM if i in scalars else pl.ANY if i in far else VMEM for i in range(len(args))]
    args = [
        pltpu.with_memory_space_constraint(arg, pltpu.HBM) if i in far else arg
        for i, arg in enumerate(args)
    ]
    return pl.pallas_call(
        kernel,
        out_shape=outs,
        in_specs=[pl.BlockSpec(memory_space=space) for space in spaces],
        out_specs=jax.tree.map(lambda _: pl.BlockSpec(memory_space=VMEM), outs),
        scratch_shapes=list(scratch),
        cost_estimate=pl.CostEstimate(flops=flops, bytes_accessed=moved, transcendentals=0),
        compiler_params=pltpu.CompilerParams(vmem_limit_bytes=32 * 1024 * 1024),
    )(*args)


def shape(*dims, dtype=jnp.float32):
    return jax.ShapeDtypeStruct(dims, dtype)


def body(
    ln_rate,
    log_state,
    sigma,
    fric_a,
    fric_b,
    slip_dist,
    leaf_of_elem,
    near_blocks,
    near_col,
    near_count,
    far_u,
    far_v,
    far_col,
    far_rank,
    coarse_u,
    coarse_v,
):
    members = lax.axis_size("blk")
    elems = ln_rate.shape[0]
    leaf_size = near_blocks.shape[1]
    groups, rank = coarse_v.shape[0], coarse_v.shape[1]
    devices = groups * members
    width = groups * rank
    lines = pl.cdiv(width, LANES)
    sent_rows = 1 << (2 + lines).bit_length()
    integer = jnp.int32

    def swap(value, axes):
        return lax.all_to_all(value, axes, split_axis=0, concat_axis=0, tiled=True)

    bases = lax.all_gather(coarse_u.reshape(width, elems), "blk", axis=0, tiled=True)
    elem_args = [
        value.reshape(1, elems)
        for value in (leaf_of_elem, ln_rate, log_state, sigma, fric_a, fric_b, slip_dist)
    ]
    scalar_args = [near_col, far_col, far_rank]
    weights = [
        near_blocks, far_u.reshape(-1, leaf_size), far_v.reshape(-1, leaf_size),
        coarse_v.reshape(width, elems),
    ]
    far_rows = weights[1].shape[0]
    sent, slot, slot_row, near_mask, far_mask, near, far_u, far_v, coarse_v = call(
        functools.partial(sort_kernel, members),
        (
            shape(members, 8 + 2 * (elems // LANES), LANES),
            shape(1, elems, dtype=integer),
            shape(1, elems, dtype=integer),
            shape(near_blocks.shape[0], members, leaf_size),
            shape(members, far_rows),
            *[shape(*value.shape, dtype=jnp.bfloat16) for value in weights],
        ),
        near_count, *elem_args, *scalar_args, *weights, scalars=(0,), far=range(1, 15),
        scratch=[VMEM(value.shape, value.dtype) for value in elem_args]
        + [SMEM(value.shape, value.dtype) for value in scalar_args]
        + [pltpu.SemaphoreType.DMA((14,))],
    )
    fields = near, far_u, far_v, near_mask, far_mask
    state, rows, out = call(
        place_kernel,
        (
            shape(8, elems),
            shape(1, elems, dtype=integer),
            shape(devices, 1, 2 * elems + lines * LANES),
        ),
        swap(sent, "blk"), coarse_v, *fields,
        scratch=[VMEM((members * (elems // LANES), LANES), jnp.float32)],
    )
    held = members * width * elems <= 1 << 21
    place = shape(members * width, elems, dtype=jnp.bfloat16)
    buffer = [VMEM(place.shape, place.dtype)]
    signal = [pltpu.SemaphoreType.DMA((1,))]
    outs = call(
        functools.partial(second_kernel, groups),
        (shape(devices, sent_rows, LANES),) + (place,) * held,
        state, rows, swap(out, ("leaf", "blk")), bases, coarse_v, *fields, far=(3,),
        scratch=signal if held else buffer + signal,
    )
    u, phi = call(
        functools.partial(finish_kernel, groups, width), (shape(1, elems), shape(1, elems)),
        swap(outs[0], ("leaf", "blk")), outs[1] if held else bases, slot, slot_row,
        far=() if held else (1,), scratch=() if held else buffer + signal,
    )
    return u.reshape(elems), phi.reshape(elems)


def solution(mesh):
    each = P(("leaf", "blk"))
    blocks = P(("leaf", "blk"), None, None)
    last = P(None, None, ("leaf", "blk"))
    in_specs = (each,) * 7 + (blocks, each, each, blocks, blocks, each, each, last, last)
    return jax.shard_map(body, mesh=mesh, in_specs=in_specs, out_specs=(each, each), check_vma=False)
```

time: 47.5 us -> 71.3 us (1.50)
  blocking collectives: 41.1 us -> 60.3 us
  starting transfers between devices: 0 us -> 2.57 us
  Pallas kernels: 4.83 us -> 6.78 us
    all_gather x0 -> x1, blocking collectives: none -> 34.9 us  [body(): lax.all_gather(coarse_u.reshape(width, elems), 'blk', axis=0, tiled=True)]
    all_to_all x4 -> x2, blocking collectives: 41.1 us -> 25.4 us  [swap(): return lax.all_to_all(value, axes, split_axis=0, concat_axis=0, tiled=True)]
    all_to_all x0 -> x1, starting transfers between devices: none -> 2.57 us  [swap(): return lax.all_to_all(value, axes, split_axis=0, concat_axis=0, tiled=True)]
    pallas_call x5 -> x4, Pallas kernels: 4.83 us -> 6.78 us  [call(): pl.pallas_call(kernel, out_shape=outs, in_specs=[pl.BlockSpec(memory_spac...]
  transfers between devices with their start and end apart: 0 -> 1, of which waited for: 0 -> 0; matrix products, arithmetic and copies ran while one was open for 0% -> 0% of each run, Pallas kernels for 0% -> 0%
where the time goes in v6:
time: 71.3 us; the launch traced here: 70.9 us
  blocking collectives  60.3 us (85%)
  Pallas kernels  6.78 us (10%)
  starting transfers between devices  2.57 us (4%)
  between operations  1.32 us (2%)
    all_gather x1, blocking collectives, body(): lax.all_gather(coarse_u.reshape(width, elems), 'blk', axis=0, tiled=True)  34.9 us
    all_to_all x2, blocking collectives, swap(): return lax.all_to_all(value, axes, split_axis=0, concat_axis=0, tiled=True)  25.4 us
    pallas_call x4, Pallas kernels, call(): pl.pallas_call(kernel, out_shape=outs, in_specs=[pl.BlockSpec(memory_spac...  6.78 us
    all_to_all x1, starting transfers between devices, swap(): return lax.all_to_all(value, axes, split_axis=0, concat_axis=0, tiled=True)  2.57 us
  transfers between devices with their start and end apart: 1, of which 0 were waited for; matrix products, arithmetic and copies ran while one was open for 0% of the time, Pallas kernels for 0%

profile of v6, /device:TPU:0, one launch (start us, length us, event | category | flops | bytes accessed | tf_op | source)
XLA Modules:
  0.0 70.9 jit_solution(9428525413745368305)
XLA Ops:
  1.3 1.7 %shard_map.167 = (f32[8,16,128]{2,1,0:T(8,128)S(1)}, s32[1,512]{1,0:T(1,128)S(1)}, s32[1,512]{1,0:T(1,128)S(1)}, f32[3,8,512]{2,1,0:T(8,128)S(1)}, f32[8,64]{1,0...) custom-call(s32[1]{0:T(128)S(6)} %copy.18.near_count, ...), custom_call_target="tpu_custom_call" | custom-call | flops 1000 | bytes 1000 | tf_op jit(solution)/shard_map/pallas_call | solution.py:323
  2.9 0.0 copy-start
  3.0 14.1 %all_to_all.15.got_ref = f32[8,16,128]{2,1,0:T(8,128)S(1)} all-to-all(f32[8,16,128]{2,1,0:T(8,128)S(1)} %get-tuple-element.18), channel_id=1, replica_groups=mesh['leaf'=4,'blk'=8] {'blk'}, dimensions={0} | all-to-all | bytes 131072 | tf_op jit(solution)/shard_map/all_to_all | solution.py:367
  17.0 1.7 %shard_map.168 = (f32[8,512]{1,0:T(8,128)S(1)}, s32[1,512]{1,0:T(1,128)S(1)}, f32[32,1,1152]{2,1,0:T(1,128)}) custom-call(f32[8,16,128]{2,1,0:T(8,128)S(1)} %all_to_all.15.got_ref, bf16[64,512]{1,0:T(8,128)(2,1)S(1)} %get-tuple-element.19.coarse_v_ref, bf16[3,512,512]{2,1,0:T(8,128)(2,1)S(1)} %get-tuple-element.20.refs_0_, ...), custom_call_target="tpu_custom_call" | custom-call | flops 1000 | bytes 1000 | tf_op jit(solution)/shard_map/pallas_call | solution.py:323
  18.8 2.6 %all-to-all-start.1 = ((f32[32,1,1152]{2,1,0:T(1,128)}), f32[32,1,1152]{2,1,0:T(1,128)S(1)}, u32[]{:S(2)}, u32[]{:S(2)}) async-start(f32[32,1,1152]{2,1,0:T(1,128)} %get-tuple-element.27), calls=%async_computation.1 | async-start | bytes 294912 | tf_op jit(solution)/shard_map/all_to_all | solution.py:367
  21.4 0.0 copy-done
  21.4 34.9 %all_gather.3.bases_ref = bf16[512,512]{1,0:T(8,128)(2,1)} all-gather(bf16[64,512]{1,0:T(8,128)(2,1)S(1)} %bitcast.16), channel_id=1, replica_groups=mesh['leaf'=4,'blk'=8] {'blk'}, dimensions={0}, use_global_device_ids=true | all-gather | bytes 589824 | tf_op jit(solution)/shard_map/all_gather | solution.py:369
  56.2 0.0 all-to-all-done.1.all_ref
  56.2 2.1 %shard_map.169 = (f32[32,4,128]{2,1,0:T(4,128)S(1)}, bf16[512,512]{1,0:T(8,128)(2,1)S(1)}) custom-call(f32[8,512]{1,0:T(8,128)S(1)} %get-tuple-element.25.state_ref, s32[1,512]{1,0:T(1,128)S(1)} %get-tuple-element.26.rows_ref, f32[32,1,1152]{2,1,0:T(1,128)S(1)} %all-to-all-done.1.all_ref, bf16[512,512]{1,0:T(8,128)(2,1)} %all_gather.3.bases_ref, ...), custom_call_target="tpu_custom_call" | custom-call | flops 1000 | bytes 1000 | tf_op jit(solution)/shard_map/pallas_call | solution.py:323
  58.4 11.3 %all_to_all.16.got_ref = f32[32,4,128]{2,1,0:T(4,128)S(1)} all-to-all(f32[32,4,128]{2,1,0:T(4,128)S(1)} %get-tuple-element.28), channel_id=1, replica_groups=mesh['leaf'=4,'blk'=8] {'leaf','blk'}, dimensions={0} | all-to-all | bytes 131072 | tf_op jit(solution)/shard_map/all_to_all | solution.py:367
  69.7 1.3 %shard_map.170 = (f32[1,512]{1,0:T(1,128)}, f32[1,512]{1,0:T(1,128)}) custom-call(f32[32,4,128]{2,1,0:T(4,128)S(1)} %all_to_all.16.got_ref, bf16[512,512]{1,0:T(8,128)(2,1)S(1)} %get-tuple-element.29.bases_ref, s32[1,512]{1,0:T(1,128)S(1)} %get-tuple-element.30.slot_ref, s32[1,512]{1,0:T(1,128)S(1)} %get-tuple-element.31.slot_row_ref), custom_call_target="tpu_custom_call" | custom-call | flops 1000 | bytes 1000 | tf_op jit(solution)/shard_map/pallas_call | solution.py:323
Async XLA Ops:
  2.9 18.4 %copy-start = (bf16[4,16,512]{2,1,0:T(8,128)(2,1)S(1)}, bf16[4,16,512]{2,1,0:T(8,128)(2,1)}, u32[]{:S(2)}) copy-start(bf16[4,16,512]{2,1,0:T(8,128)(2,1)} %param.30) | copy-start | bytes 196612
  18.8 37.5 %all-to-all-start.1 = ((f32[32,1,1152]{2,1,0:T(1,128)}), f32[32,1,1152]{2,1,0:T(1,128)S(1)}, u32[]{:S(2)}, u32[]{:S(2)}) async-start(f32[32,1,1152]{2,1,0:T(1,128)} %get-tuple-element.27), calls=%async_computation.1 | async-start | bytes 294912 | tf_op jit(solution)/shard_map/all_to_all | solution.py:367

commit v7 on v6

--- a/solution.py
+++ b/solution.py
@@ -95,7 +95,7 @@
     return copies
 
 
-def sort_kernel(members, near_count, *refs):
+def sort_kernel(members, *refs):
     elem_refs, scalar_refs, weight_refs = refs[:7], refs[7:10], refs[10:14]
     sent_ref, slot_ref, slot_row_ref, near_mask_ref, far_mask_ref = refs[14:19]
     weight_outs, elem_bufs, scalar_bufs, sems = refs[19:23], refs[23:30], refs[30:33], refs[33]
@@ -144,8 +144,7 @@
     far_width = far_mask_ref.shape[1] // far_slots
     block = lax.broadcasted_iota(jnp.int32, near_mask_ref.shape[1:], 0)
     for number in range(near_mask_ref.shape[0]):
-        column = jnp.where(number < near_count[0], near_col[number], -1)
-        near_mask_ref[number] = jnp.where(block == column, 1.0, 0.0)
+        near_mask_ref[number] = jnp.where(block == near_col[number], 1.0, 0.0)
     block = lax.broadcasted_iota(jnp.int32, far_mask_ref.shape, 0)
     lane = lax.broadcasted_iota(jnp.int32, far_mask_ref.shape, 1)
     column = jnp.full(far_mask_ref.shape, -1, jnp.int32)
@@ -167,10 +166,11 @@
     return partial
 
 
-def inside_rows(deficits, near_ref, far_u_ref, far_v_ref, near_mask_ref, far_mask_ref):
+def inside_rows(deficits, near_count, near_ref, far_u_ref, far_v_ref, near_mask_ref, far_mask_ref):
     total = jnp.zeros(deficits.shape, jnp.float32)
     for slot in range(near_ref.shape[0]):
-        source = (deficits * near_mask_ref[slot]).astype(jnp.bfloat16)
+        live = jnp.where(slot < near_count[0], 1.0, 0.0)
+        source = (deficits * (near_mask_ref[slot] * live)).astype(jnp.bfloat16)
         total = total + dot(source, near_ref[slot], NT)
     project = dot(deficits.astype(jnp.bfloat16), far_v_ref[...], NT) * far_mask_ref[...]
     project = jnp.sum(project, axis=0, keepdims=True)
@@ -193,17 +193,32 @@
     return jnp.sum(jnp.where(kept, spread, 0.0), axis=0, keepdims=True)
 
 
-def coarse_all(weights, members, bases_ref):
+def coarse_all(weights, members, bases_refs):
     width = weights.shape[1]
-    tiled = jnp.concatenate([weights] * members, axis=1)
-    lane = lax.broadcasted_iota(jnp.int32, (members, members * width), 1) // width
-    row = lax.broadcasted_iota(jnp.int32, (members, members * width), 0)
-    left = jnp.where(lane == row, tiled, 0.0).astype(jnp.bfloat16)
-    return dot(left, bases_ref[...], NN)
+    half = members // 2
+    tiled = jnp.concatenate([weights] * half, axis=1)
+    place = lax.broadcasted_iota(jnp.int32, (members, half * width), 1) // width
+    row = lax.broadcasted_iota(jnp.int32, (members, half * width), 0) ^ lax.axis_index("blk")
+    bits = members.bit_length() - 1
+    total = jnp.zeros((members, bases_refs[0].shape[1]), jnp.float32)
+    for number, ref in enumerate(bases_refs):
+        source = jnp.full(place.shape, number, jnp.int32)
+        for bit in range(bits - 1):
+            source = source | (((place >> bit) & 1) << (bits - 1 - bit))
+        left = jnp.where(source == row, tiled, 0.0).astype(jnp.bfloat16)
+        total = total + dot(left, ref[...], NN)
+    return total
+
+
+def stack_kernel(held_ref, came_ref, *refs):
+    out_ref = refs[-1]
+    count = held_ref.shape[0]
+    out_ref[0:count, :] = held_ref[...]
+    out_ref[count:2 * count, :] = came_ref[...]
 
 
 def place_kernel(got_ref, coarse_v_ref, *refs):
-    field_refs, state_ref, rows_ref, out_ref, lines_ref = refs[:5], refs[5], refs[6], refs[7], refs[8]
+    field_refs, state_ref, rows_ref, out_ref, lines_ref = refs[:6], refs[6], refs[7], refs[8], refs[9]
     members = got_ref.shape[0]
     elem_count = state_ref.shape[1]
     pieces = elem_count // LANES
@@ -243,13 +258,9 @@
     out_ref[...] = jnp.broadcast_to(sent[None], out_ref.shape)
 
 
-def second_kernel(
-    groups, state_ref, rows_ref, all_ref, bases_ref, coarse_v_ref, *refs
-):
-    field_refs, sent_ref, bases_out, sem = refs[:5], refs[5], refs[6], refs[7]
-    copy = pltpu.make_async_copy(bases_ref, bases_out, sem.at[0])
-    copy.start()
-    members, elem_count = refs[3].shape[1], state_ref.shape[1]
+def second_kernel(groups, state_ref, rows_ref, all_ref, held_ref, came_ref, coarse_v_ref, *refs):
+    field_refs, sent_ref = refs[:6], refs[6]
+    members, elem_count = refs[4].shape[1], state_ref.shape[1]
     width = coarse_v_ref.shape[0]
     mine, me = lax.axis_index("leaf"), lax.axis_index("blk")
     sums = [
@@ -261,8 +272,7 @@
     ]
     weights = coefficients(sums, width // groups)
     own = all_ref[pl.ds(mine * members, members), 0, 0:2 * elem_count]
-    copy.wait()
-    coarse = coarse_all(weights, members, bases_out)
+    coarse = coarse_all(weights, members, (held_ref, came_ref))
     u2_all = own[:, 0:elem_count] + own[:, elem_count:] * coarse
     deficits = (PLATE_RATE - jnp.exp(u2_all)).astype(jnp.bfloat16).astype(jnp.float32)
     inside = inside_rows(deficits, *field_refs)
@@ -287,12 +297,9 @@
         sent_ref[device, 3:3 + partial.shape[0], :] = partial
 
 
-def finish_kernel(groups, width, got_ref, bases_ref, slot_ref, slot_row_ref, u_ref, phi_ref, *scratch):
-    if scratch:
-        copy = pltpu.make_async_copy(bases_ref, scratch[0], scratch[1].at[0])
-        copy.start()
-        copy.wait()
-        bases_ref = scratch[0]
+def finish_kernel(
+    groups, width, got_ref, held_ref, came_ref, slot_ref, slot_row_ref, u_ref, phi_ref
+):
     elem_count = slot_ref.shape[1]
     members = got_ref.shape[0] // groups
     sums = []
@@ -300,7 +307,7 @@
         total = jnp.sum(got_ref[group * members:(group + 1) * members], axis=0)
         lines = [total[3 + i:4 + i, :] for i in range(pl.cdiv(width, LANES))]
         sums.append(jnp.concatenate(lines, axis=1)[:, 0:width])
-    coarse = coarse_all(coefficients(sums, width // groups), members, bases_ref)
+    coarse = coarse_all(coefficients(sums, width // groups), members, (held_ref, came_ref))
     row = slot_row_ref[...]
     block = lax.broadcasted_iota(jnp.int32, (members, elem_count), 0)
     lane_block = lax.broadcasted_iota(jnp.int32, (members, elem_count), 1) // (elem_count // members)
@@ -366,7 +373,9 @@
     def swap(value, axes):
         return lax.all_to_all(value, axes, split_axis=0, concat_axis=0, tiled=True)
 
-    bases = lax.all_gather(coarse_u.reshape(width, elems), "blk", axis=0, tiled=True)
+    def partner(value, bit):
+        return lax.ppermute(value, "blk", [(i, i ^ (1 << bit)) for i in range(members)])
+
     elem_args = [
         value.reshape(1, elems)
         for value in (leaf_of_elem, ln_rate, log_state, sigma, fric_a, fric_b, slip_dist)
@@ -387,12 +396,18 @@
             shape(members, far_rows),
             *[shape(*value.shape, dtype=jnp.bfloat16) for value in weights],
         ),
-        near_count, *elem_args, *scalar_args, *weights, scalars=(0,), far=range(1, 15),
+        *elem_args, *scalar_args, *weights, far=range(14),
         scratch=[VMEM(value.shape, value.dtype) for value in elem_args]
         + [SMEM(value.shape, value.dtype) for value in scalar_args]
         + [pltpu.SemaphoreType.DMA((14,))],
     )
-    fields = near, far_u, far_v, near_mask, far_mask
+    bases = coarse_u.reshape(width, elems)
+    for bit in range(members.bit_length() - 2, 0, -1):
+        came = partner(bases, bit)
+        stacked = shape(2 * bases.shape[0], elems, dtype=jnp.bfloat16)
+        bases = call(stack_kernel, stacked, bases, came, slot, flops=2**26, moved=2**22)
+    bases = bases, partner(bases, 0)
+    fields = near_count, near, far_u, far_v, near_mask, far_mask
     state, rows, out = call(
         place_kernel,
         (
@@ -400,23 +415,16 @@
             shape(1, elems, dtype=integer),
             shape(devices, 1, 2 * elems + lines * LANES),
         ),
-        swap(sent, "blk"), coarse_v, *fields,
+        swap(sent, "blk"), coarse_v, *fields, scalars=(2,),
         scratch=[VMEM((members * (elems // LANES), LANES), jnp.float32)],
     )
-    held = members * width * elems <= 1 << 21
-    place = shape(members * width, elems, dtype=jnp.bfloat16)
-    buffer = [VMEM(place.shape, place.dtype)]
-    signal = [pltpu.SemaphoreType.DMA((1,))]
-    outs = call(
-        functools.partial(second_kernel, groups),
-        (shape(devices, sent_rows, LANES),) + (place,) * held,
-        state, rows, swap(out, ("leaf", "blk")), bases, coarse_v, *fields, far=(3,),
-        scratch=signal if held else buffer + signal,
+    sent = call(
+        functools.partial(second_kernel, groups), shape(devices, sent_rows, LANES),
+        state, rows, swap(out, ("leaf", "blk")), *bases, coarse_v, *fields, scalars=(6,),
     )
     u, phi = call(
         functools.partial(finish_kernel, groups, width), (shape(1, elems), shape(1, elems)),
-        swap(outs[0], ("leaf", "blk")), outs[1] if held else bases, slot, slot_row,
-        far=() if held else (1,), scratch=() if held else buffer + signal,
+        swap(sent, ("leaf", "blk")), *bases, slot, slot_row,
     )
     return u.reshape(elems), phi.reshape(elems)
 

time: 71.3 us -> 47 us (0.66)
  blocking collectives: 60.3 us -> 12 us
  waiting for transfers between devices: 0.01 us -> 12.6 us
  starting transfers between devices: 2.57 us -> 14.2 us
    all_gather x1 -> x0, blocking collectives: 34.9 us -> none  [body(): lax.all_gather(coarse_u.reshape(width, elems), 'blk', axis=0, tiled=True)]
    all_to_all x2 -> x1, blocking collectives: 25.4 us -> 12 us  [swap(): return lax.all_to_all(value, axes, split_axis=0, concat_axis=0, tiled=True)]
    all_to_all x1 -> x2, waiting for transfers between devices: 0.01 us -> 10.5 us  [swap(): return lax.all_to_all(value, axes, split_axis=0, concat_axis=0, tiled=True)]
    ppermute x0 -> x3, starting transfers between devices: none -> 7.88 us  [partner(): lax.ppermute(value, 'blk', [(i, i ^ 1 << bit) for i in range(members)])]
    all_to_all x1 -> x2, starting transfers between devices: 2.57 us -> 6.37 us  [swap(): return lax.all_to_all(value, axes, split_axis=0, concat_axis=0, tiled=True)]
    ppermute x0 -> x3, waiting for transfers between devices: none -> 2.11 us  [partner(): lax.ppermute(value, 'blk', [(i, i ^ 1 << bit) for i in range(members)])]
    pallas_call x4 -> x6, Pallas kernels: 6.78 us -> 6.52 us  [call(): pl.pallas_call(kernel, out_shape=outs, in_specs=[pl.BlockSpec(memory_spac...]
  transfers between devices with their start and end apart: 1 -> 5, of which waited for: 0 -> 3; matrix products, arithmetic and copies ran while one was open for 0% -> 0% of each run, Pallas kernels for 0% -> 9%
where the time goes in v7:
time: 47 us; the launch traced here: 46.7 us
  starting transfers between devices  14.2 us (30%)
  waiting for transfers between devices  12.6 us (27%)
  blocking collectives  12 us (26%)
  Pallas kernels  6.52 us (14%)
  between operations  1.35 us (3%)
    all_to_all x1, blocking collectives, swap(): return lax.all_to_all(value, axes, split_axis=0, concat_axis=0, tiled=True)  12 us
    all_to_all x2, waiting for transfers between devices, swap(): return lax.all_to_all(value, axes, split_axis=0, concat_axis=0, tiled=True)  10.5 us
    ppermute x3, starting transfers between devices, partner(): lax.ppermute(value, 'blk', [(i, i ^ 1 << bit) for i in range(members)])  7.88 us
    pallas_call x6, Pallas kernels, call(): pl.pallas_call(kernel, out_shape=outs, in_specs=[pl.BlockSpec(memory_spac...  6.52 us
    all_to_all x2, starting transfers between devices, swap(): return lax.all_to_all(value, axes, split_axis=0, concat_axis=0, tiled=True)  6.37 us
    ppermute x3, waiting for transfers between devices, partner(): lax.ppermute(value, 'blk', [(i, i ^ 1 << bit) for i in range(members)])  2.11 us
  transfers between devices with their start and end apart: 5, of which 3 were waited for; matrix products, arithmetic and copies ran while one was open for 0% of the time, Pallas kernels for 9%

profile of v7, /device:TPU:0, one launch (start us, length us, event | category | flops | bytes accessed | tf_op | source)
XLA Modules:
  0.0 46.7 jit_solution(17226746009118539549)
XLA Ops:
  0.6 0.0 copy-start
  0.6 4.1 %collective-permute-start = (bf16[64,512]{1,0:T(8,128)(2,1)}, bf16[64,512]{1,0:T(8,128)(2,1)S(1)}, u32[]{:S(2)}, u32[]{:S(2)}) collective-permute-start(bf16[64,512]{1,0:T(8,128)(2,1)} %bitcast.13), channel_id=1, source_target_pairs={{0,4},{1,5},{2,6},{3,7},{4,0},{5,1},{6,2},{7,3},{8,12},{9,13},{10,... | collective-permute-start | bytes 196616 | tf_op jit(solution)/shard_map/ppermute | solution.py:377
  4.7 2.3 %shard_map.167 = (f32[8,16,128]{2,1,0:T(8,128)}, s32[1,512]{1,0:T(1,128)S(1)}, s32[1,512]{1,0:T(1,128)S(1)}, f32[3,8,512]{2,1,0:T(8,128)S(1)}, f32[8,64]{1,0:T(8...) custom-call(s32[1,512]{1,0:T(1,128)} %bitcast.18, ...), custom_call_target="tpu_custom_call" | custom-call | flops 1000 | bytes 1000 | tf_op jit(solution)/shard_map/pallas_call | solution.py:330
  7.0 3.8 %all-to-all-start = ((f32[8,16,128]{2,1,0:T(8,128)}), f32[8,16,128]{2,1,0:T(8,128)S(1)}, u32[]{:S(2)}, u32[]{:S(2)}) async-start(f32[8,16,128]{2,1,0:T(8,128)} %get-tuple-element.16), calls=%async_computation | async-start | bytes 131072 | tf_op jit(solution)/shard_map/all_to_all | solution.py:374
  10.8 0.0 collective-permute-done.came_ref
  10.8 0.0 copy-done
  10.9 2.1 %collective-permute-start.1 = (bf16[128,512]{1,0:T(8,128)(2,1)S(1)}, bf16[128,512]{1,0:T(8,128)(2,1)S(1)}, u32[]{:S(2)}, u32[]{:S(2)}) collective-permute-start(bf16[128,512]{1,0:T(8,128)(2,1)S(1)} %shard_map.169.held_ref), channel_id=1, source_target_pairs={{0,2},{1,3},{2,0},{3,1},{4,6},{5,7},{6,4},{7,5},{8,10},{9,11},{10,... | collective-permute-start | bytes 393224 | tf_op jit(solution)/shard_map/ppermute | solution.py:377
  13.6 4.4 %all-to-all-done.got_ref = f32[8,16,128]{2,1,0:T(8,128)S(1)} async-done(((f32[8,16,128]{2,1,0:T(8,128)}), f32[8,16,128]{2,1,0:T(8,128)S(1)}, u32[]{:S(2)}, u32[]{:S(2)}) %all-to-all-start) | async-done | bytes 65568 | tf_op jit(solution)/shard_map/all_to_all | solution.py:374
  18.0 1.7 %shard_map.168 = (f32[8,512]{1,0:T(8,128)S(1)}, s32[1,512]{1,0:T(1,128)S(1)}, f32[32,1,1152]{2,1,0:T(1,128)}) custom-call(f32[8,16,128]{2,1,0:T(8,128)S(1)} %all-to-all-done.got_ref, bf16[64,512]{1,0:T(8,128)(2,1)S(1)} %get-tuple-element.17.coarse_v_ref, s32[1]{0:T(128)S(6)} %copy.18.refs_0_, bf16[3,512,512]{2,1,0:T(8,128)(2,1)S(1)} %get-tuple-element.18.refs_1_, ...), custom_call_target="tpu_custom_call" | custom-call | flops 1000 | bytes 1000 | tf_op jit(solution)/shard_map/pallas_call | solution.py:330
  19.7 2.6 %all-to-all-start.1 = ((f32[32,1,1152]{2,1,0:T(1,128)}), f32[32,1,1152]{2,1,0:T(1,128)S(1)}, u32[]{:S(2)}, u32[]{:S(2)}) async-start(f32[32,1,1152]{2,1,0:T(1,128)} %get-tuple-element.25), calls=%async_computation.1 | async-start | bytes 294912 | tf_op jit(solution)/shard_map/all_to_all | solution.py:374
  22.3 0.0 collective-permute-done.1.came_ref
  22.3 1.7 %collective-permute-start.2 = (bf16[256,512]{1,0:T(8,128)(2,1)S(1)}, bf16[256,512]{1,0:T(8,128)(2,1)S(1)}, u32[]{:S(2)}, u32[]{:S(2)}) collective-permute-start(bf16[256,512]{1,0:T(8,128)(2,1)S(1)} %shard_map.170.held_ref), channel_id=1, source_target_pairs={{0,1},{1,0},{2,3},{3,2},{4,5},{5,4},{6,7},{7,6},{8,9},{9,8},{10,11... | collective-permute-start | bytes 786440 | tf_op jit(solution)/shard_map/ppermute | solution.py:377
  24.0 6.1 %all-to-all-done.1.all_ref = f32[32,1,1152]{2,1,0:T(1,128)S(1)} async-done(((f32[32,1,1152]{2,1,0:T(1,128)}), f32[32,1,1152]{2,1,0:T(1,128)S(1)}, u32[]{:S(2)}, u32[]{:S(2)}) %all-to-all-start.1) | async-done | bytes 147488 | tf_op jit(solution)/shard_map/all_to_all | solution.py:374
  30.1 2.1 %collective-permute-done.2.came_ref = bf16[256,512]{1,0:T(8,128)(2,1)S(1)} collective-permute-done((bf16[256,512]{1,0:T(8,128)(2,1)S(1)}, bf16[256,512]{1,0:T(8,128)(2,1)S(1)}, u32[]{:S(2)}, u32[]{:S(2)}) %collective-permute-start.2) | collective-permute-done | bytes 262176 | tf_op jit(solution)/shard_map/ppermute | solution.py:377
  32.2 1.2 %shard_map.171 = f32[32,4,128]{2,1,0:T(4,128)S(1)} custom-call(f32[8,512]{1,0:T(8,128)S(1)} %get-tuple-element.23.state_ref, s32[1,512]{1,0:T(1,128)S(1)} %get-tuple-element.24.rows_ref, f32[32,1,1152]{2,1,0:T(1,128)S(1)} %all-to-all-done.1.all_ref, bf16[256,512]{1,0:T(8,128)(2,1)S(1)} %shard_map.170.held_ref, ...), custom_call_target="tpu_custom_call" | custom-call | flops 1000 | bytes 1000 | tf_op jit(solution)/shard_map/pallas_call | solution.py:330
  33.4 12.0 %all_to_all.15.got_ref = f32[32,4,128]{2,1,0:T(4,128)S(1)} all-to-all(f32[32,4,128]{2,1,0:T(4,128)S(1)} %shard_map.171), channel_id=1, replica_groups=mesh['leaf'=4,'blk'=8] {'leaf','blk'}, dimensions={0} | all-to-all | bytes 131072 | tf_op jit(solution)/shard_map/all_to_all | solution.py:374
  45.5 1.3 %shard_map.172 = (f32[1,512]{1,0:T(1,128)}, f32[1,512]{1,0:T(1,128)}) custom-call(f32[32,4,128]{2,1,0:T(4,128)S(1)} %all_to_all.15.got_ref, bf16[256,512]{1,0:T(8,128)(2,1)S(1)} %shard_map.170.held_ref, bf16[256,512]{1,0:T(8,128)(2,1)S(1)} %collective-permute-done.2.came_ref, s32[1,512]{1,0:T(1,128)S(1)} %get-tuple-element.26.refs_0_.slot_ref, ...), custom_call_target="tpu_custom_call" | custom-call | flops 1000 | bytes 1000 | tf_op jit(solution)/shard_map/pallas_call | solution.py:330
  (2 shorter events, 0.0 us)
Async XLA Ops:
  0.6 10.2 %copy-start = (bf16[4,16,512]{2,1,0:T(8,128)(2,1)S(1)}, bf16[4,16,512]{2,1,0:T(8,128)(2,1)}, u32[]{:S(2)}) copy-start(bf16[4,16,512]{2,1,0:T(8,128)(2,1)} %param.30) | copy-start | bytes 196612
  0.6 10.2 %collective-permute-start = (bf16[64,512]{1,0:T(8,128)(2,1)}, bf16[64,512]{1,0:T(8,128)(2,1)S(1)}, u32[]{:S(2)}, u32[]{:S(2)}) collective-permute-start(bf16[64,512]{1,0:T(8,128)(2,1)} %bitcast.13), channel_id=1, source_target_pairs={{0,4},{1,5},{2,6},{3,7},{4,0},{5,1},{6,2},{7,3},{8,12},{9,13},{10,... | collective-permute-start | bytes 196616 | tf_op jit(solution)/shard_map/ppermute | solution.py:377
  7.0 10.9 %all-to-all-start = ((f32[8,16,128]{2,1,0:T(8,128)}), f32[8,16,128]{2,1,0:T(8,128)S(1)}, u32[]{:S(2)}, u32[]{:S(2)}) async-start(f32[8,16,128]{2,1,0:T(8,128)} %get-tuple-element.16), calls=%async_computation | async-start | bytes 131072 | tf_op jit(solution)/shard_map/all_to_all | solution.py:374
  10.9 11.4 %collective-permute-start.1 = (bf16[128,512]{1,0:T(8,128)(2,1)S(1)}, bf16[128,512]{1,0:T(8,128)(2,1)S(1)}, u32[]{:S(2)}, u32[]{:S(2)}) collective-permute-start(bf16[128,512]{1,0:T(8,128)(2,1)S(1)} %shard_map.169.held_ref), channel_id=1, source_target_pairs={{0,2},{1,3},{2,0},{3,1},{4,6},{5,7},{6,4},{7,5},{8,10},{9,11},{10,... | collective-permute-start | bytes 393224 | tf_op jit(solution)/shard_map/ppermute | solution.py:377
  19.7 10.4 %all-to-all-start.1 = ((f32[32,1,1152]{2,1,0:T(1,128)}), f32[32,1,1152]{2,1,0:T(1,128)S(1)}, u32[]{:S(2)}, u32[]{:S(2)}) async-start(f32[32,1,1152]{2,1,0:T(1,128)} %get-tuple-element.25), calls=%async_computation.1 | async-start | bytes 294912 | tf_op jit(solution)/shard_map/all_to_all | solution.py:374
  22.3 9.9 %collective-permute-start.2 = (bf16[256,512]{1,0:T(8,128)(2,1)S(1)}, bf16[256,512]{1,0:T(8,128)(2,1)S(1)}, u32[]{:S(2)}, u32[]{:S(2)}) collective-permute-start(bf16[256,512]{1,0:T(8,128)(2,1)S(1)} %shard_map.170.held_ref), channel_id=1, source_target_pairs={{0,1},{1,0},{2,3},{3,2},{4,5},{5,4},{6,7},{7,6},{8,9},{9,8},{10,11... | collective-permute-start | bytes 786440 | tf_op jit(solution)/shard_map/ppermute | solution.py:377

commit v8 on v7

--- a/solution.py
+++ b/solution.py
@@ -189,29 +189,36 @@
     across = lax.broadcasted_iota(jnp.int32, (width, width), 0) % rank
     down = lax.broadcasted_iota(jnp.int32, (width, width), 1) % rank
     spread = dot(table, jnp.where(across == down, 1.0, 0.0).astype(jnp.bfloat16), NN)
-    kept = (lane == row) & (row != mine)
-    return jnp.sum(jnp.where(kept, spread, 0.0), axis=0, keepdims=True)
+    weights = jnp.sum(jnp.where(row == mine ^ (lane + 1), spread, 0.0), axis=0, keepdims=True)
+    return weights[:, 0:width - rank]
 
 
 def coarse_all(weights, members, bases_refs):
-    width = weights.shape[1]
-    half = members // 2
-    tiled = jnp.concatenate([weights] * half, axis=1)
-    place = lax.broadcasted_iota(jnp.int32, (members, half * width), 1) // width
-    row = lax.broadcasted_iota(jnp.int32, (members, half * width), 0) ^ lax.axis_index("blk")
+    row = lax.broadcasted_iota(jnp.int32, (members, weights.shape[1]), 0) ^ lax.axis_index("blk")
     bits = members.bit_length() - 1
     total = jnp.zeros((members, bases_refs[0].shape[1]), jnp.float32)
     for number, ref in enumerate(bases_refs):
-        source = jnp.full(place.shape, number, jnp.int32)
-        for bit in range(bits - 1):
-            source = source | (((place >> bit) & 1) << (bits - 1 - bit))
-        left = jnp.where(source == row, tiled, 0.0).astype(jnp.bfloat16)
+        left = []
+        for place in range(members // 4):
+            source = number
+            for bit in range(bits - 2):
+                source |= (place >> bit & 1) << (bits - 1 - bit)
+            left.append(jnp.where(row == source, weights, 0.0))
+        left = jnp.concatenate(left, axis=1).astype(jnp.bfloat16)
         total = total + dot(left, ref[...], NN)
     return total
 
 
-def stack_kernel(held_ref, came_ref, *refs):
-    out_ref = refs[-1]
+def pair_kernel(rank, held_ref, came_ref, order_ref, out_ref):
+    groups = held_ref.shape[0] // rank
+    mine = lax.axis_index("leaf")
+    for number, ref in enumerate((held_ref, came_ref)):
+        for shift in range(1, groups):
+            place = (number * (groups - 1) + shift - 1) * rank
+            out_ref[place:place + rank, :] = ref[pl.ds((mine ^ shift) * rank, rank), :]
+
+
+def stack_kernel(held_ref, came_ref, out_ref):
     count = held_ref.shape[0]
     out_ref[0:count, :] = held_ref[...]
     out_ref[count:2 * count, :] = came_ref[...]
@@ -258,9 +265,9 @@
     out_ref[...] = jnp.broadcast_to(sent[None], out_ref.shape)
 
 
-def second_kernel(groups, state_ref, rows_ref, all_ref, held_ref, came_ref, coarse_v_ref, *refs):
-    field_refs, sent_ref = refs[:6], refs[6]
-    members, elem_count = refs[4].shape[1], state_ref.shape[1]
+def second_kernel(groups, state_ref, rows_ref, all_ref, coarse_v_ref, *refs):
+    bases_refs, field_refs, sent_ref = refs[:4], refs[4:10], refs[10]
+    members, elem_count = refs[8].shape[1], state_ref.shape[1]
     width = coarse_v_ref.shape[0]
     mine, me = lax.axis_index("leaf"), lax.axis_index("blk")
     sums = [
@@ -272,7 +279,7 @@
     ]
     weights = coefficients(sums, width // groups)
     own = all_ref[pl.ds(mine * members, members), 0, 0:2 * elem_count]
-    coarse = coarse_all(weights, members, (held_ref, came_ref))
+    coarse = coarse_all(weights, members, bases_refs)
     u2_all = own[:, 0:elem_count] + own[:, elem_count:] * coarse
     deficits = (PLATE_RATE - jnp.exp(u2_all)).astype(jnp.bfloat16).astype(jnp.float32)
     inside = inside_rows(deficits, *field_refs)
@@ -297,9 +304,8 @@
         sent_ref[device, 3:3 + partial.shape[0], :] = partial
 
 
-def finish_kernel(
-    groups, width, got_ref, held_ref, came_ref, slot_ref, slot_row_ref, u_ref, phi_ref
-):
+def finish_kernel(groups, width, got_ref, slot_ref, slot_row_ref, *refs):
+    bases_refs, u_ref, phi_ref = refs[:4], refs[4], refs[5]
     elem_count = slot_ref.shape[1]
     members = got_ref.shape[0] // groups
     sums = []
@@ -307,7 +313,7 @@
         total = jnp.sum(got_ref[group * members:(group + 1) * members], axis=0)
         lines = [total[3 + i:4 + i, :] for i in range(pl.cdiv(width, LANES))]
         sums.append(jnp.concatenate(lines, axis=1)[:, 0:width])
-    coarse = coarse_all(coefficients(sums, width // groups), members, (held_ref, came_ref))
+    coarse = coarse_all(coefficients(sums, width // groups), members, bases_refs)
     row = slot_row_ref[...]
     block = lax.broadcasted_iota(jnp.int32, (members, elem_count), 0)
     lane_block = lax.broadcasted_iota(jnp.int32, (members, elem_count), 1) // (elem_count // members)
@@ -402,11 +408,17 @@
         + [pltpu.SemaphoreType.DMA((14,))],
     )
     bases = coarse_u.reshape(width, elems)
-    for bit in range(members.bit_length() - 2, 0, -1):
-        came = partner(bases, bit)
+    top = members.bit_length() - 2
+    kept = width - rank
+    bases = call(
+        functools.partial(pair_kernel, rank), shape(2 * kept, elems, dtype=jnp.bfloat16),
+        bases, partner(bases, top), slot, flops=1 << 26, moved=1 << 22,
+    )
+    for bit in range(top - 1, 1, -1):
         stacked = shape(2 * bases.shape[0], elems, dtype=jnp.bfloat16)
-        bases = call(stack_kernel, stacked, bases, came, slot, flops=2**26, moved=2**22)
-    bases = bases, partner(bases, 0)
+        bases = call(stack_kernel, stacked, bases, partner(bases, bit))
+    across = partner(bases, 0)
+    bases = bases, across, partner(bases, 1), partner(across, 1)
     fields = near_count, near, far_u, far_v, near_mask, far_mask
     state, rows, out = call(
         place_kernel,
@@ -420,11 +432,11 @@
     )
     sent = call(
         functools.partial(second_kernel, groups), shape(devices, sent_rows, LANES),
-        state, rows, swap(out, ("leaf", "blk")), *bases, coarse_v, *fields, scalars=(6,),
+        state, rows, swap(out, ("leaf", "blk")), coarse_v, *bases, *fields, scalars=(8,),
     )
     u, phi = call(
         functools.partial(finish_kernel, groups, width), (shape(1, elems), shape(1, elems)),
-        swap(sent, ("leaf", "blk")), *bases, slot, slot_row,
+        swap(sent, ("leaf", "blk")), slot, slot_row, *bases,
     )
     return u.reshape(elems), phi.reshape(elems)
 

time: 47 us -> 54.1 us (1.15)
  waiting for transfers between devices: 12.6 us -> 21 us
  blocking collectives: 12 us -> 10.7 us
    ppermute x3 -> x4, waiting for transfers between devices: 2.11 us -> 14.7 us  [partner(): lax.ppermute(value, 'blk', [(i, i ^ 1 << bit) for i in range(members)])]
    all_to_all x2, waiting for transfers between devices: 10.5 us -> 6.26 us  [swap(): return lax.all_to_all(value, axes, split_axis=0, concat_axis=0, tiled=True)]
    ppermute x3 -> x4, starting transfers between devices: 7.88 us -> 4.27 us  [partner(): lax.ppermute(value, 'blk', [(i, i ^ 1 << bit) for i in range(members)])]
    all_to_all x2, starting transfers between devices: 6.37 us -> 9.97 us  [swap(): return lax.all_to_all(value, axes, split_axis=0, concat_axis=0, tiled=True)]
    all_to_all x1, blocking collectives: 12 us -> 10.7 us  [swap(): return lax.all_to_all(value, axes, split_axis=0, concat_axis=0, tiled=True)]
    pallas_call x6 -> x5, Pallas kernels: 6.52 us -> 6.51 us  [call(): pl.pallas_call(kernel, out_shape=outs, in_specs=[pl.BlockSpec(memory_spac...]
  transfers between devices with their start and end apart: 5 -> 6, of which waited for: 3 -> 5; matrix products, arithmetic and copies ran while one was open for 0% -> 0% of each run, Pallas kernels for 9% -> 0%
where the time goes in v8:
time: 54.1 us; the launch traced here: 53.7 us
  waiting for transfers between devices  21 us (39%)
  starting transfers between devices  14.2 us (26%)
  blocking collectives  10.7 us (20%)
  Pallas kernels  6.51 us (12%)
  between operations  1.33 us (2%)
    ppermute x4, waiting for transfers between devices, partner(): lax.ppermute(value, 'blk', [(i, i ^ 1 << bit) for i in range(members)])  14.7 us
    all_to_all x1, blocking collectives, swap(): return lax.all_to_all(value, axes, split_axis=0, concat_axis=0, tiled=True)  10.7 us
    all_to_all x2, starting transfers between devices, swap(): return lax.all_to_all(value, axes, split_axis=0, concat_axis=0, tiled=True)  9.97 us
    pallas_call x5, Pallas kernels, call(): pl.pallas_call(kernel, out_shape=outs, in_specs=[pl.BlockSpec(memory_spac...  6.51 us
    all_to_all x2, waiting for transfers between devices, swap(): return lax.all_to_all(value, axes, split_axis=0, concat_axis=0, tiled=True)  6.26 us
    ppermute x4, starting transfers between devices, partner(): lax.ppermute(value, 'blk', [(i, i ^ 1 << bit) for i in range(members)])  4.27 us
  transfers between devices with their start and end apart: 6, of which 5 were waited for; matrix products, arithmetic and copies ran while one was open for 0% of the time, Pallas kernels for 0%

profile of v8, /device:TPU:0, one launch (start us, length us, event | category | flops | bytes accessed | tf_op | source)
XLA Modules:
  0.0 53.7 jit_solution(14918637714769743188)
XLA Ops:
  0.6 2.3 %shard_map.167 = (f32[8,16,128]{2,1,0:T(8,128)}, s32[1,512]{1,0:T(1,128)S(1)}, s32[1,512]{1,0:T(1,128)S(1)}, f32[3,8,512]{2,1,0:T(8,128)S(1)}, f32[8,64]{1,0:T(8...) custom-call(s32[1,512]{1,0:T(1,128)} %bitcast.18, ...), custom_call_target="tpu_custom_call" | custom-call | flops 1000 | bytes 1000 | tf_op jit(solution)/shard_map/pallas_call | solution.py:336
  2.9 0.0 copy-start
  2.9 7.4 %all-to-all-start = ((f32[8,16,128]{2,1,0:T(8,128)}), f32[8,16,128]{2,1,0:T(8,128)S(1)}, u32[]{:S(2)}, u32[]{:S(2)}) async-start(f32[8,16,128]{2,1,0:T(8,128)} %get-tuple-element.16), calls=%async_computation | async-start | bytes 131072 | tf_op jit(solution)/shard_map/all_to_all | solution.py:380
  11.0 6.3 %all-to-all-done.got_ref = f32[8,16,128]{2,1,0:T(8,128)S(1)} async-done(((f32[8,16,128]{2,1,0:T(8,128)}), f32[8,16,128]{2,1,0:T(8,128)S(1)}, u32[]{:S(2)}, u32[]{:S(2)}) %all-to-all-start) | async-done | bytes 65568 | tf_op jit(solution)/shard_map/all_to_all | solution.py:380
  17.2 1.7 %shard_map.168 = (f32[8,512]{1,0:T(8,128)S(1)}, s32[1,512]{1,0:T(1,128)S(1)}, f32[32,1,1152]{2,1,0:T(1,128)}) custom-call(f32[8,16,128]{2,1,0:T(8,128)S(1)} %all-to-all-done.got_ref, bf16[64,512]{1,0:T(8,128)(2,1)S(1)} %get-tuple-element.17.coarse_v_ref, s32[1]{0:T(128)S(6)} %copy.18.refs_0_.refs_4_, ...), custom_call_target="tpu_custom_call" | custom-call | flops 1000 | bytes 1000 | tf_op jit(solution)/shard_map/pallas_call | solution.py:336
  19.0 2.6 %all-to-all-start.1 = ((f32[32,1,1152]{2,1,0:T(1,128)}), f32[32,1,1152]{2,1,0:T(1,128)S(1)}, u32[]{:S(2)}, u32[]{:S(2)}) async-start(f32[32,1,1152]{2,1,0:T(1,128)} %get-tuple-element.25), calls=%async_computation.1 | async-start | bytes 294912 | tf_op jit(solution)/shard_map/all_to_all | solution.py:380
  21.6 0.0 copy-done
  21.6 2.7 %collective-permute-start = (bf16[64,512]{1,0:T(8,128)(2,1)S(1)}, bf16[64,512]{1,0:T(8,128)(2,1)S(1)}, u32[]{:S(2)}, u32[]{:S(2)}) collective-permute-start(bf16[64,512]{1,0:T(8,128)(2,1)S(1)} %bitcast.13), channel_id=1, source_target_pairs={{0,4},{1,5},{2,6},{3,7},{4,0},{5,1},{6,2},{7,3},{8,12},{9,13},{10,... | collective-permute-start | bytes 196616 | tf_op jit(solution)/shard_map/ppermute | solution.py:383
  24.3 7.0 %collective-permute-done.came_ref = bf16[64,512]{1,0:T(8,128)(2,1)S(1)} collective-permute-done((bf16[64,512]{1,0:T(8,128)(2,1)S(1)}, bf16[64,512]{1,0:T(8,128)(2,1)S(1)}, u32[]{:S(2)}, u32[]{:S(2)}) %collective-permute-start) | collective-permute-done | bytes 65568 | tf_op jit(solution)/shard_map/ppermute | solution.py:383
  31.3 1.5 %collective-permute-start.1 = (bf16[96,512]{1,0:T(8,128)(2,1)S(1)}, bf16[96,512]{1,0:T(8,128)(2,1)S(1)}, u32[]{:S(2)}, u32[]{:S(2)}) collective-permute-start(bf16[96,512]{1,0:T(8,128)(2,1)S(1)} %shard_map.169.refs_0_), channel_id=1, source_target_pairs={{0,1},{1,0},{2,3},{3,2},{4,5},{5,4},{6,7},{7,6},{8,9},{9,8},{10,11... | collective-permute-start | bytes 294920 | tf_op jit(solution)/shard_map/ppermute | solution.py:383
  32.8 0.0 collective-permute-start.2
  32.8 3.1 %collective-permute-done.1.refs_1_ = bf16[96,512]{1,0:T(8,128)(2,1)S(1)} collective-permute-done((bf16[96,512]{1,0:T(8,128)(2,1)S(1)}, bf16[96,512]{1,0:T(8,128)(2,1)S(1)}, u32[]{:S(2)}, u32[]{:S(2)}) %collective-permute-start.1) | collective-permute-done | bytes 98336 | tf_op jit(solution)/shard_map/ppermute | solution.py:383
  36.0 0.0 collective-permute-start.3
  36.0 1.9 %collective-permute-done.2.refs_2_ = bf16[96,512]{1,0:T(8,128)(2,1)S(1)} collective-permute-done((bf16[96,512]{1,0:T(8,128)(2,1)S(1)}, bf16[96,512]{1,0:T(8,128)(2,1)S(1)}, u32[]{:S(2)}, u32[]{:S(2)}) %collective-permute-start.2) | collective-permute-done | bytes 98336 | tf_op jit(solution)/shard_map/ppermute | solution.py:383
  37.9 2.7 %collective-permute-done.3.refs_3_ = bf16[96,512]{1,0:T(8,128)(2,1)S(1)} collective-permute-done((bf16[96,512]{1,0:T(8,128)(2,1)S(1)}, bf16[96,512]{1,0:T(8,128)(2,1)S(1)}, u32[]{:S(2)}, u32[]{:S(2)}) %collective-permute-start.3) | collective-permute-done | bytes 98336 | tf_op jit(solution)/shard_map/ppermute | solution.py:383
  40.6 0.0 all-to-all-done.1.all_ref
  40.6 1.2 %shard_map.170 = f32[32,4,128]{2,1,0:T(4,128)S(1)} custom-call(f32[8,512]{1,0:T(8,128)S(1)} %get-tuple-element.23.state_ref, s32[1,512]{1,0:T(1,128)S(1)} %get-tuple-element.24.rows_ref, f32[32,1,1152]{2,1,0:T(1,128)S(1)} %all-to-all-done.1.all_ref, bf16[64,512]{1,0:T(8,128)(2,1)S(1)} %get-tuple-element.17.coarse_v_ref, ...), custom_call_target="tpu_custom_call" | custom-call | flops 1000 | bytes 1000 | tf_op jit(solution)/shard_map/pallas_call | solution.py:336
  41.8 10.7 %all_to_all.15.got_ref = f32[32,4,128]{2,1,0:T(4,128)S(1)} all-to-all(f32[32,4,128]{2,1,0:T(4,128)S(1)} %shard_map.170), channel_id=1, replica_groups=mesh['leaf'=4,'blk'=8] {'leaf','blk'}, dimensions={0} | all-to-all | bytes 131072 | tf_op jit(solution)/shard_map/all_to_all | solution.py:380
  52.5 1.3 %shard_map.171 = (f32[1,512]{1,0:T(1,128)}, f32[1,512]{1,0:T(1,128)}) custom-call(f32[32,4,128]{2,1,0:T(4,128)S(1)} %all_to_all.15.got_ref, s32[1,512]{1,0:T(1,128)S(1)} %get-tuple-element.26.order_ref.slot_ref, s32[1,512]{1,0:T(1,128)S(1)} %get-tuple-element.27.slot_row_ref, bf16[96,512]{1,0:T(8,128)(2,1)S(1)} %shard_map.169.refs_0_, ...), custom_call_target="tpu_custom_call" | custom-call | flops 1000 | bytes 1000 | tf_op jit(solution)/shard_map/pallas_call | solution.py:336
  (1 shorter events, 0.0 us)
Async XLA Ops:
  2.9 18.6 %copy-start = (bf16[4,16,512]{2,1,0:T(8,128)(2,1)S(1)}, bf16[4,16,512]{2,1,0:T(8,128)(2,1)}, u32[]{:S(2)}) copy-start(bf16[4,16,512]{2,1,0:T(8,128)(2,1)} %param.30) | copy-start | bytes 196612
  2.9 14.3 %all-to-all-start = ((f32[8,16,128]{2,1,0:T(8,128)}), f32[8,16,128]{2,1,0:T(8,128)S(1)}, u32[]{:S(2)}, u32[]{:S(2)}) async-start(f32[8,16,128]{2,1,0:T(8,128)} %get-tuple-element.16), calls=%async_computation | async-start | bytes 131072 | tf_op jit(solution)/shard_map/all_to_all | solution.py:380
  19.0 21.6 %all-to-all-start.1 = ((f32[32,1,1152]{2,1,0:T(1,128)}), f32[32,1,1152]{2,1,0:T(1,128)S(1)}, u32[]{:S(2)}, u32[]{:S(2)}) async-start(f32[32,1,1152]{2,1,0:T(1,128)} %get-tuple-element.25), calls=%async_computation.1 | async-start | bytes 294912 | tf_op jit(solution)/shard_map/all_to_all | solution.py:380
  21.6 9.7 %collective-permute-start = (bf16[64,512]{1,0:T(8,128)(2,1)S(1)}, bf16[64,512]{1,0:T(8,128)(2,1)S(1)}, u32[]{:S(2)}, u32[]{:S(2)}) collective-permute-start(bf16[64,512]{1,0:T(8,128)(2,1)S(1)} %bitcast.13), channel_id=1, source_target_pairs={{0,4},{1,5},{2,6},{3,7},{4,0},{5,1},{6,2},{7,3},{8,12},{9,13},{10,... | collective-permute-start | bytes 196616 | tf_op jit(solution)/shard_map/ppermute | solution.py:383
  31.3 4.7 %collective-permute-start.1 = (bf16[96,512]{1,0:T(8,128)(2,1)S(1)}, bf16[96,512]{1,0:T(8,128)(2,1)S(1)}, u32[]{:S(2)}, u32[]{:S(2)}) collective-permute-start(bf16[96,512]{1,0:T(8,128)(2,1)S(1)} %shard_map.169.refs_0_), channel_id=1, source_target_pairs={{0,1},{1,0},{2,3},{3,2},{4,5},{5,4},{6,7},{7,6},{8,9},{9,8},{10,11... | collective-permute-start | bytes 294920 | tf_op jit(solution)/shard_map/ppermute | solution.py:383
  32.8 5.1 %collective-permute-start.2 = (bf16[96,512]{1,0:T(8,128)(2,1)S(1)}, bf16[96,512]{1,0:T(8,128)(2,1)S(1)}, u32[]{:S(2)}, u32[]{:S(2)}) collective-permute-start(bf16[96,512]{1,0:T(8,128)(2,1)S(1)} %shard_map.169.refs_0_), channel_id=1, source_target_pairs={{0,2},{1,3},{2,0},{3,1},{4,6},{5,7},{6,4},{7,5},{8,10},{9,11},{10,... | collective-permute-start | bytes 294920 | tf_op jit(solution)/shard_map/ppermute | solution.py:383
  36.0 4.6 %collective-permute-start.3 = (bf16[96,512]{1,0:T(8,128)(2,1)S(1)}, bf16[96,512]{1,0:T(8,128)(2,1)S(1)}, u32[]{:S(2)}, u32[]{:S(2)}) collective-permute-start(bf16[96,512]{1,0:T(8,128)(2,1)S(1)} %collective-permute-done.1.refs_1_), channel_id=1, source_target_pairs={{0,2},{1,3},{2,0},{3,1},{4,6},{5,7},{6,4},{7,5},{8,10},{9,11},{10,... | collective-permute-start | bytes 294920 | tf_op jit(solution)/shard_map/ppermute | solution.py:383

commit v9 on v8

--- a/solution.py
+++ b/solution.py
@@ -224,7 +224,7 @@
     out_ref[count:2 * count, :] = came_ref[...]
 
 
-def place_kernel(got_ref, coarse_v_ref, *refs):
+def place_kernel(got_ref, coarse_v_ref, early_ref, *refs):
     field_refs, state_ref, rows_ref, out_ref, lines_ref = refs[:6], refs[6], refs[7], refs[8], refs[9]
     members = got_ref.shape[0]
     elem_count = state_ref.shape[1]
@@ -410,7 +410,7 @@
     bases = coarse_u.reshape(width, elems)
     top = members.bit_length() - 2
     kept = width - rank
-    bases = call(
+    early = bases = call(
         functools.partial(pair_kernel, rank), shape(2 * kept, elems, dtype=jnp.bfloat16),
         bases, partner(bases, top), slot, flops=1 << 26, moved=1 << 22,
     )
@@ -427,7 +427,7 @@
             shape(1, elems, dtype=integer),
             shape(devices, 1, 2 * elems + lines * LANES),
         ),
-        swap(sent, "blk"), coarse_v, *fields, scalars=(2,),
+        swap(sent, "blk"), coarse_v, early, *fields, scalars=(3,),
         scratch=[VMEM((members * (elems // LANES), LANES), jnp.float32)],
     )
     sent = call(

time: 54.1 us -> 49.7 us (0.919)
  waiting for transfers between devices: 21 us -> 9.82 us
  starting transfers between devices: 14.2 us -> 19.6 us
  blocking collectives: 10.7 us -> 12.2 us
    all_to_all x2, waiting for transfers between devices: 6.26 us -> 0.01 us  [swap(): return lax.all_to_all(value, axes, split_axis=0, concat_axis=0, tiled=True)]
    ppermute x4, waiting for transfers between devices: 14.7 us -> 9.82 us  [partner(): lax.ppermute(value, 'blk', [(i, i ^ 1 << bit) for i in range(members)])]
    ppermute x4, starting transfers between devices: 4.27 us -> 7.88 us  [partner(): lax.ppermute(value, 'blk', [(i, i ^ 1 << bit) for i in range(members)])]
    all_to_all x2, starting transfers between devices: 9.97 us -> 11.7 us  [swap(): return lax.all_to_all(value, axes, split_axis=0, concat_axis=0, tiled=True)]
    all_to_all x1, blocking collectives: 10.7 us -> 12.2 us  [swap(): return lax.all_to_all(value, axes, split_axis=0, concat_axis=0, tiled=True)]
  transfers between devices with their start and end apart: 6 -> 6, of which waited for: 5 -> 3; matrix products, arithmetic and copies ran while one was open for 0% -> 0% of each run, Pallas kernels for 0% -> 0%
where the time goes in v9:
time: 49.7 us; the launch traced here: 49.4 us
  starting transfers between devices  19.6 us (39%)
  blocking collectives  12.2 us (25%)
  waiting for transfers between devices  9.82 us (20%)
  Pallas kernels  6.54 us (13%)
  between operations  1.33 us (3%)
    all_to_all x1, blocking collectives, swap(): return lax.all_to_all(value, axes, split_axis=0, concat_axis=0, tiled=True)  12.2 us
    all_to_all x2, starting transfers between devices, swap(): return lax.all_to_all(value, axes, split_axis=0, concat_axis=0, tiled=True)  11.7 us
    ppermute x4, waiting for transfers between devices, partner(): lax.ppermute(value, 'blk', [(i, i ^ 1 << bit) for i in range(members)])  9.82 us
    ppermute x4, starting transfers between devices, partner(): lax.ppermute(value, 'blk', [(i, i ^ 1 << bit) for i in range(members)])  7.88 us
    pallas_call x5, Pallas kernels, call(): pl.pallas_call(kernel, out_shape=outs, in_specs=[pl.BlockSpec(memory_spac...  6.54 us
  transfers between devices with their start and end apart: 6, of which 3 were waited for; matrix products, arithmetic and copies ran while one was open for 0% of the time, Pallas kernels for 0%

profile of v9, /device:TPU:0, one launch (start us, length us, event | category | flops | bytes accessed | tf_op | source)
XLA Modules:
  0.0 49.4 jit_solution(14921949575291673488)
XLA Ops:
  0.6 0.0 copy-start
  0.6 2.3 %shard_map.167 = (f32[8,16,128]{2,1,0:T(8,128)}, s32[1,512]{1,0:T(1,128)S(1)}, s32[1,512]{1,0:T(1,128)S(1)}, f32[3,8,512]{2,1,0:T(8,128)S(1)}, f32[8,64]{1,0:T(8...) custom-call(s32[1,512]{1,0:T(1,128)} %bitcast.18, ...), custom_call_target="tpu_custom_call" | custom-call | flops 1000 | bytes 1000 | tf_op jit(solution)/shard_map/pallas_call | solution.py:336
  3.0 7.3 %all-to-all-start = ((f32[8,16,128]{2,1,0:T(8,128)}), f32[8,16,128]{2,1,0:T(8,128)S(1)}, u32[]{:S(2)}, u32[]{:S(2)}) async-start(f32[8,16,128]{2,1,0:T(8,128)} %get-tuple-element.16), calls=%async_computation | async-start | bytes 131072 | tf_op jit(solution)/shard_map/all_to_all | solution.py:380
  10.2 0.0 copy-done
  10.2 2.9 %collective-permute-start = (bf16[64,512]{1,0:T(8,128)(2,1)S(1)}, bf16[64,512]{1,0:T(8,128)(2,1)S(1)}, u32[]{:S(2)}, u32[]{:S(2)}) collective-permute-start(bf16[64,512]{1,0:T(8,128)(2,1)S(1)} %bitcast.13), channel_id=1, source_target_pairs={{0,4},{1,5},{2,6},{3,7},{4,0},{5,1},{6,2},{7,3},{8,12},{9,13},{10,... | collective-permute-start | bytes 196616 | tf_op jit(solution)/shard_map/ppermute | solution.py:383
  13.8 3.9 %collective-permute-done.came_ref = bf16[64,512]{1,0:T(8,128)(2,1)S(1)} collective-permute-done((bf16[64,512]{1,0:T(8,128)(2,1)S(1)}, bf16[64,512]{1,0:T(8,128)(2,1)S(1)}, u32[]{:S(2)}, u32[]{:S(2)}) %collective-permute-start) | collective-permute-done | bytes 65568 | tf_op jit(solution)/shard_map/ppermute | solution.py:383
  17.7 0.0 all-to-all-done.got_ref
  17.7 1.7 %shard_map.169 = (f32[8,512]{1,0:T(8,128)S(1)}, s32[1,512]{1,0:T(1,128)S(1)}, f32[32,1,1152]{2,1,0:T(1,128)}) custom-call(f32[8,16,128]{2,1,0:T(8,128)S(1)} %all-to-all-done.got_ref, bf16[64,512]{1,0:T(8,128)(2,1)S(1)} %get-tuple-element.17.coarse_v_ref, bf16[96,512]{1,0:T(8,128)(2,1)S(1)} %shard_map.168.early_ref.refs_0_, s32[1]{0:T(128)S(6)} %copy.18.refs_0_.refs_4_, ...), custom_call_target="tpu_custom_call" | custom-call | flops 1000 | bytes 1000 | tf_op jit(solution)/shard_map/pallas_call | solution.py:336
  19.5 4.4 %all-to-all-start.1 = ((f32[32,1,1152]{2,1,0:T(1,128)}), f32[32,1,1152]{2,1,0:T(1,128)S(1)}, u32[]{:S(2)}, u32[]{:S(2)}) async-start(f32[32,1,1152]{2,1,0:T(1,128)} %get-tuple-element.26), calls=%async_computation.1 | async-start | bytes 294912 | tf_op jit(solution)/shard_map/all_to_all | solution.py:380
  23.9 1.8 %collective-permute-start.1 = (bf16[96,512]{1,0:T(8,128)(2,1)S(1)}, bf16[96,512]{1,0:T(8,128)(2,1)S(1)}, u32[]{:S(2)}, u32[]{:S(2)}) collective-permute-start(bf16[96,512]{1,0:T(8,128)(2,1)S(1)} %shard_map.168.early_ref.refs_0_), channel_id=1, source_target_pairs={{0,1},{1,0},{2,3},{3,2},{4,5},{5,4},{6,7},{7,6},{8,9},{9,8},{10,11... | collective-permute-start | bytes 294920 | tf_op jit(solution)/shard_map/ppermute | solution.py:383
  25.7 1.5 %collective-permute-start.2 = (bf16[96,512]{1,0:T(8,128)(2,1)S(1)}, bf16[96,512]{1,0:T(8,128)(2,1)S(1)}, u32[]{:S(2)}, u32[]{:S(2)}) collective-permute-start(bf16[96,512]{1,0:T(8,128)(2,1)S(1)} %shard_map.168.early_ref.refs_0_), channel_id=1, source_target_pairs={{0,2},{1,3},{2,0},{3,1},{4,6},{5,7},{6,4},{7,5},{8,10},{9,11},{10,... | collective-permute-start | bytes 294920 | tf_op jit(solution)/shard_map/ppermute | solution.py:383
  27.2 3.0 %collective-permute-done.1.refs_1_ = bf16[96,512]{1,0:T(8,128)(2,1)S(1)} collective-permute-done((bf16[96,512]{1,0:T(8,128)(2,1)S(1)}, bf16[96,512]{1,0:T(8,128)(2,1)S(1)}, u32[]{:S(2)}, u32[]{:S(2)}) %collective-permute-start.1) | collective-permute-done | bytes 98336 | tf_op jit(solution)/shard_map/ppermute | solution.py:383
  30.2 1.7 %collective-permute-start.3 = (bf16[96,512]{1,0:T(8,128)(2,1)S(1)}, bf16[96,512]{1,0:T(8,128)(2,1)S(1)}, u32[]{:S(2)}, u32[]{:S(2)}) collective-permute-start(bf16[96,512]{1,0:T(8,128)(2,1)S(1)} %collective-permute-done.1.refs_1_), channel_id=1, source_target_pairs={{0,2},{1,3},{2,0},{3,1},{4,6},{5,7},{6,4},{7,5},{8,10},{9,11},{10,... | collective-permute-start | bytes 294920 | tf_op jit(solution)/shard_map/ppermute | solution.py:383
  31.8 0.0 collective-permute-done.2.refs_2_
  31.8 2.9 %collective-permute-done.3.refs_3_ = bf16[96,512]{1,0:T(8,128)(2,1)S(1)} collective-permute-done((bf16[96,512]{1,0:T(8,128)(2,1)S(1)}, bf16[96,512]{1,0:T(8,128)(2,1)S(1)}, u32[]{:S(2)}, u32[]{:S(2)}) %collective-permute-start.3) | collective-permute-done | bytes 98336 | tf_op jit(solution)/shard_map/ppermute | solution.py:383
  34.8 0.0 all-to-all-done.1.all_ref
  34.8 1.2 %shard_map.170 = f32[32,4,128]{2,1,0:T(4,128)S(1)} custom-call(f32[8,512]{1,0:T(8,128)S(1)} %get-tuple-element.24.state_ref, s32[1,512]{1,0:T(1,128)S(1)} %get-tuple-element.25.rows_ref, f32[32,1,1152]{2,1,0:T(1,128)S(1)} %all-to-all-done.1.all_ref, bf16[64,512]{1,0:T(8,128)(2,1)S(1)} %get-tuple-element.17.coarse_v_ref, ...), custom_call_target="tpu_custom_call" | custom-call | flops 1000 | bytes 1000 | tf_op jit(solution)/shard_map/pallas_call | solution.py:336
  36.0 12.2 %all_to_all.15.got_ref = f32[32,4,128]{2,1,0:T(4,128)S(1)} all-to-all(f32[32,4,128]{2,1,0:T(4,128)S(1)} %shard_map.170), channel_id=1, replica_groups=mesh['leaf'=4,'blk'=8] {'leaf','blk'}, dimensions={0} | all-to-all | bytes 131072 | tf_op jit(solution)/shard_map/all_to_all | solution.py:380
  48.2 1.3 %shard_map.171 = (f32[1,512]{1,0:T(1,128)}, f32[1,512]{1,0:T(1,128)}) custom-call(f32[32,4,128]{2,1,0:T(4,128)S(1)} %all_to_all.15.got_ref, s32[1,512]{1,0:T(1,128)S(1)} %get-tuple-element.18.order_ref.slot_ref, s32[1,512]{1,0:T(1,128)S(1)} %get-tuple-element.27.slot_row_ref, bf16[96,512]{1,0:T(8,128)(2,1)S(1)} %shard_map.168.early_ref.refs_0_, ...), custom_call_target="tpu_custom_call" | custom-call | flops 1000 | bytes 1000 | tf_op jit(solution)/shard_map/pallas_call | solution.py:336
  (1 shorter events, 0.0 us)
Async XLA Ops:
  0.6 9.6 %copy-start = (bf16[4,16,512]{2,1,0:T(8,128)(2,1)S(1)}, bf16[4,16,512]{2,1,0:T(8,128)(2,1)}, u32[]{:S(2)}) copy-start(bf16[4,16,512]{2,1,0:T(8,128)(2,1)} %param.30) | copy-start | bytes 196612
  3.0 14.8 %all-to-all-start = ((f32[8,16,128]{2,1,0:T(8,128)}), f32[8,16,128]{2,1,0:T(8,128)S(1)}, u32[]{:S(2)}, u32[]{:S(2)}) async-start(f32[8,16,128]{2,1,0:T(8,128)} %get-tuple-element.16), calls=%async_computation | async-start | bytes 131072 | tf_op jit(solution)/shard_map/all_to_all | solution.py:380
  10.2 7.5 %collective-permute-start = (bf16[64,512]{1,0:T(8,128)(2,1)S(1)}, bf16[64,512]{1,0:T(8,128)(2,1)S(1)}, u32[]{:S(2)}, u32[]{:S(2)}) collective-permute-start(bf16[64,512]{1,0:T(8,128)(2,1)S(1)} %bitcast.13), channel_id=1, source_target_pairs={{0,4},{1,5},{2,6},{3,7},{4,0},{5,1},{6,2},{7,3},{8,12},{9,13},{10,... | collective-permute-start | bytes 196616 | tf_op jit(solution)/shard_map/ppermute | solution.py:383
  19.5 15.3 %all-to-all-start.1 = ((f32[32,1,1152]{2,1,0:T(1,128)}), f32[32,1,1152]{2,1,0:T(1,128)S(1)}, u32[]{:S(2)}, u32[]{:S(2)}) async-start(f32[32,1,1152]{2,1,0:T(1,128)} %get-tuple-element.26), calls=%async_computation.1 | async-start | bytes 294912 | tf_op jit(solution)/shard_map/all_to_all | solution.py:380
  23.9 6.3 %collective-permute-start.1 = (bf16[96,512]{1,0:T(8,128)(2,1)S(1)}, bf16[96,512]{1,0:T(8,128)(2,1)S(1)}, u32[]{:S(2)}, u32[]{:S(2)}) collective-permute-start(bf16[96,512]{1,0:T(8,128)(2,1)S(1)} %shard_map.168.early_ref.refs_0_), channel_id=1, source_target_pairs={{0,1},{1,0},{2,3},{3,2},{4,5},{5,4},{6,7},{7,6},{8,9},{9,8},{10,11... | collective-permute-start | bytes 294920 | tf_op jit(solution)/shard_map/ppermute | solution.py:383
  25.7 6.1 %collective-permute-start.2 = (bf16[96,512]{1,0:T(8,128)(2,1)S(1)}, bf16[96,512]{1,0:T(8,128)(2,1)S(1)}, u32[]{:S(2)}, u32[]{:S(2)}) collective-permute-start(bf16[96,512]{1,0:T(8,128)(2,1)S(1)} %shard_map.168.early_ref.refs_0_), channel_id=1, source_target_pairs={{0,2},{1,3},{2,0},{3,1},{4,6},{5,7},{6,4},{7,5},{8,10},{9,11},{10,... | collective-permute-start | bytes 294920 | tf_op jit(solution)/shard_map/ppermute | solution.py:383
  30.2 4.6 %collective-permute-start.3 = (bf16[96,512]{1,0:T(8,128)(2,1)S(1)}, bf16[96,512]{1,0:T(8,128)(2,1)S(1)}, u32[]{:S(2)}, u32[]{:S(2)}) collective-permute-start(bf16[96,512]{1,0:T(8,128)(2,1)S(1)} %collective-permute-done.1.refs_1_), channel_id=1, source_target_pairs={{0,2},{1,3},{2,0},{3,1},{4,6},{5,7},{6,4},{7,5},{8,10},{9,11},{10,... | collective-permute-start | bytes 294920 | tf_op jit(solution)/shard_map/ppermute | solution.py:383

commit v10 on v8

--- a/solution.py
+++ b/solution.py
@@ -199,9 +199,9 @@
     total = jnp.zeros((members, bases_refs[0].shape[1]), jnp.float32)
     for number, ref in enumerate(bases_refs):
         left = []
-        for place in range(members // 4):
+        for place in range(members // 2):
             source = number
-            for bit in range(bits - 2):
+            for bit in range(bits - 1):
                 source |= (place >> bit & 1) << (bits - 1 - bit)
             left.append(jnp.where(row == source, weights, 0.0))
         left = jnp.concatenate(left, axis=1).astype(jnp.bfloat16)
@@ -266,8 +266,8 @@
 
 
 def second_kernel(groups, state_ref, rows_ref, all_ref, coarse_v_ref, *refs):
-    bases_refs, field_refs, sent_ref = refs[:4], refs[4:10], refs[10]
-    members, elem_count = refs[8].shape[1], state_ref.shape[1]
+    bases_refs, field_refs, sent_ref = refs[:2], refs[2:8], refs[8]
+    members, elem_count = refs[6].shape[1], state_ref.shape[1]
     width = coarse_v_ref.shape[0]
     mine, me = lax.axis_index("leaf"), lax.axis_index("blk")
     sums = [
@@ -305,7 +305,7 @@
 
 
 def finish_kernel(groups, width, got_ref, slot_ref, slot_row_ref, *refs):
-    bases_refs, u_ref, phi_ref = refs[:4], refs[4], refs[5]
+    bases_refs, u_ref, phi_ref = refs[:2], refs[2], refs[3]
     elem_count = slot_ref.shape[1]
     members = got_ref.shape[0] // groups
     sums = []
@@ -414,11 +414,10 @@
         functools.partial(pair_kernel, rank), shape(2 * kept, elems, dtype=jnp.bfloat16),
         bases, partner(bases, top), slot, flops=1 << 26, moved=1 << 22,
     )
-    for bit in range(top - 1, 1, -1):
+    for bit in range(top - 1, 0, -1):
         stacked = shape(2 * bases.shape[0], elems, dtype=jnp.bfloat16)
         bases = call(stack_kernel, stacked, bases, partner(bases, bit))
-    across = partner(bases, 0)
-    bases = bases, across, partner(bases, 1), partner(across, 1)
+    bases = bases, partner(bases, 0)
     fields = near_count, near, far_u, far_v, near_mask, far_mask
     state, rows, out = call(
         place_kernel,
@@ -432,7 +431,7 @@
     )
     sent = call(
         functools.partial(second_kernel, groups), shape(devices, sent_rows, LANES),
-        state, rows, swap(out, ("leaf", "blk")), coarse_v, *bases, *fields, scalars=(8,),
+        state, rows, swap(out, ("leaf", "blk")), coarse_v, *bases, *fields, scalars=(6,),
     )
     u, phi = call(
         functools.partial(finish_kernel, groups, width), (shape(1, elems), shape(1, elems)),

time: 54.1 us -> 48.5 us (0.90)
  waiting for transfers between devices: 21 us -> 11.4 us
  starting transfers between devices: 14.2 us -> 17 us
  blocking collectives: 10.7 us -> 11.9 us
    all_to_all x2, waiting for transfers between devices: 6.26 us -> 0.01 us  [swap(): return lax.all_to_all(value, axes, split_axis=0, concat_axis=0, tiled=True)]
    ppermute x4 -> x3, waiting for transfers between devices: 14.7 us -> 11.4 us  [partner(): lax.ppermute(value, 'blk', [(i, i ^ 1 << bit) for i in range(members)])]
    all_to_all x2, starting transfers between devices: 9.97 us -> 12.2 us  [swap(): return lax.all_to_all(value, axes, split_axis=0, concat_axis=0, tiled=True)]
    all_to_all x1, blocking collectives: 10.7 us -> 11.9 us  [swap(): return lax.all_to_all(value, axes, split_axis=0, concat_axis=0, tiled=True)]
    ppermute x4 -> x3, starting transfers between devices: 4.27 us -> 4.82 us  [partner(): lax.ppermute(value, 'blk', [(i, i ^ 1 << bit) for i in range(members)])]
    pallas_call x5 -> x6, Pallas kernels: 6.51 us -> 6.54 us  [call(): pl.pallas_call(kernel, out_shape=outs, in_specs=[pl.BlockSpec(memory_spac...]
  transfers between devices with their start and end apart: 6 -> 5, of which waited for: 5 -> 2; matrix products, arithmetic and copies ran while one was open for 0% -> 0% of each run, Pallas kernels for 0% -> 4%
where the time goes in v10:
time: 48.5 us; the launch traced here: 48.2 us
  starting transfers between devices  17 us (35%)
  blocking collectives  11.9 us (25%)
  waiting for transfers between devices  11.4 us (24%)
  Pallas kernels  6.54 us (13%)
  between operations  1.35 us (3%)
    all_to_all x2, starting transfers between devices, swap(): return lax.all_to_all(value, axes, split_axis=0, concat_axis=0, tiled=True)  12.2 us
    all_to_all x1, blocking collectives, swap(): return lax.all_to_all(value, axes, split_axis=0, concat_axis=0, tiled=True)  11.9 us
    ppermute x3, waiting for transfers between devices, partner(): lax.ppermute(value, 'blk', [(i, i ^ 1 << bit) for i in range(members)])  11.4 us
    pallas_call x6, Pallas kernels, call(): pl.pallas_call(kernel, out_shape=outs, in_specs=[pl.BlockSpec(memory_spac...  6.54 us
    ppermute x3, starting transfers between devices, partner(): lax.ppermute(value, 'blk', [(i, i ^ 1 << bit) for i in range(members)])  4.82 us
  transfers between devices with their start and end apart: 5, of which 2 were waited for; matrix products, arithmetic and copies ran while one was open for 0% of the time, Pallas kernels for 4%

profile of v10, /device:TPU:0, one launch (start us, length us, event | category | flops | bytes accessed | tf_op | source)
XLA Modules:
  0.0 48.2 jit_solution(7080781121732367909)
XLA Ops:
  0.6 0.0 copy-start
  0.6 2.3 %shard_map.167 = (f32[8,16,128]{2,1,0:T(8,128)}, s32[1,512]{1,0:T(1,128)S(1)}, s32[1,512]{1,0:T(1,128)S(1)}, f32[3,8,512]{2,1,0:T(8,128)S(1)}, f32[8,64]{1,0:T(8...) custom-call(s32[1,512]{1,0:T(1,128)} %bitcast.18, ...), custom_call_target="tpu_custom_call" | custom-call | flops 1000 | bytes 1000 | tf_op jit(solution)/shard_map/pallas_call | solution.py:336
  3.0 7.3 %all-to-all-start = ((f32[8,16,128]{2,1,0:T(8,128)}), f32[8,16,128]{2,1,0:T(8,128)S(1)}, u32[]{:S(2)}, u32[]{:S(2)}) async-start(f32[8,16,128]{2,1,0:T(8,128)} %get-tuple-element.16), calls=%async_computation | async-start | bytes 131072 | tf_op jit(solution)/shard_map/all_to_all | solution.py:380
  10.2 0.0 copy-done
  10.2 2.9 %collective-permute-start = (bf16[64,512]{1,0:T(8,128)(2,1)S(1)}, bf16[64,512]{1,0:T(8,128)(2,1)S(1)}, u32[]{:S(2)}, u32[]{:S(2)}) collective-permute-start(bf16[64,512]{1,0:T(8,128)(2,1)S(1)} %bitcast.13), channel_id=1, source_target_pairs={{0,4},{1,5},{2,6},{3,7},{4,0},{5,1},{6,2},{7,3},{8,12},{9,13},{10,... | collective-permute-start | bytes 196616 | tf_op jit(solution)/shard_map/ppermute | solution.py:383
  13.2 4.6 %collective-permute-done.came_ref = bf16[64,512]{1,0:T(8,128)(2,1)S(1)} collective-permute-done((bf16[64,512]{1,0:T(8,128)(2,1)S(1)}, bf16[64,512]{1,0:T(8,128)(2,1)S(1)}, u32[]{:S(2)}, u32[]{:S(2)}) %collective-permute-start) | collective-permute-done | bytes 65568 | tf_op jit(solution)/shard_map/ppermute | solution.py:383
  17.8 0.1 collective-permute-start.1
  18.5 0.0 all-to-all-done.got_ref
  18.5 1.7 %shard_map.168 = (f32[8,512]{1,0:T(8,128)S(1)}, s32[1,512]{1,0:T(1,128)S(1)}, f32[32,1,1152]{2,1,0:T(1,128)}) custom-call(f32[8,16,128]{2,1,0:T(8,128)S(1)} %all-to-all-done.got_ref, bf16[64,512]{1,0:T(8,128)(2,1)S(1)} %get-tuple-element.17.coarse_v_ref, s32[1]{0:T(128)S(6)} %copy.18.refs_0_.refs_2_, ...), custom_call_target="tpu_custom_call" | custom-call | flops 1000 | bytes 1000 | tf_op jit(solution)/shard_map/pallas_call | solution.py:336
  20.3 4.9 %all-to-all-start.1 = ((f32[32,1,1152]{2,1,0:T(1,128)}), f32[32,1,1152]{2,1,0:T(1,128)S(1)}, u32[]{:S(2)}, u32[]{:S(2)}) async-start(f32[32,1,1152]{2,1,0:T(1,128)} %get-tuple-element.25), calls=%async_computation.1 | async-start | bytes 294912 | tf_op jit(solution)/shard_map/all_to_all | solution.py:380
  25.2 0.0 collective-permute-done.1.came_ref
  25.2 1.8 %collective-permute-start.2 = (bf16[192,512]{1,0:T(8,128)(2,1)S(1)}, bf16[192,512]{1,0:T(8,128)(2,1)S(1)}, u32[]{:S(2)}, u32[]{:S(2)}) collective-permute-start(bf16[192,512]{1,0:T(8,128)(2,1)S(1)} %shard_map.170.refs_0_), channel_id=1, source_target_pairs={{0,1},{1,0},{2,3},{3,2},{4,5},{5,4},{6,7},{7,6},{8,9},{9,8},{10,11... | collective-permute-start | bytes 589832 | tf_op jit(solution)/shard_map/ppermute | solution.py:383
  27.1 6.8 %collective-permute-done.2.refs_1_ = bf16[192,512]{1,0:T(8,128)(2,1)S(1)} collective-permute-done((bf16[192,512]{1,0:T(8,128)(2,1)S(1)}, bf16[192,512]{1,0:T(8,128)(2,1)S(1)}, u32[]{:S(2)}, u32[]{:S(2)}) %collective-permute-start.2) | collective-permute-done | bytes 196640 | tf_op jit(solution)/shard_map/ppermute | solution.py:383
  33.9 0.0 all-to-all-done.1.all_ref
  33.9 1.2 %shard_map.171 = f32[32,4,128]{2,1,0:T(4,128)S(1)} custom-call(f32[8,512]{1,0:T(8,128)S(1)} %get-tuple-element.23.state_ref, s32[1,512]{1,0:T(1,128)S(1)} %get-tuple-element.24.rows_ref, f32[32,1,1152]{2,1,0:T(1,128)S(1)} %all-to-all-done.1.all_ref, bf16[64,512]{1,0:T(8,128)(2,1)S(1)} %get-tuple-element.17.coarse_v_ref, ...), custom_call_target="tpu_custom_call" | custom-call | flops 1000 | bytes 1000 | tf_op jit(solution)/shard_map/pallas_call | solution.py:336
  35.1 11.9 %all_to_all.15.got_ref = f32[32,4,128]{2,1,0:T(4,128)S(1)} all-to-all(f32[32,4,128]{2,1,0:T(4,128)S(1)} %shard_map.171), channel_id=1, replica_groups=mesh['leaf'=4,'blk'=8] {'leaf','blk'}, dimensions={0} | all-to-all | bytes 131072 | tf_op jit(solution)/shard_map/all_to_all | solution.py:380
  47.0 1.3 %shard_map.172 = (f32[1,512]{1,0:T(1,128)}, f32[1,512]{1,0:T(1,128)}) custom-call(f32[32,4,128]{2,1,0:T(4,128)S(1)} %all_to_all.15.got_ref, s32[1,512]{1,0:T(1,128)S(1)} %get-tuple-element.26.order_ref.slot_ref, s32[1,512]{1,0:T(1,128)S(1)} %get-tuple-element.27.slot_row_ref, bf16[192,512]{1,0:T(8,128)(2,1)S(1)} %shard_map.170.refs_0_, ...), custom_call_target="tpu_custom_call" | custom-call | flops 1000 | bytes 1000 | tf_op jit(solution)/shard_map/pallas_call | solution.py:336
  (2 shorter events, 0.0 us)
Async XLA Ops:
  0.6 9.6 %copy-start = (bf16[4,16,512]{2,1,0:T(8,128)(2,1)S(1)}, bf16[4,16,512]{2,1,0:T(8,128)(2,1)}, u32[]{:S(2)}) copy-start(bf16[4,16,512]{2,1,0:T(8,128)(2,1)} %param.30) | copy-start | bytes 196612
  3.0 15.6 %all-to-all-start = ((f32[8,16,128]{2,1,0:T(8,128)}), f32[8,16,128]{2,1,0:T(8,128)S(1)}, u32[]{:S(2)}, u32[]{:S(2)}) async-start(f32[8,16,128]{2,1,0:T(8,128)} %get-tuple-element.16), calls=%async_computation | async-start | bytes 131072 | tf_op jit(solution)/shard_map/all_to_all | solution.py:380
  10.2 7.5 %collective-permute-start = (bf16[64,512]{1,0:T(8,128)(2,1)S(1)}, bf16[64,512]{1,0:T(8,128)(2,1)S(1)}, u32[]{:S(2)}, u32[]{:S(2)}) collective-permute-start(bf16[64,512]{1,0:T(8,128)(2,1)S(1)} %bitcast.13), channel_id=1, source_target_pairs={{0,4},{1,5},{2,6},{3,7},{4,0},{5,1},{6,2},{7,3},{8,12},{9,13},{10,... | collective-permute-start | bytes 196616 | tf_op jit(solution)/shard_map/ppermute | solution.py:383
  17.8 7.4 %collective-permute-start.1 = (bf16[96,512]{1,0:T(8,128)(2,1)S(1)}, bf16[96,512]{1,0:T(8,128)(2,1)S(1)}, u32[]{:S(2)}, u32[]{:S(2)}) collective-permute-start(bf16[96,512]{1,0:T(8,128)(2,1)S(1)} %shard_map.169.held_ref), channel_id=1, source_target_pairs={{0,2},{1,3},{2,0},{3,1},{4,6},{5,7},{6,4},{7,5},{8,10},{9,11},{10,... | collective-permute-start | bytes 294920 | tf_op jit(solution)/shard_map/ppermute | solution.py:383
  20.3 13.6 %all-to-all-start.1 = ((f32[32,1,1152]{2,1,0:T(1,128)}), f32[32,1,1152]{2,1,0:T(1,128)S(1)}, u32[]{:S(2)}, u32[]{:S(2)}) async-start(f32[32,1,1152]{2,1,0:T(1,128)} %get-tuple-element.25), calls=%async_computation.1 | async-start | bytes 294912 | tf_op jit(solution)/shard_map/all_to_all | solution.py:380
  25.2 8.6 %collective-permute-start.2 = (bf16[192,512]{1,0:T(8,128)(2,1)S(1)}, bf16[192,512]{1,0:T(8,128)(2,1)S(1)}, u32[]{:S(2)}, u32[]{:S(2)}) collective-permute-start(bf16[192,512]{1,0:T(8,128)(2,1)S(1)} %shard_map.170.refs_0_), channel_id=1, source_target_pairs={{0,1},{1,0},{2,3},{3,2},{4,5},{5,4},{6,7},{7,6},{8,9},{9,8},{10,11... | collective-permute-start | bytes 589832 | tf_op jit(solution)/shard_map/ppermute | solution.py:383

commit v11 on v10

--- a/solution.py
+++ b/solution.py
@@ -209,19 +209,23 @@
     return total
 
 
-def pair_kernel(rank, held_ref, came_ref, order_ref, out_ref):
-    groups = held_ref.shape[0] // rank
-    mine = lax.axis_index("leaf")
-    for number, ref in enumerate((held_ref, came_ref)):
-        for shift in range(1, groups):
-            place = (number * (groups - 1) + shift - 1) * rank
-            out_ref[place:place + rank, :] = ref[pl.ds((mine ^ shift) * rank, rank), :]
-
-
-def stack_kernel(held_ref, came_ref, out_ref):
+def stack_kernel(held_ref, came_ref, *refs):
+    out_ref = refs[-1]
     count = held_ref.shape[0]
     out_ref[0:count, :] = held_ref[...]
     out_ref[count:2 * count, :] = came_ref[...]
+
+
+def stack_foreign_kernel(groups, rank, held_ref, came_ref, *refs):
+    out_ref = refs[-1]
+    width = groups * rank
+    mine = lax.axis_index("leaf")
+    place = 0
+    for ref in (held_ref, came_ref):
+        for low in range(0, ref.shape[0], width):
+            for shift in range(1, groups):
+                out_ref[place:place + rank, :] = ref[pl.ds(low + (mine ^ shift) * rank, rank), :]
+                place += rank
 
 
 def place_kernel(got_ref, coarse_v_ref, *refs):
@@ -408,15 +412,16 @@
         + [pltpu.SemaphoreType.DMA((14,))],
     )
     bases = coarse_u.reshape(width, elems)
-    top = members.bit_length() - 2
-    kept = width - rank
-    bases = call(
-        functools.partial(pair_kernel, rank), shape(2 * kept, elems, dtype=jnp.bfloat16),
-        bases, partner(bases, top), slot, flops=1 << 26, moved=1 << 22,
-    )
-    for bit in range(top - 1, 0, -1):
-        stacked = shape(2 * bases.shape[0], elems, dtype=jnp.bfloat16)
-        bases = call(stack_kernel, stacked, bases, partner(bases, bit))
+    for bit in range(members.bit_length() - 2, 0, -1):
+        rows_out = 2 * bases.shape[0]
+        kernel = stack_kernel
+        if bit == 1:
+            rows_out = rows_out // groups * (groups - 1)
+            kernel = functools.partial(stack_foreign_kernel, groups, rank)
+        bases = call(
+            kernel, shape(rows_out, elems, dtype=jnp.bfloat16),
+            bases, partner(bases, bit), slot, flops=1 << 26, moved=1 << 22,
+        )
     bases = bases, partner(bases, 0)
     fields = near_count, near, far_u, far_v, near_mask, far_mask
     state, rows, out = call(

time: 48.5 us -> 45.6 us (0.940)
  starting transfers between devices: 17 us -> 14.2 us
    all_to_all x2, starting transfers between devices: 12.2 us -> 6.37 us  [swap(): return lax.all_to_all(value, axes, split_axis=0, concat_axis=0, tiled=True)]
    ppermute x3, waiting for transfers between devices: 11.4 us -> 6.79 us  [partner(): lax.ppermute(value, 'blk', [(i, i ^ 1 << bit) for i in range(members)])]
    all_to_all x2, waiting for transfers between devices: 0.01 us -> 4.38 us  [swap(): return lax.all_to_all(value, axes, split_axis=0, concat_axis=0, tiled=True)]
    ppermute x3, starting transfers between devices: 4.82 us -> 7.88 us  [partner(): lax.ppermute(value, 'blk', [(i, i ^ 1 << bit) for i in range(members)])]
  transfers between devices with their start and end apart: 5 -> 5, of which waited for: 2 -> 2; matrix products, arithmetic and copies ran while one was open for 0% -> 0% of each run, Pallas kernels for 4% -> 9%
where the time goes in v11:
time: 45.6 us; the launch traced here: 45.3 us
  starting transfers between devices  14.2 us (31%)
  blocking collectives  12 us (26%)
  waiting for transfers between devices  11.2 us (25%)
  Pallas kernels  6.51 us (14%)
  between operations  1.35 us (3%)
    all_to_all x1, blocking collectives, swap(): return lax.all_to_all(value, axes, split_axis=0, concat_axis=0, tiled=True)  12 us
    ppermute x3, starting transfers between devices, partner(): lax.ppermute(value, 'blk', [(i, i ^ 1 << bit) for i in range(members)])  7.88 us
    ppermute x3, waiting for transfers between devices, partner(): lax.ppermute(value, 'blk', [(i, i ^ 1 << bit) for i in range(members)])  6.79 us
    pallas_call x6, Pallas kernels, call(): pl.pallas_call(kernel, out_shape=outs, in_specs=[pl.BlockSpec(memory_spac...  6.51 us
    all_to_all x2, starting transfers between devices, swap(): return lax.all_to_all(value, axes, split_axis=0, concat_axis=0, tiled=True)  6.37 us
    all_to_all x2, waiting for transfers between devices, swap(): return lax.all_to_all(value, axes, split_axis=0, concat_axis=0, tiled=True)  4.38 us
  transfers between devices with their start and end apart: 5, of which 2 were waited for; matrix products, arithmetic and copies ran while one was open for 0% of the time, Pallas kernels for 9%

profile of v11, /device:TPU:0, one launch (start us, length us, event | category | flops | bytes accessed | tf_op | source)
XLA Modules:
  0.0 45.3 jit_solution(9881667427328978997)
XLA Ops:
  0.6 0.0 copy-start
  0.6 4.1 %collective-permute-start = (bf16[64,512]{1,0:T(8,128)(2,1)}, bf16[64,512]{1,0:T(8,128)(2,1)S(1)}, u32[]{:S(2)}, u32[]{:S(2)}) collective-permute-start(bf16[64,512]{1,0:T(8,128)(2,1)} %bitcast.13), channel_id=1, source_target_pairs={{0,4},{1,5},{2,6},{3,7},{4,0},{5,1},{6,2},{7,3},{8,12},{9,13},{10,... | collective-permute-start | bytes 196616 | tf_op jit(solution)/shard_map/ppermute | solution.py:387
  4.7 2.3 %shard_map.167 = (f32[8,16,128]{2,1,0:T(8,128)}, s32[1,512]{1,0:T(1,128)S(1)}, s32[1,512]{1,0:T(1,128)S(1)}, f32[3,8,512]{2,1,0:T(8,128)S(1)}, f32[8,64]{1,0:T(8...) custom-call(s32[1,512]{1,0:T(1,128)} %bitcast.18, ...), custom_call_target="tpu_custom_call" | custom-call | flops 1000 | bytes 1000 | tf_op jit(solution)/shard_map/pallas_call | solution.py:340
  7.0 3.8 %all-to-all-start = ((f32[8,16,128]{2,1,0:T(8,128)}), f32[8,16,128]{2,1,0:T(8,128)S(1)}, u32[]{:S(2)}, u32[]{:S(2)}) async-start(f32[8,16,128]{2,1,0:T(8,128)} %get-tuple-element.16), calls=%async_computation | async-start | bytes 131072 | tf_op jit(solution)/shard_map/all_to_all | solution.py:384
  10.8 0.0 collective-permute-done.came_ref
  10.8 0.0 copy-done
  10.9 2.1 %collective-permute-start.1 = (bf16[128,512]{1,0:T(8,128)(2,1)S(1)}, bf16[128,512]{1,0:T(8,128)(2,1)S(1)}, u32[]{:S(2)}, u32[]{:S(2)}) collective-permute-start(bf16[128,512]{1,0:T(8,128)(2,1)S(1)} %shard_map.169.held_ref), channel_id=1, source_target_pairs={{0,2},{1,3},{2,0},{3,1},{4,6},{5,7},{6,4},{7,5},{8,10},{9,11},{10,... | collective-permute-start | bytes 393224 | tf_op jit(solution)/shard_map/ppermute | solution.py:387
  13.6 4.4 %all-to-all-done.got_ref = f32[8,16,128]{2,1,0:T(8,128)S(1)} async-done(((f32[8,16,128]{2,1,0:T(8,128)}), f32[8,16,128]{2,1,0:T(8,128)S(1)}, u32[]{:S(2)}, u32[]{:S(2)}) %all-to-all-start) | async-done | bytes 65568 | tf_op jit(solution)/shard_map/all_to_all | solution.py:384
  18.0 1.7 %shard_map.168 = (f32[8,512]{1,0:T(8,128)S(1)}, s32[1,512]{1,0:T(1,128)S(1)}, f32[32,1,1152]{2,1,0:T(1,128)}) custom-call(f32[8,16,128]{2,1,0:T(8,128)S(1)} %all-to-all-done.got_ref, bf16[64,512]{1,0:T(8,128)(2,1)S(1)} %get-tuple-element.17.coarse_v_ref, s32[1]{0:T(128)S(6)} %copy.18.refs_0_.refs_2_, ...), custom_call_target="tpu_custom_call" | custom-call | flops 1000 | bytes 1000 | tf_op jit(solution)/shard_map/pallas_call | solution.py:340
  19.7 2.6 %all-to-all-start.1 = ((f32[32,1,1152]{2,1,0:T(1,128)}), f32[32,1,1152]{2,1,0:T(1,128)S(1)}, u32[]{:S(2)}, u32[]{:S(2)}) async-start(f32[32,1,1152]{2,1,0:T(1,128)} %get-tuple-element.25), calls=%async_computation.1 | async-start | bytes 294912 | tf_op jit(solution)/shard_map/all_to_all | solution.py:384
  22.3 0.0 collective-permute-done.1.came_ref
  22.3 1.7 %collective-permute-start.2 = (bf16[192,512]{1,0:T(8,128)(2,1)S(1)}, bf16[192,512]{1,0:T(8,128)(2,1)S(1)}, u32[]{:S(2)}, u32[]{:S(2)}) collective-permute-start(bf16[192,512]{1,0:T(8,128)(2,1)S(1)} %shard_map.170.refs_0_), channel_id=1, source_target_pairs={{0,1},{1,0},{2,3},{3,2},{4,5},{5,4},{6,7},{7,6},{8,9},{9,8},{10,11... | collective-permute-start | bytes 589832 | tf_op jit(solution)/shard_map/ppermute | solution.py:387
  24.0 6.8 %collective-permute-done.2.refs_1_ = bf16[192,512]{1,0:T(8,128)(2,1)S(1)} collective-permute-done((bf16[192,512]{1,0:T(8,128)(2,1)S(1)}, bf16[192,512]{1,0:T(8,128)(2,1)S(1)}, u32[]{:S(2)}, u32[]{:S(2)}) %collective-permute-start.2) | collective-permute-done | bytes 196640 | tf_op jit(solution)/shard_map/ppermute | solution.py:387
  30.8 0.0 all-to-all-done.1.all_ref
  30.8 1.2 %shard_map.171 = f32[32,4,128]{2,1,0:T(4,128)S(1)} custom-call(f32[8,512]{1,0:T(8,128)S(1)} %get-tuple-element.23.state_ref, s32[1,512]{1,0:T(1,128)S(1)} %get-tuple-element.24.rows_ref, f32[32,1,1152]{2,1,0:T(1,128)S(1)} %all-to-all-done.1.all_ref, bf16[64,512]{1,0:T(8,128)(2,1)S(1)} %get-tuple-element.17.coarse_v_ref, ...), custom_call_target="tpu_custom_call" | custom-call | flops 1000 | bytes 1000 | tf_op jit(solution)/shard_map/pallas_call | solution.py:340
  32.0 12.0 %all_to_all.15.got_ref = f32[32,4,128]{2,1,0:T(4,128)S(1)} all-to-all(f32[32,4,128]{2,1,0:T(4,128)S(1)} %shard_map.171), channel_id=1, replica_groups=mesh['leaf'=4,'blk'=8] {'leaf','blk'}, dimensions={0} | all-to-all | bytes 131072 | tf_op jit(solution)/shard_map/all_to_all | solution.py:384
  44.1 1.3 %shard_map.172 = (f32[1,512]{1,0:T(1,128)}, f32[1,512]{1,0:T(1,128)}) custom-call(f32[32,4,128]{2,1,0:T(4,128)S(1)} %all_to_all.15.got_ref, s32[1,512]{1,0:T(1,128)S(1)} %get-tuple-element.26.refs_0_.slot_ref, s32[1,512]{1,0:T(1,128)S(1)} %get-tuple-element.27.slot_row_ref, bf16[192,512]{1,0:T(8,128)(2,1)S(1)} %shard_map.170.refs_0_, ...), custom_call_target="tpu_custom_call" | custom-call | flops 1000 | bytes 1000 | tf_op jit(solution)/shard_map/pallas_call | solution.py:340
  (2 shorter events, 0.0 us)
Async XLA Ops:
  0.6 10.2 %copy-start = (bf16[4,16,512]{2,1,0:T(8,128)(2,1)S(1)}, bf16[4,16,512]{2,1,0:T(8,128)(2,1)}, u32[]{:S(2)}) copy-start(bf16[4,16,512]{2,1,0:T(8,128)(2,1)} %param.30) | copy-start | bytes 196612
  0.6 10.2 %collective-permute-start = (bf16[64,512]{1,0:T(8,128)(2,1)}, bf16[64,512]{1,0:T(8,128)(2,1)S(1)}, u32[]{:S(2)}, u32[]{:S(2)}) collective-permute-start(bf16[64,512]{1,0:T(8,128)(2,1)} %bitcast.13), channel_id=1, source_target_pairs={{0,4},{1,5},{2,6},{3,7},{4,0},{5,1},{6,2},{7,3},{8,12},{9,13},{10,... | collective-permute-start | bytes 196616 | tf_op jit(solution)/shard_map/ppermute | solution.py:387
  7.0 10.9 %all-to-all-start = ((f32[8,16,128]{2,1,0:T(8,128)}), f32[8,16,128]{2,1,0:T(8,128)S(1)}, u32[]{:S(2)}, u32[]{:S(2)}) async-start(f32[8,16,128]{2,1,0:T(8,128)} %get-tuple-element.16), calls=%async_computation | async-start | bytes 131072 | tf_op jit(solution)/shard_map/all_to_all | solution.py:384
  10.9 11.4 %collective-permute-start.1 = (bf16[128,512]{1,0:T(8,128)(2,1)S(1)}, bf16[128,512]{1,0:T(8,128)(2,1)S(1)}, u32[]{:S(2)}, u32[]{:S(2)}) collective-permute-start(bf16[128,512]{1,0:T(8,128)(2,1)S(1)} %shard_map.169.held_ref), channel_id=1, source_target_pairs={{0,2},{1,3},{2,0},{3,1},{4,6},{5,7},{6,4},{7,5},{8,10},{9,11},{10,... | collective-permute-start | bytes 393224 | tf_op jit(solution)/shard_map/ppermute | solution.py:387
  19.7 11.1 %all-to-all-start.1 = ((f32[32,1,1152]{2,1,0:T(1,128)}), f32[32,1,1152]{2,1,0:T(1,128)S(1)}, u32[]{:S(2)}, u32[]{:S(2)}) async-start(f32[32,1,1152]{2,1,0:T(1,128)} %get-tuple-element.25), calls=%async_computation.1 | async-start | bytes 294912 | tf_op jit(solution)/shard_map/all_to_all | solution.py:384
  22.3 8.5 %collective-permute-start.2 = (bf16[192,512]{1,0:T(8,128)(2,1)S(1)}, bf16[192,512]{1,0:T(8,128)(2,1)S(1)}, u32[]{:S(2)}, u32[]{:S(2)}) collective-permute-start(bf16[192,512]{1,0:T(8,128)(2,1)S(1)} %shard_map.170.refs_0_), channel_id=1, source_target_pairs={{0,1},{1,0},{2,3},{3,2},{4,5},{5,4},{6,7},{7,6},{8,9},{9,8},{10,11... | collective-permute-start | bytes 589832 | tf_op jit(solution)/shard_map/ppermute | solution.py:387

commit v12 on v11

--- a/solution.py
+++ b/solution.py
@@ -228,6 +228,10 @@
                 place += rank
 
 
+def mark_kernel(came_ref, out_ref):
+    out_ref[...] = came_ref[0:16, 0:LANES].astype(jnp.float32)
+
+
 def place_kernel(got_ref, coarse_v_ref, *refs):
     field_refs, state_ref, rows_ref, out_ref, lines_ref = refs[:6], refs[6], refs[7], refs[8], refs[9]
     members = got_ref.shape[0]
@@ -269,7 +273,7 @@
     out_ref[...] = jnp.broadcast_to(sent[None], out_ref.shape)
 
 
-def second_kernel(groups, state_ref, rows_ref, all_ref, coarse_v_ref, *refs):
+def second_kernel(groups, state_ref, rows_ref, all_ref, complete_ref, coarse_v_ref, *refs):
     bases_refs, field_refs, sent_ref = refs[:2], refs[2:8], refs[8]
     members, elem_count = refs[6].shape[1], state_ref.shape[1]
     width = coarse_v_ref.shape[0]
@@ -423,6 +427,7 @@
             bases, partner(bases, bit), slot, flops=1 << 26, moved=1 << 22,
         )
     bases = bases, partner(bases, 0)
+    complete = call(mark_kernel, shape(16, LANES), bases[1], flops=1 << 34, moved=1 << 26)
     fields = near_count, near, far_u, far_v, near_mask, far_mask
     state, rows, out = call(
         place_kernel,
@@ -436,7 +441,7 @@
     )
     sent = call(
         functools.partial(second_kernel, groups), shape(devices, sent_rows, LANES),
-        state, rows, swap(out, ("leaf", "blk")), coarse_v, *bases, *fields, scalars=(6,),
+        state, rows, swap(out, ("leaf", "blk")), complete, coarse_v, *bases, *fields, scalars=(7,),
     )
     u, phi = call(
         functools.partial(finish_kernel, groups, width), (shape(1, elems), shape(1, elems)),

time: 45.6 us -> 51.5 us (1.13)
  waiting for transfers between devices: 11.2 us -> 19.9 us
  blocking collectives: 12 us -> 9.7 us
    all_to_all x2, waiting for transfers between devices: 4.38 us -> 14.1 us  [swap(): return lax.all_to_all(value, axes, split_axis=0, concat_axis=0, tiled=True)]
    all_to_all x1, blocking collectives: 12 us -> 9.7 us  [swap(): return lax.all_to_all(value, axes, split_axis=0, concat_axis=0, tiled=True)]
    ppermute x3, starting transfers between devices: 7.88 us -> 6.6 us  [partner(): lax.ppermute(value, 'blk', [(i, i ^ 1 << bit) for i in range(members)])]
    ppermute x3, waiting for transfers between devices: 6.79 us -> 5.87 us  [partner(): lax.ppermute(value, 'blk', [(i, i ^ 1 << bit) for i in range(members)])]
    all_to_all x2, starting transfers between devices: 6.37 us -> 7.13 us  [swap(): return lax.all_to_all(value, axes, split_axis=0, concat_axis=0, tiled=True)]
    pallas_call x6 -> x7, Pallas kernels: 6.51 us -> 6.5 us  [call(): pl.pallas_call(kernel, out_shape=outs, in_specs=[pl.BlockSpec(memory_spac...]
  transfers between devices with their start and end apart: 5 -> 5, of which waited for: 2 -> 4; matrix products, arithmetic and copies ran while one was open for 0% -> 0% of each run, Pallas kernels for 9% -> 8%
where the time goes in v12:
time: 51.5 us; the launch traced here: 51.2 us
  waiting for transfers between devices  19.9 us (39%)
  starting transfers between devices  13.7 us (27%)
  blocking collectives  9.7 us (19%)
  Pallas kernels  6.5 us (13%)
  between operations  1.34 us (3%)
    all_to_all x2, waiting for transfers between devices, swap(): return lax.all_to_all(value, axes, split_axis=0, concat_axis=0, tiled=True)  14.1 us
    all_to_all x1, blocking collectives, swap(): return lax.all_to_all(value, axes, split_axis=0, concat_axis=0, tiled=True)  9.7 us
    all_to_all x2, starting transfers between devices, swap(): return lax.all_to_all(value, axes, split_axis=0, concat_axis=0, tiled=True)  7.13 us
    ppermute x3, starting transfers between devices, partner(): lax.ppermute(value, 'blk', [(i, i ^ 1 << bit) for i in range(members)])  6.6 us
    pallas_call x7, Pallas kernels, call(): pl.pallas_call(kernel, out_shape=outs, in_specs=[pl.BlockSpec(memory_spac...  6.5 us
    ppermute x3, waiting for transfers between devices, partner(): lax.ppermute(value, 'blk', [(i, i ^ 1 << bit) for i in range(members)])  5.87 us
  transfers between devices with their start and end apart: 5, of which 4 were waited for; matrix products, arithmetic and copies ran while one was open for 0% of the time, Pallas kernels for 8%

profile of v12, /device:TPU:0, one launch (start us, length us, event | category | flops | bytes accessed | tf_op | source)
XLA Modules:
  0.0 51.2 jit_solution(8047230685941975725)
XLA Ops:
  0.6 0.0 copy-start
  0.6 4.1 %collective-permute-start = (bf16[64,512]{1,0:T(8,128)(2,1)}, bf16[64,512]{1,0:T(8,128)(2,1)S(1)}, u32[]{:S(2)}, u32[]{:S(2)}) collective-permute-start(bf16[64,512]{1,0:T(8,128)(2,1)} %bitcast.13), channel_id=1, source_target_pairs={{0,4},{1,5},{2,6},{3,7},{4,0},{5,1},{6,2},{7,3},{8,12},{9,13},{10,... | collective-permute-start | bytes 196616 | tf_op jit(solution)/shard_map/ppermute | solution.py:391
  4.7 2.3 %shard_map.167 = (f32[8,16,128]{2,1,0:T(8,128)}, s32[1,512]{1,0:T(1,128)S(1)}, s32[1,512]{1,0:T(1,128)S(1)}, f32[3,8,512]{2,1,0:T(8,128)S(1)}, f32[8,64]{1,0:T(8...) custom-call(s32[1,512]{1,0:T(1,128)} %bitcast.18, ...), custom_call_target="tpu_custom_call" | custom-call | flops 1000 | bytes 1000 | tf_op jit(solution)/shard_map/pallas_call | solution.py:344
  7.0 1.6 %collective-permute-done.came_ref = bf16[64,512]{1,0:T(8,128)(2,1)S(1)} collective-permute-done((bf16[64,512]{1,0:T(8,128)(2,1)}, bf16[64,512]{1,0:T(8,128)(2,1)S(1)}, u32[]{:S(2)}, u32[]{:S(2)}) %collective-permute-start) | collective-permute-done | bytes 65568 | tf_op jit(solution)/shard_map/ppermute | solution.py:391
  8.6 0.0 copy-done
  8.6 0.7 %collective-permute-start.1 = (bf16[128,512]{1,0:T(8,128)(2,1)S(1)}, bf16[128,512]{1,0:T(8,128)(2,1)S(1)}, u32[]{:S(2)}, u32[]{:S(2)}) collective-permute-start(bf16[128,512]{1,0:T(8,128)(2,1)S(1)} %shard_map.169.held_ref), channel_id=1, source_target_pairs={{0,2},{1,3},{2,0},{3,1},{4,6},{5,7},{6,4},{7,5},{8,10},{9,11},{10,... | collective-permute-start | bytes 393224 | tf_op jit(solution)/shard_map/ppermute | solution.py:391
  9.4 4.3 %collective-permute-done.1.came_ref = bf16[128,512]{1,0:T(8,128)(2,1)S(1)} collective-permute-done((bf16[128,512]{1,0:T(8,128)(2,1)S(1)}, bf16[128,512]{1,0:T(8,128)(2,1)S(1)}, u32[]{:S(2)}, u32[]{:S(2)}) %collective-permute-start.1) | collective-permute-done | bytes 131104 | tf_op jit(solution)/shard_map/ppermute | solution.py:391
  13.7 1.8 %collective-permute-start.2 = (bf16[192,512]{1,0:T(8,128)(2,1)S(1)}, bf16[192,512]{1,0:T(8,128)(2,1)S(1)}, u32[]{:S(2)}, u32[]{:S(2)}) collective-permute-start(bf16[192,512]{1,0:T(8,128)(2,1)S(1)} %shard_map.170.refs_0_), channel_id=1, source_target_pairs={{0,1},{1,0},{2,3},{3,2},{4,5},{5,4},{6,7},{7,6},{8,9},{9,8},{10,11... | collective-permute-start | bytes 589832 | tf_op jit(solution)/shard_map/ppermute | solution.py:391
  15.4 4.6 %all-to-all-start = ((f32[8,16,128]{2,1,0:T(8,128)}), f32[8,16,128]{2,1,0:T(8,128)S(1)}, u32[]{:S(2)}, u32[]{:S(2)}) async-start(f32[8,16,128]{2,1,0:T(8,128)} %get-tuple-element.16), calls=%async_computation | async-start | bytes 131072 | tf_op jit(solution)/shard_map/all_to_all | solution.py:388
  20.6 6.3 %all-to-all-done.got_ref = f32[8,16,128]{2,1,0:T(8,128)S(1)} async-done(((f32[8,16,128]{2,1,0:T(8,128)}), f32[8,16,128]{2,1,0:T(8,128)S(1)}, u32[]{:S(2)}, u32[]{:S(2)}) %all-to-all-start) | async-done | bytes 65568 | tf_op jit(solution)/shard_map/all_to_all | solution.py:388
  26.9 1.7 %shard_map.168 = (f32[8,512]{1,0:T(8,128)S(1)}, s32[1,512]{1,0:T(1,128)S(1)}, f32[32,1,1152]{2,1,0:T(1,128)}) custom-call(f32[8,16,128]{2,1,0:T(8,128)S(1)} %all-to-all-done.got_ref, bf16[64,512]{1,0:T(8,128)(2,1)S(1)} %get-tuple-element.17.coarse_v_ref, s32[1]{0:T(128)S(6)} %copy.18.refs_0_.refs_2_, ...), custom_call_target="tpu_custom_call" | custom-call | flops 1000 | bytes 1000 | tf_op jit(solution)/shard_map/pallas_call | solution.py:344
  28.6 2.6 %all-to-all-start.1 = ((f32[32,1,1152]{2,1,0:T(1,128)}), f32[32,1,1152]{2,1,0:T(1,128)S(1)}, u32[]{:S(2)}, u32[]{:S(2)}) async-start(f32[32,1,1152]{2,1,0:T(1,128)} %get-tuple-element.25), calls=%async_computation.1 | async-start | bytes 294912 | tf_op jit(solution)/shard_map/all_to_all | solution.py:388
  31.2 0.0 collective-permute-done.2.came_ref.refs_1_
  31.2 7.8 %all-to-all-done.1.all_ref = f32[32,1,1152]{2,1,0:T(1,128)S(1)} async-done(((f32[32,1,1152]{2,1,0:T(1,128)}), f32[32,1,1152]{2,1,0:T(1,128)S(1)}, u32[]{:S(2)}, u32[]{:S(2)}) %all-to-all-start.1) | async-done | bytes 147488 | tf_op jit(solution)/shard_map/all_to_all | solution.py:388
  39.0 1.2 %shard_map.172 = f32[32,4,128]{2,1,0:T(4,128)S(1)} custom-call(f32[8,512]{1,0:T(8,128)S(1)} %get-tuple-element.23.state_ref, s32[1,512]{1,0:T(1,128)S(1)} %get-tuple-element.24.rows_ref, f32[32,1,1152]{2,1,0:T(1,128)S(1)} %all-to-all-done.1.all_ref, f32[16,128]{1,0:T(8,128)S(1)} %shard_map.171.complete_ref, ...), custom_call_target="tpu_custom_call" | custom-call | flops 1000 | bytes 1000 | tf_op jit(solution)/shard_map/pallas_call | solution.py:344
  40.2 9.7 %all_to_all.15.got_ref = f32[32,4,128]{2,1,0:T(4,128)S(1)} all-to-all(f32[32,4,128]{2,1,0:T(4,128)S(1)} %shard_map.172), channel_id=1, replica_groups=mesh['leaf'=4,'blk'=8] {'leaf','blk'}, dimensions={0} | all-to-all | bytes 131072 | tf_op jit(solution)/shard_map/all_to_all | solution.py:388
  49.9 1.3 %shard_map.173 = (f32[1,512]{1,0:T(1,128)}, f32[1,512]{1,0:T(1,128)}) custom-call(f32[32,4,128]{2,1,0:T(4,128)S(1)} %all_to_all.15.got_ref, s32[1,512]{1,0:T(1,128)S(1)} %get-tuple-element.26.refs_0_.slot_ref, s32[1,512]{1,0:T(1,128)S(1)} %get-tuple-element.27.slot_row_ref, bf16[192,512]{1,0:T(8,128)(2,1)S(1)} %shard_map.170.refs_0_, ...), custom_call_target="tpu_custom_call" | custom-call | flops 1000 | bytes 1000 | tf_op jit(solution)/shard_map/pallas_call | solution.py:344
  (3 shorter events, 0.0 us)
Async XLA Ops:
  0.6 8.0 %copy-start = (bf16[4,16,512]{2,1,0:T(8,128)(2,1)S(1)}, bf16[4,16,512]{2,1,0:T(8,128)(2,1)}, u32[]{:S(2)}) copy-start(bf16[4,16,512]{2,1,0:T(8,128)(2,1)} %param.30) | copy-start | bytes 196612
  0.6 8.0 %collective-permute-start = (bf16[64,512]{1,0:T(8,128)(2,1)}, bf16[64,512]{1,0:T(8,128)(2,1)S(1)}, u32[]{:S(2)}, u32[]{:S(2)}) collective-permute-start(bf16[64,512]{1,0:T(8,128)(2,1)} %bitcast.13), channel_id=1, source_target_pairs={{0,4},{1,5},{2,6},{3,7},{4,0},{5,1},{6,2},{7,3},{8,12},{9,13},{10,... | collective-permute-start | bytes 196616 | tf_op jit(solution)/shard_map/ppermute | solution.py:391
  8.6 5.0 %collective-permute-start.1 = (bf16[128,512]{1,0:T(8,128)(2,1)S(1)}, bf16[128,512]{1,0:T(8,128)(2,1)S(1)}, u32[]{:S(2)}, u32[]{:S(2)}) collective-permute-start(bf16[128,512]{1,0:T(8,128)(2,1)S(1)} %shard_map.169.held_ref), channel_id=1, source_target_pairs={{0,2},{1,3},{2,0},{3,1},{4,6},{5,7},{6,4},{7,5},{8,10},{9,11},{10,... | collective-permute-start | bytes 393224 | tf_op jit(solution)/shard_map/ppermute | solution.py:391
  13.7 17.5 %collective-permute-start.2 = (bf16[192,512]{1,0:T(8,128)(2,1)S(1)}, bf16[192,512]{1,0:T(8,128)(2,1)S(1)}, u32[]{:S(2)}, u32[]{:S(2)}) collective-permute-start(bf16[192,512]{1,0:T(8,128)(2,1)S(1)} %shard_map.170.refs_0_), channel_id=1, source_target_pairs={{0,1},{1,0},{2,3},{3,2},{4,5},{5,4},{6,7},{7,6},{8,9},{9,8},{10,11... | collective-permute-start | bytes 589832 | tf_op jit(solution)/shard_map/ppermute | solution.py:391
  15.4 11.5 %all-to-all-start = ((f32[8,16,128]{2,1,0:T(8,128)}), f32[8,16,128]{2,1,0:T(8,128)S(1)}, u32[]{:S(2)}, u32[]{:S(2)}) async-start(f32[8,16,128]{2,1,0:T(8,128)} %get-tuple-element.16), calls=%async_computation | async-start | bytes 131072 | tf_op jit(solution)/shard_map/all_to_all | solution.py:388
  28.6 10.4 %all-to-all-start.1 = ((f32[32,1,1152]{2,1,0:T(1,128)}), f32[32,1,1152]{2,1,0:T(1,128)S(1)}, u32[]{:S(2)}, u32[]{:S(2)}) async-start(f32[32,1,1152]{2,1,0:T(1,128)} %get-tuple-element.25), calls=%async_computation.1 | async-start | bytes 294912 | tf_op jit(solution)/shard_map/all_to_all | solution.py:388

commit v13 on v12

--- a/solution.py
+++ b/solution.py
@@ -17,6 +17,7 @@
 SMEM = pltpu.SMEM
 
 LANES = 128
+HALF = 64
 
 
 def dot(left, right, dims):
@@ -128,14 +129,19 @@
     for copy in copies[1:7]:
         copy.wait()
     u, phi, sigma, fric_a, fric_b, dist = (buf[...] for buf in elem_bufs[1:])
-    deficit = (PLATE_RATE - jnp.exp(u)).astype(jnp.bfloat16).astype(jnp.float32)
-    rows = [u, phi, sigma * fric_a, sigma * fric_b, dist, target_row.astype(jnp.float32), deficit]
+    velocity = jnp.exp(u)
+    deficit = (PLATE_RATE - velocity).astype(jnp.bfloat16).astype(jnp.float32)
+    sa = sigma * fric_a
+    factor = TIME_STEP / (sa + DAMPING * velocity)
+    rows = [u, phi, sa, sigma * fric_b, dist, target_row.astype(jnp.float32), deficit, factor]
     values = scattered(padded(rows, 8), slot)
     slot_row_ref[...] = values[5:6].astype(jnp.int32)
-    everyone = jnp.concatenate([as_lines(values[6:7]), as_lines(values[5:6])], axis=0)
+    everyone = jnp.concatenate([as_lines(values[i:i + 1]) for i in (6, 5, 7)], axis=0)
     for peer in range(members):
-        sent_ref[peer, 0:8, 0:peer_rows] = values[:, peer * peer_rows:(peer + 1) * peer_rows]
-        sent_ref[peer, 8:8 + 2 * pieces, :] = everyone
+        sent_ref[peer, 0:3 * pieces, :] = everyone
+        part = values[0:6, peer * peer_rows:(peer + 1) * peer_rows]
+        sent_ref[peer, 3 * pieces:3 * pieces + 4, 0:peer_rows] = part[0:4]
+        sent_ref[peer, 3 * pieces:3 * pieces + 2, HALF:HALF + peer_rows] = part[4:6]
 
     for copy in copies[7:10]:
         copy.wait()
@@ -233,62 +239,81 @@
 
 
 def place_kernel(got_ref, coarse_v_ref, *refs):
-    field_refs, state_ref, rows_ref, out_ref, lines_ref = refs[:6], refs[6], refs[7], refs[8], refs[9]
+    field_refs, state_ref, factor_ref, rows_ref, out_ref, lines_ref = refs[:6], *refs[6:]
     members = got_ref.shape[0]
     elem_count = state_ref.shape[1]
     pieces = elem_count // LANES
     peer_rows = elem_count // members
-    per_line = LANES // peer_rows
-    line_block = lax.broadcasted_iota(jnp.int32, (per_line * pieces, LANES), 0) // pieces
-    line_piece = lax.broadcasted_iota(jnp.int32, (per_line * pieces, LANES), 0) % pieces
-    lane_block = lax.broadcasted_iota(jnp.int32, (per_line * pieces, LANES), 1) // peer_rows
-    own_lane = line_block == lane_block
+    count = LANES // peer_rows * pieces
+    line_row = lax.broadcasted_iota(jnp.int32, (count, LANES), 0)
+    lane_block = lax.broadcasted_iota(jnp.int32, (count, LANES), 1) // peer_rows
+    own_lane = line_row // pieces == lane_block
     for line in range(pieces):
+        rows = got_ref[:, pieces + line, :].astype(jnp.int32)
+        parts = [got_ref[:, line, :]]
+        split = three_parts(got_ref[:, 2 * pieces + line, :])
+        parts += [split[i * members:(i + 1) * members] for i in range(3)]
         left, right = [], []
         for peer in range(members):
-            value = got_ref[peer, 8 + line:9 + line, :]
-            row = got_ref[peer, 8 + pieces + line:9 + pieces + line, :].astype(jnp.int32)
-            left.append(jnp.where(own_lane & (line_piece == row // LANES), value, 0.0))
+            row = rows[peer:peer + 1]
+            kept = own_lane & (line_row % pieces == row // LANES)
+            left.append(
+                jnp.concatenate([jnp.where(kept, part[peer:peer + 1], 0.0) for part in parts], axis=0)
+            )
             right.append(low_matrix(row))
         left = jnp.concatenate(left, axis=1).astype(jnp.bfloat16)
-        count = per_line * pieces
-        lines_ref[line * count:(line + 1) * count, :] = dot(left, jnp.concatenate(right, axis=1), NT)
-    deficits = jnp.concatenate(
-        [lines_ref[pl.ds(piece, members, stride=pieces), :] for piece in range(pieces)], axis=1
-    )
-    inside = inside_rows(deficits, *field_refs)
-
-    flat = peer_lanes(got_ref, 0, members, 8, elem_count)
-    rows = flat[5:6].astype(jnp.int32)
+        placed = dot(left, jnp.concatenate(right, axis=1), NT)
+        lines_ref[0, line * count:(line + 1) * count, :] = placed[0:count]
+        lines_ref[1, line * count:(line + 1) * count, :] = joined(placed[count:])
+
+    def blocks(number):
+        return jnp.concatenate(
+            [lines_ref[number, pl.ds(piece, members, stride=pieces), :] for piece in range(pieces)],
+            axis=1,
+        )
+
+    factor_ref[...] = blocks(1)
+    inside = inside_rows(blocks(0), *field_refs)
+
+    first = 3 * pieces
+    flat = jnp.concatenate(
+        [got_ref[peer, first:first + 4, 0:peer_rows] for peer in range(members)], axis=1
+    )
+    rest = jnp.concatenate(
+        [got_ref[peer, first:first + 2, HALF:HALF + peer_rows] for peer in range(members)], axis=1
+    )
+    rows = rest[1:2].astype(jnp.int32)
     rows_ref[...] = rows
-    state = scattered(flat, rows)
+    fields = [flat[i:i + 1] for i in range(4)] + [rest[0:1]]
+    state = scattered(padded(fields, 8), rows)
     u, phi, sa, sb, dist = (state[i:i + 1] for i in range(5))
     velocity = jnp.exp(u)
+    deficit = (PLATE_RATE - velocity).astype(jnp.bfloat16).astype(jnp.float32)
     k1p = (jnp.exp(-phi) - velocity) / dist
-    inverse = 1.0 / (sa + DAMPING * velocity)
-    u2 = u + TIME_STEP * ((inside - sb * k1p) * inverse)
-    factor = TIME_STEP * inverse
-    state_ref[...] = jnp.concatenate([u, phi, sa, sb, dist, k1p, u2, factor], axis=0)
-    sent = jnp.concatenate([u2, factor, partial_row(state[6:7], coarse_v_ref)], axis=1)
+    u2 = u + TIME_STEP * ((inside - sb * k1p) / (sa + DAMPING * velocity))
+    state_ref[...] = padded([u, phi, sa, sb, dist, k1p], 8)
+    sent = jnp.concatenate([u2, partial_row(deficit, coarse_v_ref)], axis=1)
     out_ref[...] = jnp.broadcast_to(sent[None], out_ref.shape)
 
 
-def second_kernel(groups, state_ref, rows_ref, all_ref, complete_ref, coarse_v_ref, *refs):
+def second_kernel(
+    groups, state_ref, factor_ref, rows_ref, all_ref, complete_ref, coarse_v_ref, *refs
+):
     bases_refs, field_refs, sent_ref = refs[:2], refs[2:8], refs[8]
     members, elem_count = refs[6].shape[1], state_ref.shape[1]
     width = coarse_v_ref.shape[0]
     mine, me = lax.axis_index("leaf"), lax.axis_index("blk")
     sums = [
         jnp.sum(
-            all_ref[group * members:(group + 1) * members, 0, 2 * elem_count:2 * elem_count + width],
+            all_ref[group * members:(group + 1) * members, 0, elem_count:elem_count + width],
             axis=0, keepdims=True,
         )
         for group in range(groups)
     ]
     weights = coefficients(sums, width // groups)
-    own = all_ref[pl.ds(mine * members, members), 0, 0:2 * elem_count]
+    own = all_ref[pl.ds(mine * members, members), 0, 0:elem_count]
     coarse = coarse_all(weights, members, bases_refs)
-    u2_all = own[:, 0:elem_count] + own[:, elem_count:] * coarse
+    u2_all = own + factor_ref[...] * coarse
     deficits = (PLATE_RATE - jnp.exp(u2_all)).astype(jnp.bfloat16).astype(jnp.float32)
     inside = inside_rows(deficits, *field_refs)
 
@@ -403,7 +428,7 @@
     sent, slot, slot_row, near_mask, far_mask, near, far_u, far_v, coarse_v = call(
         functools.partial(sort_kernel, members),
         (
-            shape(members, 8 + 2 * (elems // LANES), LANES),
+            shape(members, -(-(3 * (elems // LANES) + 4) // 8) * 8, LANES),
             shape(1, elems, dtype=integer),
             shape(1, elems, dtype=integer),
             shape(near_blocks.shape[0], members, leaf_size),
@@ -415,33 +440,34 @@
         + [SMEM(value.shape, value.dtype) for value in scalar_args]
         + [pltpu.SemaphoreType.DMA((14,))],
     )
+    fields = near_count, near, far_u, far_v, near_mask, far_mask
+    state, factor, rows, out = call(
+        place_kernel,
+        (
+            shape(8, elems),
+            shape(members, elems),
+            shape(1, elems, dtype=integer),
+            shape(devices, 1, elems + lines * LANES),
+        ),
+        swap(sent, "blk"), coarse_v, *fields, scalars=(2,),
+        scratch=[VMEM((2, members * (elems // LANES), LANES), jnp.float32)],
+    )
     bases = coarse_u.reshape(width, elems)
     for bit in range(members.bit_length() - 2, 0, -1):
         rows_out = 2 * bases.shape[0]
-        kernel = stack_kernel
+        kernel, after = stack_kernel, slot
         if bit == 1:
             rows_out = rows_out // groups * (groups - 1)
-            kernel = functools.partial(stack_foreign_kernel, groups, rank)
+            kernel, after = functools.partial(stack_foreign_kernel, groups, rank), rows
         bases = call(
             kernel, shape(rows_out, elems, dtype=jnp.bfloat16),
-            bases, partner(bases, bit), slot, flops=1 << 26, moved=1 << 22,
+            bases, partner(bases, bit), after, flops=1 << 26, moved=1 << 22,
         )
     bases = bases, partner(bases, 0)
     complete = call(mark_kernel, shape(16, LANES), bases[1], flops=1 << 34, moved=1 << 26)
-    fields = near_count, near, far_u, far_v, near_mask, far_mask
-    state, rows, out = call(
-        place_kernel,
-        (
-            shape(8, elems),
-            shape(1, elems, dtype=integer),
-            shape(devices, 1, 2 * elems + lines * LANES),
-        ),
-        swap(sent, "blk"), coarse_v, *fields, scalars=(2,),
-        scratch=[VMEM((members * (elems // LANES), LANES), jnp.float32)],
-    )
     sent = call(
         functools.partial(second_kernel, groups), shape(devices, sent_rows, LANES),
-        state, rows, swap(out, ("leaf", "blk")), complete, coarse_v, *bases, *fields, scalars=(7,),
+        state, factor, rows, swap(out, ("leaf", "blk")), complete, coarse_v, *bases, *fields, scalars=(8,),
     )
     u, phi = call(
         functools.partial(finish_kernel, groups, width), (shape(1, elems), shape(1, elems)),

time: 51.5 us -> 46.2 us (0.90)
  waiting for transfers between devices: 19.9 us -> 15.3 us
  blocking collectives: 9.7 us -> 8.96 us
    all_to_all x2, waiting for transfers between devices: 14.1 us -> 11.4 us  [swap(): return lax.all_to_all(value, axes, split_axis=0, concat_axis=0, tiled=True)]
    ppermute x3, waiting for transfers between devices: 5.87 us -> 3.89 us  [partner(): lax.ppermute(value, 'blk', [(i, i ^ 1 << bit) for i in range(members)])]
    ppermute x3, starting transfers between devices: 6.6 us -> 5.29 us  [partner(): lax.ppermute(value, 'blk', [(i, i ^ 1 << bit) for i in range(members)])]
    all_to_all x2, starting transfers between devices: 7.13 us -> 8.44 us  [swap(): return lax.all_to_all(value, axes, split_axis=0, concat_axis=0, tiled=True)]
    all_to_all x1, blocking collectives: 9.7 us -> 8.96 us  [swap(): return lax.all_to_all(value, axes, split_axis=0, concat_axis=0, tiled=True)]
  transfers between devices with their start and end apart: 5 -> 5, of which waited for: 4 -> 4; matrix products, arithmetic and copies ran while one was open for 0% -> 0% of each run, Pallas kernels for 8% -> 9%
where the time goes in v13:
time: 46.2 us; the launch traced here: 45.9 us
  waiting for transfers between devices  15.3 us (33%)
  starting transfers between devices  13.7 us (30%)
  blocking collectives  8.96 us (19%)
  Pallas kernels  6.61 us (14%)
  between operations  1.33 us (3%)
    all_to_all x2, waiting for transfers between devices, swap(): return lax.all_to_all(value, axes, split_axis=0, concat_axis=0, tiled=True)  11.4 us
    all_to_all x1, blocking collectives, swap(): return lax.all_to_all(value, axes, split_axis=0, concat_axis=0, tiled=True)  8.96 us
    all_to_all x2, starting transfers between devices, swap(): return lax.all_to_all(value, axes, split_axis=0, concat_axis=0, tiled=True)  8.44 us
    pallas_call x7, Pallas kernels, call(): pl.pallas_call(kernel, out_shape=outs, in_specs=[pl.BlockSpec(memory_spac...  6.61 us
    ppermute x3, starting transfers between devices, partner(): lax.ppermute(value, 'blk', [(i, i ^ 1 << bit) for i in range(members)])  5.29 us
    ppermute x3, waiting for transfers between devices, partner(): lax.ppermute(value, 'blk', [(i, i ^ 1 << bit) for i in range(members)])  3.89 us
  transfers between devices with their start and end apart: 5, of which 4 were waited for; matrix products, arithmetic and copies ran while one was open for 0% of the time, Pallas kernels for 9%

profile of v13, /device:TPU:0, one launch (start us, length us, event | category | flops | bytes accessed | tf_op | source)
XLA Modules:
  0.0 45.9 jit_solution(11784170221786827150)
XLA Ops:
  0.6 0.0 copy-start
  0.6 4.1 %collective-permute-start = (bf16[64,512]{1,0:T(8,128)(2,1)}, bf16[64,512]{1,0:T(8,128)(2,1)S(1)}, u32[]{:S(2)}, u32[]{:S(2)}) collective-permute-start(bf16[64,512]{1,0:T(8,128)(2,1)} %bitcast.13), channel_id=1, source_target_pairs={{0,4},{1,5},{2,6},{3,7},{4,0},{5,1},{6,2},{7,3},{8,12},{9,13},{10,... | collective-permute-start | bytes 196616 | tf_op jit(solution)/shard_map/ppermute | solution.py:416
  4.7 2.3 %shard_map.167 = (f32[8,16,128]{2,1,0:T(8,128)}, s32[1,512]{1,0:T(1,128)S(1)}, s32[1,512]{1,0:T(1,128)S(1)}, f32[3,8,512]{2,1,0:T(8,128)S(1)}, f32[8,64]{1,0:T(8...) custom-call(s32[1,512]{1,0:T(1,128)} %bitcast.18, ...), custom_call_target="tpu_custom_call" | custom-call | flops 1000 | bytes 1000 | tf_op jit(solution)/shard_map/pallas_call | solution.py:369
  7.0 1.6 %collective-permute-done.came_ref = bf16[64,512]{1,0:T(8,128)(2,1)S(1)} collective-permute-done((bf16[64,512]{1,0:T(8,128)(2,1)}, bf16[64,512]{1,0:T(8,128)(2,1)S(1)}, u32[]{:S(2)}, u32[]{:S(2)}) %collective-permute-start) | collective-permute-done | bytes 65568 | tf_op jit(solution)/shard_map/ppermute | solution.py:416
  8.6 0.0 copy-done
  8.6 0.7 %collective-permute-start.1 = (bf16[128,512]{1,0:T(8,128)(2,1)S(1)}, bf16[128,512]{1,0:T(8,128)(2,1)S(1)}, u32[]{:S(2)}, u32[]{:S(2)}) collective-permute-start(bf16[128,512]{1,0:T(8,128)(2,1)S(1)} %shard_map.169.held_ref), channel_id=1, source_target_pairs={{0,2},{1,3},{2,0},{3,1},{4,6},{5,7},{6,4},{7,5},{8,10},{9,11},{10,... | collective-permute-start | bytes 393224 | tf_op jit(solution)/shard_map/ppermute | solution.py:416
  9.4 5.5 %all-to-all-start = ((f32[8,16,128]{2,1,0:T(8,128)}), f32[8,16,128]{2,1,0:T(8,128)S(1)}, u32[]{:S(2)}, u32[]{:S(2)}) async-start(f32[8,16,128]{2,1,0:T(8,128)} %get-tuple-element.17), calls=%async_computation | async-start | bytes 131072 | tf_op jit(solution)/shard_map/all_to_all | solution.py:413
  15.5 6.3 %all-to-all-done.got_ref = f32[8,16,128]{2,1,0:T(8,128)S(1)} async-done(((f32[8,16,128]{2,1,0:T(8,128)}), f32[8,16,128]{2,1,0:T(8,128)S(1)}, u32[]{:S(2)}, u32[]{:S(2)}) %all-to-all-start) | async-done | bytes 65568 | tf_op jit(solution)/shard_map/all_to_all | solution.py:413
  21.7 1.8 %shard_map.168 = (f32[8,512]{1,0:T(8,128)S(1)}, f32[8,512]{1,0:T(8,128)S(1)}, s32[1,512]{1,0:T(1,128)S(1)}, f32[32,1,640]{2,1,0:T(1,128)}) custom-call(f32[8,16,128]{2,1,0:T(8,128)S(1)} %all-to-all-done.got_ref, bf16[64,512]{1,0:T(8,128)(2,1)S(1)} %get-tuple-element.18.coarse_v_ref, s32[1]{0:T(128)S(6)} %copy.18.refs_0_.refs_2_, ...), custom_call_target="tpu_custom_call" | custom-call | flops 1000 | bytes 1000 | tf_op jit(solution)/shard_map/pallas_call | solution.py:369
  23.6 0.0 collective-permute-done.1.came_ref
  23.6 0.5 collective-permute-start.2
  24.1 3.0 %all-to-all-start.1 = ((f32[32,1,640]{2,1,0:T(1,128)}), f32[32,1,640]{2,1,0:T(1,128)S(1)}, u32[]{:S(2)}, u32[]{:S(2)}) async-start(f32[32,1,640]{2,1,0:T(1,128)} %get-tuple-element.27), calls=%async_computation.1 | async-start | bytes 163840 | tf_op jit(solution)/shard_map/all_to_all | solution.py:413
  27.0 2.3 %collective-permute-done.2.came_ref.refs_1_ = bf16[192,512]{1,0:T(8,128)(2,1)S(1)} collective-permute-done((bf16[192,512]{1,0:T(8,128)(2,1)S(1)}, bf16[192,512]{1,0:T(8,128)(2,1)S(1)}, u32[]{:S(2)}, u32[]{:S(2)}) %collective-permute-start.2) | collective-permute-done | bytes 196640 | tf_op jit(solution)/shard_map/ppermute | solution.py:416
  29.4 5.1 %all-to-all-done.1.all_ref = f32[32,1,640]{2,1,0:T(1,128)S(1)} async-done(((f32[32,1,640]{2,1,0:T(1,128)}), f32[32,1,640]{2,1,0:T(1,128)S(1)}, u32[]{:S(2)}, u32[]{:S(2)}) %all-to-all-start.1) | async-done | bytes 81952 | tf_op jit(solution)/shard_map/all_to_all | solution.py:413
  34.5 1.2 %shard_map.172 = f32[32,4,128]{2,1,0:T(4,128)S(1)} custom-call(f32[8,512]{1,0:T(8,128)S(1)} %get-tuple-element.24.state_ref, f32[8,512]{1,0:T(8,128)S(1)} %get-tuple-element.25.factor_ref, s32[1,512]{1,0:T(1,128)S(1)} %get-tuple-element.26.refs_0_.rows_ref, f32[32,1,640]{2,1,0:T(1,128)S(1)} %all-to-all-done.1.all_ref, ...), custom_call_target="tpu_custom_call" | custom-call | flops 1000 | bytes 1000 | tf_op jit(solution)/shard_map/pallas_call | solution.py:369
  35.7 9.0 %all_to_all.15.got_ref = f32[32,4,128]{2,1,0:T(4,128)S(1)} all-to-all(f32[32,4,128]{2,1,0:T(4,128)S(1)} %shard_map.172), channel_id=1, replica_groups=mesh['leaf'=4,'blk'=8] {'leaf','blk'}, dimensions={0} | all-to-all | bytes 131072 | tf_op jit(solution)/shard_map/all_to_all | solution.py:413
  44.6 1.3 %shard_map.173 = (f32[1,512]{1,0:T(1,128)}, f32[1,512]{1,0:T(1,128)}) custom-call(f32[32,4,128]{2,1,0:T(4,128)S(1)} %all_to_all.15.got_ref, s32[1,512]{1,0:T(1,128)S(1)} %get-tuple-element.28.refs_0_.slot_ref, s32[1,512]{1,0:T(1,128)S(1)} %get-tuple-element.29.slot_row_ref, bf16[192,512]{1,0:T(8,128)(2,1)S(1)} %shard_map.170.refs_0_, ...), custom_call_target="tpu_custom_call" | custom-call | flops 1000 | bytes 1000 | tf_op jit(solution)/shard_map/pallas_call | solution.py:369
  (3 shorter events, 0.0 us)
Async XLA Ops:
  0.6 8.0 %copy-start = (bf16[4,16,512]{2,1,0:T(8,128)(2,1)S(1)}, bf16[4,16,512]{2,1,0:T(8,128)(2,1)}, u32[]{:S(2)}) copy-start(bf16[4,16,512]{2,1,0:T(8,128)(2,1)} %param.30) | copy-start | bytes 196612
  0.6 8.0 %collective-permute-start = (bf16[64,512]{1,0:T(8,128)(2,1)}, bf16[64,512]{1,0:T(8,128)(2,1)S(1)}, u32[]{:S(2)}, u32[]{:S(2)}) collective-permute-start(bf16[64,512]{1,0:T(8,128)(2,1)} %bitcast.13), channel_id=1, source_target_pairs={{0,4},{1,5},{2,6},{3,7},{4,0},{5,1},{6,2},{7,3},{8,12},{9,13},{10,... | collective-permute-start | bytes 196616 | tf_op jit(solution)/shard_map/ppermute | solution.py:416
  8.6 15.0 %collective-permute-start.1 = (bf16[128,512]{1,0:T(8,128)(2,1)S(1)}, bf16[128,512]{1,0:T(8,128)(2,1)S(1)}, u32[]{:S(2)}, u32[]{:S(2)}) collective-permute-start(bf16[128,512]{1,0:T(8,128)(2,1)S(1)} %shard_map.169.held_ref), channel_id=1, source_target_pairs={{0,2},{1,3},{2,0},{3,1},{4,6},{5,7},{6,4},{7,5},{8,10},{9,11},{10,... | collective-permute-start | bytes 393224 | tf_op jit(solution)/shard_map/ppermute | solution.py:416
  9.4 12.4 %all-to-all-start = ((f32[8,16,128]{2,1,0:T(8,128)}), f32[8,16,128]{2,1,0:T(8,128)S(1)}, u32[]{:S(2)}, u32[]{:S(2)}) async-start(f32[8,16,128]{2,1,0:T(8,128)} %get-tuple-element.17), calls=%async_computation | async-start | bytes 131072 | tf_op jit(solution)/shard_map/all_to_all | solution.py:413
  23.6 5.7 %collective-permute-start.2 = (bf16[192,512]{1,0:T(8,128)(2,1)S(1)}, bf16[192,512]{1,0:T(8,128)(2,1)S(1)}, u32[]{:S(2)}, u32[]{:S(2)}) collective-permute-start(bf16[192,512]{1,0:T(8,128)(2,1)S(1)} %shard_map.170.refs_0_), channel_id=1, source_target_pairs={{0,1},{1,0},{2,3},{3,2},{4,5},{5,4},{6,7},{7,6},{8,9},{9,8},{10,11... | collective-permute-start | bytes 589832 | tf_op jit(solution)/shard_map/ppermute | solution.py:416
  24.1 10.4 %all-to-all-start.1 = ((f32[32,1,640]{2,1,0:T(1,128)}), f32[32,1,640]{2,1,0:T(1,128)S(1)}, u32[]{:S(2)}, u32[]{:S(2)}) async-start(f32[32,1,640]{2,1,0:T(1,128)} %get-tuple-element.27), calls=%async_computation.1 | async-start | bytes 163840 | tf_op jit(solution)/shard_map/all_to_all | solution.py:413

commit v14 on v13

--- a/solution.py
+++ b/solution.py
@@ -451,6 +451,7 @@
         ),
         swap(sent, "blk"), coarse_v, *fields, scalars=(2,),
         scratch=[VMEM((2, members * (elems // LANES), LANES), jnp.float32)],
+        flops=1 << 33, moved=1 << 25,
     )
     bases = coarse_u.reshape(width, elems)
     for bit in range(members.bit_length() - 2, 0, -1):

time: 46.2 us -> 47 us (1.017)
  starting transfers between devices: 13.7 us -> 15.2 us
  waiting for transfers between devices: 15.3 us -> 14.5 us
    all_to_all x2, waiting for transfers between devices: 11.4 us -> 6.7 us  [swap(): return lax.all_to_all(value, axes, split_axis=0, concat_axis=0, tiled=True)]
    ppermute x3, waiting for transfers between devices: 3.89 us -> 7.81 us  [partner(): lax.ppermute(value, 'blk', [(i, i ^ 1 << bit) for i in range(members)])]
    all_to_all x2, starting transfers between devices: 8.44 us -> 10.8 us  [swap(): return lax.all_to_all(value, axes, split_axis=0, concat_axis=0, tiled=True)]
    ppermute x3, starting transfers between devices: 5.29 us -> 4.48 us  [partner(): lax.ppermute(value, 'blk', [(i, i ^ 1 << bit) for i in range(members)])]
  transfers between devices with their start and end apart: 5 -> 5, of which waited for: 4 -> 4; matrix products, arithmetic and copies ran while one was open for 0% -> 0% of each run, Pallas kernels for 9% -> 4%
where the time goes in v14:
time: 47 us; the launch traced here: 46.7 us
  starting transfers between devices  15.2 us (32%)
  waiting for transfers between devices  14.5 us (31%)
  blocking collectives  8.96 us (19%)
  Pallas kernels  6.65 us (14%)
  between operations  1.34 us (3%)
    all_to_all x2, starting transfers between devices, swap(): return lax.all_to_all(value, axes, split_axis=0, concat_axis=0, tiled=True)  10.8 us
    all_to_all x1, blocking collectives, swap(): return lax.all_to_all(value, axes, split_axis=0, concat_axis=0, tiled=True)  8.96 us
    ppermute x3, waiting for transfers between devices, partner(): lax.ppermute(value, 'blk', [(i, i ^ 1 << bit) for i in range(members)])  7.81 us
    all_to_all x2, waiting for transfers between devices, swap(): return lax.all_to_all(value, axes, split_axis=0, concat_axis=0, tiled=True)  6.7 us
    pallas_call x7, Pallas kernels, call(): pl.pallas_call(kernel, out_shape=outs, in_specs=[pl.BlockSpec(memory_spac...  6.65 us
    ppermute x3, starting transfers between devices, partner(): lax.ppermute(value, 'blk', [(i, i ^ 1 << bit) for i in range(members)])  4.48 us
  transfers between devices with their start and end apart: 5, of which 4 were waited for; matrix products, arithmetic and copies ran while one was open for 0% of the time, Pallas kernels for 4%

profile of v14, /device:TPU:0, one launch (start us, length us, event | category | flops | bytes accessed | tf_op | source)
XLA Modules:
  0.0 46.7 jit_solution(14013891024774247034)
XLA Ops:
  0.6 0.0 copy-start
  0.6 2.3 %shard_map.167 = (f32[8,16,128]{2,1,0:T(8,128)}, s32[1,512]{1,0:T(1,128)S(1)}, s32[1,512]{1,0:T(1,128)S(1)}, f32[3,8,512]{2,1,0:T(8,128)S(1)}, f32[8,64]{1,0:T(8...) custom-call(s32[1,512]{1,0:T(1,128)} %bitcast.18, ...), custom_call_target="tpu_custom_call" | custom-call | flops 1000 | bytes 1000 | tf_op jit(solution)/shard_map/pallas_call | solution.py:369
  3.0 7.3 %all-to-all-start = ((f32[8,16,128]{2,1,0:T(8,128)}), f32[8,16,128]{2,1,0:T(8,128)S(1)}, u32[]{:S(2)}, u32[]{:S(2)}) async-start(f32[8,16,128]{2,1,0:T(8,128)} %get-tuple-element.17), calls=%async_computation | async-start | bytes 131072 | tf_op jit(solution)/shard_map/all_to_all | solution.py:413
  10.2 0.0 copy-done
  10.2 2.9 %collective-permute-start = (bf16[64,512]{1,0:T(8,128)(2,1)S(1)}, bf16[64,512]{1,0:T(8,128)(2,1)S(1)}, u32[]{:S(2)}, u32[]{:S(2)}) collective-permute-start(bf16[64,512]{1,0:T(8,128)(2,1)S(1)} %bitcast.13), channel_id=1, source_target_pairs={{0,4},{1,5},{2,6},{3,7},{4,0},{5,1},{6,2},{7,3},{8,12},{9,13},{10,... | collective-permute-start | bytes 196616 | tf_op jit(solution)/shard_map/ppermute | solution.py:416
  13.8 4.0 %collective-permute-done.came_ref = bf16[64,512]{1,0:T(8,128)(2,1)S(1)} collective-permute-done((bf16[64,512]{1,0:T(8,128)(2,1)S(1)}, bf16[64,512]{1,0:T(8,128)(2,1)S(1)}, u32[]{:S(2)}, u32[]{:S(2)}) %collective-permute-start) | collective-permute-done | bytes 65568 | tf_op jit(solution)/shard_map/ppermute | solution.py:416
  17.8 0.1 collective-permute-start.1
  17.9 0.0 all-to-all-done.got_ref
  17.9 1.9 %shard_map.168 = (f32[8,512]{1,0:T(8,128)S(1)}, f32[8,512]{1,0:T(8,128)S(1)}, s32[1,512]{1,0:T(1,128)S(1)}, f32[32,1,640]{2,1,0:T(1,128)}) custom-call(f32[8,16,128]{2,1,0:T(8,128)S(1)} %all-to-all-done.got_ref, bf16[64,512]{1,0:T(8,128)(2,1)S(1)} %get-tuple-element.18.coarse_v_ref, s32[1]{0:T(128)S(6)} %copy.18.refs_0_.refs_2_, ...), custom_call_target="tpu_custom_call" | custom-call | flops 8589934592 | bytes 33554432 | tf_op jit(solution)/shard_map/pallas_call | solution.py:369
  19.7 3.1 %collective-permute-done.1.came_ref = bf16[128,512]{1,0:T(8,128)(2,1)S(1)} collective-permute-done((bf16[128,512]{1,0:T(8,128)(2,1)S(1)}, bf16[128,512]{1,0:T(8,128)(2,1)S(1)}, u32[]{:S(2)}, u32[]{:S(2)}) %collective-permute-start.1) | collective-permute-done | bytes 131104 | tf_op jit(solution)/shard_map/ppermute | solution.py:416
  22.9 1.5 %collective-permute-start.2 = (bf16[192,512]{1,0:T(8,128)(2,1)S(1)}, bf16[192,512]{1,0:T(8,128)(2,1)S(1)}, u32[]{:S(2)}, u32[]{:S(2)}) collective-permute-start(bf16[192,512]{1,0:T(8,128)(2,1)S(1)} %shard_map.170.refs_0_), channel_id=1, source_target_pairs={{0,1},{1,0},{2,3},{3,2},{4,5},{5,4},{6,7},{7,6},{8,9},{9,8},{10,11... | collective-permute-start | bytes 589832 | tf_op jit(solution)/shard_map/ppermute | solution.py:416
  24.3 3.5 %all-to-all-start.1 = ((f32[32,1,640]{2,1,0:T(1,128)}), f32[32,1,640]{2,1,0:T(1,128)S(1)}, u32[]{:S(2)}, u32[]{:S(2)}) async-start(f32[32,1,640]{2,1,0:T(1,128)} %get-tuple-element.27), calls=%async_computation.1 | async-start | bytes 163840 | tf_op jit(solution)/shard_map/all_to_all | solution.py:413
  27.8 0.7 %collective-permute-done.2.came_ref.refs_1_ = bf16[192,512]{1,0:T(8,128)(2,1)S(1)} collective-permute-done((bf16[192,512]{1,0:T(8,128)(2,1)S(1)}, bf16[192,512]{1,0:T(8,128)(2,1)S(1)}, u32[]{:S(2)}, u32[]{:S(2)}) %collective-permute-start.2) | collective-permute-done | bytes 196640 | tf_op jit(solution)/shard_map/ppermute | solution.py:416
  28.6 6.7 %all-to-all-done.1.all_ref = f32[32,1,640]{2,1,0:T(1,128)S(1)} async-done(((f32[32,1,640]{2,1,0:T(1,128)}), f32[32,1,640]{2,1,0:T(1,128)S(1)}, u32[]{:S(2)}, u32[]{:S(2)}) %all-to-all-start.1) | async-done | bytes 81952 | tf_op jit(solution)/shard_map/all_to_all | solution.py:413
  35.3 1.2 %shard_map.172 = f32[32,4,128]{2,1,0:T(4,128)S(1)} custom-call(f32[8,512]{1,0:T(8,128)S(1)} %get-tuple-element.24.state_ref, f32[8,512]{1,0:T(8,128)S(1)} %get-tuple-element.25.factor_ref, s32[1,512]{1,0:T(1,128)S(1)} %get-tuple-element.26.refs_0_.rows_ref, f32[32,1,640]{2,1,0:T(1,128)S(1)} %all-to-all-done.1.all_ref, ...), custom_call_target="tpu_custom_call" | custom-call | flops 1000 | bytes 1000 | tf_op jit(solution)/shard_map/pallas_call | solution.py:369
  36.5 9.0 %all_to_all.15.got_ref = f32[32,4,128]{2,1,0:T(4,128)S(1)} all-to-all(f32[32,4,128]{2,1,0:T(4,128)S(1)} %shard_map.172), channel_id=1, replica_groups=mesh['leaf'=4,'blk'=8] {'leaf','blk'}, dimensions={0} | all-to-all | bytes 131072 | tf_op jit(solution)/shard_map/all_to_all | solution.py:413
  45.4 1.3 %shard_map.173 = (f32[1,512]{1,0:T(1,128)}, f32[1,512]{1,0:T(1,128)}) custom-call(f32[32,4,128]{2,1,0:T(4,128)S(1)} %all_to_all.15.got_ref, s32[1,512]{1,0:T(1,128)S(1)} %get-tuple-element.28.refs_0_.slot_ref, s32[1,512]{1,0:T(1,128)S(1)} %get-tuple-element.29.slot_row_ref, bf16[192,512]{1,0:T(8,128)(2,1)S(1)} %shard_map.170.refs_0_, ...), custom_call_target="tpu_custom_call" | custom-call | flops 1000 | bytes 1000 | tf_op jit(solution)/shard_map/pallas_call | solution.py:369
  (3 shorter events, 0.0 us)
Async XLA Ops:
  0.6 9.6 %copy-start = (bf16[4,16,512]{2,1,0:T(8,128)(2,1)S(1)}, bf16[4,16,512]{2,1,0:T(8,128)(2,1)}, u32[]{:S(2)}) copy-start(bf16[4,16,512]{2,1,0:T(8,128)(2,1)} %param.30) | copy-start | bytes 196612
  3.0 14.9 %all-to-all-start = ((f32[8,16,128]{2,1,0:T(8,128)}), f32[8,16,128]{2,1,0:T(8,128)S(1)}, u32[]{:S(2)}, u32[]{:S(2)}) async-start(f32[8,16,128]{2,1,0:T(8,128)} %get-tuple-element.17), calls=%async_computation | async-start | bytes 131072 | tf_op jit(solution)/shard_map/all_to_all | solution.py:413
  10.2 7.5 %collective-permute-start = (bf16[64,512]{1,0:T(8,128)(2,1)S(1)}, bf16[64,512]{1,0:T(8,128)(2,1)S(1)}, u32[]{:S(2)}, u32[]{:S(2)}) collective-permute-start(bf16[64,512]{1,0:T(8,128)(2,1)S(1)} %bitcast.13), channel_id=1, source_target_pairs={{0,4},{1,5},{2,6},{3,7},{4,0},{5,1},{6,2},{7,3},{8,12},{9,13},{10,... | collective-permute-start | bytes 196616 | tf_op jit(solution)/shard_map/ppermute | solution.py:416
  17.8 5.0 %collective-permute-start.1 = (bf16[128,512]{1,0:T(8,128)(2,1)S(1)}, bf16[128,512]{1,0:T(8,128)(2,1)S(1)}, u32[]{:S(2)}, u32[]{:S(2)}) collective-permute-start(bf16[128,512]{1,0:T(8,128)(2,1)S(1)} %shard_map.169.held_ref), channel_id=1, source_target_pairs={{0,2},{1,3},{2,0},{3,1},{4,6},{5,7},{6,4},{7,5},{8,10},{9,11},{10,... | collective-permute-start | bytes 393224 | tf_op jit(solution)/shard_map/ppermute | solution.py:416
  22.9 5.7 %collective-permute-start.2 = (bf16[192,512]{1,0:T(8,128)(2,1)S(1)}, bf16[192,512]{1,0:T(8,128)(2,1)S(1)}, u32[]{:S(2)}, u32[]{:S(2)}) collective-permute-start(bf16[192,512]{1,0:T(8,128)(2,1)S(1)} %shard_map.170.refs_0_), channel_id=1, source_target_pairs={{0,1},{1,0},{2,3},{3,2},{4,5},{5,4},{6,7},{7,6},{8,9},{9,8},{10,11... | collective-permute-start | bytes 589832 | tf_op jit(solution)/shard_map/ppermute | solution.py:416
  24.3 10.9 %all-to-all-start.1 = ((f32[32,1,640]{2,1,0:T(1,128)}), f32[32,1,640]{2,1,0:T(1,128)S(1)}, u32[]{:S(2)}, u32[]{:S(2)}) async-start(f32[32,1,640]{2,1,0:T(1,128)} %get-tuple-element.27), calls=%async_computation.1 | async-start | bytes 163840 | tf_op jit(solution)/shard_map/all_to_all | solution.py:413

commit v15 on v14

--- a/solution.py
+++ b/solution.py
@@ -462,7 +462,7 @@
             kernel, after = functools.partial(stack_foreign_kernel, groups, rank), rows
         bases = call(
             kernel, shape(rows_out, elems, dtype=jnp.bfloat16),
-            bases, partner(bases, bit), after, flops=1 << 26, moved=1 << 22,
+            bases, partner(bases, bit), after, flops=1 << 34, moved=1 << 26,
         )
     bases = bases, partner(bases, 0)
     complete = call(mark_kernel, shape(16, LANES), bases[1], flops=1 << 34, moved=1 << 26)

time: 47 us -> 42.6 us (0.906)
  waiting for transfers between devices: 14.5 us -> 12 us
  starting transfers between devices: 15.2 us -> 13.4 us
    ppermute x3, waiting for transfers between devices: 7.81 us -> 2.32 us  [partner(): lax.ppermute(value, 'blk', [(i, i ^ 1 << bit) for i in range(members)])]
    all_to_all x2, starting transfers between devices: 10.8 us -> 6.93 us  [swap(): return lax.all_to_all(value, axes, split_axis=0, concat_axis=0, tiled=True)]
    all_to_all x2, waiting for transfers between devices: 6.7 us -> 9.66 us  [swap(): return lax.all_to_all(value, axes, split_axis=0, concat_axis=0, tiled=True)]
    ppermute x3, starting transfers between devices: 4.48 us -> 6.47 us  [partner(): lax.ppermute(value, 'blk', [(i, i ^ 1 << bit) for i in range(members)])]
  transfers between devices with their start and end apart: 5 -> 5, of which waited for: 4 -> 3; matrix products, arithmetic and copies ran while one was open for 0% -> 0% of each run, Pallas kernels for 4% -> 10%
where the time goes in v15:
time: 42.6 us; the launch traced here: 42.3 us
  starting transfers between devices  13.4 us (31%)
  waiting for transfers between devices  12 us (28%)
  blocking collectives  8.96 us (21%)
  Pallas kernels  6.61 us (16%)
  between operations  1.34 us (3%)
    all_to_all x2, waiting for transfers between devices, swap(): return lax.all_to_all(value, axes, split_axis=0, concat_axis=0, tiled=True)  9.66 us
    all_to_all x1, blocking collectives, swap(): return lax.all_to_all(value, axes, split_axis=0, concat_axis=0, tiled=True)  8.96 us
    all_to_all x2, starting transfers between devices, swap(): return lax.all_to_all(value, axes, split_axis=0, concat_axis=0, tiled=True)  6.93 us
    pallas_call x7, Pallas kernels, call(): pl.pallas_call(kernel, out_shape=outs, in_specs=[pl.BlockSpec(memory_spac...  6.61 us
    ppermute x3, starting transfers between devices, partner(): lax.ppermute(value, 'blk', [(i, i ^ 1 << bit) for i in range(members)])  6.47 us
    ppermute x3, waiting for transfers between devices, partner(): lax.ppermute(value, 'blk', [(i, i ^ 1 << bit) for i in range(members)])  2.32 us
  transfers between devices with their start and end apart: 5, of which 3 were waited for; matrix products, arithmetic and copies ran while one was open for 0% of the time, Pallas kernels for 10%

profile of v15, /device:TPU:0, one launch (start us, length us, event | category | flops | bytes accessed | tf_op | source)
XLA Modules:
  0.0 42.3 jit_solution(17467578510038614094)
XLA Ops:
  0.6 0.0 copy-start
  0.6 4.1 %collective-permute-start = (bf16[64,512]{1,0:T(8,128)(2,1)}, bf16[64,512]{1,0:T(8,128)(2,1)S(1)}, u32[]{:S(2)}, u32[]{:S(2)}) collective-permute-start(bf16[64,512]{1,0:T(8,128)(2,1)} %bitcast.13), channel_id=1, source_target_pairs={{0,4},{1,5},{2,6},{3,7},{4,0},{5,1},{6,2},{7,3},{8,12},{9,13},{10,... | collective-permute-start | bytes 196616 | tf_op jit(solution)/shard_map/ppermute | solution.py:416
  4.7 2.3 %shard_map.167 = (f32[8,16,128]{2,1,0:T(8,128)}, s32[1,512]{1,0:T(1,128)S(1)}, s32[1,512]{1,0:T(1,128)S(1)}, f32[3,8,512]{2,1,0:T(8,128)S(1)}, f32[8,64]{1,0:T(8...) custom-call(s32[1,512]{1,0:T(1,128)} %bitcast.18, ...), custom_call_target="tpu_custom_call" | custom-call | flops 1000 | bytes 1000 | tf_op jit(solution)/shard_map/pallas_call | solution.py:369
  7.0 3.8 %all-to-all-start = ((f32[8,16,128]{2,1,0:T(8,128)}), f32[8,16,128]{2,1,0:T(8,128)S(1)}, u32[]{:S(2)}, u32[]{:S(2)}) async-start(f32[8,16,128]{2,1,0:T(8,128)} %get-tuple-element.17), calls=%async_computation | async-start | bytes 131072 | tf_op jit(solution)/shard_map/all_to_all | solution.py:413
  11.5 0.0 collective-permute-done.came_ref
  11.5 0.0 copy-done
  11.5 2.1 %collective-permute-start.1 = (bf16[128,512]{1,0:T(8,128)(2,1)S(1)}, bf16[128,512]{1,0:T(8,128)(2,1)S(1)}, u32[]{:S(2)}, u32[]{:S(2)}) collective-permute-start(bf16[128,512]{1,0:T(8,128)(2,1)S(1)} %shard_map.169.held_ref), channel_id=1, source_target_pairs={{0,2},{1,3},{2,0},{3,1},{4,6},{5,7},{6,4},{7,5},{8,10},{9,11},{10,... | collective-permute-start | bytes 393224 | tf_op jit(solution)/shard_map/ppermute | solution.py:416
  13.6 4.5 %all-to-all-done.got_ref = f32[8,16,128]{2,1,0:T(8,128)S(1)} async-done(((f32[8,16,128]{2,1,0:T(8,128)}), f32[8,16,128]{2,1,0:T(8,128)S(1)}, u32[]{:S(2)}, u32[]{:S(2)}) %all-to-all-start) | async-done | bytes 65568 | tf_op jit(solution)/shard_map/all_to_all | solution.py:413
  18.1 1.9 %shard_map.168 = (f32[8,512]{1,0:T(8,128)S(1)}, f32[8,512]{1,0:T(8,128)S(1)}, s32[1,512]{1,0:T(1,128)S(1)}, f32[32,1,640]{2,1,0:T(1,128)}) custom-call(f32[8,16,128]{2,1,0:T(8,128)S(1)} %all-to-all-done.got_ref, bf16[64,512]{1,0:T(8,128)(2,1)S(1)} %get-tuple-element.18.coarse_v_ref, s32[1]{0:T(128)S(6)} %copy.18.refs_0_.refs_2_, ...), custom_call_target="tpu_custom_call" | custom-call | flops 8589934592 | bytes 33554432 | tf_op jit(solution)/shard_map/pallas_call | solution.py:369
  20.0 0.0 collective-permute-done.1.came_ref
  20.0 0.3 collective-permute-start.2
  20.3 3.1 %all-to-all-start.1 = ((f32[32,1,640]{2,1,0:T(1,128)}), f32[32,1,640]{2,1,0:T(1,128)S(1)}, u32[]{:S(2)}, u32[]{:S(2)}) async-start(f32[32,1,640]{2,1,0:T(1,128)} %get-tuple-element.27), calls=%async_computation.1 | async-start | bytes 163840 | tf_op jit(solution)/shard_map/all_to_all | solution.py:413
  23.4 2.3 %collective-permute-done.2.came_ref.refs_1_ = bf16[192,512]{1,0:T(8,128)(2,1)S(1)} collective-permute-done((bf16[192,512]{1,0:T(8,128)(2,1)S(1)}, bf16[192,512]{1,0:T(8,128)(2,1)S(1)}, u32[]{:S(2)}, u32[]{:S(2)}) %collective-permute-start.2) | collective-permute-done | bytes 196640 | tf_op jit(solution)/shard_map/ppermute | solution.py:416
  25.8 5.1 %all-to-all-done.1.all_ref = f32[32,1,640]{2,1,0:T(1,128)S(1)} async-done(((f32[32,1,640]{2,1,0:T(1,128)}), f32[32,1,640]{2,1,0:T(1,128)S(1)}, u32[]{:S(2)}, u32[]{:S(2)}) %all-to-all-start.1) | async-done | bytes 81952 | tf_op jit(solution)/shard_map/all_to_all | solution.py:413
  30.9 1.2 %shard_map.172 = f32[32,4,128]{2,1,0:T(4,128)S(1)} custom-call(f32[8,512]{1,0:T(8,128)S(1)} %get-tuple-element.24.state_ref, f32[8,512]{1,0:T(8,128)S(1)} %get-tuple-element.25.factor_ref, s32[1,512]{1,0:T(1,128)S(1)} %get-tuple-element.26.refs_0_.rows_ref, f32[32,1,640]{2,1,0:T(1,128)S(1)} %all-to-all-done.1.all_ref, ...), custom_call_target="tpu_custom_call" | custom-call | flops 1000 | bytes 1000 | tf_op jit(solution)/shard_map/pallas_call | solution.py:369
  32.1 9.0 %all_to_all.15.got_ref = f32[32,4,128]{2,1,0:T(4,128)S(1)} all-to-all(f32[32,4,128]{2,1,0:T(4,128)S(1)} %shard_map.172), channel_id=1, replica_groups=mesh['leaf'=4,'blk'=8] {'leaf','blk'}, dimensions={0} | all-to-all | bytes 131072 | tf_op jit(solution)/shard_map/all_to_all | solution.py:413
  41.0 1.3 %shard_map.173 = (f32[1,512]{1,0:T(1,128)}, f32[1,512]{1,0:T(1,128)}) custom-call(f32[32,4,128]{2,1,0:T(4,128)S(1)} %all_to_all.15.got_ref, s32[1,512]{1,0:T(1,128)S(1)} %get-tuple-element.28.refs_0_.slot_ref, s32[1,512]{1,0:T(1,128)S(1)} %get-tuple-element.29.slot_row_ref, bf16[192,512]{1,0:T(8,128)(2,1)S(1)} %shard_map.170.refs_0_, ...), custom_call_target="tpu_custom_call" | custom-call | flops 1000 | bytes 1000 | tf_op jit(solution)/shard_map/pallas_call | solution.py:369
  (3 shorter events, 0.0 us)
Async XLA Ops:
  0.6 10.9 %copy-start = (bf16[4,16,512]{2,1,0:T(8,128)(2,1)S(1)}, bf16[4,16,512]{2,1,0:T(8,128)(2,1)}, u32[]{:S(2)}) copy-start(bf16[4,16,512]{2,1,0:T(8,128)(2,1)} %param.30) | copy-start | bytes 196612
  0.6 10.8 %collective-permute-start = (bf16[64,512]{1,0:T(8,128)(2,1)}, bf16[64,512]{1,0:T(8,128)(2,1)S(1)}, u32[]{:S(2)}, u32[]{:S(2)}) collective-permute-start(bf16[64,512]{1,0:T(8,128)(2,1)} %bitcast.13), channel_id=1, source_target_pairs={{0,4},{1,5},{2,6},{3,7},{4,0},{5,1},{6,2},{7,3},{8,12},{9,13},{10,... | collective-permute-start | bytes 196616 | tf_op jit(solution)/shard_map/ppermute | solution.py:416
  7.0 11.1 %all-to-all-start = ((f32[8,16,128]{2,1,0:T(8,128)}), f32[8,16,128]{2,1,0:T(8,128)S(1)}, u32[]{:S(2)}, u32[]{:S(2)}) async-start(f32[8,16,128]{2,1,0:T(8,128)} %get-tuple-element.17), calls=%async_computation | async-start | bytes 131072 | tf_op jit(solution)/shard_map/all_to_all | solution.py:413
  11.5 8.5 %collective-permute-start.1 = (bf16[128,512]{1,0:T(8,128)(2,1)S(1)}, bf16[128,512]{1,0:T(8,128)(2,1)S(1)}, u32[]{:S(2)}, u32[]{:S(2)}) collective-permute-start(bf16[128,512]{1,0:T(8,128)(2,1)S(1)} %shard_map.169.held_ref), channel_id=1, source_target_pairs={{0,2},{1,3},{2,0},{3,1},{4,6},{5,7},{6,4},{7,5},{8,10},{9,11},{10,... | collective-permute-start | bytes 393224 | tf_op jit(solution)/shard_map/ppermute | solution.py:416
  20.0 5.7 %collective-permute-start.2 = (bf16[192,512]{1,0:T(8,128)(2,1)S(1)}, bf16[192,512]{1,0:T(8,128)(2,1)S(1)}, u32[]{:S(2)}, u32[]{:S(2)}) collective-permute-start(bf16[192,512]{1,0:T(8,128)(2,1)S(1)} %shard_map.170.refs_0_), channel_id=1, source_target_pairs={{0,1},{1,0},{2,3},{3,2},{4,5},{5,4},{6,7},{7,6},{8,9},{9,8},{10,11... | collective-permute-start | bytes 589832 | tf_op jit(solution)/shard_map/ppermute | solution.py:416
  20.3 10.6 %all-to-all-start.1 = ((f32[32,1,640]{2,1,0:T(1,128)}), f32[32,1,640]{2,1,0:T(1,128)S(1)}, u32[]{:S(2)}, u32[]{:S(2)}) async-start(f32[32,1,640]{2,1,0:T(1,128)} %get-tuple-element.27), calls=%async_computation.1 | async-start | bytes 163840 | tf_op jit(solution)/shard_map/all_to_all | solution.py:413

commit v16 on v15

--- a/solution.py
+++ b/solution.py
@@ -97,12 +97,9 @@
 
 
 def sort_kernel(members, *refs):
-    elem_refs, scalar_refs, weight_refs = refs[:7], refs[7:10], refs[10:14]
-    sent_ref, slot_ref, slot_row_ref, near_mask_ref, far_mask_ref = refs[14:19]
-    weight_outs, elem_bufs, scalar_bufs, sems = refs[19:23], refs[23:30], refs[30:33], refs[33]
-    copies = start_copies(
-        [*elem_refs, *scalar_refs, *weight_refs], [*elem_bufs, *scalar_bufs, *weight_outs], sems
-    )
+    elem_refs, sent_ref, slot_ref, elem_row_ref = refs[:7], refs[7], refs[8], refs[9]
+    elem_bufs, sems = refs[10:17], refs[17]
+    copies = start_copies(elem_refs, elem_bufs, sems)
     mine = lax.axis_index("leaf")
     elem_count = elem_bufs[0].shape[1]
     peer_rows = elem_count // members
@@ -126,7 +123,8 @@
         passed = passed + jnp.sum(line, axis=1, keepdims=True)
     slot = target * peer_rows + jnp.concatenate(ranks, axis=1).astype(jnp.int32)
     slot_ref[...] = slot
-    for copy in copies[1:7]:
+    elem_row_ref[...] = target_row
+    for copy in copies[1:]:
         copy.wait()
     u, phi, sigma, fric_a, fric_b, dist = (buf[...] for buf in elem_bufs[1:])
     velocity = jnp.exp(u)
@@ -135,7 +133,6 @@
     factor = TIME_STEP / (sa + DAMPING * velocity)
     rows = [u, phi, sa, sigma * fric_b, dist, target_row.astype(jnp.float32), deficit, factor]
     values = scattered(padded(rows, 8), slot)
-    slot_row_ref[...] = values[5:6].astype(jnp.int32)
     everyone = jnp.concatenate([as_lines(values[i:i + 1]) for i in (6, 5, 7)], axis=0)
     for peer in range(members):
         sent_ref[peer, 0:3 * pieces, :] = everyone
@@ -143,7 +140,12 @@
         sent_ref[peer, 3 * pieces:3 * pieces + 4, 0:peer_rows] = part[0:4]
         sent_ref[peer, 3 * pieces:3 * pieces + 2, HALF:HALF + peer_rows] = part[4:6]
 
-    for copy in copies[7:10]:
+
+def load_kernel(*refs):
+    scalar_refs, weight_refs, near_mask_ref, far_mask_ref = refs[:3], refs[3:7], refs[7], refs[8]
+    weight_outs, scalar_bufs, sems = refs[9:13], refs[13:16], refs[16]
+    copies = start_copies([*scalar_refs, *weight_refs], [*scalar_bufs, *weight_outs], sems)
+    for copy in copies[:3]:
         copy.wait()
     near_col, far_col, far_rank = scalar_bufs
     far_slots = far_col.shape[0]
@@ -159,7 +161,7 @@
         kept = (lane >= low) & (lane < low + far_rank[number])
         column = jnp.where(kept, far_col[number], column)
     far_mask_ref[...] = jnp.where(block == column, 1.0, 0.0)
-    for copy in copies[10:]:
+    for copy in copies[3:]:
         copy.wait()
 
 
@@ -206,9 +208,7 @@
     for number, ref in enumerate(bases_refs):
         left = []
         for place in range(members // 2):
-            source = number
-            for bit in range(bits - 1):
-                source |= (place >> bit & 1) << (bits - 1 - bit)
+            source = relative_member(place, number, bits)
             left.append(jnp.where(row == source, weights, 0.0))
         left = jnp.concatenate(left, axis=1).astype(jnp.bfloat16)
         total = total + dot(left, ref[...], NN)
@@ -224,18 +224,40 @@
 
 def stack_foreign_kernel(groups, rank, held_ref, came_ref, *refs):
     out_ref = refs[-1]
-    width = groups * rank
     mine = lax.axis_index("leaf")
     place = 0
     for ref in (held_ref, came_ref):
-        for low in range(0, ref.shape[0], width):
-            for shift in range(1, groups):
-                out_ref[place:place + rank, :] = ref[pl.ds(low + (mine ^ shift) * rank, rank), :]
-                place += rank
-
-
-def mark_kernel(came_ref, out_ref):
-    out_ref[...] = came_ref[0:16, 0:LANES].astype(jnp.float32)
+        for shift in range(1, groups):
+            out_ref[place:place + rank, :] = ref[pl.ds((mine ^ shift) * rank, rank), :]
+            place += rank
+
+
+def relative_member(place, number, bits):
+    for bit in range(bits - 1):
+        number |= (place >> bit & 1) << (bits - 1 - bit)
+    return number
+
+
+def element_kernel(members, held_ref, came_ref, slot_ref, elem_row_ref, out_ref):
+    slot, row = slot_ref[...], elem_row_ref[...]
+    elem_count = row.shape[1]
+    kept = out_ref.shape[0]
+    pieces = elem_count // LANES
+    owner = (slot // (elem_count // members)) ^ lax.axis_index("blk")
+    low, high = low_matrix(row), row // LANES
+    total = jnp.zeros(out_ref.shape, jnp.float32)
+    for number, ref in enumerate((held_ref, came_ref)):
+        for place in range(members // 2):
+            part = ref[place * kept:(place + 1) * kept, :]
+            left = jnp.concatenate(
+                [part[:, piece * LANES:(piece + 1) * LANES] for piece in range(pieces)], axis=0
+            )
+            found = dot(left, low, NN)
+            ours = owner == relative_member(place, number, members.bit_length() - 1)
+            for piece in range(pieces):
+                here = ours & (high == piece)
+                total = jnp.where(here, found[piece * kept:(piece + 1) * kept], total)
+    out_ref[...] = total.astype(jnp.bfloat16)
 
 
 def place_kernel(got_ref, coarse_v_ref, *refs):
@@ -297,7 +319,7 @@
 
 
 def second_kernel(
-    groups, state_ref, factor_ref, rows_ref, all_ref, complete_ref, coarse_v_ref, *refs
+    groups, state_ref, factor_ref, rows_ref, all_ref, elem_bases_ref, coarse_v_ref, *refs
 ):
     bases_refs, field_refs, sent_ref = refs[:2], refs[2:8], refs[8]
     members, elem_count = refs[6].shape[1], state_ref.shape[1]
@@ -337,27 +359,22 @@
         sent_ref[device, 3:3 + partial.shape[0], :] = partial
 
 
-def finish_kernel(groups, width, got_ref, slot_ref, slot_row_ref, *refs):
-    bases_refs, u_ref, phi_ref = refs[:2], refs[2], refs[3]
+def finish_kernel(groups, width, got_ref, slot_ref, elem_bases_ref, u_ref, phi_ref):
     elem_count = slot_ref.shape[1]
     members = got_ref.shape[0] // groups
+    first = lax.axis_index("leaf") * members
+    flat = peer_lanes(got_ref, first, members, 3, elem_count)
+    out = gathered(padded([flat[i:i + 1] for i in range(3)], 8), slot_ref[...])
     sums = []
     for group in range(groups):
         total = jnp.sum(got_ref[group * members:(group + 1) * members], axis=0)
         lines = [total[3 + i:4 + i, :] for i in range(pl.cdiv(width, LANES))]
         sums.append(jnp.concatenate(lines, axis=1)[:, 0:width])
-    coarse = coarse_all(coefficients(sums, width // groups), members, bases_refs)
-    row = slot_row_ref[...]
-    block = lax.broadcasted_iota(jnp.int32, (members, elem_count), 0)
-    lane_block = lax.broadcasted_iota(jnp.int32, (members, elem_count), 1) // (elem_count // members)
-    rows = gathered(coarse, row)
-    found = jnp.sum(jnp.where(block == lane_block, rows, 0.0), axis=0, keepdims=True)
-    first = lax.axis_index("leaf") * members
-    flat = peer_lanes(got_ref, first, members, 3, elem_count)
-    u_next = flat[0:1] + flat[1:2] * found
-    out = gathered(padded([u_next, flat[2:3]], 8), slot_ref[...])
-    u_ref[...] = out[0:1]
-    phi_ref[...] = out[1:2]
+    weights = coefficients(sums, width // groups)
+    weights = jnp.broadcast_to(weights, (8, weights.shape[1])).astype(jnp.bfloat16)
+    coarse = dot(weights, elem_bases_ref[...], NN)[0:1]
+    u_ref[...] = out[0:1] + out[1:2] * coarse
+    phi_ref[...] = out[2:3]
 
 
 def call(kernel, outs, *args, scalars=(), far=(), scratch=(), flops=1000, moved=1000):
@@ -425,20 +442,28 @@
         coarse_v.reshape(width, elems),
     ]
     far_rows = weights[1].shape[0]
-    sent, slot, slot_row, near_mask, far_mask, near, far_u, far_v, coarse_v = call(
+    sent, slot, elem_row = call(
         functools.partial(sort_kernel, members),
         (
             shape(members, -(-(3 * (elems // LANES) + 4) // 8) * 8, LANES),
             shape(1, elems, dtype=integer),
             shape(1, elems, dtype=integer),
+        ),
+        *elem_args, far=range(7),
+        scratch=[VMEM(value.shape, value.dtype) for value in elem_args]
+        + [pltpu.SemaphoreType.DMA((7,))],
+    )
+    near_mask, far_mask, near, far_u, far_v, coarse_v = call(
+        load_kernel,
+        (
             shape(near_blocks.shape[0], members, leaf_size),
             shape(members, far_rows),
             *[shape(*value.shape, dtype=jnp.bfloat16) for value in weights],
         ),
-        *elem_args, *scalar_args, *weights, far=range(14),
-        scratch=[VMEM(value.shape, value.dtype) for value in elem_args]
-        + [SMEM(value.shape, value.dtype) for value in scalar_args]
-        + [pltpu.SemaphoreType.DMA((14,))],
+        *scalar_args, *weights, far=range(7),
+        scratch=[SMEM(value.shape, value.dtype) for value in scalar_args]
+        + [pltpu.SemaphoreType.DMA((7,))],
+        flops=1 << 30, moved=1 << 22,
     )
     fields = near_count, near, far_u, far_v, near_mask, far_mask
     state, factor, rows, out = call(
@@ -454,25 +479,28 @@
         flops=1 << 33, moved=1 << 25,
     )
     bases = coarse_u.reshape(width, elems)
-    for bit in range(members.bit_length() - 2, 0, -1):
-        rows_out = 2 * bases.shape[0]
-        kernel, after = stack_kernel, slot
-        if bit == 1:
-            rows_out = rows_out // groups * (groups - 1)
-            kernel, after = functools.partial(stack_foreign_kernel, groups, rank), rows
+    top = members.bit_length() - 2
+    for bit in range(top, 0, -1):
+        kernel, rows_out = stack_kernel, 2 * bases.shape[0]
+        if bit == top:
+            kernel = functools.partial(stack_foreign_kernel, groups, rank)
+            rows_out = 2 * (width - rank)
         bases = call(
             kernel, shape(rows_out, elems, dtype=jnp.bfloat16),
-            bases, partner(bases, bit), after, flops=1 << 34, moved=1 << 26,
+            bases, partner(bases, bit), slot if bit == top else rows, flops=1 << 34, moved=1 << 26,
         )
     bases = bases, partner(bases, 0)
-    complete = call(mark_kernel, shape(16, LANES), bases[1], flops=1 << 34, moved=1 << 26)
+    elem_bases = call(
+        functools.partial(element_kernel, members), shape(width - rank, elems, dtype=jnp.bfloat16),
+        *bases, slot, elem_row, flops=1 << 34, moved=1 << 26,
+    )
     sent = call(
         functools.partial(second_kernel, groups), shape(devices, sent_rows, LANES),
-        state, factor, rows, swap(out, ("leaf", "blk")), complete, coarse_v, *bases, *fields, scalars=(8,),
+        state, factor, rows, swap(out, ("leaf", "blk")), elem_bases, coarse_v, *bases, *fields, scalars=(8,),
     )
     u, phi = call(
         functools.partial(finish_kernel, groups, width), (shape(1, elems), shape(1, elems)),
-        swap(sent, ("leaf", "blk")), slot, slot_row, *bases,
+        swap(sent, ("leaf", "blk")), slot, elem_bases,
     )
     return u.reshape(elems), phi.reshape(elems)
 

time: 42.6 us -> 46 us (1.080)
  starting transfers between devices: 13.4 us -> 15.5 us
  Pallas kernels: 6.61 us -> 7.9 us
    all_to_all x2, starting transfers between devices: 6.93 us -> 11 us  [swap(): return lax.all_to_all(value, axes, split_axis=0, concat_axis=0, tiled=True)]
    ppermute x3, waiting for transfers between devices: 2.32 us -> 5.72 us  [partner(): lax.ppermute(value, 'blk', [(i, i ^ 1 << bit) for i in range(members)])]
    all_to_all x2, waiting for transfers between devices: 9.66 us -> 6.32 us  [swap(): return lax.all_to_all(value, axes, split_axis=0, concat_axis=0, tiled=True)]
    ppermute x3, starting transfers between devices: 6.47 us -> 4.48 us  [partner(): lax.ppermute(value, 'blk', [(i, i ^ 1 << bit) for i in range(members)])]
    pallas_call x7 -> x8, Pallas kernels: 6.61 us -> 7.9 us  [call(): pl.pallas_call(kernel, out_shape=outs, in_specs=[pl.BlockSpec(memory_spac...]
  transfers between devices with their start and end apart: 5 -> 5, of which waited for: 3 -> 4; matrix products, arithmetic and copies ran while one was open for 0% -> 0% of each run, Pallas kernels for 10% -> 9%
where the time goes in v16:
time: 46 us; the launch traced here: 45.7 us
  starting transfers between devices  15.5 us (34%)
  waiting for transfers between devices  12 us (26%)
  blocking collectives  8.96 us (19%)
  Pallas kernels  7.9 us (17%)
  between operations  1.35 us (3%)
    all_to_all x2, starting transfers between devices, swap(): return lax.all_to_all(value, axes, split_axis=0, concat_axis=0, tiled=True)  11 us
    all_to_all x1, blocking collectives, swap(): return lax.all_to_all(value, axes, split_axis=0, concat_axis=0, tiled=True)  8.96 us
    pallas_call x8, Pallas kernels, call(): pl.pallas_call(kernel, out_shape=outs, in_specs=[pl.BlockSpec(memory_spac...  7.9 us
    all_to_all x2, waiting for transfers between devices, swap(): return lax.all_to_all(value, axes, split_axis=0, concat_axis=0, tiled=True)  6.32 us
    ppermute x3, waiting for transfers between devices, partner(): lax.ppermute(value, 'blk', [(i, i ^ 1 << bit) for i in range(members)])  5.72 us
    ppermute x3, starting transfers between devices, partner(): lax.ppermute(value, 'blk', [(i, i ^ 1 << bit) for i in range(members)])  4.48 us
  transfers between devices with their start and end apart: 5, of which 4 were waited for; matrix products, arithmetic and copies ran while one was open for 0% of the time, Pallas kernels for 9%

profile of v16, /device:TPU:0, one launch (start us, length us, event | category | flops | bytes accessed | tf_op | source)
XLA Modules:
  0.0 45.7 jit_solution(12108652510840499386)
XLA Ops:
  0.6 1.8 %shard_map.167 = (f32[8,16,128]{2,1,0:T(8,128)}, s32[1,512]{1,0:T(1,128)S(1)}, s32[1,512]{1,0:T(1,128)S(1)}) custom-call(s32[1,512]{1,0:T(1,128)} %bitcast.15, f32[1,512]{1,0:T(1,128)} %bitcast.16, f32[1,512]{1,0:T(1,128)} %bitcast.17, f32[1,512]{1,0:T(1,128)} %bitcast.18, f32[1,512]{1,0:T(1,128)} %bitcast.19, f32[1,512]{1,0:T(1,128)} %bitcast.20, ...), custom_call_target="tpu_custom_call" | custom-call | flops 1000 | bytes 1000 | tf_op jit(solution)/shard_map/pallas_call | solution.py:386
  2.4 7.3 %all-to-all-start = ((f32[8,16,128]{2,1,0:T(8,128)}), f32[8,16,128]{2,1,0:T(8,128)S(1)}, u32[]{:S(2)}, u32[]{:S(2)}) async-start(f32[8,16,128]{2,1,0:T(8,128)} %get-tuple-element.17), calls=%async_computation | async-start | bytes 131072 | tf_op jit(solution)/shard_map/all_to_all | solution.py:430
  9.7 2.9 %collective-permute-start = (bf16[64,512]{1,0:T(8,128)(2,1)}, bf16[64,512]{1,0:T(8,128)(2,1)S(1)}, u32[]{:S(2)}, u32[]{:S(2)}) collective-permute-start(bf16[64,512]{1,0:T(8,128)(2,1)} %bitcast.13), channel_id=1, source_target_pairs={{0,4},{1,5},{2,6},{3,7},{4,0},{5,1},{6,2},{7,3},{8,12},{9,13},{10,... | collective-permute-start | bytes 196616 | tf_op jit(solution)/shard_map/ppermute | solution.py:433
  13.3 0.0 copy-start
  13.3 1.5 %shard_map.168 = (f32[3,8,512]{2,1,0:T(8,128)S(1)}, f32[8,64]{1,0:T(8,128)S(1)}, bf16[3,512,512]{2,1,0:T(8,128)(2,1)S(1)}, bf16[64,512]{1,0:T(8,128)(2,1)S(1)}, ...) custom-call(s32[3]{0:T(128)} %refs_0_.2, s32[4]{0:T(128)} %refs_1_.1, s32[4]{0:T(128)} %refs_2_.2, ...), custom_call_target="tpu_custom_call" | custom-call | flops 1073741824 | bytes 4194304 | tf_op jit(solution)/shard_map/pallas_call | solution.py:386
  14.8 2.4 %collective-permute-done.came_ref = bf16[64,512]{1,0:T(8,128)(2,1)S(1)} collective-permute-done((bf16[64,512]{1,0:T(8,128)(2,1)}, bf16[64,512]{1,0:T(8,128)(2,1)S(1)}, u32[]{:S(2)}, u32[]{:S(2)}) %collective-permute-start) | collective-permute-done | bytes 65568 | tf_op jit(solution)/shard_map/ppermute | solution.py:433
  17.2 0.0 copy-done
  17.3 0.1 collective-permute-start.1
  17.3 0.0 all-to-all-done.got_ref
  17.4 1.9 %shard_map.169 = (f32[8,512]{1,0:T(8,128)S(1)}, f32[8,512]{1,0:T(8,128)S(1)}, s32[1,512]{1,0:T(1,128)S(1)}, f32[32,1,640]{2,1,0:T(1,128)}) custom-call(f32[8,16,128]{2,1,0:T(8,128)S(1)} %all-to-all-done.got_ref, bf16[64,512]{1,0:T(8,128)(2,1)S(1)} %get-tuple-element.18.coarse_v_ref, s32[1]{0:T(128)S(6)} %copy.18.refs_0_.refs_2_, ...), custom_call_target="tpu_custom_call" | custom-call | flops 8589934592 | bytes 33554432 | tf_op jit(solution)/shard_map/pallas_call | solution.py:386
  19.2 2.7 %collective-permute-done.1.came_ref = bf16[96,512]{1,0:T(8,128)(2,1)S(1)} collective-permute-done((bf16[96,512]{1,0:T(8,128)(2,1)S(1)}, bf16[96,512]{1,0:T(8,128)(2,1)S(1)}, u32[]{:S(2)}, u32[]{:S(2)}) %collective-permute-start.1) | collective-permute-done | bytes 98336 | tf_op jit(solution)/shard_map/ppermute | solution.py:433
  22.0 1.5 %collective-permute-start.2 = (bf16[192,512]{1,0:T(8,128)(2,1)S(1)}, bf16[192,512]{1,0:T(8,128)(2,1)S(1)}, u32[]{:S(2)}, u32[]{:S(2)}) collective-permute-start(bf16[192,512]{1,0:T(8,128)(2,1)S(1)} %shard_map.171.held_ref.refs_0_), channel_id=1, source_target_pairs={{0,1},{1,0},{2,3},{3,2},{4,5},{5,4},{6,7},{7,6},{8,9},{9,8},{10,11... | collective-permute-start | bytes 589832 | tf_op jit(solution)/shard_map/ppermute | solution.py:433
  23.4 3.7 %all-to-all-start.1 = ((f32[32,1,640]{2,1,0:T(1,128)}), f32[32,1,640]{2,1,0:T(1,128)S(1)}, u32[]{:S(2)}, u32[]{:S(2)}) async-start(f32[32,1,640]{2,1,0:T(1,128)} %get-tuple-element.27), calls=%async_computation.1 | async-start | bytes 163840 | tf_op jit(solution)/shard_map/all_to_all | solution.py:430
  27.2 0.5 %collective-permute-done.2.came_ref.refs_1_ = bf16[192,512]{1,0:T(8,128)(2,1)S(1)} collective-permute-done((bf16[192,512]{1,0:T(8,128)(2,1)S(1)}, bf16[192,512]{1,0:T(8,128)(2,1)S(1)}, u32[]{:S(2)}, u32[]{:S(2)}) %collective-permute-start.2) | collective-permute-done | bytes 196640 | tf_op jit(solution)/shard_map/ppermute | solution.py:433
  27.7 0.6 %shard_map.172.elem_bases_ref = bf16[48,512]{1,0:T(8,128)(2,1)S(1)} custom-call(bf16[192,512]{1,0:T(8,128)(2,1)S(1)} %shard_map.171.held_ref.refs_0_, bf16[192,512]{1,0:T(8,128)(2,1)S(1)} %collective-permute-done.2.came_ref.refs_1_, s32[1,512]{1,0:T(1,128)S(1)} %get-tuple-element.28.refs_0_.slot_ref, s32[1,512]{1,0:T(1,128)S(1)} %get-tuple-element.29.elem_row_ref), custom_call_target="tpu_custom_call" | custom-call | flops 17179869184 | bytes 67108864 | tf_op jit(solution)/shard_map/pallas_call | solution.py:386
  28.3 6.3 %all-to-all-done.1.all_ref = f32[32,1,640]{2,1,0:T(1,128)S(1)} async-done(((f32[32,1,640]{2,1,0:T(1,128)}), f32[32,1,640]{2,1,0:T(1,128)S(1)}, u32[]{:S(2)}, u32[]{:S(2)}) %all-to-all-start.1) | async-done | bytes 81952 | tf_op jit(solution)/shard_map/all_to_all | solution.py:430
  34.6 1.2 %shard_map.173 = f32[32,4,128]{2,1,0:T(4,128)S(1)} custom-call(f32[8,512]{1,0:T(8,128)S(1)} %get-tuple-element.24.state_ref, f32[8,512]{1,0:T(8,128)S(1)} %get-tuple-element.25.factor_ref, s32[1,512]{1,0:T(1,128)S(1)} %get-tuple-element.26.refs_0_.rows_ref, f32[32,1,640]{2,1,0:T(1,128)S(1)} %all-to-all-done.1.all_ref, ...), custom_call_target="tpu_custom_call" | custom-call | flops 1000 | bytes 1000 | tf_op jit(solution)/shard_map/pallas_call | solution.py:386
  35.8 9.0 %all_to_all.15.got_ref = f32[32,4,128]{2,1,0:T(4,128)S(1)} all-to-all(f32[32,4,128]{2,1,0:T(4,128)S(1)} %shard_map.173), channel_id=1, replica_groups=mesh['leaf'=4,'blk'=8] {'leaf','blk'}, dimensions={0} | all-to-all | bytes 131072 | tf_op jit(solution)/shard_map/all_to_all | solution.py:430
  44.8 0.9 %shard_map.174 = (f32[1,512]{1,0:T(1,128)}, f32[1,512]{1,0:T(1,128)}) custom-call(f32[32,4,128]{2,1,0:T(4,128)S(1)} %all_to_all.15.got_ref, s32[1,512]{1,0:T(1,128)S(1)} %get-tuple-element.28.refs_0_.slot_ref, bf16[48,512]{1,0:T(8,128)(2,1)S(1)} %shard_map.172.elem_bases_ref), custom_call_target="tpu_custom_call" | custom-call | flops 1000 | bytes 1000 | tf_op jit(solution)/shard_map/pallas_call | solution.py:386
  (2 shorter events, 0.0 us)
Async XLA Ops:
  2.4 14.9 %all-to-all-start = ((f32[8,16,128]{2,1,0:T(8,128)}), f32[8,16,128]{2,1,0:T(8,128)S(1)}, u32[]{:S(2)}, u32[]{:S(2)}) async-start(f32[8,16,128]{2,1,0:T(8,128)} %get-tuple-element.17), calls=%async_computation | async-start | bytes 131072 | tf_op jit(solution)/shard_map/all_to_all | solution.py:430
  9.7 7.6 %collective-permute-start = (bf16[64,512]{1,0:T(8,128)(2,1)}, bf16[64,512]{1,0:T(8,128)(2,1)S(1)}, u32[]{:S(2)}, u32[]{:S(2)}) collective-permute-start(bf16[64,512]{1,0:T(8,128)(2,1)} %bitcast.13), channel_id=1, source_target_pairs={{0,4},{1,5},{2,6},{3,7},{4,0},{5,1},{6,2},{7,3},{8,12},{9,13},{10,... | collective-permute-start | bytes 196616 | tf_op jit(solution)/shard_map/ppermute | solution.py:433
  13.3 4.0 %copy-start = (bf16[4,16,512]{2,1,0:T(8,128)(2,1)S(1)}, bf16[4,16,512]{2,1,0:T(8,128)(2,1)}, u32[]{:S(2)}) copy-start(bf16[4,16,512]{2,1,0:T(8,128)(2,1)} %param.30) | copy-start | bytes 196612
  17.3 4.7 %collective-permute-start.1 = (bf16[96,512]{1,0:T(8,128)(2,1)S(1)}, bf16[96,512]{1,0:T(8,128)(2,1)S(1)}, u32[]{:S(2)}, u32[]{:S(2)}) collective-permute-start(bf16[96,512]{1,0:T(8,128)(2,1)S(1)} %shard_map.170.held_ref), channel_id=1, source_target_pairs={{0,2},{1,3},{2,0},{3,1},{4,6},{5,7},{6,4},{7,5},{8,10},{9,11},{10,... | collective-permute-start | bytes 294920 | tf_op jit(solution)/shard_map/ppermute | solution.py:433
  22.0 5.7 %collective-permute-start.2 = (bf16[192,512]{1,0:T(8,128)(2,1)S(1)}, bf16[192,512]{1,0:T(8,128)(2,1)S(1)}, u32[]{:S(2)}, u32[]{:S(2)}) collective-permute-start(bf16[192,512]{1,0:T(8,128)(2,1)S(1)} %shard_map.171.held_ref.refs_0_), channel_id=1, source_target_pairs={{0,1},{1,0},{2,3},{3,2},{4,5},{5,4},{6,7},{7,6},{8,9},{9,8},{10,11... | collective-permute-start | bytes 589832 | tf_op jit(solution)/shard_map/ppermute | solution.py:433
  23.4 11.2 %all-to-all-start.1 = ((f32[32,1,640]{2,1,0:T(1,128)}), f32[32,1,640]{2,1,0:T(1,128)S(1)}, u32[]{:S(2)}, u32[]{:S(2)}) async-start(f32[32,1,640]{2,1,0:T(1,128)} %get-tuple-element.27), calls=%async_computation.1 | async-start | bytes 163840 | tf_op jit(solution)/shard_map/all_to_all | solution.py:430

commit v17 on v16

--- a/solution.py
+++ b/solution.py
@@ -141,7 +141,7 @@
         sent_ref[peer, 3 * pieces:3 * pieces + 2, HALF:HALF + peer_rows] = part[4:6]
 
 
-def load_kernel(*refs):
+def load_kernel(early_ref, *refs):
     scalar_refs, weight_refs, near_mask_ref, far_mask_ref = refs[:3], refs[3:7], refs[7], refs[8]
     weight_outs, scalar_bufs, sems = refs[9:13], refs[13:16], refs[16]
     copies = start_copies([*scalar_refs, *weight_refs], [*scalar_bufs, *weight_outs], sems)
@@ -453,6 +453,13 @@
         scratch=[VMEM(value.shape, value.dtype) for value in elem_args]
         + [pltpu.SemaphoreType.DMA((7,))],
     )
+    bases = coarse_u.reshape(width, elems)
+    top = members.bit_length() - 2
+    early = bases = call(
+        functools.partial(stack_foreign_kernel, groups, rank),
+        shape(2 * (width - rank), elems, dtype=jnp.bfloat16),
+        bases, partner(bases, top), slot, flops=1 << 34, moved=1 << 26,
+    )
     near_mask, far_mask, near, far_u, far_v, coarse_v = call(
         load_kernel,
         (
@@ -460,7 +467,7 @@
             shape(members, far_rows),
             *[shape(*value.shape, dtype=jnp.bfloat16) for value in weights],
         ),
-        *scalar_args, *weights, far=range(7),
+        early, *scalar_args, *weights, far=range(1, 8),
         scratch=[SMEM(value.shape, value.dtype) for value in scalar_args]
         + [pltpu.SemaphoreType.DMA((7,))],
         flops=1 << 30, moved=1 << 22,
@@ -478,16 +485,10 @@
         scratch=[VMEM((2, members * (elems // LANES), LANES), jnp.float32)],
         flops=1 << 33, moved=1 << 25,
     )
-    bases = coarse_u.reshape(width, elems)
-    top = members.bit_length() - 2
-    for bit in range(top, 0, -1):
-        kernel, rows_out = stack_kernel, 2 * bases.shape[0]
-        if bit == top:
-            kernel = functools.partial(stack_foreign_kernel, groups, rank)
-            rows_out = 2 * (width - rank)
+    for bit in range(top - 1, 0, -1):
         bases = call(
-            kernel, shape(rows_out, elems, dtype=jnp.bfloat16),
-            bases, partner(bases, bit), slot if bit == top else rows, flops=1 << 34, moved=1 << 26,
+            stack_kernel, shape(2 * bases.shape[0], elems, dtype=jnp.bfloat16),
+            bases, partner(bases, bit), rows, flops=1 << 34, moved=1 << 26,
         )
     bases = bases, partner(bases, 0)
     elem_bases = call(

time: 46 us -> 42.1 us (0.915)
  waiting for transfers between devices: 12 us -> 9.12 us
  starting transfers between devices: 15.5 us -> 13.6 us
  local copies, waits for them, and re-layouts: 0.01 us -> 0.83 us
    all_to_all x2, starting transfers between devices: 11 us -> 7.18 us  [swap(): return lax.all_to_all(value, axes, split_axis=0, concat_axis=0, tiled=True)]
    ppermute x3, waiting for transfers between devices: 5.72 us -> 2.06 us  [partner(): lax.ppermute(value, 'blk', [(i, i ^ 1 << bit) for i in range(members)])]
    ppermute x3, starting transfers between devices: 4.48 us -> 6.47 us  [partner(): lax.ppermute(value, 'blk', [(i, i ^ 1 << bit) for i in range(members)])]
    unnamed x2, local copies, waits for them, and re-layouts: 0.01 us -> 0.83 us
    all_to_all x2, waiting for transfers between devices: 6.32 us -> 7.05 us  [swap(): return lax.all_to_all(value, axes, split_axis=0, concat_axis=0, tiled=True)]
  transfers between devices with their start and end apart: 5 -> 5, of which waited for: 4 -> 3; matrix products, arithmetic and copies ran while one was open for 0% -> 0% of each run, Pallas kernels for 9% -> 14%
where the time goes in v17:
time: 42.1 us; the launch traced here: 41.8 us
  starting transfers between devices  13.6 us (32%)
  waiting for transfers between devices  9.12 us (22%)
  blocking collectives  8.96 us (21%)
  Pallas kernels  7.86 us (19%)
  between operations  1.34 us (3%)
  local copies, waits for them, and re-layouts  0.83 us (2%)
    all_to_all x1, blocking collectives, swap(): return lax.all_to_all(value, axes, split_axis=0, concat_axis=0, tiled=True)  8.96 us
    pallas_call x8, Pallas kernels, call(): pl.pallas_call(kernel, out_shape=outs, in_specs=[pl.BlockSpec(memory_spac...  7.86 us
    all_to_all x2, starting transfers between devices, swap(): return lax.all_to_all(value, axes, split_axis=0, concat_axis=0, tiled=True)  7.18 us
    all_to_all x2, waiting for transfers between devices, swap(): return lax.all_to_all(value, axes, split_axis=0, concat_axis=0, tiled=True)  7.05 us
    ppermute x3, starting transfers between devices, partner(): lax.ppermute(value, 'blk', [(i, i ^ 1 << bit) for i in range(members)])  6.47 us
    ppermute x3, waiting for transfers between devices, partner(): lax.ppermute(value, 'blk', [(i, i ^ 1 << bit) for i in range(members)])  2.06 us
  transfers between devices with their start and end apart: 5, of which 3 were waited for; matrix products, arithmetic and copies ran while one was open for 0% of the time, Pallas kernels for 14%

profile of v17, /device:TPU:0, one launch (start us, length us, event | category | flops | bytes accessed | tf_op | source)
XLA Modules:
  0.0 41.8 jit_solution(11105737473595161061)
XLA Ops:
  0.6 4.1 %collective-permute-start = (bf16[64,512]{1,0:T(8,128)(2,1)}, bf16[64,512]{1,0:T(8,128)(2,1)S(1)}, u32[]{:S(2)}, u32[]{:S(2)}) collective-permute-start(bf16[64,512]{1,0:T(8,128)(2,1)} %bitcast.13), channel_id=1, source_target_pairs={{0,4},{1,5},{2,6},{3,7},{4,0},{5,1},{6,2},{7,3},{8,12},{9,13},{10,... | collective-permute-start | bytes 196616 | tf_op jit(solution)/shard_map/ppermute | solution.py:433
  4.7 1.8 %shard_map.167 = (f32[8,16,128]{2,1,0:T(8,128)}, s32[1,512]{1,0:T(1,128)S(1)}, s32[1,512]{1,0:T(1,128)S(1)}) custom-call(s32[1,512]{1,0:T(1,128)} %bitcast.15, f32[1,512]{1,0:T(1,128)} %bitcast.16, f32[1,512]{1,0:T(1,128)} %bitcast.17, f32[1,512]{1,0:T(1,128)} %bitcast.18, f32[1,512]{1,0:T(1,128)} %bitcast.19, f32[1,512]{1,0:T(1,128)} %bitcast.20, ...), custom_call_target="tpu_custom_call" | custom-call | flops 1000 | bytes 1000 | tf_op jit(solution)/shard_map/pallas_call | solution.py:386
  6.5 3.8 %all-to-all-start = ((f32[8,16,128]{2,1,0:T(8,128)}), f32[8,16,128]{2,1,0:T(8,128)S(1)}, u32[]{:S(2)}, u32[]{:S(2)}) async-start(f32[8,16,128]{2,1,0:T(8,128)} %get-tuple-element.17), calls=%async_computation | async-start | bytes 131072 | tf_op jit(solution)/shard_map/all_to_all | solution.py:430
  11.0 0.0 collective-permute-done.came_ref
  11.0 0.0 copy-start
  11.0 0.8 %copy-done = bf16[4,16,512]{2,1,0:T(8,128)(2,1)S(1)} copy-done((bf16[4,16,512]{2,1,0:T(8,128)(2,1)S(1)}, bf16[4,16,512]{2,1,0:T(8,128)(2,1)}, u32[]{:S(2)}) %copy-start) | copy-done | bytes 65560
  11.8 2.1 %collective-permute-start.1 = (bf16[96,512]{1,0:T(8,128)(2,1)S(1)}, bf16[96,512]{1,0:T(8,128)(2,1)S(1)}, u32[]{:S(2)}, u32[]{:S(2)}) collective-permute-start(bf16[96,512]{1,0:T(8,128)(2,1)S(1)} %shard_map.168.early_ref.held_ref), channel_id=1, source_target_pairs={{0,2},{1,3},{2,0},{3,1},{4,6},{5,7},{6,4},{7,5},{8,10},{9,11},{10,... | collective-permute-start | bytes 294920 | tf_op jit(solution)/shard_map/ppermute | solution.py:433
  13.9 1.5 %shard_map.169 = (f32[3,8,512]{2,1,0:T(8,128)S(1)}, f32[8,64]{1,0:T(8,128)S(1)}, bf16[3,512,512]{2,1,0:T(8,128)(2,1)S(1)}, bf16[64,512]{1,0:T(8,128)(2,1)S(1)}, ...) custom-call(bf16[96,512]{1,0:T(8,128)(2,1)S(1)} %shard_map.168.early_ref.held_ref, s32[3]{0:T(128)} %refs_0_.2, ...), custom_call_target="tpu_custom_call" | custom-call | flops 1073741824 | bytes 4194304 | tf_op jit(solution)/shard_map/pallas_call | solution.py:386
  15.4 2.3 %all-to-all-done.got_ref = f32[8,16,128]{2,1,0:T(8,128)S(1)} async-done(((f32[8,16,128]{2,1,0:T(8,128)}), f32[8,16,128]{2,1,0:T(8,128)S(1)}, u32[]{:S(2)}, u32[]{:S(2)}) %all-to-all-start) | async-done | bytes 65568 | tf_op jit(solution)/shard_map/all_to_all | solution.py:430
  17.7 1.8 %shard_map.170 = (f32[8,512]{1,0:T(8,128)S(1)}, f32[8,512]{1,0:T(8,128)S(1)}, s32[1,512]{1,0:T(1,128)S(1)}, f32[32,1,640]{2,1,0:T(1,128)}) custom-call(f32[8,16,128]{2,1,0:T(8,128)S(1)} %all-to-all-done.got_ref, bf16[64,512]{1,0:T(8,128)(2,1)S(1)} %get-tuple-element.19.coarse_v_ref, s32[1]{0:T(128)S(6)} %copy.18.refs_0_.refs_2_, ...), custom_call_target="tpu_custom_call" | custom-call | flops 8589934592 | bytes 33554432 | tf_op jit(solution)/shard_map/pallas_call | solution.py:386
  19.5 0.0 collective-permute-done.1.came_ref
  19.5 0.3 collective-permute-start.2
  19.8 3.4 %all-to-all-start.1 = ((f32[32,1,640]{2,1,0:T(1,128)}), f32[32,1,640]{2,1,0:T(1,128)S(1)}, u32[]{:S(2)}, u32[]{:S(2)}) async-start(f32[32,1,640]{2,1,0:T(1,128)} %get-tuple-element.28), calls=%async_computation.1 | async-start | bytes 163840 | tf_op jit(solution)/shard_map/all_to_all | solution.py:430
  23.2 2.1 %collective-permute-done.2.came_ref.refs_1_ = bf16[192,512]{1,0:T(8,128)(2,1)S(1)} collective-permute-done((bf16[192,512]{1,0:T(8,128)(2,1)S(1)}, bf16[192,512]{1,0:T(8,128)(2,1)S(1)}, u32[]{:S(2)}, u32[]{:S(2)}) %collective-permute-start.2) | collective-permute-done | bytes 196640 | tf_op jit(solution)/shard_map/ppermute | solution.py:433
  25.3 0.6 %shard_map.172.elem_bases_ref = bf16[48,512]{1,0:T(8,128)(2,1)S(1)} custom-call(bf16[192,512]{1,0:T(8,128)(2,1)S(1)} %shard_map.171.held_ref.refs_0_, bf16[192,512]{1,0:T(8,128)(2,1)S(1)} %collective-permute-done.2.came_ref.refs_1_, s32[1,512]{1,0:T(1,128)S(1)} %get-tuple-element.18.refs_0_.slot_ref, s32[1,512]{1,0:T(1,128)S(1)} %get-tuple-element.29.elem_row_ref), custom_call_target="tpu_custom_call" | custom-call | flops 17179869184 | bytes 67108864 | tf_op jit(solution)/shard_map/pallas_call | solution.py:386
  25.9 4.8 %all-to-all-done.1.all_ref = f32[32,1,640]{2,1,0:T(1,128)S(1)} async-done(((f32[32,1,640]{2,1,0:T(1,128)}), f32[32,1,640]{2,1,0:T(1,128)S(1)}, u32[]{:S(2)}, u32[]{:S(2)}) %all-to-all-start.1) | async-done | bytes 81952 | tf_op jit(solution)/shard_map/all_to_all | solution.py:430
  30.7 1.2 %shard_map.173 = f32[32,4,128]{2,1,0:T(4,128)S(1)} custom-call(f32[8,512]{1,0:T(8,128)S(1)} %get-tuple-element.25.state_ref, f32[8,512]{1,0:T(8,128)S(1)} %get-tuple-element.26.factor_ref, s32[1,512]{1,0:T(1,128)S(1)} %get-tuple-element.27.refs_0_.rows_ref, f32[32,1,640]{2,1,0:T(1,128)S(1)} %all-to-all-done.1.all_ref, ...), custom_call_target="tpu_custom_call" | custom-call | flops 1000 | bytes 1000 | tf_op jit(solution)/shard_map/pallas_call | solution.py:386
  31.9 9.0 %all_to_all.15.got_ref = f32[32,4,128]{2,1,0:T(4,128)S(1)} all-to-all(f32[32,4,128]{2,1,0:T(4,128)S(1)} %shard_map.173), channel_id=1, replica_groups=mesh['leaf'=4,'blk'=8] {'leaf','blk'}, dimensions={0} | all-to-all | bytes 131072 | tf_op jit(solution)/shard_map/all_to_all | solution.py:430
  40.8 0.9 %shard_map.174 = (f32[1,512]{1,0:T(1,128)}, f32[1,512]{1,0:T(1,128)}) custom-call(f32[32,4,128]{2,1,0:T(4,128)S(1)} %all_to_all.15.got_ref, s32[1,512]{1,0:T(1,128)S(1)} %get-tuple-element.18.refs_0_.slot_ref, bf16[48,512]{1,0:T(8,128)(2,1)S(1)} %shard_map.172.elem_bases_ref), custom_call_target="tpu_custom_call" | custom-call | flops 1000 | bytes 1000 | tf_op jit(solution)/shard_map/pallas_call | solution.py:386
  (2 shorter events, 0.0 us)
Async XLA Ops:
  0.6 10.3 %collective-permute-start = (bf16[64,512]{1,0:T(8,128)(2,1)}, bf16[64,512]{1,0:T(8,128)(2,1)S(1)}, u32[]{:S(2)}, u32[]{:S(2)}) collective-permute-start(bf16[64,512]{1,0:T(8,128)(2,1)} %bitcast.13), channel_id=1, source_target_pairs={{0,4},{1,5},{2,6},{3,7},{4,0},{5,1},{6,2},{7,3},{8,12},{9,13},{10,... | collective-permute-start | bytes 196616 | tf_op jit(solution)/shard_map/ppermute | solution.py:433
  6.5 11.1 %all-to-all-start = ((f32[8,16,128]{2,1,0:T(8,128)}), f32[8,16,128]{2,1,0:T(8,128)S(1)}, u32[]{:S(2)}, u32[]{:S(2)}) async-start(f32[8,16,128]{2,1,0:T(8,128)} %get-tuple-element.17), calls=%async_computation | async-start | bytes 131072 | tf_op jit(solution)/shard_map/all_to_all | solution.py:430
  11.0 0.8 %copy-start = (bf16[4,16,512]{2,1,0:T(8,128)(2,1)S(1)}, bf16[4,16,512]{2,1,0:T(8,128)(2,1)}, u32[]{:S(2)}) copy-start(bf16[4,16,512]{2,1,0:T(8,128)(2,1)} %param.30) | copy-start | bytes 196612
  11.8 7.7 %collective-permute-start.1 = (bf16[96,512]{1,0:T(8,128)(2,1)S(1)}, bf16[96,512]{1,0:T(8,128)(2,1)S(1)}, u32[]{:S(2)}, u32[]{:S(2)}) collective-permute-start(bf16[96,512]{1,0:T(8,128)(2,1)S(1)} %shard_map.168.early_ref.held_ref), channel_id=1, source_target_pairs={{0,2},{1,3},{2,0},{3,1},{4,6},{5,7},{6,4},{7,5},{8,10},{9,11},{10,... | collective-permute-start | bytes 294920 | tf_op jit(solution)/shard_map/ppermute | solution.py:433
  19.5 5.7 %collective-permute-start.2 = (bf16[192,512]{1,0:T(8,128)(2,1)S(1)}, bf16[192,512]{1,0:T(8,128)(2,1)S(1)}, u32[]{:S(2)}, u32[]{:S(2)}) collective-permute-start(bf16[192,512]{1,0:T(8,128)(2,1)S(1)} %shard_map.171.held_ref.refs_0_), channel_id=1, source_target_pairs={{0,1},{1,0},{2,3},{3,2},{4,5},{5,4},{6,7},{7,6},{8,9},{9,8},{10,11... | collective-permute-start | bytes 589832 | tf_op jit(solution)/shard_map/ppermute | solution.py:433
  19.8 10.8 %all-to-all-start.1 = ((f32[32,1,640]{2,1,0:T(1,128)}), f32[32,1,640]{2,1,0:T(1,128)S(1)}, u32[]{:S(2)}, u32[]{:S(2)}) async-start(f32[32,1,640]{2,1,0:T(1,128)} %get-tuple-element.28), calls=%async_computation.1 | async-start | bytes 163840 | tf_op jit(solution)/shard_map/all_to_all | solution.py:430

commit v18 on v17

--- a/solution.py
+++ b/solution.py
@@ -26,7 +26,10 @@
 
 def low_matrix(index_row):
     rows = lax.broadcasted_iota(jnp.int32, (LANES, index_row.shape[1]), 0)
-    return jnp.where(rows == (index_row & (LANES - 1)), 1.0, 0.0).astype(jnp.bfloat16)
+    rows = rows.astype(jnp.float32).astype(jnp.bfloat16)
+    low = (index_row & (LANES - 1)).astype(jnp.float32).astype(jnp.bfloat16)
+    one = jnp.ones((), jnp.bfloat16)
+    return jnp.where(rows == low, one, jnp.zeros_like(one))
 
 
 def three_parts(values):
@@ -97,9 +100,9 @@
 
 
 def sort_kernel(members, *refs):
-    elem_refs, sent_ref, slot_ref, elem_row_ref = refs[:7], refs[7], refs[8], refs[9]
-    elem_bufs, sems = refs[10:17], refs[17]
-    copies = start_copies(elem_refs, elem_bufs, sems)
+    elem_refs, bases_ref, sent_ref, slot_ref, elem_row_ref, bases_out = refs[:7], *refs[7:12]
+    elem_bufs, sems = refs[12:19], refs[19]
+    copies = start_copies([*elem_refs, bases_ref], [*elem_bufs, bases_out], sems)
     mine = lax.axis_index("leaf")
     elem_count = elem_bufs[0].shape[1]
     peer_rows = elem_count // members
@@ -124,7 +127,7 @@
     slot = target * peer_rows + jnp.concatenate(ranks, axis=1).astype(jnp.int32)
     slot_ref[...] = slot
     elem_row_ref[...] = target_row
-    for copy in copies[1:]:
+    for copy in copies[1:7]:
         copy.wait()
     u, phi, sigma, fric_a, fric_b, dist = (buf[...] for buf in elem_bufs[1:])
     velocity = jnp.exp(u)
@@ -139,6 +142,7 @@
         part = values[0:6, peer * peer_rows:(peer + 1) * peer_rows]
         sent_ref[peer, 3 * pieces:3 * pieces + 4, 0:peer_rows] = part[0:4]
         sent_ref[peer, 3 * pieces:3 * pieces + 2, HALF:HALF + peer_rows] = part[4:6]
+    copies[7].wait()
 
 
 def load_kernel(early_ref, *refs):
@@ -442,23 +446,24 @@
         coarse_v.reshape(width, elems),
     ]
     far_rows = weights[1].shape[0]
-    sent, slot, elem_row = call(
+    bases = coarse_u.reshape(width, elems)
+    sent, slot, elem_row, held = call(
         functools.partial(sort_kernel, members),
         (
             shape(members, -(-(3 * (elems // LANES) + 4) // 8) * 8, LANES),
             shape(1, elems, dtype=integer),
             shape(1, elems, dtype=integer),
+            shape(width, elems, dtype=jnp.bfloat16),
         ),
-        *elem_args, far=range(7),
+        *elem_args, bases, far=range(8),
         scratch=[VMEM(value.shape, value.dtype) for value in elem_args]
-        + [pltpu.SemaphoreType.DMA((7,))],
-    )
-    bases = coarse_u.reshape(width, elems)
+        + [pltpu.SemaphoreType.DMA((8,))],
+    )
     top = members.bit_length() - 2
     early = bases = call(
         functools.partial(stack_foreign_kernel, groups, rank),
         shape(2 * (width - rank), elems, dtype=jnp.bfloat16),
-        bases, partner(bases, top), slot, flops=1 << 34, moved=1 << 26,
+        held, partner(bases, top), slot, flops=1 << 34, moved=1 << 26,
     )
     near_mask, far_mask, near, far_u, far_v, coarse_v = call(
         load_kernel,

time: 42.1 us -> 41.6 us (0.988)
  local copies, waits for them, and re-layouts: 0.83 us -> 0 us
  waiting for transfers between devices: 9.12 us -> 9.7 us
    unnamed x2 -> x0, local copies, waits for them, and re-layouts: 0.83 us -> none
    all_to_all x2, starting transfers between devices: 7.18 us -> 6.7 us  [swap(): return lax.all_to_all(value, axes, split_axis=0, concat_axis=0, tiled=True)]
where the time goes in v18:
time: 41.6 us; the launch traced here: 41.2 us
  starting transfers between devices  13.4 us (32%)
  waiting for transfers between devices  9.7 us (23%)
  blocking collectives  8.96 us (22%)
  Pallas kernels  7.82 us (19%)
  between operations  1.34 us (3%)
    all_to_all x1, blocking collectives, swap(): return lax.all_to_all(value, axes, split_axis=0, concat_axis=0, tiled=True)  8.96 us
    pallas_call x8, Pallas kernels, call(): pl.pallas_call(kernel, out_shape=outs, in_specs=[pl.BlockSpec(memory_spac...  7.82 us
    all_to_all x2, waiting for transfers between devices, swap(): return lax.all_to_all(value, axes, split_axis=0, concat_axis=0, tiled=True)  7.41 us
    ppermute x3, starting transfers between devices, partner(): lax.ppermute(value, 'blk', [(i, i ^ 1 << bit) for i in range(members)])  6.73 us
    all_to_all x2, starting transfers between devices, swap(): return lax.all_to_all(value, axes, split_axis=0, concat_axis=0, tiled=True)  6.7 us
    ppermute x3, waiting for transfers between devices, partner(): lax.ppermute(value, 'blk', [(i, i ^ 1 << bit) for i in range(members)])  2.29 us
  transfers between devices with their start and end apart: 5, of which 3 were waited for; matrix products, arithmetic and copies ran while one was open for 0% of the time, Pallas kernels for 14%

profile of v18, /device:TPU:0, one launch (start us, length us, event | category | flops | bytes accessed | tf_op | source)
XLA Modules:
  0.0 41.2 jit_solution(3408863704737252049)
XLA Ops:
  0.6 4.1 %collective-permute-start = (bf16[64,512]{1,0:T(8,128)(2,1)}, bf16[64,512]{1,0:T(8,128)(2,1)S(1)}, u32[]{:S(2)}, u32[]{:S(2)}) collective-permute-start(bf16[64,512]{1,0:T(8,128)(2,1)} %bitcast.13), channel_id=1, source_target_pairs={{0,4},{1,5},{2,6},{3,7},{4,0},{5,1},{6,2},{7,3},{8,12},{9,13},{10,... | collective-permute-start | bytes 196616 | tf_op jit(solution)/shard_map/ppermute | solution.py:437
  4.7 1.8 %shard_map.167 = (f32[8,16,128]{2,1,0:T(8,128)}, s32[1,512]{1,0:T(1,128)S(1)}, s32[1,512]{1,0:T(1,128)S(1)}, bf16[64,512]{1,0:T(8,128)(2,1)S(1)}) custom-call(s32[1,512]{1,0:T(1,128)} %bitcast.15, f32[1,512]{1,0:T(1,128)} %bitcast.16, f32[1,512]{1,0:T(1,128)} %bitcast.17, f32[1,512]{1,0:T(1,128)} %bitcast.18, f32[1,512]{1,0:T(1,128)} %bitcast.19, ...), custom_call_target="tpu_custom_call" | custom-call | flops 1000 | bytes 1000 | tf_op jit(solution)/shard_map/pallas_call | solution.py:390
  6.5 3.8 %all-to-all-start = ((f32[8,16,128]{2,1,0:T(8,128)}), f32[8,16,128]{2,1,0:T(8,128)S(1)}, u32[]{:S(2)}, u32[]{:S(2)}) async-start(f32[8,16,128]{2,1,0:T(8,128)} %get-tuple-element.18), calls=%async_computation | async-start | bytes 131072 | tf_op jit(solution)/shard_map/all_to_all | solution.py:434
  11.0 0.0 collective-permute-done.came_ref
  11.0 2.1 %collective-permute-start.1 = (bf16[96,512]{1,0:T(8,128)(2,1)S(1)}, bf16[96,512]{1,0:T(8,128)(2,1)S(1)}, u32[]{:S(2)}, u32[]{:S(2)}) collective-permute-start(bf16[96,512]{1,0:T(8,128)(2,1)S(1)} %shard_map.168.early_ref.held_ref), channel_id=1, source_target_pairs={{0,2},{1,3},{2,0},{3,1},{4,6},{5,7},{6,4},{7,5},{8,10},{9,11},{10,... | collective-permute-start | bytes 294920 | tf_op jit(solution)/shard_map/ppermute | solution.py:437
  13.1 1.5 %shard_map.169 = (f32[3,8,512]{2,1,0:T(8,128)S(1)}, f32[8,64]{1,0:T(8,128)S(1)}, bf16[3,512,512]{2,1,0:T(8,128)(2,1)S(1)}, bf16[64,512]{1,0:T(8,128)(2,1)S(1)}, ...) custom-call(bf16[96,512]{1,0:T(8,128)(2,1)S(1)} %shard_map.168.early_ref.held_ref, s32[3]{0:T(128)} %refs_0_.2, ...), custom_call_target="tpu_custom_call" | custom-call | flops 1073741824 | bytes 4194304 | tf_op jit(solution)/shard_map/pallas_call | solution.py:390
  14.6 2.8 %all-to-all-done.got_ref = f32[8,16,128]{2,1,0:T(8,128)S(1)} async-done(((f32[8,16,128]{2,1,0:T(8,128)}), f32[8,16,128]{2,1,0:T(8,128)S(1)}, u32[]{:S(2)}, u32[]{:S(2)}) %all-to-all-start) | async-done | bytes 65568 | tf_op jit(solution)/shard_map/all_to_all | solution.py:434
  17.4 1.8 %shard_map.170 = (f32[8,512]{1,0:T(8,128)S(1)}, f32[8,512]{1,0:T(8,128)S(1)}, s32[1,512]{1,0:T(1,128)S(1)}, f32[32,1,640]{2,1,0:T(1,128)}) custom-call(f32[8,16,128]{2,1,0:T(8,128)S(1)} %all-to-all-done.got_ref, bf16[64,512]{1,0:T(8,128)(2,1)S(1)} %get-tuple-element.21.coarse_v_ref, s32[1]{0:T(128)S(6)} %copy.18.refs_0_.refs_2_, ...), custom_call_target="tpu_custom_call" | custom-call | flops 8589934592 | bytes 33554432 | tf_op jit(solution)/shard_map/pallas_call | solution.py:390
  19.2 0.0 collective-permute-done.1.came_ref
  19.2 0.5 %collective-permute-start.2 = (bf16[192,512]{1,0:T(8,128)(2,1)S(1)}, bf16[192,512]{1,0:T(8,128)(2,1)S(1)}, u32[]{:S(2)}, u32[]{:S(2)}) collective-permute-start(bf16[192,512]{1,0:T(8,128)(2,1)S(1)} %shard_map.171.held_ref.refs_0_), channel_id=1, source_target_pairs={{0,1},{1,0},{2,3},{3,2},{4,5},{5,4},{6,7},{7,6},{8,9},{9,8},{10,11... | collective-permute-start | bytes 589832 | tf_op jit(solution)/shard_map/ppermute | solution.py:437
  19.8 2.9 %all-to-all-start.1 = ((f32[32,1,640]{2,1,0:T(1,128)}), f32[32,1,640]{2,1,0:T(1,128)S(1)}, u32[]{:S(2)}, u32[]{:S(2)}) async-start(f32[32,1,640]{2,1,0:T(1,128)} %get-tuple-element.30), calls=%async_computation.1 | async-start | bytes 163840 | tf_op jit(solution)/shard_map/all_to_all | solution.py:434
  22.7 2.3 %collective-permute-done.2.came_ref.refs_1_ = bf16[192,512]{1,0:T(8,128)(2,1)S(1)} collective-permute-done((bf16[192,512]{1,0:T(8,128)(2,1)S(1)}, bf16[192,512]{1,0:T(8,128)(2,1)S(1)}, u32[]{:S(2)}, u32[]{:S(2)}) %collective-permute-start.2) | collective-permute-done | bytes 196640 | tf_op jit(solution)/shard_map/ppermute | solution.py:437
  25.0 0.6 %shard_map.172.elem_bases_ref = bf16[48,512]{1,0:T(8,128)(2,1)S(1)} custom-call(bf16[192,512]{1,0:T(8,128)(2,1)S(1)} %shard_map.171.held_ref.refs_0_, bf16[192,512]{1,0:T(8,128)(2,1)S(1)} %collective-permute-done.2.came_ref.refs_1_, s32[1,512]{1,0:T(1,128)S(1)} %get-tuple-element.20.refs_0_.slot_ref, s32[1,512]{1,0:T(1,128)S(1)} %get-tuple-element.31.elem_row_ref), custom_call_target="tpu_custom_call" | custom-call | flops 17179869184 | bytes 67108864 | tf_op jit(solution)/shard_map/pallas_call | solution.py:390
  25.6 4.6 %all-to-all-done.1.all_ref = f32[32,1,640]{2,1,0:T(1,128)S(1)} async-done(((f32[32,1,640]{2,1,0:T(1,128)}), f32[32,1,640]{2,1,0:T(1,128)S(1)}, u32[]{:S(2)}, u32[]{:S(2)}) %all-to-all-start.1) | async-done | bytes 81952 | tf_op jit(solution)/shard_map/all_to_all | solution.py:434
  30.1 1.2 %shard_map.173 = f32[32,4,128]{2,1,0:T(4,128)S(1)} custom-call(f32[8,512]{1,0:T(8,128)S(1)} %get-tuple-element.27.state_ref, f32[8,512]{1,0:T(8,128)S(1)} %get-tuple-element.28.factor_ref, s32[1,512]{1,0:T(1,128)S(1)} %get-tuple-element.29.refs_0_.rows_ref, f32[32,1,640]{2,1,0:T(1,128)S(1)} %all-to-all-done.1.all_ref, ...), custom_call_target="tpu_custom_call" | custom-call | flops 1000 | bytes 1000 | tf_op jit(solution)/shard_map/pallas_call | solution.py:390
  31.3 9.0 %all_to_all.15.got_ref = f32[32,4,128]{2,1,0:T(4,128)S(1)} all-to-all(f32[32,4,128]{2,1,0:T(4,128)S(1)} %shard_map.173), channel_id=1, replica_groups=mesh['leaf'=4,'blk'=8] {'leaf','blk'}, dimensions={0} | all-to-all | bytes 131072 | tf_op jit(solution)/shard_map/all_to_all | solution.py:434
  40.3 0.9 %shard_map.174 = (f32[1,512]{1,0:T(1,128)}, f32[1,512]{1,0:T(1,128)}) custom-call(f32[32,4,128]{2,1,0:T(4,128)S(1)} %all_to_all.15.got_ref, s32[1,512]{1,0:T(1,128)S(1)} %get-tuple-element.20.refs_0_.slot_ref, bf16[48,512]{1,0:T(8,128)(2,1)S(1)} %shard_map.172.elem_bases_ref), custom_call_target="tpu_custom_call" | custom-call | flops 1000 | bytes 1000 | tf_op jit(solution)/shard_map/pallas_call | solution.py:390
  (2 shorter events, 0.0 us)
Async XLA Ops:
  0.6 10.4 %collective-permute-start = (bf16[64,512]{1,0:T(8,128)(2,1)}, bf16[64,512]{1,0:T(8,128)(2,1)S(1)}, u32[]{:S(2)}, u32[]{:S(2)}) collective-permute-start(bf16[64,512]{1,0:T(8,128)(2,1)} %bitcast.13), channel_id=1, source_target_pairs={{0,4},{1,5},{2,6},{3,7},{4,0},{5,1},{6,2},{7,3},{8,12},{9,13},{10,... | collective-permute-start | bytes 196616 | tf_op jit(solution)/shard_map/ppermute | solution.py:437
  6.5 10.9 %all-to-all-start = ((f32[8,16,128]{2,1,0:T(8,128)}), f32[8,16,128]{2,1,0:T(8,128)S(1)}, u32[]{:S(2)}, u32[]{:S(2)}) async-start(f32[8,16,128]{2,1,0:T(8,128)} %get-tuple-element.18), calls=%async_computation | async-start | bytes 131072 | tf_op jit(solution)/shard_map/all_to_all | solution.py:434
  11.0 8.2 %collective-permute-start.1 = (bf16[96,512]{1,0:T(8,128)(2,1)S(1)}, bf16[96,512]{1,0:T(8,128)(2,1)S(1)}, u32[]{:S(2)}, u32[]{:S(2)}) collective-permute-start(bf16[96,512]{1,0:T(8,128)(2,1)S(1)} %shard_map.168.early_ref.held_ref), channel_id=1, source_target_pairs={{0,2},{1,3},{2,0},{3,1},{4,6},{5,7},{6,4},{7,5},{8,10},{9,11},{10,... | collective-permute-start | bytes 294920 | tf_op jit(solution)/shard_map/ppermute | solution.py:437
  19.2 5.7 %collective-permute-start.2 = (bf16[192,512]{1,0:T(8,128)(2,1)S(1)}, bf16[192,512]{1,0:T(8,128)(2,1)S(1)}, u32[]{:S(2)}, u32[]{:S(2)}) collective-permute-start(bf16[192,512]{1,0:T(8,128)(2,1)S(1)} %shard_map.171.held_ref.refs_0_), channel_id=1, source_target_pairs={{0,1},{1,0},{2,3},{3,2},{4,5},{5,4},{6,7},{7,6},{8,9},{9,8},{10,11... | collective-permute-start | bytes 589832 | tf_op jit(solution)/shard_map/ppermute | solution.py:437
  19.8 10.4 %all-to-all-start.1 = ((f32[32,1,640]{2,1,0:T(1,128)}), f32[32,1,640]{2,1,0:T(1,128)S(1)}, u32[]{:S(2)}, u32[]{:S(2)}) async-start(f32[32,1,640]{2,1,0:T(1,128)} %get-tuple-element.30), calls=%async_computation.1 | async-start | bytes 163840 | tf_op jit(solution)/shard_map/all_to_all | solution.py:434

commit v19 on v18

--- a/solution.py
+++ b/solution.py
@@ -179,16 +179,17 @@
 
 
 def inside_rows(deficits, near_count, near_ref, far_u_ref, far_v_ref, near_mask_ref, far_mask_ref):
-    total = jnp.zeros(deficits.shape, jnp.float32)
+    total = jnp.zeros((near_ref.shape[1], deficits.shape[0]), jnp.float32)
     for slot in range(near_ref.shape[0]):
         live = jnp.where(slot < near_count[0], 1.0, 0.0)
         source = (deficits * (near_mask_ref[slot] * live)).astype(jnp.bfloat16)
-        total = total + dot(source, near_ref[slot], NT)
+        total = total + dot(near_ref[slot], source, NT)
+    near = jnp.sum(total.T, axis=0, keepdims=True)
     project = dot(deficits.astype(jnp.bfloat16), far_v_ref[...], NT) * far_mask_ref[...]
     project = jnp.sum(project, axis=0, keepdims=True)
     project = jnp.broadcast_to(project, (8, project.shape[1])).astype(jnp.bfloat16)
     far = dot(project, far_u_ref[...], NN)
-    return jnp.sum(total, axis=0, keepdims=True) + far[0:1]
+    return near + far[0:1]
 
 
 def coefficients(sums, rank):
@@ -207,12 +208,11 @@
 
 def coarse_all(weights, members, bases_refs):
     row = lax.broadcasted_iota(jnp.int32, (members, weights.shape[1]), 0) ^ lax.axis_index("blk")
-    bits = members.bit_length() - 1
     total = jnp.zeros((members, bases_refs[0].shape[1]), jnp.float32)
     for number, ref in enumerate(bases_refs):
         left = []
         for place in range(members // 2):
-            source = relative_member(place, number, bits)
+            source = relative_member(place, number, members)
             left.append(jnp.where(row == source, weights, 0.0))
         left = jnp.concatenate(left, axis=1).astype(jnp.bfloat16)
         total = total + dot(left, ref[...], NN)
@@ -236,10 +236,17 @@
             place += rank
 
 
-def relative_member(place, number, bits):
-    for bit in range(bits - 1):
-        number |= (place >> bit & 1) << (bits - 1 - bit)
-    return number
+def step_bits(members):
+    bits = list(range(members.bit_length() - 2, -1, -1))
+    return bits[:-2] + [bits[-1], bits[-2]]
+
+
+def relative_member(place, number, members):
+    order = step_bits(members)
+    found = number << order[-1]
+    for step, bit in enumerate(order[:-1]):
+        found |= (place >> step & 1) << bit
+    return found
 
 
 def element_kernel(members, held_ref, came_ref, slot_ref, elem_row_ref, out_ref):
@@ -257,7 +264,7 @@
                 [part[:, piece * LANES:(piece + 1) * LANES] for piece in range(pieces)], axis=0
             )
             found = dot(left, low, NN)
-            ours = owner == relative_member(place, number, members.bit_length() - 1)
+            ours = owner == relative_member(place, number, members)
             for piece in range(pieces):
                 here = ours & (high == piece)
                 total = jnp.where(here, found[piece * kept:(piece + 1) * kept], total)
@@ -459,11 +466,11 @@
         scratch=[VMEM(value.shape, value.dtype) for value in elem_args]
         + [pltpu.SemaphoreType.DMA((8,))],
     )
-    top = members.bit_length() - 2
+    steps = step_bits(members)
     early = bases = call(
         functools.partial(stack_foreign_kernel, groups, rank),
         shape(2 * (width - rank), elems, dtype=jnp.bfloat16),
-        held, partner(bases, top), slot, flops=1 << 34, moved=1 << 26,
+        held, partner(bases, steps[0]), slot, flops=1 << 34, moved=1 << 26,
     )
     near_mask, far_mask, near, far_u, far_v, coarse_v = call(
         load_kernel,
@@ -490,12 +497,12 @@
         scratch=[VMEM((2, members * (elems // LANES), LANES), jnp.float32)],
         flops=1 << 33, moved=1 << 25,
     )
-    for bit in range(top - 1, 0, -1):
+    for bit in steps[1:-1]:
         bases = call(
             stack_kernel, shape(2 * bases.shape[0], elems, dtype=jnp.bfloat16),
             bases, partner(bases, bit), rows, flops=1 << 34, moved=1 << 26,
         )
-    bases = bases, partner(bases, 0)
+    bases = bases, partner(bases, steps[-1])
     elem_bases = call(
         functools.partial(element_kernel, members), shape(width - rank, elems, dtype=jnp.bfloat16),
         *bases, slot, elem_row, flops=1 << 34, moved=1 << 26,

time: 41.6 us -> 41.6 us (level)
  no operation moved by 1% of the time
where the time goes in v19:
time: 41.6 us; the launch traced here: 41.2 us
  starting transfers between devices  13.4 us (32%)
  waiting for transfers between devices  9.51 us (23%)
  blocking collectives  8.96 us (22%)
  Pallas kernels  8.02 us (19%)
  between operations  1.34 us (3%)
    all_to_all x1, blocking collectives, swap(): return lax.all_to_all(value, axes, split_axis=0, concat_axis=0, tiled=True)  8.96 us
    pallas_call x8, Pallas kernels, call(): pl.pallas_call(kernel, out_shape=outs, in_specs=[pl.BlockSpec(memory_spac...  8.02 us
    all_to_all x2, waiting for transfers between devices, swap(): return lax.all_to_all(value, axes, split_axis=0, concat_axis=0, tiled=True)  7.2 us
    all_to_all x2, starting transfers between devices, swap(): return lax.all_to_all(value, axes, split_axis=0, concat_axis=0, tiled=True)  6.82 us
    ppermute x3, starting transfers between devices, partner(): lax.ppermute(value, 'blk', [(i, i ^ 1 << bit) for i in range(members)])  6.58 us
    ppermute x3, waiting for transfers between devices, partner(): lax.ppermute(value, 'blk', [(i, i ^ 1 << bit) for i in range(members)])  2.31 us
  transfers between devices with their start and end apart: 5, of which 3 were waited for; matrix products, arithmetic and copies ran while one was open for 0% of the time, Pallas kernels for 14%

profile of v19, /device:TPU:0, one launch (start us, length us, event | category | flops | bytes accessed | tf_op | source)
XLA Modules:
  0.0 41.2 jit_solution(2446392973285016536)
XLA Ops:
  0.6 4.1 %collective-permute-start = (bf16[64,512]{1,0:T(8,128)(2,1)}, bf16[64,512]{1,0:T(8,128)(2,1)S(1)}, u32[]{:S(2)}, u32[]{:S(2)}) collective-permute-start(bf16[64,512]{1,0:T(8,128)(2,1)} %bitcast.13), channel_id=1, source_target_pairs={{0,4},{1,5},{2,6},{3,7},{4,0},{5,1},{6,2},{7,3},{8,12},{9,13},{10,... | collective-permute-start | bytes 196616 | tf_op jit(solution)/shard_map/ppermute | solution.py:444
  4.7 1.8 %shard_map.167 = (f32[8,16,128]{2,1,0:T(8,128)}, s32[1,512]{1,0:T(1,128)S(1)}, s32[1,512]{1,0:T(1,128)S(1)}, bf16[64,512]{1,0:T(8,128)(2,1)S(1)}) custom-call(s32[1,512]{1,0:T(1,128)} %bitcast.15, f32[1,512]{1,0:T(1,128)} %bitcast.16, f32[1,512]{1,0:T(1,128)} %bitcast.17, f32[1,512]{1,0:T(1,128)} %bitcast.18, f32[1,512]{1,0:T(1,128)} %bitcast.19, ...), custom_call_target="tpu_custom_call" | custom-call | flops 1000 | bytes 1000 | tf_op jit(solution)/shard_map/pallas_call | solution.py:397
  6.5 3.8 %all-to-all-start = ((f32[8,16,128]{2,1,0:T(8,128)}), f32[8,16,128]{2,1,0:T(8,128)S(1)}, u32[]{:S(2)}, u32[]{:S(2)}) async-start(f32[8,16,128]{2,1,0:T(8,128)} %get-tuple-element.18), calls=%async_computation | async-start | bytes 131072 | tf_op jit(solution)/shard_map/all_to_all | solution.py:441
  11.0 0.0 collective-permute-done.came_ref
  11.0 2.1 %collective-permute-start.1 = (bf16[96,512]{1,0:T(8,128)(2,1)S(1)}, bf16[96,512]{1,0:T(8,128)(2,1)S(1)}, u32[]{:S(2)}, u32[]{:S(2)}) collective-permute-start(bf16[96,512]{1,0:T(8,128)(2,1)S(1)} %shard_map.168.early_ref.held_ref), channel_id=1, source_target_pairs={{0,1},{1,0},{2,3},{3,2},{4,5},{5,4},{6,7},{7,6},{8,9},{9,8},{10,11... | collective-permute-start | bytes 294920 | tf_op jit(solution)/shard_map/ppermute | solution.py:444
  13.1 1.5 %shard_map.169 = (f32[3,8,512]{2,1,0:T(8,128)S(1)}, f32[8,64]{1,0:T(8,128)S(1)}, bf16[3,512,512]{2,1,0:T(8,128)(2,1)S(1)}, bf16[64,512]{1,0:T(8,128)(2,1)S(1)}, ...) custom-call(bf16[96,512]{1,0:T(8,128)(2,1)S(1)} %shard_map.168.early_ref.held_ref, s32[3]{0:T(128)} %refs_0_.2, ...), custom_call_target="tpu_custom_call" | custom-call | flops 1073741824 | bytes 4194304 | tf_op jit(solution)/shard_map/pallas_call | solution.py:397
  14.6 2.6 %all-to-all-done.got_ref = f32[8,16,128]{2,1,0:T(8,128)S(1)} async-done(((f32[8,16,128]{2,1,0:T(8,128)}), f32[8,16,128]{2,1,0:T(8,128)S(1)}, u32[]{:S(2)}, u32[]{:S(2)}) %all-to-all-start) | async-done | bytes 65568 | tf_op jit(solution)/shard_map/all_to_all | solution.py:441
  17.2 2.0 %shard_map.170 = (f32[8,512]{1,0:T(8,128)S(1)}, f32[8,512]{1,0:T(8,128)S(1)}, s32[1,512]{1,0:T(1,128)S(1)}, f32[32,1,640]{2,1,0:T(1,128)}) custom-call(f32[8,16,128]{2,1,0:T(8,128)S(1)} %all-to-all-done.got_ref, bf16[64,512]{1,0:T(8,128)(2,1)S(1)} %get-tuple-element.21.coarse_v_ref, s32[1]{0:T(128)S(6)} %copy.18.refs_0_.refs_2_, ...), custom_call_target="tpu_custom_call" | custom-call | flops 8589934592 | bytes 33554432 | tf_op jit(solution)/shard_map/pallas_call | solution.py:397
  19.2 0.0 collective-permute-done.1.came_ref
  19.2 0.4 collective-permute-start.2
  19.6 3.0 %all-to-all-start.1 = ((f32[32,1,640]{2,1,0:T(1,128)}), f32[32,1,640]{2,1,0:T(1,128)S(1)}, u32[]{:S(2)}, u32[]{:S(2)}) async-start(f32[32,1,640]{2,1,0:T(1,128)} %get-tuple-element.30), calls=%async_computation.1 | async-start | bytes 163840 | tf_op jit(solution)/shard_map/all_to_all | solution.py:441
  22.6 2.3 %collective-permute-done.2.came_ref.refs_1_ = bf16[192,512]{1,0:T(8,128)(2,1)S(1)} collective-permute-done((bf16[192,512]{1,0:T(8,128)(2,1)S(1)}, bf16[192,512]{1,0:T(8,128)(2,1)S(1)}, u32[]{:S(2)}, u32[]{:S(2)}) %collective-permute-start.2) | collective-permute-done | bytes 196640 | tf_op jit(solution)/shard_map/ppermute | solution.py:444
  25.0 0.6 %shard_map.172.elem_bases_ref = bf16[48,512]{1,0:T(8,128)(2,1)S(1)} custom-call(bf16[192,512]{1,0:T(8,128)(2,1)S(1)} %shard_map.171.held_ref.refs_0_, bf16[192,512]{1,0:T(8,128)(2,1)S(1)} %collective-permute-done.2.came_ref.refs_1_, s32[1,512]{1,0:T(1,128)S(1)} %get-tuple-element.20.refs_0_.slot_ref, s32[1,512]{1,0:T(1,128)S(1)} %get-tuple-element.31.elem_row_ref), custom_call_target="tpu_custom_call" | custom-call | flops 17179869184 | bytes 67108864 | tf_op jit(solution)/shard_map/pallas_call | solution.py:397
  25.5 4.6 %all-to-all-done.1.all_ref = f32[32,1,640]{2,1,0:T(1,128)S(1)} async-done(((f32[32,1,640]{2,1,0:T(1,128)}), f32[32,1,640]{2,1,0:T(1,128)S(1)}, u32[]{:S(2)}, u32[]{:S(2)}) %all-to-all-start.1) | async-done | bytes 81952 | tf_op jit(solution)/shard_map/all_to_all | solution.py:441
  30.1 1.2 %shard_map.173 = f32[32,4,128]{2,1,0:T(4,128)S(1)} custom-call(f32[8,512]{1,0:T(8,128)S(1)} %get-tuple-element.27.state_ref, f32[8,512]{1,0:T(8,128)S(1)} %get-tuple-element.28.factor_ref, s32[1,512]{1,0:T(1,128)S(1)} %get-tuple-element.29.refs_0_.rows_ref, f32[32,1,640]{2,1,0:T(1,128)S(1)} %all-to-all-done.1.all_ref, ...), custom_call_target="tpu_custom_call" | custom-call | flops 1000 | bytes 1000 | tf_op jit(solution)/shard_map/pallas_call | solution.py:397
  31.3 9.0 %all_to_all.15.got_ref = f32[32,4,128]{2,1,0:T(4,128)S(1)} all-to-all(f32[32,4,128]{2,1,0:T(4,128)S(1)} %shard_map.173), channel_id=1, replica_groups=mesh['leaf'=4,'blk'=8] {'leaf','blk'}, dimensions={0} | all-to-all | bytes 131072 | tf_op jit(solution)/shard_map/all_to_all | solution.py:441
  40.3 0.9 %shard_map.174 = (f32[1,512]{1,0:T(1,128)}, f32[1,512]{1,0:T(1,128)}) custom-call(f32[32,4,128]{2,1,0:T(4,128)S(1)} %all_to_all.15.got_ref, s32[1,512]{1,0:T(1,128)S(1)} %get-tuple-element.20.refs_0_.slot_ref, bf16[48,512]{1,0:T(8,128)(2,1)S(1)} %shard_map.172.elem_bases_ref), custom_call_target="tpu_custom_call" | custom-call | flops 1000 | bytes 1000 | tf_op jit(solution)/shard_map/pallas_call | solution.py:397
  (2 shorter events, 0.0 us)
Async XLA Ops:
  0.6 10.4 %collective-permute-start = (bf16[64,512]{1,0:T(8,128)(2,1)}, bf16[64,512]{1,0:T(8,128)(2,1)S(1)}, u32[]{:S(2)}, u32[]{:S(2)}) collective-permute-start(bf16[64,512]{1,0:T(8,128)(2,1)} %bitcast.13), channel_id=1, source_target_pairs={{0,4},{1,5},{2,6},{3,7},{4,0},{5,1},{6,2},{7,3},{8,12},{9,13},{10,... | collective-permute-start | bytes 196616 | tf_op jit(solution)/shard_map/ppermute | solution.py:444
  6.5 10.7 %all-to-all-start = ((f32[8,16,128]{2,1,0:T(8,128)}), f32[8,16,128]{2,1,0:T(8,128)S(1)}, u32[]{:S(2)}, u32[]{:S(2)}) async-start(f32[8,16,128]{2,1,0:T(8,128)} %get-tuple-element.18), calls=%async_computation | async-start | bytes 131072 | tf_op jit(solution)/shard_map/all_to_all | solution.py:441
  11.0 8.2 %collective-permute-start.1 = (bf16[96,512]{1,0:T(8,128)(2,1)S(1)}, bf16[96,512]{1,0:T(8,128)(2,1)S(1)}, u32[]{:S(2)}, u32[]{:S(2)}) collective-permute-start(bf16[96,512]{1,0:T(8,128)(2,1)S(1)} %shard_map.168.early_ref.held_ref), channel_id=1, source_target_pairs={{0,1},{1,0},{2,3},{3,2},{4,5},{5,4},{6,7},{7,6},{8,9},{9,8},{10,11... | collective-permute-start | bytes 294920 | tf_op jit(solution)/shard_map/ppermute | solution.py:444
  19.2 5.7 %collective-permute-start.2 = (bf16[192,512]{1,0:T(8,128)(2,1)S(1)}, bf16[192,512]{1,0:T(8,128)(2,1)S(1)}, u32[]{:S(2)}, u32[]{:S(2)}) collective-permute-start(bf16[192,512]{1,0:T(8,128)(2,1)S(1)} %shard_map.171.held_ref.refs_0_), channel_id=1, source_target_pairs={{0,2},{1,3},{2,0},{3,1},{4,6},{5,7},{6,4},{7,5},{8,10},{9,11},{10,... | collective-permute-start | bytes 589832 | tf_op jit(solution)/shard_map/ppermute | solution.py:444
  19.6 10.5 %all-to-all-start.1 = ((f32[32,1,640]{2,1,0:T(1,128)}), f32[32,1,640]{2,1,0:T(1,128)S(1)}, u32[]{:S(2)}, u32[]{:S(2)}) async-start(f32[32,1,640]{2,1,0:T(1,128)} %get-tuple-element.30), calls=%async_computation.1 | async-start | bytes 163840 | tf_op jit(solution)/shard_map/all_to_all | solution.py:441

commit v20 on v19

--- a/solution.py
+++ b/solution.py
@@ -148,7 +148,14 @@
 def load_kernel(early_ref, *refs):
     scalar_refs, weight_refs, near_mask_ref, far_mask_ref = refs[:3], refs[3:7], refs[7], refs[8]
     weight_outs, scalar_bufs, sems = refs[9:13], refs[13:16], refs[16]
-    copies = start_copies([*scalar_refs, *weight_refs], [*scalar_bufs, *weight_outs], sems)
+    sources, targets = [*scalar_refs, *weight_refs[:3]], [*scalar_bufs, *weight_outs[:3]]
+    coarse_v_ref, coarse_v_out = weight_refs[3], weight_outs[3]
+    groups, rank = coarse_v_ref.shape[0], coarse_v_ref.shape[1]
+    for shift in range(groups):
+        place = (shift - 1) % groups * rank
+        sources.append(coarse_v_ref.at[lax.axis_index("leaf") ^ shift])
+        targets.append(coarse_v_out.at[pl.ds(place, rank), :])
+    copies = start_copies(sources, targets, sems)
     for copy in copies[:3]:
         copy.wait()
     near_col, far_col, far_rank = scalar_bufs
@@ -179,31 +186,26 @@
 
 
 def inside_rows(deficits, near_count, near_ref, far_u_ref, far_v_ref, near_mask_ref, far_mask_ref):
-    total = jnp.zeros((near_ref.shape[1], deficits.shape[0]), jnp.float32)
+    total = jnp.zeros(deficits.shape, jnp.float32)
     for slot in range(near_ref.shape[0]):
         live = jnp.where(slot < near_count[0], 1.0, 0.0)
         source = (deficits * (near_mask_ref[slot] * live)).astype(jnp.bfloat16)
-        total = total + dot(near_ref[slot], source, NT)
-    near = jnp.sum(total.T, axis=0, keepdims=True)
+        total = total + dot(source, near_ref[slot], NT)
     project = dot(deficits.astype(jnp.bfloat16), far_v_ref[...], NT) * far_mask_ref[...]
     project = jnp.sum(project, axis=0, keepdims=True)
     project = jnp.broadcast_to(project, (8, project.shape[1])).astype(jnp.bfloat16)
     far = dot(project, far_u_ref[...], NN)
-    return near + far[0:1]
-
-
-def coefficients(sums, rank):
-    groups, width = len(sums), sums[0].shape[1]
+    return jnp.sum(total, axis=0, keepdims=True) + far[0:1]
+
+
+def coefficients(parts_of, groups, rank):
     mine = lax.axis_index("leaf")
-    table = padded(sums, -(-groups // 8) * 8)
-    lane = lax.broadcasted_iota(jnp.int32, table.shape, 1) // rank
-    row = lax.broadcasted_iota(jnp.int32, table.shape, 0)
-    table = jnp.where(lane == mine, table, 0.0).astype(jnp.bfloat16)
-    across = lax.broadcasted_iota(jnp.int32, (width, width), 0) % rank
-    down = lax.broadcasted_iota(jnp.int32, (width, width), 1) % rank
-    spread = dot(table, jnp.where(across == down, 1.0, 0.0).astype(jnp.bfloat16), NN)
-    weights = jnp.sum(jnp.where(row == mine ^ (lane + 1), spread, 0.0), axis=0, keepdims=True)
-    return weights[:, 0:width - rank]
+    lane = lax.broadcasted_iota(jnp.int32, (1, groups * rank), 1) // rank
+    weights = jnp.zeros(lane.shape, jnp.float32)
+    for shift in range(1, groups):
+        total = jnp.sum(parts_of(mine ^ shift), axis=0, keepdims=True)
+        weights = jnp.where(lane == shift - 1, total, weights)
+    return weights[:, 0:(groups - 1) * rank]
 
 
 def coarse_all(weights, members, bases_refs):
@@ -336,14 +338,11 @@
     members, elem_count = refs[6].shape[1], state_ref.shape[1]
     width = coarse_v_ref.shape[0]
     mine, me = lax.axis_index("leaf"), lax.axis_index("blk")
-    sums = [
-        jnp.sum(
-            all_ref[group * members:(group + 1) * members, 0, elem_count:elem_count + width],
-            axis=0, keepdims=True,
-        )
-        for group in range(groups)
-    ]
-    weights = coefficients(sums, width // groups)
+
+    def parts_of(group):
+        return all_ref[pl.ds(group * members, members), 0, elem_count:elem_count + width]
+
+    weights = coefficients(parts_of, groups, width // groups)
     own = all_ref[pl.ds(mine * members, members), 0, 0:elem_count]
     coarse = coarse_all(weights, members, bases_refs)
     u2_all = own + factor_ref[...] * coarse
@@ -376,12 +375,13 @@
     first = lax.axis_index("leaf") * members
     flat = peer_lanes(got_ref, first, members, 3, elem_count)
     out = gathered(padded([flat[i:i + 1] for i in range(3)], 8), slot_ref[...])
-    sums = []
-    for group in range(groups):
-        total = jnp.sum(got_ref[group * members:(group + 1) * members], axis=0)
-        lines = [total[3 + i:4 + i, :] for i in range(pl.cdiv(width, LANES))]
-        sums.append(jnp.concatenate(lines, axis=1)[:, 0:width])
-    weights = coefficients(sums, width // groups)
+
+    def parts_of(group):
+        sent = pl.ds(group * members, members)
+        lines = [got_ref[sent, 3 + i, :] for i in range(pl.cdiv(width, LANES))]
+        return jnp.concatenate(lines, axis=1)[:, 0:width]
+
+    weights = coefficients(parts_of, groups, width // groups)
     weights = jnp.broadcast_to(weights, (8, weights.shape[1])).astype(jnp.bfloat16)
     coarse = dot(weights, elem_bases_ref[...], NN)[0:1]
     u_ref[...] = out[0:1] + out[1:2] * coarse
@@ -449,8 +449,7 @@
     ]
     scalar_args = [near_col, far_col, far_rank]
     weights = [
-        near_blocks, far_u.reshape(-1, leaf_size), far_v.reshape(-1, leaf_size),
-        coarse_v.reshape(width, elems),
+        near_blocks, far_u.reshape(-1, leaf_size), far_v.reshape(-1, leaf_size), coarse_v
     ]
     far_rows = weights[1].shape[0]
     bases = coarse_u.reshape(width, elems)
@@ -477,11 +476,12 @@
         (
             shape(near_blocks.shape[0], members, leaf_size),
             shape(members, far_rows),
-            *[shape(*value.shape, dtype=jnp.bfloat16) for value in weights],
+            *[shape(*value.shape, dtype=jnp.bfloat16) for value in weights[:3]],
+            shape(width, elems, dtype=jnp.bfloat16),
         ),
         early, *scalar_args, *weights, far=range(1, 8),
         scratch=[SMEM(value.shape, value.dtype) for value in scalar_args]
-        + [pltpu.SemaphoreType.DMA((7,))],
+        + [pltpu.SemaphoreType.DMA((6 + groups,))],
         flops=1 << 30, moved=1 << 22,
     )
     fields = near_count, near, far_u, far_v, near_mask, far_mask

time: 41.6 us -> 41.1 us (0.988)
  Pallas kernels: 8.02 us -> 7.6 us
    pallas_call x8, Pallas kernels: 8.02 us -> 7.6 us  [call(): pl.pallas_call(kernel, out_shape=outs, in_specs=[pl.BlockSpec(memory_spac...]
where the time goes in v20:
time: 41.1 us; the launch traced here: 40.8 us
  starting transfers between devices  13.4 us (33%)
  waiting for transfers between devices  9.48 us (23%)
  blocking collectives  8.96 us (22%)
  Pallas kernels  7.6 us (18%)
  between operations  1.34 us (3%)
    all_to_all x1, blocking collectives, swap(): return lax.all_to_all(value, axes, split_axis=0, concat_axis=0, tiled=True)  8.96 us
    pallas_call x8, Pallas kernels, call(): pl.pallas_call(kernel, out_shape=outs, in_specs=[pl.BlockSpec(memory_spac...  7.6 us
    all_to_all x2, waiting for transfers between devices, swap(): return lax.all_to_all(value, axes, split_axis=0, concat_axis=0, tiled=True)  7.18 us
    all_to_all x2, starting transfers between devices, swap(): return lax.all_to_all(value, axes, split_axis=0, concat_axis=0, tiled=True)  6.84 us
    ppermute x3, starting transfers between devices, partner(): lax.ppermute(value, 'blk', [(i, i ^ 1 << bit) for i in range(members)])  6.58 us
    ppermute x3, waiting for transfers between devices, partner(): lax.ppermute(value, 'blk', [(i, i ^ 1 << bit) for i in range(members)])  2.3 us
  transfers between devices with their start and end apart: 5, of which 3 were waited for; matrix products, arithmetic and copies ran while one was open for 0% of the time, Pallas kernels for 14%

profile of v20, /device:TPU:0, one launch (start us, length us, event | category | flops | bytes accessed | tf_op | source)
XLA Modules:
  0.0 40.8 jit_solution(11537387602364067682)
XLA Ops:
  0.6 4.1 %collective-permute-start = (bf16[64,512]{1,0:T(8,128)(2,1)}, bf16[64,512]{1,0:T(8,128)(2,1)S(1)}, u32[]{:S(2)}, u32[]{:S(2)}) collective-permute-start(bf16[64,512]{1,0:T(8,128)(2,1)} %bitcast.12), channel_id=1, source_target_pairs={{0,4},{1,5},{2,6},{3,7},{4,0},{5,1},{6,2},{7,3},{8,12},{9,13},{10,... | collective-permute-start | bytes 196616 | tf_op jit(solution)/shard_map/ppermute | solution.py:444
  4.7 1.8 %shard_map.167 = (f32[8,16,128]{2,1,0:T(8,128)}, s32[1,512]{1,0:T(1,128)S(1)}, s32[1,512]{1,0:T(1,128)S(1)}, bf16[64,512]{1,0:T(8,128)(2,1)S(1)}) custom-call(s32[1,512]{1,0:T(1,128)} %bitcast.14, f32[1,512]{1,0:T(1,128)} %bitcast.15, f32[1,512]{1,0:T(1,128)} %bitcast.16, f32[1,512]{1,0:T(1,128)} %bitcast.17, f32[1,512]{1,0:T(1,128)} %bitcast.18, ...), custom_call_target="tpu_custom_call" | custom-call | flops 1000 | bytes 1000 | tf_op jit(solution)/shard_map/pallas_call | solution.py:397
  6.5 3.8 %all-to-all-start = ((f32[8,16,128]{2,1,0:T(8,128)}), f32[8,16,128]{2,1,0:T(8,128)S(1)}, u32[]{:S(2)}, u32[]{:S(2)}) async-start(f32[8,16,128]{2,1,0:T(8,128)} %get-tuple-element.18), calls=%async_computation | async-start | bytes 131072 | tf_op jit(solution)/shard_map/all_to_all | solution.py:441
  11.0 0.0 collective-permute-done.came_ref
  11.0 2.1 %collective-permute-start.1 = (bf16[96,512]{1,0:T(8,128)(2,1)S(1)}, bf16[96,512]{1,0:T(8,128)(2,1)S(1)}, u32[]{:S(2)}, u32[]{:S(2)}) collective-permute-start(bf16[96,512]{1,0:T(8,128)(2,1)S(1)} %shard_map.168.early_ref.held_ref), channel_id=1, source_target_pairs={{0,1},{1,0},{2,3},{3,2},{4,5},{5,4},{6,7},{7,6},{8,9},{9,8},{10,11... | collective-permute-start | bytes 294920 | tf_op jit(solution)/shard_map/ppermute | solution.py:444
  13.1 1.5 %shard_map.169 = (f32[3,8,512]{2,1,0:T(8,128)S(1)}, f32[8,64]{1,0:T(8,128)S(1)}, bf16[3,512,512]{2,1,0:T(8,128)(2,1)S(1)}, bf16[64,512]{1,0:T(8,128)(2,1)S(1)}, ...) custom-call(bf16[96,512]{1,0:T(8,128)(2,1)S(1)} %shard_map.168.early_ref.held_ref, s32[3]{0:T(128)} %refs_0_.2, ...), custom_call_target="tpu_custom_call" | custom-call | flops 1073741824 | bytes 4194304 | tf_op jit(solution)/shard_map/pallas_call | solution.py:397
  14.6 2.6 %all-to-all-done.got_ref = f32[8,16,128]{2,1,0:T(8,128)S(1)} async-done(((f32[8,16,128]{2,1,0:T(8,128)}), f32[8,16,128]{2,1,0:T(8,128)S(1)}, u32[]{:S(2)}, u32[]{:S(2)}) %all-to-all-start) | async-done | bytes 65568 | tf_op jit(solution)/shard_map/all_to_all | solution.py:441
  17.2 1.8 %shard_map.170 = (f32[8,512]{1,0:T(8,128)S(1)}, f32[8,512]{1,0:T(8,128)S(1)}, s32[1,512]{1,0:T(1,128)S(1)}, f32[32,1,640]{2,1,0:T(1,128)}) custom-call(f32[8,16,128]{2,1,0:T(8,128)S(1)} %all-to-all-done.got_ref, bf16[64,512]{1,0:T(8,128)(2,1)S(1)} %get-tuple-element.21.coarse_v_ref, s32[1]{0:T(128)S(6)} %copy.18.refs_0_.refs_2_, ...), custom_call_target="tpu_custom_call" | custom-call | flops 8589934592 | bytes 33554432 | tf_op jit(solution)/shard_map/pallas_call | solution.py:397
  19.0 0.0 collective-permute-done.1.came_ref
  19.1 0.4 collective-permute-start.2
  19.4 3.0 %all-to-all-start.1 = ((f32[32,1,640]{2,1,0:T(1,128)}), f32[32,1,640]{2,1,0:T(1,128)S(1)}, u32[]{:S(2)}, u32[]{:S(2)}) async-start(f32[32,1,640]{2,1,0:T(1,128)} %get-tuple-element.30), calls=%async_computation.1 | async-start | bytes 163840 | tf_op jit(solution)/shard_map/all_to_all | solution.py:441
  22.5 2.3 %collective-permute-done.2.came_ref.refs_1_ = bf16[192,512]{1,0:T(8,128)(2,1)S(1)} collective-permute-done((bf16[192,512]{1,0:T(8,128)(2,1)S(1)}, bf16[192,512]{1,0:T(8,128)(2,1)S(1)}, u32[]{:S(2)}, u32[]{:S(2)}) %collective-permute-start.2) | collective-permute-done | bytes 196640 | tf_op jit(solution)/shard_map/ppermute | solution.py:444
  24.8 0.6 %shard_map.172.elem_bases_ref = bf16[48,512]{1,0:T(8,128)(2,1)S(1)} custom-call(bf16[192,512]{1,0:T(8,128)(2,1)S(1)} %shard_map.171.held_ref.refs_0_, bf16[192,512]{1,0:T(8,128)(2,1)S(1)} %collective-permute-done.2.came_ref.refs_1_, s32[1,512]{1,0:T(1,128)S(1)} %get-tuple-element.20.refs_0_.slot_ref, s32[1,512]{1,0:T(1,128)S(1)} %get-tuple-element.31.elem_row_ref), custom_call_target="tpu_custom_call" | custom-call | flops 17179869184 | bytes 67108864 | tf_op jit(solution)/shard_map/pallas_call | solution.py:397
  25.4 4.6 %all-to-all-done.1.all_ref = f32[32,1,640]{2,1,0:T(1,128)S(1)} async-done(((f32[32,1,640]{2,1,0:T(1,128)}), f32[32,1,640]{2,1,0:T(1,128)S(1)}, u32[]{:S(2)}, u32[]{:S(2)}) %all-to-all-start.1) | async-done | bytes 81952 | tf_op jit(solution)/shard_map/all_to_all | solution.py:441
  29.9 1.1 %shard_map.173 = f32[32,4,128]{2,1,0:T(4,128)S(1)} custom-call(f32[8,512]{1,0:T(8,128)S(1)} %get-tuple-element.27.state_ref, f32[8,512]{1,0:T(8,128)S(1)} %get-tuple-element.28.factor_ref, s32[1,512]{1,0:T(1,128)S(1)} %get-tuple-element.29.refs_0_.rows_ref, f32[32,1,640]{2,1,0:T(1,128)S(1)} %all-to-all-done.1.all_ref, ...), custom_call_target="tpu_custom_call" | custom-call | flops 1000 | bytes 1000 | tf_op jit(solution)/shard_map/pallas_call | solution.py:397
  31.0 9.0 %all_to_all.15.got_ref = f32[32,4,128]{2,1,0:T(4,128)S(1)} all-to-all(f32[32,4,128]{2,1,0:T(4,128)S(1)} %shard_map.173), channel_id=1, replica_groups=mesh['leaf'=4,'blk'=8] {'leaf','blk'}, dimensions={0} | all-to-all | bytes 131072 | tf_op jit(solution)/shard_map/all_to_all | solution.py:441
  40.0 0.8 %shard_map.174 = (f32[1,512]{1,0:T(1,128)}, f32[1,512]{1,0:T(1,128)}) custom-call(f32[32,4,128]{2,1,0:T(4,128)S(1)} %all_to_all.15.got_ref, s32[1,512]{1,0:T(1,128)S(1)} %get-tuple-element.20.refs_0_.slot_ref, bf16[48,512]{1,0:T(8,128)(2,1)S(1)} %shard_map.172.elem_bases_ref), custom_call_target="tpu_custom_call" | custom-call | flops 1000 | bytes 1000 | tf_op jit(solution)/shard_map/pallas_call | solution.py:397
  (2 shorter events, 0.0 us)
Async XLA Ops:
  0.6 10.4 %collective-permute-start = (bf16[64,512]{1,0:T(8,128)(2,1)}, bf16[64,512]{1,0:T(8,128)(2,1)S(1)}, u32[]{:S(2)}, u32[]{:S(2)}) collective-permute-start(bf16[64,512]{1,0:T(8,128)(2,1)} %bitcast.12), channel_id=1, source_target_pairs={{0,4},{1,5},{2,6},{3,7},{4,0},{5,1},{6,2},{7,3},{8,12},{9,13},{10,... | collective-permute-start | bytes 196616 | tf_op jit(solution)/shard_map/ppermute | solution.py:444
  6.5 10.7 %all-to-all-start = ((f32[8,16,128]{2,1,0:T(8,128)}), f32[8,16,128]{2,1,0:T(8,128)S(1)}, u32[]{:S(2)}, u32[]{:S(2)}) async-start(f32[8,16,128]{2,1,0:T(8,128)} %get-tuple-element.18), calls=%async_computation | async-start | bytes 131072 | tf_op jit(solution)/shard_map/all_to_all | solution.py:441
  11.0 8.0 %collective-permute-start.1 = (bf16[96,512]{1,0:T(8,128)(2,1)S(1)}, bf16[96,512]{1,0:T(8,128)(2,1)S(1)}, u32[]{:S(2)}, u32[]{:S(2)}) collective-permute-start(bf16[96,512]{1,0:T(8,128)(2,1)S(1)} %shard_map.168.early_ref.held_ref), channel_id=1, source_target_pairs={{0,1},{1,0},{2,3},{3,2},{4,5},{5,4},{6,7},{7,6},{8,9},{9,8},{10,11... | collective-permute-start | bytes 294920 | tf_op jit(solution)/shard_map/ppermute | solution.py:444
  19.1 5.7 %collective-permute-start.2 = (bf16[192,512]{1,0:T(8,128)(2,1)S(1)}, bf16[192,512]{1,0:T(8,128)(2,1)S(1)}, u32[]{:S(2)}, u32[]{:S(2)}) collective-permute-start(bf16[192,512]{1,0:T(8,128)(2,1)S(1)} %shard_map.171.held_ref.refs_0_), channel_id=1, source_target_pairs={{0,2},{1,3},{2,0},{3,1},{4,6},{5,7},{6,4},{7,5},{8,10},{9,11},{10,... | collective-permute-start | bytes 589832 | tf_op jit(solution)/shard_map/ppermute | solution.py:444
  19.4 10.5 %all-to-all-start.1 = ((f32[32,1,640]{2,1,0:T(1,128)}), f32[32,1,640]{2,1,0:T(1,128)S(1)}, u32[]{:S(2)}, u32[]{:S(2)}) async-start(f32[32,1,640]{2,1,0:T(1,128)} %get-tuple-element.30), calls=%async_computation.1 | async-start | bytes 163840 | tf_op jit(solution)/shard_map/all_to_all | solution.py:441

commit v21 on v20

--- a/solution.py
+++ b/solution.py
@@ -482,7 +482,6 @@
         early, *scalar_args, *weights, far=range(1, 8),
         scratch=[SMEM(value.shape, value.dtype) for value in scalar_args]
         + [pltpu.SemaphoreType.DMA((6 + groups,))],
-        flops=1 << 30, moved=1 << 22,
     )
     fields = near_count, near, far_u, far_v, near_mask, far_mask
     state, factor, rows, out = call(
@@ -495,7 +494,7 @@
         ),
         swap(sent, "blk"), coarse_v, *fields, scalars=(2,),
         scratch=[VMEM((2, members * (elems // LANES), LANES), jnp.float32)],
-        flops=1 << 33, moved=1 << 25,
+        flops=1 << 20, moved=1 << 22,
     )
     for bit in steps[1:-1]:
         bases = call(

time: 41.1 us -> 41.1 us (level)
  no operation moved by 1% of the time
where the time goes in v21:
time: 41.1 us; the launch traced here: 40.8 us
  starting transfers between devices  13.4 us (33%)
  waiting for transfers between devices  9.5 us (23%)
  blocking collectives  8.96 us (22%)
  Pallas kernels  7.61 us (19%)
  between operations  1.34 us (3%)
    all_to_all x1, blocking collectives, swap(): return lax.all_to_all(value, axes, split_axis=0, concat_axis=0, tiled=True)  8.96 us
    pallas_call x8, Pallas kernels, call(): pl.pallas_call(kernel, out_shape=outs, in_specs=[pl.BlockSpec(memory_spac...  7.61 us
    all_to_all x2, waiting for transfers between devices, swap(): return lax.all_to_all(value, axes, split_axis=0, concat_axis=0, tiled=True)  7.2 us
    all_to_all x2, starting transfers between devices, swap(): return lax.all_to_all(value, axes, split_axis=0, concat_axis=0, tiled=True)  6.94 us
    ppermute x3, starting transfers between devices, partner(): lax.ppermute(value, 'blk', [(i, i ^ 1 << bit) for i in range(members)])  6.45 us
    ppermute x3, waiting for transfers between devices, partner(): lax.ppermute(value, 'blk', [(i, i ^ 1 << bit) for i in range(members)])  2.3 us
  transfers between devices with their start and end apart: 5, of which 3 were waited for; matrix products, arithmetic and copies ran while one was open for 0% of the time, Pallas kernels for 14%

profile of v21, /device:TPU:0, one launch (start us, length us, event | category | flops | bytes accessed | tf_op | source)
XLA Modules:
  0.0 40.8 jit_solution(14449339711218190283)
XLA Ops:
  0.6 4.1 %collective-permute-start = (bf16[64,512]{1,0:T(8,128)(2,1)}, bf16[64,512]{1,0:T(8,128)(2,1)S(1)}, u32[]{:S(2)}, u32[]{:S(2)}) collective-permute-start(bf16[64,512]{1,0:T(8,128)(2,1)} %bitcast.14), channel_id=1, source_target_pairs={{0,4},{1,5},{2,6},{3,7},{4,0},{5,1},{6,2},{7,3},{8,12},{9,13},{10,... | collective-permute-start | bytes 196616 | tf_op jit(solution)/shard_map/ppermute | solution.py:444
  4.7 1.8 %shard_map.167 = (f32[8,16,128]{2,1,0:T(8,128)}, s32[1,512]{1,0:T(1,128)S(1)}, s32[1,512]{1,0:T(1,128)S(1)}, bf16[64,512]{1,0:T(8,128)(2,1)S(1)}) custom-call(s32[1,512]{1,0:T(1,128)} %bitcast.16, f32[1,512]{1,0:T(1,128)} %bitcast.17, f32[1,512]{1,0:T(1,128)} %bitcast.18, f32[1,512]{1,0:T(1,128)} %bitcast.19, f32[1,512]{1,0:T(1,128)} %bitcast.20, ...), custom_call_target="tpu_custom_call" | custom-call | flops 1000 | bytes 1000 | tf_op jit(solution)/shard_map/pallas_call | solution.py:397
  6.5 3.8 %all-to-all-start = ((f32[8,16,128]{2,1,0:T(8,128)}), f32[8,16,128]{2,1,0:T(8,128)S(1)}, u32[]{:S(2)}, u32[]{:S(2)}) async-start(f32[8,16,128]{2,1,0:T(8,128)} %get-tuple-element.18), calls=%async_computation | async-start | bytes 131072 | tf_op jit(solution)/shard_map/all_to_all | solution.py:441
  10.3 0.0 collective-permute-done.came_ref
  10.4 2.1 %collective-permute-start.1 = (bf16[96,512]{1,0:T(8,128)(2,1)S(1)}, bf16[96,512]{1,0:T(8,128)(2,1)S(1)}, u32[]{:S(2)}, u32[]{:S(2)}) collective-permute-start(bf16[96,512]{1,0:T(8,128)(2,1)S(1)} %shard_map.168.early_ref.held_ref), channel_id=1, source_target_pairs={{0,1},{1,0},{2,3},{3,2},{4,5},{5,4},{6,7},{7,6},{8,9},{9,8},{10,11... | collective-permute-start | bytes 294920 | tf_op jit(solution)/shard_map/ppermute | solution.py:444
  13.1 1.5 %shard_map.169 = (f32[3,8,512]{2,1,0:T(8,128)S(1)}, f32[8,64]{1,0:T(8,128)S(1)}, bf16[3,512,512]{2,1,0:T(8,128)(2,1)S(1)}, bf16[64,512]{1,0:T(8,128)(2,1)S(1)}, ...) custom-call(bf16[96,512]{1,0:T(8,128)(2,1)S(1)} %shard_map.168.early_ref.held_ref, s32[3]{0:T(128)} %refs_0_.2, ...), custom_call_target="tpu_custom_call" | custom-call | flops 1000 | bytes 1000 | tf_op jit(solution)/shard_map/pallas_call | solution.py:397
  14.6 2.6 %all-to-all-done.got_ref = f32[8,16,128]{2,1,0:T(8,128)S(1)} async-done(((f32[8,16,128]{2,1,0:T(8,128)}), f32[8,16,128]{2,1,0:T(8,128)S(1)}, u32[]{:S(2)}, u32[]{:S(2)}) %all-to-all-start) | async-done | bytes 65568 | tf_op jit(solution)/shard_map/all_to_all | solution.py:441
  17.2 1.8 %shard_map.170 = (f32[8,512]{1,0:T(8,128)S(1)}, f32[8,512]{1,0:T(8,128)S(1)}, s32[1,512]{1,0:T(1,128)S(1)}, f32[32,1,640]{2,1,0:T(1,128)}) custom-call(f32[8,16,128]{2,1,0:T(8,128)S(1)} %all-to-all-done.got_ref, bf16[64,512]{1,0:T(8,128)(2,1)S(1)} %get-tuple-element.21.coarse_v_ref, s32[1]{0:T(128)S(6)} %copy.18.refs_0_.refs_2_, ...), custom_call_target="tpu_custom_call" | custom-call | flops 1048576 | bytes 4194304 | tf_op jit(solution)/shard_map/pallas_call | solution.py:397
  19.0 0.0 collective-permute-done.1.came_ref
  19.1 0.3 collective-permute-start.2
  19.3 3.2 %all-to-all-start.1 = ((f32[32,1,640]{2,1,0:T(1,128)}), f32[32,1,640]{2,1,0:T(1,128)S(1)}, u32[]{:S(2)}, u32[]{:S(2)}) async-start(f32[32,1,640]{2,1,0:T(1,128)} %get-tuple-element.30), calls=%async_computation.1 | async-start | bytes 163840 | tf_op jit(solution)/shard_map/all_to_all | solution.py:441
  22.5 2.3 %collective-permute-done.2.came_ref.refs_1_ = bf16[192,512]{1,0:T(8,128)(2,1)S(1)} collective-permute-done((bf16[192,512]{1,0:T(8,128)(2,1)S(1)}, bf16[192,512]{1,0:T(8,128)(2,1)S(1)}, u32[]{:S(2)}, u32[]{:S(2)}) %collective-permute-start.2) | collective-permute-done | bytes 196640 | tf_op jit(solution)/shard_map/ppermute | solution.py:444
  24.8 0.6 %shard_map.172.elem_bases_ref = bf16[48,512]{1,0:T(8,128)(2,1)S(1)} custom-call(bf16[192,512]{1,0:T(8,128)(2,1)S(1)} %shard_map.171.held_ref.refs_0_, bf16[192,512]{1,0:T(8,128)(2,1)S(1)} %collective-permute-done.2.came_ref.refs_1_, s32[1,512]{1,0:T(1,128)S(1)} %get-tuple-element.20.refs_0_.slot_ref, s32[1,512]{1,0:T(1,128)S(1)} %get-tuple-element.31.elem_row_ref), custom_call_target="tpu_custom_call" | custom-call | flops 17179869184 | bytes 67108864 | tf_op jit(solution)/shard_map/pallas_call | solution.py:397
  25.4 4.6 %all-to-all-done.1.all_ref = f32[32,1,640]{2,1,0:T(1,128)S(1)} async-done(((f32[32,1,640]{2,1,0:T(1,128)}), f32[32,1,640]{2,1,0:T(1,128)S(1)}, u32[]{:S(2)}, u32[]{:S(2)}) %all-to-all-start.1) | async-done | bytes 81952 | tf_op jit(solution)/shard_map/all_to_all | solution.py:441
  29.9 1.1 %shard_map.173 = f32[32,4,128]{2,1,0:T(4,128)S(1)} custom-call(f32[8,512]{1,0:T(8,128)S(1)} %get-tuple-element.27.state_ref, f32[8,512]{1,0:T(8,128)S(1)} %get-tuple-element.28.factor_ref, s32[1,512]{1,0:T(1,128)S(1)} %get-tuple-element.29.refs_0_.rows_ref, f32[32,1,640]{2,1,0:T(1,128)S(1)} %all-to-all-done.1.all_ref, ...), custom_call_target="tpu_custom_call" | custom-call | flops 1000 | bytes 1000 | tf_op jit(solution)/shard_map/pallas_call | solution.py:397
  31.0 9.0 %all_to_all.15.got_ref = f32[32,4,128]{2,1,0:T(4,128)S(1)} all-to-all(f32[32,4,128]{2,1,0:T(4,128)S(1)} %shard_map.173), channel_id=1, replica_groups=mesh['leaf'=4,'blk'=8] {'leaf','blk'}, dimensions={0} | all-to-all | bytes 131072 | tf_op jit(solution)/shard_map/all_to_all | solution.py:441
  40.0 0.8 %shard_map.174 = (f32[1,512]{1,0:T(1,128)}, f32[1,512]{1,0:T(1,128)}) custom-call(f32[32,4,128]{2,1,0:T(4,128)S(1)} %all_to_all.15.got_ref, s32[1,512]{1,0:T(1,128)S(1)} %get-tuple-element.20.refs_0_.slot_ref, bf16[48,512]{1,0:T(8,128)(2,1)S(1)} %shard_map.172.elem_bases_ref), custom_call_target="tpu_custom_call" | custom-call | flops 1000 | bytes 1000 | tf_op jit(solution)/shard_map/pallas_call | solution.py:397
  (2 shorter events, 0.0 us)
Async XLA Ops:
  0.6 9.7 %collective-permute-start = (bf16[64,512]{1,0:T(8,128)(2,1)}, bf16[64,512]{1,0:T(8,128)(2,1)S(1)}, u32[]{:S(2)}, u32[]{:S(2)}) collective-permute-start(bf16[64,512]{1,0:T(8,128)(2,1)} %bitcast.14), channel_id=1, source_target_pairs={{0,4},{1,5},{2,6},{3,7},{4,0},{5,1},{6,2},{7,3},{8,12},{9,13},{10,... | collective-permute-start | bytes 196616 | tf_op jit(solution)/shard_map/ppermute | solution.py:444
  6.5 10.7 %all-to-all-start = ((f32[8,16,128]{2,1,0:T(8,128)}), f32[8,16,128]{2,1,0:T(8,128)S(1)}, u32[]{:S(2)}, u32[]{:S(2)}) async-start(f32[8,16,128]{2,1,0:T(8,128)} %get-tuple-element.18), calls=%async_computation | async-start | bytes 131072 | tf_op jit(solution)/shard_map/all_to_all | solution.py:441
  10.4 8.7 %collective-permute-start.1 = (bf16[96,512]{1,0:T(8,128)(2,1)S(1)}, bf16[96,512]{1,0:T(8,128)(2,1)S(1)}, u32[]{:S(2)}, u32[]{:S(2)}) collective-permute-start(bf16[96,512]{1,0:T(8,128)(2,1)S(1)} %shard_map.168.early_ref.held_ref), channel_id=1, source_target_pairs={{0,1},{1,0},{2,3},{3,2},{4,5},{5,4},{6,7},{7,6},{8,9},{9,8},{10,11... | collective-permute-start | bytes 294920 | tf_op jit(solution)/shard_map/ppermute | solution.py:444
  19.1 5.7 %collective-permute-start.2 = (bf16[192,512]{1,0:T(8,128)(2,1)S(1)}, bf16[192,512]{1,0:T(8,128)(2,1)S(1)}, u32[]{:S(2)}, u32[]{:S(2)}) collective-permute-start(bf16[192,512]{1,0:T(8,128)(2,1)S(1)} %shard_map.171.held_ref.refs_0_), channel_id=1, source_target_pairs={{0,2},{1,3},{2,0},{3,1},{4,6},{5,7},{6,4},{7,5},{8,10},{9,11},{10,... | collective-permute-start | bytes 589832 | tf_op jit(solution)/shard_map/ppermute | solution.py:444
  19.3 10.6 %all-to-all-start.1 = ((f32[32,1,640]{2,1,0:T(1,128)}), f32[32,1,640]{2,1,0:T(1,128)S(1)}, u32[]{:S(2)}, u32[]{:S(2)}) async-start(f32[32,1,640]{2,1,0:T(1,128)} %get-tuple-element.30), calls=%async_computation.1 | async-start | bytes 163840 | tf_op jit(solution)/shard_map/all_to_all | solution.py:441

commit v22 on v21

--- a/solution.py
+++ b/solution.py
@@ -82,11 +82,6 @@
     return jnp.concatenate(
         [row[:, i * LANES:(i + 1) * LANES] for i in range(row.shape[1] // LANES)], axis=0
     )
-
-
-def peer_lanes(ref, first, members, rows, elem_count):
-    width = elem_count // members
-    return jnp.concatenate([ref[first + peer, 0:rows, 0:width] for peer in range(members)], axis=1)
 
 
 def start_copies(sources, targets, sems):
@@ -361,24 +356,37 @@
     u_next = 0.5 * (u + u2) + (inside - sb * k2p) * inverse
     phi_next = phi + 0.5 * TIME_STEP * (k1p + k2p)
     sent = gathered(padded([u_next, inverse, phi_next], 8), rows_ref[...])
-    partial = as_lines(partial_row(deficit, coarse_v_ref))
+    partial = partial_row(deficit, coarse_v_ref)
     peer_rows = elem_count // members
     for device in range(groups * members):
-        peer = device % members
-        sent_ref[device, 0:3, 0:peer_rows] = sent[0:3, peer * peer_rows:(peer + 1) * peer_rows]
-        sent_ref[device, 3:3 + partial.shape[0], :] = partial
+        span = slice(device % members * peer_rows, (device % members + 1) * peer_rows)
+        sent_ref[device, 0:1, 0:peer_rows] = sent[0:1, span]
+        sent_ref[device, 0:1, HALF:HALF + peer_rows] = sent[1:2, span]
+        sent_ref[device, 1:2, 0:peer_rows] = sent[2:3, span]
+        if width <= LANES - HALF:
+            sent_ref[device, 1:2, HALF:HALF + width] = partial[:, 0:width]
+        else:
+            sent_ref[device, 2:2 + partial.shape[1] // LANES, :] = as_lines(partial)
 
 
 def finish_kernel(groups, width, got_ref, slot_ref, elem_bases_ref, u_ref, phi_ref):
     elem_count = slot_ref.shape[1]
     members = got_ref.shape[0] // groups
     first = lax.axis_index("leaf") * members
-    flat = peer_lanes(got_ref, first, members, 3, elem_count)
-    out = gathered(padded([flat[i:i + 1] for i in range(3)], 8), slot_ref[...])
+    peer_rows = elem_count // members
+
+    def side_by_side(row, low):
+        parts = [got_ref[first + peer, row:row + 1, low:low + peer_rows] for peer in range(members)]
+        return jnp.concatenate(parts, axis=1)
+
+    rows = [side_by_side(0, 0), side_by_side(0, HALF), side_by_side(1, 0)]
+    out = gathered(padded(rows, 8), slot_ref[...])
 
     def parts_of(group):
         sent = pl.ds(group * members, members)
-        lines = [got_ref[sent, 3 + i, :] for i in range(pl.cdiv(width, LANES))]
+        if width <= LANES - HALF:
+            return got_ref[sent, 1, HALF:HALF + width]
+        lines = [got_ref[sent, 2 + i, :] for i in range(pl.cdiv(width, LANES))]
         return jnp.concatenate(lines, axis=1)[:, 0:width]
 
     weights = coefficients(parts_of, groups, width // groups)
@@ -434,7 +442,7 @@
     devices = groups * members
     width = groups * rank
     lines = pl.cdiv(width, LANES)
-    sent_rows = 1 << (2 + lines).bit_length()
+    sent_rows = 2 if width <= LANES - HALF else 1 << (1 + lines).bit_length()
     integer = jnp.int32
 
     def swap(value, axes):

time: 41.1 us -> 41.1 us (level)
  no operation moved by 1% of the time
where the time goes in v22:
time: 41.1 us; the launch traced here: 40.8 us
  starting transfers between devices  13.4 us (33%)
  waiting for transfers between devices  9.5 us (23%)
  blocking collectives  8.88 us (22%)
  Pallas kernels  7.64 us (19%)
  between operations  1.34 us (3%)
    all_to_all x1, blocking collectives, swap(): return lax.all_to_all(value, axes, split_axis=0, concat_axis=0, tiled=True)  8.88 us
    pallas_call x8, Pallas kernels, call(): pl.pallas_call(kernel, out_shape=outs, in_specs=[pl.BlockSpec(memory_spac...  7.64 us
    all_to_all x2, waiting for transfers between devices, swap(): return lax.all_to_all(value, axes, split_axis=0, concat_axis=0, tiled=True)  7.2 us
    all_to_all x2, starting transfers between devices, swap(): return lax.all_to_all(value, axes, split_axis=0, concat_axis=0, tiled=True)  6.94 us
    ppermute x3, starting transfers between devices, partner(): lax.ppermute(value, 'blk', [(i, i ^ 1 << bit) for i in range(members)])  6.45 us
    ppermute x3, waiting for transfers between devices, partner(): lax.ppermute(value, 'blk', [(i, i ^ 1 << bit) for i in range(members)])  2.3 us
  transfers between devices with their start and end apart: 5, of which 3 were waited for; matrix products, arithmetic and copies ran while one was open for 0% of the time, Pallas kernels for 14%

profile of v22, /device:TPU:0, one launch (start us, length us, event | category | flops | bytes accessed | tf_op | source)
XLA Modules:
  0.0 40.8 jit_solution(13985349628261563239)
XLA Ops:
  0.6 4.1 %collective-permute-start = (bf16[64,512]{1,0:T(8,128)(2,1)}, bf16[64,512]{1,0:T(8,128)(2,1)S(1)}, u32[]{:S(2)}, u32[]{:S(2)}) collective-permute-start(bf16[64,512]{1,0:T(8,128)(2,1)} %bitcast.14), channel_id=1, source_target_pairs={{0,4},{1,5},{2,6},{3,7},{4,0},{5,1},{6,2},{7,3},{8,12},{9,13},{10,... | collective-permute-start | bytes 196616 | tf_op jit(solution)/shard_map/ppermute | solution.py:452
  4.7 1.8 %shard_map.167 = (f32[8,16,128]{2,1,0:T(8,128)}, s32[1,512]{1,0:T(1,128)S(1)}, s32[1,512]{1,0:T(1,128)S(1)}, bf16[64,512]{1,0:T(8,128)(2,1)S(1)}) custom-call(s32[1,512]{1,0:T(1,128)} %bitcast.16, f32[1,512]{1,0:T(1,128)} %bitcast.17, f32[1,512]{1,0:T(1,128)} %bitcast.18, f32[1,512]{1,0:T(1,128)} %bitcast.19, f32[1,512]{1,0:T(1,128)} %bitcast.20, ...), custom_call_target="tpu_custom_call" | custom-call | flops 1000 | bytes 1000 | tf_op jit(solution)/shard_map/pallas_call | solution.py:405
  6.5 3.8 %all-to-all-start = ((f32[8,16,128]{2,1,0:T(8,128)}), f32[8,16,128]{2,1,0:T(8,128)S(1)}, u32[]{:S(2)}, u32[]{:S(2)}) async-start(f32[8,16,128]{2,1,0:T(8,128)} %get-tuple-element.18), calls=%async_computation | async-start | bytes 131072 | tf_op jit(solution)/shard_map/all_to_all | solution.py:449
  10.3 0.0 collective-permute-done.came_ref
  10.4 2.1 %collective-permute-start.1 = (bf16[96,512]{1,0:T(8,128)(2,1)S(1)}, bf16[96,512]{1,0:T(8,128)(2,1)S(1)}, u32[]{:S(2)}, u32[]{:S(2)}) collective-permute-start(bf16[96,512]{1,0:T(8,128)(2,1)S(1)} %shard_map.168.early_ref.held_ref), channel_id=1, source_target_pairs={{0,1},{1,0},{2,3},{3,2},{4,5},{5,4},{6,7},{7,6},{8,9},{9,8},{10,11... | collective-permute-start | bytes 294920 | tf_op jit(solution)/shard_map/ppermute | solution.py:452
  13.1 1.5 %shard_map.169 = (f32[3,8,512]{2,1,0:T(8,128)S(1)}, f32[8,64]{1,0:T(8,128)S(1)}, bf16[3,512,512]{2,1,0:T(8,128)(2,1)S(1)}, bf16[64,512]{1,0:T(8,128)(2,1)S(1)}, ...) custom-call(bf16[96,512]{1,0:T(8,128)(2,1)S(1)} %shard_map.168.early_ref.held_ref, s32[3]{0:T(128)} %refs_0_.2, ...), custom_call_target="tpu_custom_call" | custom-call | flops 1000 | bytes 1000 | tf_op jit(solution)/shard_map/pallas_call | solution.py:405
  14.6 2.6 %all-to-all-done.got_ref = f32[8,16,128]{2,1,0:T(8,128)S(1)} async-done(((f32[8,16,128]{2,1,0:T(8,128)}), f32[8,16,128]{2,1,0:T(8,128)S(1)}, u32[]{:S(2)}, u32[]{:S(2)}) %all-to-all-start) | async-done | bytes 65568 | tf_op jit(solution)/shard_map/all_to_all | solution.py:449
  17.2 1.8 %shard_map.170 = (f32[8,512]{1,0:T(8,128)S(1)}, f32[8,512]{1,0:T(8,128)S(1)}, s32[1,512]{1,0:T(1,128)S(1)}, f32[32,1,640]{2,1,0:T(1,128)}) custom-call(f32[8,16,128]{2,1,0:T(8,128)S(1)} %all-to-all-done.got_ref, bf16[64,512]{1,0:T(8,128)(2,1)S(1)} %get-tuple-element.21.coarse_v_ref, s32[1]{0:T(128)S(6)} %copy.18.refs_0_.refs_2_, ...), custom_call_target="tpu_custom_call" | custom-call | flops 1048576 | bytes 4194304 | tf_op jit(solution)/shard_map/pallas_call | solution.py:405
  19.0 0.0 collective-permute-done.1.came_ref
  19.1 0.3 collective-permute-start.2
  19.3 3.2 %all-to-all-start.1 = ((f32[32,1,640]{2,1,0:T(1,128)}), f32[32,1,640]{2,1,0:T(1,128)S(1)}, u32[]{:S(2)}, u32[]{:S(2)}) async-start(f32[32,1,640]{2,1,0:T(1,128)} %get-tuple-element.30), calls=%async_computation.1 | async-start | bytes 163840 | tf_op jit(solution)/shard_map/all_to_all | solution.py:449
  22.5 2.3 %collective-permute-done.2.came_ref.refs_1_ = bf16[192,512]{1,0:T(8,128)(2,1)S(1)} collective-permute-done((bf16[192,512]{1,0:T(8,128)(2,1)S(1)}, bf16[192,512]{1,0:T(8,128)(2,1)S(1)}, u32[]{:S(2)}, u32[]{:S(2)}) %collective-permute-start.2) | collective-permute-done | bytes 196640 | tf_op jit(solution)/shard_map/ppermute | solution.py:452
  24.8 0.6 %shard_map.172.elem_bases_ref = bf16[48,512]{1,0:T(8,128)(2,1)S(1)} custom-call(bf16[192,512]{1,0:T(8,128)(2,1)S(1)} %shard_map.171.held_ref.refs_0_, bf16[192,512]{1,0:T(8,128)(2,1)S(1)} %collective-permute-done.2.came_ref.refs_1_, s32[1,512]{1,0:T(1,128)S(1)} %get-tuple-element.20.refs_0_.slot_ref, s32[1,512]{1,0:T(1,128)S(1)} %get-tuple-element.31.elem_row_ref), custom_call_target="tpu_custom_call" | custom-call | flops 17179869184 | bytes 67108864 | tf_op jit(solution)/shard_map/pallas_call | solution.py:405
  25.4 4.6 %all-to-all-done.1.all_ref = f32[32,1,640]{2,1,0:T(1,128)S(1)} async-done(((f32[32,1,640]{2,1,0:T(1,128)}), f32[32,1,640]{2,1,0:T(1,128)S(1)}, u32[]{:S(2)}, u32[]{:S(2)}) %all-to-all-start.1) | async-done | bytes 81952 | tf_op jit(solution)/shard_map/all_to_all | solution.py:449
  29.9 1.1 %shard_map.173 = f32[32,2,128]{2,1,0:T(2,128)S(1)} custom-call(f32[8,512]{1,0:T(8,128)S(1)} %get-tuple-element.27.state_ref, f32[8,512]{1,0:T(8,128)S(1)} %get-tuple-element.28.factor_ref, s32[1,512]{1,0:T(1,128)S(1)} %get-tuple-element.29.refs_0_.rows_ref, f32[32,1,640]{2,1,0:T(1,128)S(1)} %all-to-all-done.1.all_ref, ...), custom_call_target="tpu_custom_call" | custom-call | flops 1000 | bytes 1000 | tf_op jit(solution)/shard_map/pallas_call | solution.py:405
  31.0 8.9 %all_to_all.15.got_ref = f32[32,2,128]{2,1,0:T(2,128)S(1)} all-to-all(f32[32,2,128]{2,1,0:T(2,128)S(1)} %shard_map.173), channel_id=1, replica_groups=mesh['leaf'=4,'blk'=8] {'leaf','blk'}, dimensions={0} | all-to-all | bytes 65536 | tf_op jit(solution)/shard_map/all_to_all | solution.py:449
  39.9 0.8 %shard_map.174 = (f32[1,512]{1,0:T(1,128)}, f32[1,512]{1,0:T(1,128)}) custom-call(f32[32,2,128]{2,1,0:T(2,128)S(1)} %all_to_all.15.got_ref, s32[1,512]{1,0:T(1,128)S(1)} %get-tuple-element.20.refs_0_.slot_ref, bf16[48,512]{1,0:T(8,128)(2,1)S(1)} %shard_map.172.elem_bases_ref), custom_call_target="tpu_custom_call" | custom-call | flops 1000 | bytes 1000 | tf_op jit(solution)/shard_map/pallas_call | solution.py:405
  (2 shorter events, 0.0 us)
Async XLA Ops:
  0.6 9.7 %collective-permute-start = (bf16[64,512]{1,0:T(8,128)(2,1)}, bf16[64,512]{1,0:T(8,128)(2,1)S(1)}, u32[]{:S(2)}, u32[]{:S(2)}) collective-permute-start(bf16[64,512]{1,0:T(8,128)(2,1)} %bitcast.14), channel_id=1, source_target_pairs={{0,4},{1,5},{2,6},{3,7},{4,0},{5,1},{6,2},{7,3},{8,12},{9,13},{10,... | collective-permute-start | bytes 196616 | tf_op jit(solution)/shard_map/ppermute | solution.py:452
  6.5 10.7 %all-to-all-start = ((f32[8,16,128]{2,1,0:T(8,128)}), f32[8,16,128]{2,1,0:T(8,128)S(1)}, u32[]{:S(2)}, u32[]{:S(2)}) async-start(f32[8,16,128]{2,1,0:T(8,128)} %get-tuple-element.18), calls=%async_computation | async-start | bytes 131072 | tf_op jit(solution)/shard_map/all_to_all | solution.py:449
  10.4 8.7 %collective-permute-start.1 = (bf16[96,512]{1,0:T(8,128)(2,1)S(1)}, bf16[96,512]{1,0:T(8,128)(2,1)S(1)}, u32[]{:S(2)}, u32[]{:S(2)}) collective-permute-start(bf16[96,512]{1,0:T(8,128)(2,1)S(1)} %shard_map.168.early_ref.held_ref), channel_id=1, source_target_pairs={{0,1},{1,0},{2,3},{3,2},{4,5},{5,4},{6,7},{7,6},{8,9},{9,8},{10,11... | collective-permute-start | bytes 294920 | tf_op jit(solution)/shard_map/ppermute | solution.py:452
  19.1 5.7 %collective-permute-start.2 = (bf16[192,512]{1,0:T(8,128)(2,1)S(1)}, bf16[192,512]{1,0:T(8,128)(2,1)S(1)}, u32[]{:S(2)}, u32[]{:S(2)}) collective-permute-start(bf16[192,512]{1,0:T(8,128)(2,1)S(1)} %shard_map.171.held_ref.refs_0_), channel_id=1, source_target_pairs={{0,2},{1,3},{2,0},{3,1},{4,6},{5,7},{6,4},{7,5},{8,10},{9,11},{10,... | collective-permute-start | bytes 589832 | tf_op jit(solution)/shard_map/ppermute | solution.py:452
  19.3 10.6 %all-to-all-start.1 = ((f32[32,1,640]{2,1,0:T(1,128)}), f32[32,1,640]{2,1,0:T(1,128)S(1)}, u32[]{:S(2)}, u32[]{:S(2)}) async-start(f32[32,1,640]{2,1,0:T(1,128)} %get-tuple-element.30), calls=%async_computation.1 | async-start | bytes 163840 | tf_op jit(solution)/shard_map/all_to_all | solution.py:449

commit v23 on v21

--- a/solution.py
+++ b/solution.py
@@ -100,9 +100,10 @@
 
 
 def sort_kernel(members, *refs):
-    elem_refs, bases_ref, sent_ref, slot_ref, elem_row_ref, bases_out = refs[:7], *refs[7:12]
-    elem_bufs, sems = refs[12:19], refs[19]
-    copies = start_copies([*elem_refs, bases_ref], [*elem_bufs, bases_out], sems)
+    elem_refs, weight_refs = refs[:7], refs[7:9]
+    sent_ref, slot_ref, elem_row_ref = refs[9:12]
+    weight_outs, elem_bufs, sems = refs[12:14], refs[14:21], refs[21]
+    copies = start_copies([*elem_refs, *weight_refs], [*elem_bufs, *weight_outs], sems)
     mine = lax.axis_index("leaf")
     elem_count = elem_bufs[0].shape[1]
     peer_rows = elem_count // members
@@ -142,14 +143,15 @@
         part = values[0:6, peer * peer_rows:(peer + 1) * peer_rows]
         sent_ref[peer, 3 * pieces:3 * pieces + 4, 0:peer_rows] = part[0:4]
         sent_ref[peer, 3 * pieces:3 * pieces + 2, HALF:HALF + peer_rows] = part[4:6]
-    copies[7].wait()
+    for copy in copies[7:]:
+        copy.wait()
 
 
 def load_kernel(early_ref, *refs):
-    scalar_refs, weight_refs, near_mask_ref, far_mask_ref = refs[:3], refs[3:7], refs[7], refs[8]
-    weight_outs, scalar_bufs, sems = refs[9:13], refs[13:16], refs[16]
-    sources, targets = [*scalar_refs, *weight_refs[:3]], [*scalar_bufs, *weight_outs[:3]]
-    coarse_v_ref, coarse_v_out = weight_refs[3], weight_outs[3]
+    scalar_refs, weight_refs, near_mask_ref, far_mask_ref = refs[:3], refs[3:6], refs[6], refs[7]
+    weight_outs, scalar_bufs, sems = refs[8:11], refs[11:14], refs[14]
+    sources, targets = [*scalar_refs, *weight_refs[:2]], [*scalar_bufs, *weight_outs[:2]]
+    coarse_v_ref, coarse_v_out = weight_refs[2], weight_outs[2]
     groups, rank = coarse_v_ref.shape[0], coarse_v_ref.shape[1]
     for shift in range(groups):
         place = (shift - 1) % groups * rank
@@ -449,21 +451,22 @@
     ]
     scalar_args = [near_col, far_col, far_rank]
     weights = [
-        near_blocks, far_u.reshape(-1, leaf_size), far_v.reshape(-1, leaf_size), coarse_v
+        far_u.reshape(-1, leaf_size), far_v.reshape(-1, leaf_size), coarse_v
     ]
-    far_rows = weights[1].shape[0]
+    far_rows = weights[0].shape[0]
     bases = coarse_u.reshape(width, elems)
-    sent, slot, elem_row, held = call(
+    sent, slot, elem_row, held, near = call(
         functools.partial(sort_kernel, members),
         (
             shape(members, -(-(3 * (elems // LANES) + 4) // 8) * 8, LANES),
             shape(1, elems, dtype=integer),
             shape(1, elems, dtype=integer),
             shape(width, elems, dtype=jnp.bfloat16),
+            shape(*near_blocks.shape, dtype=jnp.bfloat16),
         ),
-        *elem_args, bases, far=range(8),
+        *elem_args, bases, near_blocks, far=range(9),
         scratch=[VMEM(value.shape, value.dtype) for value in elem_args]
-        + [pltpu.SemaphoreType.DMA((8,))],
+        + [pltpu.SemaphoreType.DMA((9,))],
     )
     steps = step_bits(members)
     early = bases = call(
@@ -471,17 +474,17 @@
         shape(2 * (width - rank), elems, dtype=jnp.bfloat16),
         held, partner(bases, steps[0]), slot, flops=1 << 34, moved=1 << 26,
     )
-    near_mask, far_mask, near, far_u, far_v, coarse_v = call(
+    near_mask, far_mask, far_u, far_v, coarse_v = call(
         load_kernel,
         (
             shape(near_blocks.shape[0], members, leaf_size),
             shape(members, far_rows),
-            *[shape(*value.shape, dtype=jnp.bfloat16) for value in weights[:3]],
+            *[shape(*value.shape, dtype=jnp.bfloat16) for value in weights[:2]],
             shape(width, elems, dtype=jnp.bfloat16),
         ),
-        early, *scalar_args, *weights, far=range(1, 8),
+        early, *scalar_args, *weights, far=range(1, 7),
         scratch=[SMEM(value.shape, value.dtype) for value in scalar_args]
-        + [pltpu.SemaphoreType.DMA((6 + groups,))],
+        + [pltpu.SemaphoreType.DMA((5 + groups,))],
     )
     fields = near_count, near, far_u, far_v, near_mask, far_mask
     state, factor, rows, out = call(

time: 41.1 us -> 41.6 us (1.012)
  waiting for transfers between devices: 9.5 us -> 10 us
    all_to_all x2, waiting for transfers between devices: 7.2 us -> 7.75 us  [swap(): return lax.all_to_all(value, axes, split_axis=0, concat_axis=0, tiled=True)]
where the time goes in v23:
time: 41.6 us; the launch traced here: 41.3 us
  starting transfers between devices  13.4 us (32%)
  waiting for transfers between devices  10 us (24%)
  blocking collectives  8.96 us (22%)
  Pallas kernels  7.52 us (18%)
  between operations  1.34 us (3%)
    all_to_all x1, blocking collectives, swap(): return lax.all_to_all(value, axes, split_axis=0, concat_axis=0, tiled=True)  8.96 us
    all_to_all x2, waiting for transfers between devices, swap(): return lax.all_to_all(value, axes, split_axis=0, concat_axis=0, tiled=True)  7.75 us
    pallas_call x8, Pallas kernels, call(): pl.pallas_call(kernel, out_shape=outs, in_specs=[pl.BlockSpec(memory_spac...  7.52 us
    all_to_all x2, starting transfers between devices, swap(): return lax.all_to_all(value, axes, split_axis=0, concat_axis=0, tiled=True)  6.94 us
    ppermute x3, starting transfers between devices, partner(): lax.ppermute(value, 'blk', [(i, i ^ 1 << bit) for i in range(members)])  6.45 us
    ppermute x3, waiting for transfers between devices, partner(): lax.ppermute(value, 'blk', [(i, i ^ 1 << bit) for i in range(members)])  2.3 us
  transfers between devices with their start and end apart: 5, of which 3 were waited for; matrix products, arithmetic and copies ran while one was open for 0% of the time, Pallas kernels for 14%

profile of v23, /device:TPU:0, one launch (start us, length us, event | category | flops | bytes accessed | tf_op | source)
XLA Modules:
  0.0 41.3 jit_solution(10279770613956905954)
XLA Ops:
  0.6 4.1 %collective-permute-start = (bf16[64,512]{1,0:T(8,128)(2,1)}, bf16[64,512]{1,0:T(8,128)(2,1)S(1)}, u32[]{:S(2)}, u32[]{:S(2)}) collective-permute-start(bf16[64,512]{1,0:T(8,128)(2,1)} %bitcast.12), channel_id=1, source_target_pairs={{0,4},{1,5},{2,6},{3,7},{4,0},{5,1},{6,2},{7,3},{8,12},{9,13},{10,... | collective-permute-start | bytes 196616 | tf_op jit(solution)/shard_map/ppermute | solution.py:446
  4.7 2.3 %shard_map.167 = (f32[8,16,128]{2,1,0:T(8,128)}, s32[1,512]{1,0:T(1,128)S(1)}, s32[1,512]{1,0:T(1,128)S(1)}, bf16[64,512]{1,0:T(8,128)(2,1)S(1)}, bf16[3,512,512]{2,1,0:T(8,128)(2,1)S(1)}) custom-call(s32[1,512]{1,0:T(1,128)} %bitcast.16, f32[1,512]{1,0:T(1,128)} %bitcast.17, f32[1,512]{1,0:T(1,128)} %bitcast.18, f32[1,512]{1,0:T(1,128)} %bitcast.19, ...), custom_call_target="tpu_custom_call" | custom-call | flops 1000 | bytes 1000 | tf_op jit(solution)/shard_map/pallas_call | solution.py:399
  7.0 3.8 %all-to-all-start = ((f32[8,16,128]{2,1,0:T(8,128)}), f32[8,16,128]{2,1,0:T(8,128)S(1)}, u32[]{:S(2)}, u32[]{:S(2)}) async-start(f32[8,16,128]{2,1,0:T(8,128)} %get-tuple-element.18), calls=%async_computation | async-start | bytes 131072 | tf_op jit(solution)/shard_map/all_to_all | solution.py:443
  10.8 0.0 collective-permute-done.came_ref
  10.8 2.1 %collective-permute-start.1 = (bf16[96,512]{1,0:T(8,128)(2,1)S(1)}, bf16[96,512]{1,0:T(8,128)(2,1)S(1)}, u32[]{:S(2)}, u32[]{:S(2)}) collective-permute-start(bf16[96,512]{1,0:T(8,128)(2,1)S(1)} %shard_map.168.early_ref.held_ref), channel_id=1, source_target_pairs={{0,1},{1,0},{2,3},{3,2},{4,5},{5,4},{6,7},{7,6},{8,9},{9,8},{10,11... | collective-permute-start | bytes 294920 | tf_op jit(solution)/shard_map/ppermute | solution.py:446
  13.5 1.0 %shard_map.169 = (f32[3,8,512]{2,1,0:T(8,128)S(1)}, f32[8,64]{1,0:T(8,128)S(1)}, bf16[64,512]{1,0:T(8,128)(2,1)S(1)}, bf16[64,512]{1,0:T(8,128)(2,1)S(1)}, bf16[64,512]{1,0:T(8,128)(2,1)S(1)}) custom-call(bf16[96,512]{1,0:T(8,128)(2,1)S(1)} %shard_map.168.early_ref.held_ref, s32[3]{0:T(128)} %refs_0_.2, s32[4]{0:T(128)} %refs_1_.1, s32[4]{0:T(128)} %refs_2_.2, ...), custom_call_target="tpu_custom_call" | custom-call | flops 1000 | bytes 1000 | tf_op jit(solution)/shard_map/pallas_call | solution.py:399
  14.5 3.2 %all-to-all-done.got_ref = f32[8,16,128]{2,1,0:T(8,128)S(1)} async-done(((f32[8,16,128]{2,1,0:T(8,128)}), f32[8,16,128]{2,1,0:T(8,128)S(1)}, u32[]{:S(2)}, u32[]{:S(2)}) %all-to-all-start) | async-done | bytes 65568 | tf_op jit(solution)/shard_map/all_to_all | solution.py:443
  17.7 1.8 %shard_map.170 = (f32[8,512]{1,0:T(8,128)S(1)}, f32[8,512]{1,0:T(8,128)S(1)}, s32[1,512]{1,0:T(1,128)S(1)}, f32[32,1,640]{2,1,0:T(1,128)}) custom-call(f32[8,16,128]{2,1,0:T(8,128)S(1)} %all-to-all-done.got_ref, bf16[64,512]{1,0:T(8,128)(2,1)S(1)} %get-tuple-element.21.coarse_v_ref, s32[1]{0:T(128)S(6)} %copy.18.refs_0_.refs_2_, ...), custom_call_target="tpu_custom_call" | custom-call | flops 1048576 | bytes 4194304 | tf_op jit(solution)/shard_map/pallas_call | solution.py:399
  19.5 0.0 collective-permute-done.1.came_ref
  19.5 0.3 collective-permute-start.2
  19.8 3.2 %all-to-all-start.1 = ((f32[32,1,640]{2,1,0:T(1,128)}), f32[32,1,640]{2,1,0:T(1,128)S(1)}, u32[]{:S(2)}, u32[]{:S(2)}) async-start(f32[32,1,640]{2,1,0:T(1,128)} %get-tuple-element.30), calls=%async_computation.1 | async-start | bytes 163840 | tf_op jit(solution)/shard_map/all_to_all | solution.py:443
  22.9 2.3 %collective-permute-done.2.came_ref.refs_1_ = bf16[192,512]{1,0:T(8,128)(2,1)S(1)} collective-permute-done((bf16[192,512]{1,0:T(8,128)(2,1)S(1)}, bf16[192,512]{1,0:T(8,128)(2,1)S(1)}, u32[]{:S(2)}, u32[]{:S(2)}) %collective-permute-start.2) | collective-permute-done | bytes 196640 | tf_op jit(solution)/shard_map/ppermute | solution.py:446
  25.2 0.6 %shard_map.172.elem_bases_ref = bf16[48,512]{1,0:T(8,128)(2,1)S(1)} custom-call(bf16[192,512]{1,0:T(8,128)(2,1)S(1)} %shard_map.171.held_ref.refs_0_, bf16[192,512]{1,0:T(8,128)(2,1)S(1)} %collective-permute-done.2.came_ref.refs_1_, s32[1,512]{1,0:T(1,128)S(1)} %get-tuple-element.20.refs_0_.slot_ref, s32[1,512]{1,0:T(1,128)S(1)} %get-tuple-element.31.elem_row_ref), custom_call_target="tpu_custom_call" | custom-call | flops 17179869184 | bytes 67108864 | tf_op jit(solution)/shard_map/pallas_call | solution.py:399
  25.8 4.6 %all-to-all-done.1.all_ref = f32[32,1,640]{2,1,0:T(1,128)S(1)} async-done(((f32[32,1,640]{2,1,0:T(1,128)}), f32[32,1,640]{2,1,0:T(1,128)S(1)}, u32[]{:S(2)}, u32[]{:S(2)}) %all-to-all-start.1) | async-done | bytes 81952 | tf_op jit(solution)/shard_map/all_to_all | solution.py:443
  30.4 1.1 %shard_map.173 = f32[32,4,128]{2,1,0:T(4,128)S(1)} custom-call(f32[8,512]{1,0:T(8,128)S(1)} %get-tuple-element.27.state_ref, f32[8,512]{1,0:T(8,128)S(1)} %get-tuple-element.28.factor_ref, s32[1,512]{1,0:T(1,128)S(1)} %get-tuple-element.29.refs_0_.rows_ref, f32[32,1,640]{2,1,0:T(1,128)S(1)} %all-to-all-done.1.all_ref, ...), custom_call_target="tpu_custom_call" | custom-call | flops 1000 | bytes 1000 | tf_op jit(solution)/shard_map/pallas_call | solution.py:399
  31.5 9.0 %all_to_all.15.got_ref = f32[32,4,128]{2,1,0:T(4,128)S(1)} all-to-all(f32[32,4,128]{2,1,0:T(4,128)S(1)} %shard_map.173), channel_id=1, replica_groups=mesh['leaf'=4,'blk'=8] {'leaf','blk'}, dimensions={0} | all-to-all | bytes 131072 | tf_op jit(solution)/shard_map/all_to_all | solution.py:443
  40.4 0.8 %shard_map.174 = (f32[1,512]{1,0:T(1,128)}, f32[1,512]{1,0:T(1,128)}) custom-call(f32[32,4,128]{2,1,0:T(4,128)S(1)} %all_to_all.15.got_ref, s32[1,512]{1,0:T(1,128)S(1)} %get-tuple-element.20.refs_0_.slot_ref, bf16[48,512]{1,0:T(8,128)(2,1)S(1)} %shard_map.172.elem_bases_ref), custom_call_target="tpu_custom_call" | custom-call | flops 1000 | bytes 1000 | tf_op jit(solution)/shard_map/pallas_call | solution.py:399
  (2 shorter events, 0.0 us)
Async XLA Ops:
  0.6 10.2 %collective-permute-start = (bf16[64,512]{1,0:T(8,128)(2,1)}, bf16[64,512]{1,0:T(8,128)(2,1)S(1)}, u32[]{:S(2)}, u32[]{:S(2)}) collective-permute-start(bf16[64,512]{1,0:T(8,128)(2,1)} %bitcast.12), channel_id=1, source_target_pairs={{0,4},{1,5},{2,6},{3,7},{4,0},{5,1},{6,2},{7,3},{8,12},{9,13},{10,... | collective-permute-start | bytes 196616 | tf_op jit(solution)/shard_map/ppermute | solution.py:446
  7.0 10.7 %all-to-all-start = ((f32[8,16,128]{2,1,0:T(8,128)}), f32[8,16,128]{2,1,0:T(8,128)S(1)}, u32[]{:S(2)}, u32[]{:S(2)}) async-start(f32[8,16,128]{2,1,0:T(8,128)} %get-tuple-element.18), calls=%async_computation | async-start | bytes 131072 | tf_op jit(solution)/shard_map/all_to_all | solution.py:443
  10.8 8.7 %collective-permute-start.1 = (bf16[96,512]{1,0:T(8,128)(2,1)S(1)}, bf16[96,512]{1,0:T(8,128)(2,1)S(1)}, u32[]{:S(2)}, u32[]{:S(2)}) collective-permute-start(bf16[96,512]{1,0:T(8,128)(2,1)S(1)} %shard_map.168.early_ref.held_ref), channel_id=1, source_target_pairs={{0,1},{1,0},{2,3},{3,2},{4,5},{5,4},{6,7},{7,6},{8,9},{9,8},{10,11... | collective-permute-start | bytes 294920 | tf_op jit(solution)/shard_map/ppermute | solution.py:446
  19.5 5.7 %collective-permute-start.2 = (bf16[192,512]{1,0:T(8,128)(2,1)S(1)}, bf16[192,512]{1,0:T(8,128)(2,1)S(1)}, u32[]{:S(2)}, u32[]{:S(2)}) collective-permute-start(bf16[192,512]{1,0:T(8,128)(2,1)S(1)} %shard_map.171.held_ref.refs_0_), channel_id=1, source_target_pairs={{0,2},{1,3},{2,0},{3,1},{4,6},{5,7},{6,4},{7,5},{8,10},{9,11},{10,... | collective-permute-start | bytes 589832 | tf_op jit(solution)/shard_map/ppermute | solution.py:446
  19.8 10.6 %all-to-all-start.1 = ((f32[32,1,640]{2,1,0:T(1,128)}), f32[32,1,640]{2,1,0:T(1,128)S(1)}, u32[]{:S(2)}, u32[]{:S(2)}) async-start(f32[32,1,640]{2,1,0:T(1,128)} %get-tuple-element.30), calls=%async_computation.1 | async-start | bytes 163840 | tf_op jit(solution)/shard_map/all_to_all | solution.py:443

commit v24 on v21

--- a/solution.py
+++ b/solution.py
@@ -251,7 +251,10 @@
     return found
 
 
-def element_kernel(members, held_ref, came_ref, slot_ref, elem_row_ref, out_ref):
+def element_kernel(
+    members, held_ref, came_ref, slot_ref, elem_row_ref, got_ref, out_ref, factor_ref, lines_ref
+):
+    factor_ref[...] = placed_blocks(got_ref, 2 * (slot_ref.shape[1] // LANES), 3, lines_ref)
     slot, row = slot_ref[...], elem_row_ref[...]
     elem_count = row.shape[1]
     kept = out_ref.shape[0]
@@ -273,21 +276,21 @@
     out_ref[...] = total.astype(jnp.bfloat16)
 
 
-def place_kernel(got_ref, coarse_v_ref, *refs):
-    field_refs, state_ref, factor_ref, rows_ref, out_ref, lines_ref = refs[:6], *refs[6:]
+def placed_blocks(got_ref, first, count, lines_ref):
     members = got_ref.shape[0]
-    elem_count = state_ref.shape[1]
-    pieces = elem_count // LANES
-    peer_rows = elem_count // members
-    count = LANES // peer_rows * pieces
-    line_row = lax.broadcasted_iota(jnp.int32, (count, LANES), 0)
-    lane_block = lax.broadcasted_iota(jnp.int32, (count, LANES), 1) // peer_rows
+    pieces = lines_ref.shape[0] // members
+    peer_rows = pieces * LANES // members
+    rows_here = LANES // peer_rows * pieces
+    line_row = lax.broadcasted_iota(jnp.int32, (rows_here, LANES), 0)
+    lane_block = lax.broadcasted_iota(jnp.int32, (rows_here, LANES), 1) // peer_rows
     own_lane = line_row // pieces == lane_block
     for line in range(pieces):
         rows = got_ref[:, pieces + line, :].astype(jnp.int32)
-        parts = [got_ref[:, line, :]]
-        split = three_parts(got_ref[:, 2 * pieces + line, :])
-        parts += [split[i * members:(i + 1) * members] for i in range(3)]
+        value = got_ref[:, first + line, :]
+        parts = [value]
+        if count == 3:
+            split = three_parts(value)
+            parts = [split[i * members:(i + 1) * members] for i in range(3)]
         left, right = [], []
         for peer in range(members):
             row = rows[peer:peer + 1]
@@ -298,17 +301,20 @@
             right.append(low_matrix(row))
         left = jnp.concatenate(left, axis=1).astype(jnp.bfloat16)
         placed = dot(left, jnp.concatenate(right, axis=1), NT)
-        lines_ref[0, line * count:(line + 1) * count, :] = placed[0:count]
-        lines_ref[1, line * count:(line + 1) * count, :] = joined(placed[count:])
-
-    def blocks(number):
-        return jnp.concatenate(
-            [lines_ref[number, pl.ds(piece, members, stride=pieces), :] for piece in range(pieces)],
-            axis=1,
-        )
-
-    factor_ref[...] = blocks(1)
-    inside = inside_rows(blocks(0), *field_refs)
+        lines_ref[line * rows_here:(line + 1) * rows_here, :] = joined(placed) if count == 3 else placed
+    return jnp.concatenate(
+        [lines_ref[pl.ds(piece, members, stride=pieces), :] for piece in range(pieces)], axis=1
+    )
+
+
+def place_kernel(got_ref, coarse_v_ref, *refs):
+    field_refs, state_ref, rows_ref, out_ref, lines_ref = refs[:6], *refs[6:]
+    members = got_ref.shape[0]
+    elem_count = state_ref.shape[1]
+    pieces = elem_count // LANES
+    peer_rows = elem_count // members
+    deficits = placed_blocks(got_ref, 0, 1, lines_ref)
+    inside = inside_rows(deficits, *field_refs)
 
     first = 3 * pieces
     flat = jnp.concatenate(
@@ -484,16 +490,16 @@
         + [pltpu.SemaphoreType.DMA((6 + groups,))],
     )
     fields = near_count, near, far_u, far_v, near_mask, far_mask
-    state, factor, rows, out = call(
+    got = swap(sent, "blk")
+    state, rows, out = call(
         place_kernel,
         (
             shape(8, elems),
-            shape(members, elems),
             shape(1, elems, dtype=integer),
             shape(devices, 1, elems + lines * LANES),
         ),
-        swap(sent, "blk"), coarse_v, *fields, scalars=(2,),
-        scratch=[VMEM((2, members * (elems // LANES), LANES), jnp.float32)],
+        got, coarse_v, *fields, scalars=(2,),
+        scratch=[VMEM((members * (elems // LANES), LANES), jnp.float32)],
         flops=1 << 20, moved=1 << 22,
     )
     for bit in steps[1:-1]:
@@ -502,9 +508,12 @@
             bases, partner(bases, bit), rows, flops=1 << 34, moved=1 << 26,
         )
     bases = bases, partner(bases, steps[-1])
-    elem_bases = call(
-        functools.partial(element_kernel, members), shape(width - rank, elems, dtype=jnp.bfloat16),
-        *bases, slot, elem_row, flops=1 << 34, moved=1 << 26,
+    elem_bases, factor = call(
+        functools.partial(element_kernel, members),
+        (shape(width - rank, elems, dtype=jnp.bfloat16), shape(members, elems)),
+        *bases, slot, elem_row, got,
+        scratch=[VMEM((members * (elems // LANES), LANES), jnp.float32)],
+        flops=1 << 34, moved=1 << 26,
     )
     sent = call(
         functools.partial(second_kernel, groups), shape(devices, sent_rows, LANES),

time: 41.1 us -> 41.1 us (level)
  transfers between devices with their start and end apart: 5 -> 5, of which waited for: 3 -> 3; matrix products, arithmetic and copies ran while one was open for 0% -> 0% of each run, Pallas kernels for 14% -> 15%
where the time goes in v24:
time: 41.1 us; the launch traced here: 40.7 us
  starting transfers between devices  13.4 us (33%)
  waiting for transfers between devices  9.17 us (22%)
  blocking collectives  8.96 us (22%)
  Pallas kernels  7.87 us (19%)
  between operations  1.34 us (3%)
    all_to_all x1, blocking collectives, swap(): return lax.all_to_all(value, axes, split_axis=0, concat_axis=0, tiled=True)  8.96 us
    pallas_call x8, Pallas kernels, call(): pl.pallas_call(kernel, out_shape=outs, in_specs=[pl.BlockSpec(memory_spac...  7.87 us
    all_to_all x2, starting transfers between devices, swap(): return lax.all_to_all(value, axes, split_axis=0, concat_axis=0, tiled=True)  6.94 us
    all_to_all x2, waiting for transfers between devices, swap(): return lax.all_to_all(value, axes, split_axis=0, concat_axis=0, tiled=True)  6.86 us
    ppermute x3, starting transfers between devices, partner(): lax.ppermute(value, 'blk', [(i, i ^ 1 << bit) for i in range(members)])  6.45 us
    ppermute x3, waiting for transfers between devices, partner(): lax.ppermute(value, 'blk', [(i, i ^ 1 << bit) for i in range(members)])  2.3 us
  transfers between devices with their start and end apart: 5, of which 3 were waited for; matrix products, arithmetic and copies ran while one was open for 0% of the time, Pallas kernels for 15%

profile of v24, /device:TPU:0, one launch (start us, length us, event | category | flops | bytes accessed | tf_op | source)
XLA Modules:
  0.0 40.7 jit_solution(5609873993749067427)
XLA Ops:
  0.6 4.1 %collective-permute-start = (bf16[64,512]{1,0:T(8,128)(2,1)}, bf16[64,512]{1,0:T(8,128)(2,1)S(1)}, u32[]{:S(2)}, u32[]{:S(2)}) collective-permute-start(bf16[64,512]{1,0:T(8,128)(2,1)} %bitcast.14), channel_id=1, source_target_pairs={{0,4},{1,5},{2,6},{3,7},{4,0},{5,1},{6,2},{7,3},{8,12},{9,13},{10,... | collective-permute-start | bytes 196616 | tf_op jit(solution)/shard_map/ppermute | solution.py:450
  4.7 1.8 %shard_map.167 = (f32[8,16,128]{2,1,0:T(8,128)}, s32[1,512]{1,0:T(1,128)S(1)}, s32[1,512]{1,0:T(1,128)S(1)}, bf16[64,512]{1,0:T(8,128)(2,1)S(1)}) custom-call(s32[1,512]{1,0:T(1,128)} %bitcast.16, f32[1,512]{1,0:T(1,128)} %bitcast.17, f32[1,512]{1,0:T(1,128)} %bitcast.18, f32[1,512]{1,0:T(1,128)} %bitcast.19, f32[1,512]{1,0:T(1,128)} %bitcast.20, ...), custom_call_target="tpu_custom_call" | custom-call | flops 1000 | bytes 1000 | tf_op jit(solution)/shard_map/pallas_call | solution.py:403
  6.5 3.8 %all-to-all-start = ((f32[8,16,128]{2,1,0:T(8,128)}), f32[8,16,128]{2,1,0:T(8,128)S(1)}, u32[]{:S(2)}, u32[]{:S(2)}) async-start(f32[8,16,128]{2,1,0:T(8,128)} %get-tuple-element.19), calls=%async_computation | async-start | bytes 131072 | tf_op jit(solution)/shard_map/all_to_all | solution.py:447
  10.3 0.0 collective-permute-done.came_ref
  10.4 2.1 %collective-permute-start.1 = (bf16[96,512]{1,0:T(8,128)(2,1)S(1)}, bf16[96,512]{1,0:T(8,128)(2,1)S(1)}, u32[]{:S(2)}, u32[]{:S(2)}) collective-permute-start(bf16[96,512]{1,0:T(8,128)(2,1)S(1)} %shard_map.168.early_ref.held_ref), channel_id=1, source_target_pairs={{0,1},{1,0},{2,3},{3,2},{4,5},{5,4},{6,7},{7,6},{8,9},{9,8},{10,11... | collective-permute-start | bytes 294920 | tf_op jit(solution)/shard_map/ppermute | solution.py:450
  13.1 1.5 %shard_map.169 = (f32[3,8,512]{2,1,0:T(8,128)S(1)}, f32[8,64]{1,0:T(8,128)S(1)}, bf16[3,512,512]{2,1,0:T(8,128)(2,1)S(1)}, bf16[64,512]{1,0:T(8,128)(2,1)S(1)}, ...) custom-call(bf16[96,512]{1,0:T(8,128)(2,1)S(1)} %shard_map.168.early_ref.held_ref, s32[3]{0:T(128)} %refs_0_.2, ...), custom_call_target="tpu_custom_call" | custom-call | flops 1000 | bytes 1000 | tf_op jit(solution)/shard_map/pallas_call | solution.py:403
  14.6 2.6 %all-to-all-done.got_ref = f32[8,16,128]{2,1,0:T(8,128)S(1)} async-done(((f32[8,16,128]{2,1,0:T(8,128)}), f32[8,16,128]{2,1,0:T(8,128)S(1)}, u32[]{:S(2)}, u32[]{:S(2)}) %all-to-all-start) | async-done | bytes 65568 | tf_op jit(solution)/shard_map/all_to_all | solution.py:447
  17.2 1.7 %shard_map.170 = (f32[8,512]{1,0:T(8,128)S(1)}, s32[1,512]{1,0:T(1,128)S(1)}, f32[32,1,640]{2,1,0:T(1,128)}) custom-call(f32[8,16,128]{2,1,0:T(8,128)S(1)} %all-to-all-done.got_ref, bf16[64,512]{1,0:T(8,128)(2,1)S(1)} %get-tuple-element.22.coarse_v_ref, s32[1]{0:T(128)S(6)} %copy.18.refs_0_.refs_2_, ...), custom_call_target="tpu_custom_call" | custom-call | flops 1048576 | bytes 4194304 | tf_op jit(solution)/shard_map/pallas_call | solution.py:403
  19.0 0.0 collective-permute-done.1.came_ref
  19.0 0.3 collective-permute-start.2
  19.3 3.2 %all-to-all-start.1 = ((f32[32,1,640]{2,1,0:T(1,128)}), f32[32,1,640]{2,1,0:T(1,128)S(1)}, u32[]{:S(2)}, u32[]{:S(2)}) async-start(f32[32,1,640]{2,1,0:T(1,128)} %get-tuple-element.32), calls=%async_computation.1 | async-start | bytes 163840 | tf_op jit(solution)/shard_map/all_to_all | solution.py:447
  22.4 2.3 %collective-permute-done.2.came_ref.refs_1_ = bf16[192,512]{1,0:T(8,128)(2,1)S(1)} collective-permute-done((bf16[192,512]{1,0:T(8,128)(2,1)S(1)}, bf16[192,512]{1,0:T(8,128)(2,1)S(1)}, u32[]{:S(2)}, u32[]{:S(2)}) %collective-permute-start.2) | collective-permute-done | bytes 196640 | tf_op jit(solution)/shard_map/ppermute | solution.py:450
  24.7 0.9 %shard_map.172 = (bf16[48,512]{1,0:T(8,128)(2,1)S(1)}, f32[8,512]{1,0:T(8,128)S(1)}) custom-call(bf16[192,512]{1,0:T(8,128)(2,1)S(1)} %shard_map.171.held_ref.refs_0_, bf16[192,512]{1,0:T(8,128)(2,1)S(1)} %collective-permute-done.2.came_ref.refs_1_, s32[1,512]{1,0:T(1,128)S(1)} %get-tuple-element.21.refs_0_.slot_ref, ...), custom_call_target="tpu_custom_call" | custom-call | flops 17179869184 | bytes 67108864 | tf_op jit(solution)/shard_map/pallas_call | solution.py:403
  25.6 4.2 %all-to-all-done.1.all_ref = f32[32,1,640]{2,1,0:T(1,128)S(1)} async-done(((f32[32,1,640]{2,1,0:T(1,128)}), f32[32,1,640]{2,1,0:T(1,128)S(1)}, u32[]{:S(2)}, u32[]{:S(2)}) %all-to-all-start.1) | async-done | bytes 81952 | tf_op jit(solution)/shard_map/all_to_all | solution.py:447
  29.9 1.1 %shard_map.173 = f32[32,4,128]{2,1,0:T(4,128)S(1)} custom-call(f32[8,512]{1,0:T(8,128)S(1)} %get-tuple-element.28.state_ref, f32[8,512]{1,0:T(8,128)S(1)} %get-tuple-element.31.factor_ref, s32[1,512]{1,0:T(1,128)S(1)} %get-tuple-element.29.refs_0_.rows_ref, f32[32,1,640]{2,1,0:T(1,128)S(1)} %all-to-all-done.1.all_ref, ...), custom_call_target="tpu_custom_call" | custom-call | flops 1000 | bytes 1000 | tf_op jit(solution)/shard_map/pallas_call | solution.py:403
  30.9 9.0 %all_to_all.15.got_ref = f32[32,4,128]{2,1,0:T(4,128)S(1)} all-to-all(f32[32,4,128]{2,1,0:T(4,128)S(1)} %shard_map.173), channel_id=1, replica_groups=mesh['leaf'=4,'blk'=8] {'leaf','blk'}, dimensions={0} | all-to-all | bytes 131072 | tf_op jit(solution)/shard_map/all_to_all | solution.py:447
  39.9 0.8 %shard_map.174 = (f32[1,512]{1,0:T(1,128)}, f32[1,512]{1,0:T(1,128)}) custom-call(f32[32,4,128]{2,1,0:T(4,128)S(1)} %all_to_all.15.got_ref, s32[1,512]{1,0:T(1,128)S(1)} %get-tuple-element.21.refs_0_.slot_ref, bf16[48,512]{1,0:T(8,128)(2,1)S(1)} %get-tuple-element.33.elem_bases_ref), custom_call_target="tpu_custom_call" | custom-call | flops 1000 | bytes 1000 | tf_op jit(solution)/shard_map/pallas_call | solution.py:403
  (2 shorter events, 0.0 us)
Async XLA Ops:
  0.6 9.7 %collective-permute-start = (bf16[64,512]{1,0:T(8,128)(2,1)}, bf16[64,512]{1,0:T(8,128)(2,1)S(1)}, u32[]{:S(2)}, u32[]{:S(2)}) collective-permute-start(bf16[64,512]{1,0:T(8,128)(2,1)} %bitcast.14), channel_id=1, source_target_pairs={{0,4},{1,5},{2,6},{3,7},{4,0},{5,1},{6,2},{7,3},{8,12},{9,13},{10,... | collective-permute-start | bytes 196616 | tf_op jit(solution)/shard_map/ppermute | solution.py:450
  6.5 10.7 %all-to-all-start = ((f32[8,16,128]{2,1,0:T(8,128)}), f32[8,16,128]{2,1,0:T(8,128)S(1)}, u32[]{:S(2)}, u32[]{:S(2)}) async-start(f32[8,16,128]{2,1,0:T(8,128)} %get-tuple-element.19), calls=%async_computation | async-start | bytes 131072 | tf_op jit(solution)/shard_map/all_to_all | solution.py:447
  10.4 8.6 %collective-permute-start.1 = (bf16[96,512]{1,0:T(8,128)(2,1)S(1)}, bf16[96,512]{1,0:T(8,128)(2,1)S(1)}, u32[]{:S(2)}, u32[]{:S(2)}) collective-permute-start(bf16[96,512]{1,0:T(8,128)(2,1)S(1)} %shard_map.168.early_ref.held_ref), channel_id=1, source_target_pairs={{0,1},{1,0},{2,3},{3,2},{4,5},{5,4},{6,7},{7,6},{8,9},{9,8},{10,11... | collective-permute-start | bytes 294920 | tf_op jit(solution)/shard_map/ppermute | solution.py:450
  19.0 5.7 %collective-permute-start.2 = (bf16[192,512]{1,0:T(8,128)(2,1)S(1)}, bf16[192,512]{1,0:T(8,128)(2,1)S(1)}, u32[]{:S(2)}, u32[]{:S(2)}) collective-permute-start(bf16[192,512]{1,0:T(8,128)(2,1)S(1)} %shard_map.171.held_ref.refs_0_), channel_id=1, source_target_pairs={{0,2},{1,3},{2,0},{3,1},{4,6},{5,7},{6,4},{7,5},{8,10},{9,11},{10,... | collective-permute-start | bytes 589832 | tf_op jit(solution)/shard_map/ppermute | solution.py:450
  19.3 10.6 %all-to-all-start.1 = ((f32[32,1,640]{2,1,0:T(1,128)}), f32[32,1,640]{2,1,0:T(1,128)S(1)}, u32[]{:S(2)}, u32[]{:S(2)}) async-start(f32[32,1,640]{2,1,0:T(1,128)} %get-tuple-element.32), calls=%async_computation.1 | async-start | bytes 163840 | tf_op jit(solution)/shard_map/all_to_all | solution.py:447

commit v25 on v24

--- a/solution.py
+++ b/solution.py
@@ -239,8 +239,7 @@
 
 
 def step_bits(members):
-    bits = list(range(members.bit_length() - 2, -1, -1))
-    return bits[:-2] + [bits[-1], bits[-2]]
+    return list(range(members.bit_length() - 2, -1, -1))
 
 
 def relative_member(place, number, members):

time: 41.1 us -> 41.3 us (level)
  no operation moved by 1% of the time
where the time goes in v25:
time: 41.3 us; the launch traced here: 40.9 us
  starting transfers between devices  13.6 us (33%)
  waiting for transfers between devices  9.17 us (22%)
  blocking collectives  8.96 us (22%)
  Pallas kernels  7.87 us (19%)
  between operations  1.34 us (3%)
    all_to_all x1, blocking collectives, swap(): return lax.all_to_all(value, axes, split_axis=0, concat_axis=0, tiled=True)  8.96 us
    pallas_call x8, Pallas kernels, call(): pl.pallas_call(kernel, out_shape=outs, in_specs=[pl.BlockSpec(memory_spac...  7.87 us
    all_to_all x2, waiting for transfers between devices, swap(): return lax.all_to_all(value, axes, split_axis=0, concat_axis=0, tiled=True)  7.05 us
    all_to_all x2, starting transfers between devices, swap(): return lax.all_to_all(value, axes, split_axis=0, concat_axis=0, tiled=True)  6.95 us
    ppermute x3, starting transfers between devices, partner(): lax.ppermute(value, 'blk', [(i, i ^ 1 << bit) for i in range(members)])  6.62 us
    ppermute x3, waiting for transfers between devices, partner(): lax.ppermute(value, 'blk', [(i, i ^ 1 << bit) for i in range(members)])  2.12 us
  transfers between devices with their start and end apart: 5, of which 3 were waited for; matrix products, arithmetic and copies ran while one was open for 0% of the time, Pallas kernels for 15%

profile of v25, /device:TPU:0, one launch (start us, length us, event | category | flops | bytes accessed | tf_op | source)
XLA Modules:
  0.0 40.9 jit_solution(8371984623716464489)
XLA Ops:
  0.6 4.1 %collective-permute-start = (bf16[64,512]{1,0:T(8,128)(2,1)}, bf16[64,512]{1,0:T(8,128)(2,1)S(1)}, u32[]{:S(2)}, u32[]{:S(2)}) collective-permute-start(bf16[64,512]{1,0:T(8,128)(2,1)} %bitcast.14), channel_id=1, source_target_pairs={{0,4},{1,5},{2,6},{3,7},{4,0},{5,1},{6,2},{7,3},{8,12},{9,13},{10,... | collective-permute-start | bytes 196616 | tf_op jit(solution)/shard_map/ppermute | solution.py:449
  4.7 1.8 %shard_map.167 = (f32[8,16,128]{2,1,0:T(8,128)}, s32[1,512]{1,0:T(1,128)S(1)}, s32[1,512]{1,0:T(1,128)S(1)}, bf16[64,512]{1,0:T(8,128)(2,1)S(1)}) custom-call(s32[1,512]{1,0:T(1,128)} %bitcast.16, f32[1,512]{1,0:T(1,128)} %bitcast.17, f32[1,512]{1,0:T(1,128)} %bitcast.18, f32[1,512]{1,0:T(1,128)} %bitcast.19, f32[1,512]{1,0:T(1,128)} %bitcast.20, ...), custom_call_target="tpu_custom_call" | custom-call | flops 1000 | bytes 1000 | tf_op jit(solution)/shard_map/pallas_call | solution.py:402
  6.5 3.8 %all-to-all-start = ((f32[8,16,128]{2,1,0:T(8,128)}), f32[8,16,128]{2,1,0:T(8,128)S(1)}, u32[]{:S(2)}, u32[]{:S(2)}) async-start(f32[8,16,128]{2,1,0:T(8,128)} %get-tuple-element.19), calls=%async_computation | async-start | bytes 131072 | tf_op jit(solution)/shard_map/all_to_all | solution.py:446
  10.3 0.0 collective-permute-done.came_ref
  10.4 2.1 %collective-permute-start.1 = (bf16[96,512]{1,0:T(8,128)(2,1)S(1)}, bf16[96,512]{1,0:T(8,128)(2,1)S(1)}, u32[]{:S(2)}, u32[]{:S(2)}) collective-permute-start(bf16[96,512]{1,0:T(8,128)(2,1)S(1)} %shard_map.168.early_ref.held_ref), channel_id=1, source_target_pairs={{0,2},{1,3},{2,0},{3,1},{4,6},{5,7},{6,4},{7,5},{8,10},{9,11},{10,... | collective-permute-start | bytes 294920 | tf_op jit(solution)/shard_map/ppermute | solution.py:449
  13.1 1.5 %shard_map.169 = (f32[3,8,512]{2,1,0:T(8,128)S(1)}, f32[8,64]{1,0:T(8,128)S(1)}, bf16[3,512,512]{2,1,0:T(8,128)(2,1)S(1)}, bf16[64,512]{1,0:T(8,128)(2,1)S(1)}, ...) custom-call(bf16[96,512]{1,0:T(8,128)(2,1)S(1)} %shard_map.168.early_ref.held_ref, s32[3]{0:T(128)} %refs_0_.2, ...), custom_call_target="tpu_custom_call" | custom-call | flops 1000 | bytes 1000 | tf_op jit(solution)/shard_map/pallas_call | solution.py:402
  14.6 2.6 %all-to-all-done.got_ref = f32[8,16,128]{2,1,0:T(8,128)S(1)} async-done(((f32[8,16,128]{2,1,0:T(8,128)}), f32[8,16,128]{2,1,0:T(8,128)S(1)}, u32[]{:S(2)}, u32[]{:S(2)}) %all-to-all-start) | async-done | bytes 65568 | tf_op jit(solution)/shard_map/all_to_all | solution.py:446
  17.2 1.7 %shard_map.170 = (f32[8,512]{1,0:T(8,128)S(1)}, s32[1,512]{1,0:T(1,128)S(1)}, f32[32,1,640]{2,1,0:T(1,128)}) custom-call(f32[8,16,128]{2,1,0:T(8,128)S(1)} %all-to-all-done.got_ref, bf16[64,512]{1,0:T(8,128)(2,1)S(1)} %get-tuple-element.22.coarse_v_ref, s32[1]{0:T(128)S(6)} %copy.18.refs_0_.refs_2_, ...), custom_call_target="tpu_custom_call" | custom-call | flops 1048576 | bytes 4194304 | tf_op jit(solution)/shard_map/pallas_call | solution.py:402
  19.0 0.0 collective-permute-done.1.came_ref
  19.0 0.5 %collective-permute-start.2 = (bf16[192,512]{1,0:T(8,128)(2,1)S(1)}, bf16[192,512]{1,0:T(8,128)(2,1)S(1)}, u32[]{:S(2)}, u32[]{:S(2)}) collective-permute-start(bf16[192,512]{1,0:T(8,128)(2,1)S(1)} %shard_map.171.held_ref.refs_0_), channel_id=1, source_target_pairs={{0,1},{1,0},{2,3},{3,2},{4,5},{5,4},{6,7},{7,6},{8,9},{9,8},{10,11... | collective-permute-start | bytes 589832 | tf_op jit(solution)/shard_map/ppermute | solution.py:449
  19.4 3.2 %all-to-all-start.1 = ((f32[32,1,640]{2,1,0:T(1,128)}), f32[32,1,640]{2,1,0:T(1,128)S(1)}, u32[]{:S(2)}, u32[]{:S(2)}) async-start(f32[32,1,640]{2,1,0:T(1,128)} %get-tuple-element.32), calls=%async_computation.1 | async-start | bytes 163840 | tf_op jit(solution)/shard_map/all_to_all | solution.py:446
  22.6 2.1 %collective-permute-done.2.came_ref.refs_1_ = bf16[192,512]{1,0:T(8,128)(2,1)S(1)} collective-permute-done((bf16[192,512]{1,0:T(8,128)(2,1)S(1)}, bf16[192,512]{1,0:T(8,128)(2,1)S(1)}, u32[]{:S(2)}, u32[]{:S(2)}) %collective-permute-start.2) | collective-permute-done | bytes 196640 | tf_op jit(solution)/shard_map/ppermute | solution.py:449
  24.7 0.9 %shard_map.172 = (bf16[48,512]{1,0:T(8,128)(2,1)S(1)}, f32[8,512]{1,0:T(8,128)S(1)}) custom-call(bf16[192,512]{1,0:T(8,128)(2,1)S(1)} %shard_map.171.held_ref.refs_0_, bf16[192,512]{1,0:T(8,128)(2,1)S(1)} %collective-permute-done.2.came_ref.refs_1_, s32[1,512]{1,0:T(1,128)S(1)} %get-tuple-element.21.refs_0_.slot_ref, ...), custom_call_target="tpu_custom_call" | custom-call | flops 17179869184 | bytes 67108864 | tf_op jit(solution)/shard_map/pallas_call | solution.py:402
  25.6 4.4 %all-to-all-done.1.all_ref = f32[32,1,640]{2,1,0:T(1,128)S(1)} async-done(((f32[32,1,640]{2,1,0:T(1,128)}), f32[32,1,640]{2,1,0:T(1,128)S(1)}, u32[]{:S(2)}, u32[]{:S(2)}) %all-to-all-start.1) | async-done | bytes 81952 | tf_op jit(solution)/shard_map/all_to_all | solution.py:446
  30.0 1.1 %shard_map.173 = f32[32,4,128]{2,1,0:T(4,128)S(1)} custom-call(f32[8,512]{1,0:T(8,128)S(1)} %get-tuple-element.28.state_ref, f32[8,512]{1,0:T(8,128)S(1)} %get-tuple-element.31.factor_ref, s32[1,512]{1,0:T(1,128)S(1)} %get-tuple-element.29.refs_0_.rows_ref, f32[32,1,640]{2,1,0:T(1,128)S(1)} %all-to-all-done.1.all_ref, ...), custom_call_target="tpu_custom_call" | custom-call | flops 1000 | bytes 1000 | tf_op jit(solution)/shard_map/pallas_call | solution.py:402
  31.1 9.0 %all_to_all.15.got_ref = f32[32,4,128]{2,1,0:T(4,128)S(1)} all-to-all(f32[32,4,128]{2,1,0:T(4,128)S(1)} %shard_map.173), channel_id=1, replica_groups=mesh['leaf'=4,'blk'=8] {'leaf','blk'}, dimensions={0} | all-to-all | bytes 131072 | tf_op jit(solution)/shard_map/all_to_all | solution.py:446
  40.1 0.8 %shard_map.174 = (f32[1,512]{1,0:T(1,128)}, f32[1,512]{1,0:T(1,128)}) custom-call(f32[32,4,128]{2,1,0:T(4,128)S(1)} %all_to_all.15.got_ref, s32[1,512]{1,0:T(1,128)S(1)} %get-tuple-element.21.refs_0_.slot_ref, bf16[48,512]{1,0:T(8,128)(2,1)S(1)} %get-tuple-element.33.elem_bases_ref), custom_call_target="tpu_custom_call" | custom-call | flops 1000 | bytes 1000 | tf_op jit(solution)/shard_map/pallas_call | solution.py:402
  (2 shorter events, 0.0 us)
Async XLA Ops:
  0.6 9.7 %collective-permute-start = (bf16[64,512]{1,0:T(8,128)(2,1)}, bf16[64,512]{1,0:T(8,128)(2,1)S(1)}, u32[]{:S(2)}, u32[]{:S(2)}) collective-permute-start(bf16[64,512]{1,0:T(8,128)(2,1)} %bitcast.14), channel_id=1, source_target_pairs={{0,4},{1,5},{2,6},{3,7},{4,0},{5,1},{6,2},{7,3},{8,12},{9,13},{10,... | collective-permute-start | bytes 196616 | tf_op jit(solution)/shard_map/ppermute | solution.py:449
  6.5 10.7 %all-to-all-start = ((f32[8,16,128]{2,1,0:T(8,128)}), f32[8,16,128]{2,1,0:T(8,128)S(1)}, u32[]{:S(2)}, u32[]{:S(2)}) async-start(f32[8,16,128]{2,1,0:T(8,128)} %get-tuple-element.19), calls=%async_computation | async-start | bytes 131072 | tf_op jit(solution)/shard_map/all_to_all | solution.py:446
  10.4 8.6 %collective-permute-start.1 = (bf16[96,512]{1,0:T(8,128)(2,1)S(1)}, bf16[96,512]{1,0:T(8,128)(2,1)S(1)}, u32[]{:S(2)}, u32[]{:S(2)}) collective-permute-start(bf16[96,512]{1,0:T(8,128)(2,1)S(1)} %shard_map.168.early_ref.held_ref), channel_id=1, source_target_pairs={{0,2},{1,3},{2,0},{3,1},{4,6},{5,7},{6,4},{7,5},{8,10},{9,11},{10,... | collective-permute-start | bytes 294920 | tf_op jit(solution)/shard_map/ppermute | solution.py:449
  19.0 5.7 %collective-permute-start.2 = (bf16[192,512]{1,0:T(8,128)(2,1)S(1)}, bf16[192,512]{1,0:T(8,128)(2,1)S(1)}, u32[]{:S(2)}, u32[]{:S(2)}) collective-permute-start(bf16[192,512]{1,0:T(8,128)(2,1)S(1)} %shard_map.171.held_ref.refs_0_), channel_id=1, source_target_pairs={{0,1},{1,0},{2,3},{3,2},{4,5},{5,4},{6,7},{7,6},{8,9},{9,8},{10,11... | collective-permute-start | bytes 589832 | tf_op jit(solution)/shard_map/ppermute | solution.py:449
  19.4 10.6 %all-to-all-start.1 = ((f32[32,1,640]{2,1,0:T(1,128)}), f32[32,1,640]{2,1,0:T(1,128)S(1)}, u32[]{:S(2)}, u32[]{:S(2)}) async-start(f32[32,1,640]{2,1,0:T(1,128)} %get-tuple-element.32), calls=%async_computation.1 | async-start | bytes 163840 | tf_op jit(solution)/shard_map/all_to_all | solution.py:446

commit v26 on v24

--- a/solution.py
+++ b/solution.py
@@ -56,7 +56,7 @@
     )
 
 
-def gathered(values, index_row):
+def gathered(values, index_row, low):
     parts = three_parts(values)
     count = parts.shape[0]
     high = index_row // LANES
@@ -64,7 +64,7 @@
     left = jnp.concatenate(
         [parts[:, piece * LANES:(piece + 1) * LANES] for piece in range(pieces)], axis=0
     )
-    moved = dot(left.astype(jnp.bfloat16), low_matrix(index_row), NN)
+    moved = dot(left.astype(jnp.bfloat16), low, NN)
     total = jnp.zeros((count, index_row.shape[1]), jnp.float32)
     for piece in range(pieces):
         total = jnp.where(high == piece, moved[piece * count:(piece + 1) * count], total)
@@ -252,8 +252,11 @@
 
 
 def element_kernel(
-    members, held_ref, came_ref, slot_ref, elem_row_ref, got_ref, out_ref, factor_ref, lines_ref
+    members, held_ref, came_ref, slot_ref, elem_row_ref, got_ref, rows_ref,
+    out_ref, factor_ref, rows_low_ref, slot_low_ref, lines_ref
 ):
+    rows_low_ref[...] = low_matrix(rows_ref[...])
+    slot_low_ref[...] = low_matrix(slot_ref[...])
     factor_ref[...] = placed_blocks(got_ref, 2 * (slot_ref.shape[1] // LANES), 3, lines_ref)
     slot, row = slot_ref[...], elem_row_ref[...]
     elem_count = row.shape[1]
@@ -338,7 +341,7 @@
 
 
 def second_kernel(
-    groups, state_ref, factor_ref, rows_ref, all_ref, elem_bases_ref, coarse_v_ref, *refs
+    groups, state_ref, factor_ref, rows_ref, rows_low_ref, all_ref, elem_bases_ref, coarse_v_ref, *refs
 ):
     bases_refs, field_refs, sent_ref = refs[:2], refs[2:8], refs[8]
     members, elem_count = refs[6].shape[1], state_ref.shape[1]
@@ -366,7 +369,7 @@
     inverse = 0.5 * TIME_STEP / (sa + DAMPING * velocity)
     u_next = 0.5 * (u + u2) + (inside - sb * k2p) * inverse
     phi_next = phi + 0.5 * TIME_STEP * (k1p + k2p)
-    sent = gathered(padded([u_next, inverse, phi_next], 8), rows_ref[...])
+    sent = gathered(padded([u_next, inverse, phi_next], 8), rows_ref[...], rows_low_ref[...])
     partial = as_lines(partial_row(deficit, coarse_v_ref))
     peer_rows = elem_count // members
     for device in range(groups * members):
@@ -375,12 +378,12 @@
         sent_ref[device, 3:3 + partial.shape[0], :] = partial
 
 
-def finish_kernel(groups, width, got_ref, slot_ref, elem_bases_ref, u_ref, phi_ref):
+def finish_kernel(groups, width, got_ref, slot_ref, slot_low_ref, elem_bases_ref, u_ref, phi_ref):
     elem_count = slot_ref.shape[1]
     members = got_ref.shape[0] // groups
     first = lax.axis_index("leaf") * members
     flat = peer_lanes(got_ref, first, members, 3, elem_count)
-    out = gathered(padded([flat[i:i + 1] for i in range(3)], 8), slot_ref[...])
+    out = gathered(padded([flat[i:i + 1] for i in range(3)], 8), slot_ref[...], slot_low_ref[...])
 
     def parts_of(group):
         sent = pl.ds(group * members, members)
@@ -508,20 +511,25 @@
             bases, partner(bases, bit), rows, flops=1 << 34, moved=1 << 26,
         )
     bases = bases, partner(bases, steps[-1])
-    elem_bases, factor = call(
+    elem_bases, factor, rows_low, slot_low = call(
         functools.partial(element_kernel, members),
-        (shape(width - rank, elems, dtype=jnp.bfloat16), shape(members, elems)),
-        *bases, slot, elem_row, got,
+        (
+            shape(width - rank, elems, dtype=jnp.bfloat16),
+            shape(members, elems),
+            shape(LANES, elems, dtype=jnp.bfloat16),
+            shape(LANES, elems, dtype=jnp.bfloat16),
+        ),
+        *bases, slot, elem_row, got, rows,
         scratch=[VMEM((members * (elems // LANES), LANES), jnp.float32)],
         flops=1 << 34, moved=1 << 26,
     )
     sent = call(
         functools.partial(second_kernel, groups), shape(devices, sent_rows, LANES),
-        state, factor, rows, swap(out, ("leaf", "blk")), elem_bases, coarse_v, *bases, *fields, scalars=(8,),
+        state, factor, rows, rows_low, swap(out, ("leaf", "blk")), elem_bases, coarse_v, *bases, *fields, scalars=(9,),
     )
     u, phi = call(
         functools.partial(finish_kernel, groups, width), (shape(1, elems), shape(1, elems)),
-        swap(sent, ("leaf", "blk")), slot, elem_bases,
+        swap(sent, ("leaf", "blk")), slot, slot_low, elem_bases,
     )
     return u.reshape(elems), phi.reshape(elems)
 

time: 41.1 us -> 41.1 us (level)
  no operation moved by 1% of the time
where the time goes in v26:
time: 41.1 us; the launch traced here: 40.7 us
  starting transfers between devices  13.4 us (33%)
  waiting for transfers between devices  9.16 us (22%)
  blocking collectives  8.96 us (22%)
  Pallas kernels  7.88 us (19%)
  between operations  1.34 us (3%)
    all_to_all x1, blocking collectives, swap(): return lax.all_to_all(value, axes, split_axis=0, concat_axis=0, tiled=True)  8.96 us
    pallas_call x8, Pallas kernels, call(): pl.pallas_call(kernel, out_shape=outs, in_specs=[pl.BlockSpec(memory_spac...  7.88 us
    all_to_all x2, starting transfers between devices, swap(): return lax.all_to_all(value, axes, split_axis=0, concat_axis=0, tiled=True)  6.94 us
    all_to_all x2, waiting for transfers between devices, swap(): return lax.all_to_all(value, axes, split_axis=0, concat_axis=0, tiled=True)  6.86 us
    ppermute x3, starting transfers between devices, partner(): lax.ppermute(value, 'blk', [(i, i ^ 1 << bit) for i in range(members)])  6.45 us
    ppermute x3, waiting for transfers between devices, partner(): lax.ppermute(value, 'blk', [(i, i ^ 1 << bit) for i in range(members)])  2.3 us
  transfers between devices with their start and end apart: 5, of which 3 were waited for; matrix products, arithmetic and copies ran while one was open for 0% of the time, Pallas kernels for 15%

profile of v26, /device:TPU:0, one launch (start us, length us, event | category | flops | bytes accessed | tf_op | source)
XLA Modules:
  0.0 40.7 jit_solution(8829296263660669858)
XLA Ops:
  0.6 4.1 %collective-permute-start = (bf16[64,512]{1,0:T(8,128)(2,1)}, bf16[64,512]{1,0:T(8,128)(2,1)S(1)}, u32[]{:S(2)}, u32[]{:S(2)}) collective-permute-start(bf16[64,512]{1,0:T(8,128)(2,1)} %bitcast.14), channel_id=1, source_target_pairs={{0,4},{1,5},{2,6},{3,7},{4,0},{5,1},{6,2},{7,3},{8,12},{9,13},{10,... | collective-permute-start | bytes 196616 | tf_op jit(solution)/shard_map/ppermute | solution.py:453
  4.7 1.8 %shard_map.167 = (f32[8,16,128]{2,1,0:T(8,128)}, s32[1,512]{1,0:T(1,128)S(1)}, s32[1,512]{1,0:T(1,128)S(1)}, bf16[64,512]{1,0:T(8,128)(2,1)S(1)}) custom-call(s32[1,512]{1,0:T(1,128)} %bitcast.16, f32[1,512]{1,0:T(1,128)} %bitcast.17, f32[1,512]{1,0:T(1,128)} %bitcast.18, f32[1,512]{1,0:T(1,128)} %bitcast.19, f32[1,512]{1,0:T(1,128)} %bitcast.20, ...), custom_call_target="tpu_custom_call" | custom-call | flops 1000 | bytes 1000 | tf_op jit(solution)/shard_map/pallas_call | solution.py:406
  6.5 3.8 %all-to-all-start = ((f32[8,16,128]{2,1,0:T(8,128)}), f32[8,16,128]{2,1,0:T(8,128)S(1)}, u32[]{:S(2)}, u32[]{:S(2)}) async-start(f32[8,16,128]{2,1,0:T(8,128)} %get-tuple-element.21), calls=%async_computation | async-start | bytes 131072 | tf_op jit(solution)/shard_map/all_to_all | solution.py:450
  10.3 0.0 collective-permute-done.came_ref
  10.4 2.1 %collective-permute-start.1 = (bf16[96,512]{1,0:T(8,128)(2,1)S(1)}, bf16[96,512]{1,0:T(8,128)(2,1)S(1)}, u32[]{:S(2)}, u32[]{:S(2)}) collective-permute-start(bf16[96,512]{1,0:T(8,128)(2,1)S(1)} %shard_map.168.early_ref.held_ref), channel_id=1, source_target_pairs={{0,1},{1,0},{2,3},{3,2},{4,5},{5,4},{6,7},{7,6},{8,9},{9,8},{10,11... | collective-permute-start | bytes 294920 | tf_op jit(solution)/shard_map/ppermute | solution.py:453
  13.1 1.5 %shard_map.169 = (f32[3,8,512]{2,1,0:T(8,128)S(1)}, f32[8,64]{1,0:T(8,128)S(1)}, bf16[3,512,512]{2,1,0:T(8,128)(2,1)S(1)}, bf16[64,512]{1,0:T(8,128)(2,1)S(1)}, ...) custom-call(bf16[96,512]{1,0:T(8,128)(2,1)S(1)} %shard_map.168.early_ref.held_ref, s32[3]{0:T(128)} %refs_0_.2, ...), custom_call_target="tpu_custom_call" | custom-call | flops 1000 | bytes 1000 | tf_op jit(solution)/shard_map/pallas_call | solution.py:406
  14.6 2.6 %all-to-all-done.got_ref = f32[8,16,128]{2,1,0:T(8,128)S(1)} async-done(((f32[8,16,128]{2,1,0:T(8,128)}), f32[8,16,128]{2,1,0:T(8,128)S(1)}, u32[]{:S(2)}, u32[]{:S(2)}) %all-to-all-start) | async-done | bytes 65568 | tf_op jit(solution)/shard_map/all_to_all | solution.py:450
  17.2 1.7 %shard_map.170 = (f32[8,512]{1,0:T(8,128)S(1)}, s32[1,512]{1,0:T(1,128)S(1)}, f32[32,1,640]{2,1,0:T(1,128)}) custom-call(f32[8,16,128]{2,1,0:T(8,128)S(1)} %all-to-all-done.got_ref, bf16[64,512]{1,0:T(8,128)(2,1)S(1)} %get-tuple-element.24.coarse_v_ref, s32[1]{0:T(128)S(6)} %copy.18.refs_0_.refs_2_, ...), custom_call_target="tpu_custom_call" | custom-call | flops 1048576 | bytes 4194304 | tf_op jit(solution)/shard_map/pallas_call | solution.py:406
  19.0 0.0 collective-permute-done.1.came_ref
  19.0 0.3 collective-permute-start.2
  19.3 3.2 %all-to-all-start.1 = ((f32[32,1,640]{2,1,0:T(1,128)}), f32[32,1,640]{2,1,0:T(1,128)S(1)}, u32[]{:S(2)}, u32[]{:S(2)}) async-start(f32[32,1,640]{2,1,0:T(1,128)} %get-tuple-element.35), calls=%async_computation.1 | async-start | bytes 163840 | tf_op jit(solution)/shard_map/all_to_all | solution.py:450
  22.4 2.3 %collective-permute-done.2.came_ref.refs_1_ = bf16[192,512]{1,0:T(8,128)(2,1)S(1)} collective-permute-done((bf16[192,512]{1,0:T(8,128)(2,1)S(1)}, bf16[192,512]{1,0:T(8,128)(2,1)S(1)}, u32[]{:S(2)}, u32[]{:S(2)}) %collective-permute-start.2) | collective-permute-done | bytes 196640 | tf_op jit(solution)/shard_map/ppermute | solution.py:453
  24.7 0.9 %shard_map.172 = (bf16[48,512]{1,0:T(8,128)(2,1)S(1)}, f32[8,512]{1,0:T(8,128)S(1)}, bf16[128,512]{1,0:T(8,128)(2,1)S(1)}, bf16[128,512]{1,0:T(8,128)(2,1)S(1)}) custom-call(bf16[192,512]{1,0:T(8,128)(2,1)S(1)} %shard_map.171.held_ref.refs_0_, bf16[192,512]{1,0:T(8,128)(2,1)S(1)} %collective-permute-done.2.came_ref.refs_1_, ...), custom_call_target="tpu_custom_call" | custom-call | flops 17179869184 | bytes 67108864 | tf_op jit(solution)/shard_map/pallas_call | solution.py:406
  25.6 4.2 %all-to-all-done.1.all_ref = f32[32,1,640]{2,1,0:T(1,128)S(1)} async-done(((f32[32,1,640]{2,1,0:T(1,128)}), f32[32,1,640]{2,1,0:T(1,128)S(1)}, u32[]{:S(2)}, u32[]{:S(2)}) %all-to-all-start.1) | async-done | bytes 81952 | tf_op jit(solution)/shard_map/all_to_all | solution.py:450
  29.9 1.1 %shard_map.173 = f32[32,4,128]{2,1,0:T(4,128)S(1)} custom-call(f32[8,512]{1,0:T(8,128)S(1)} %get-tuple-element.30.state_ref, f32[8,512]{1,0:T(8,128)S(1)} %get-tuple-element.33.factor_ref, s32[1,512]{1,0:T(1,128)S(1)} %get-tuple-element.31.refs_0_.rows_ref, bf16[128,512]{1,0:T(8,128)(2,1)S(1)} %get-tuple-element.34.rows_low_ref, ...), custom_call_target="tpu_custom_call" | custom-call | flops 1000 | bytes 1000 | tf_op jit(solution)/shard_map/pallas_call | solution.py:406
  30.9 9.0 %all_to_all.15.got_ref = f32[32,4,128]{2,1,0:T(4,128)S(1)} all-to-all(f32[32,4,128]{2,1,0:T(4,128)S(1)} %shard_map.173), channel_id=1, replica_groups=mesh['leaf'=4,'blk'=8] {'leaf','blk'}, dimensions={0} | all-to-all | bytes 131072 | tf_op jit(solution)/shard_map/all_to_all | solution.py:450
  39.9 0.8 %shard_map.174 = (f32[1,512]{1,0:T(1,128)}, f32[1,512]{1,0:T(1,128)}) custom-call(f32[32,4,128]{2,1,0:T(4,128)S(1)} %all_to_all.15.got_ref, s32[1,512]{1,0:T(1,128)S(1)} %get-tuple-element.23.refs_0_.slot_ref, bf16[128,512]{1,0:T(8,128)(2,1)S(1)} %get-tuple-element.37.slot_low_ref, bf16[48,512]{1,0:T(8,128)(2,1)S(1)} %get-tuple-element.36.elem_bases_ref), custom_call_target="tpu_custom_call" | custom-call | flops 1000 | bytes 1000 | tf_op jit(solution)/shard_map/pallas_call | solution.py:406
  (2 shorter events, 0.0 us)
Async XLA Ops:
  0.6 9.7 %collective-permute-start = (bf16[64,512]{1,0:T(8,128)(2,1)}, bf16[64,512]{1,0:T(8,128)(2,1)S(1)}, u32[]{:S(2)}, u32[]{:S(2)}) collective-permute-start(bf16[64,512]{1,0:T(8,128)(2,1)} %bitcast.14), channel_id=1, source_target_pairs={{0,4},{1,5},{2,6},{3,7},{4,0},{5,1},{6,2},{7,3},{8,12},{9,13},{10,... | collective-permute-start | bytes 196616 | tf_op jit(solution)/shard_map/ppermute | solution.py:453
  6.5 10.7 %all-to-all-start = ((f32[8,16,128]{2,1,0:T(8,128)}), f32[8,16,128]{2,1,0:T(8,128)S(1)}, u32[]{:S(2)}, u32[]{:S(2)}) async-start(f32[8,16,128]{2,1,0:T(8,128)} %get-tuple-element.21), calls=%async_computation | async-start | bytes 131072 | tf_op jit(solution)/shard_map/all_to_all | solution.py:450
  10.4 8.6 %collective-permute-start.1 = (bf16[96,512]{1,0:T(8,128)(2,1)S(1)}, bf16[96,512]{1,0:T(8,128)(2,1)S(1)}, u32[]{:S(2)}, u32[]{:S(2)}) collective-permute-start(bf16[96,512]{1,0:T(8,128)(2,1)S(1)} %shard_map.168.early_ref.held_ref), channel_id=1, source_target_pairs={{0,1},{1,0},{2,3},{3,2},{4,5},{5,4},{6,7},{7,6},{8,9},{9,8},{10,11... | collective-permute-start | bytes 294920 | tf_op jit(solution)/shard_map/ppermute | solution.py:453
  19.0 5.7 %collective-permute-start.2 = (bf16[192,512]{1,0:T(8,128)(2,1)S(1)}, bf16[192,512]{1,0:T(8,128)(2,1)S(1)}, u32[]{:S(2)}, u32[]{:S(2)}) collective-permute-start(bf16[192,512]{1,0:T(8,128)(2,1)S(1)} %shard_map.171.held_ref.refs_0_), channel_id=1, source_target_pairs={{0,2},{1,3},{2,0},{3,1},{4,6},{5,7},{6,4},{7,5},{8,10},{9,11},{10,... | collective-permute-start | bytes 589832 | tf_op jit(solution)/shard_map/ppermute | solution.py:453
  19.3 10.6 %all-to-all-start.1 = ((f32[32,1,640]{2,1,0:T(1,128)}), f32[32,1,640]{2,1,0:T(1,128)S(1)}, u32[]{:S(2)}, u32[]{:S(2)}) async-start(f32[32,1,640]{2,1,0:T(1,128)} %get-tuple-element.35), calls=%async_computation.1 | async-start | bytes 163840 | tf_op jit(solution)/shard_map/all_to_all | solution.py:450
